TPU v7x, 32 devices: a whole 2x2x4 slice. The times are simulated.
32 devices in a mesh: groups: 2 (over x), gx: 16 (over z, y, core).
Axes of the slice: x: 2, y: 2, z: 4, core: 2. Of those that a mesh axis runs over, the one named last changes fastest.
Arguments:
- slab: bfloat16 [4096, 64, 256], P(('groups', 'gx')), parts along dimension 0, may hold values from -6 to 6
- factor: bfloat16 [4096, 128], P(('groups', 'gx')), parts along dimension 0, may hold values from -0.125 to 0.125
Outputs:
- gram: float32 [4096, 2048], P(('groups', 'gx')), parts along dimension 0
- core: float32 [32768, 128], P(('groups', 'gx')), parts along dimension 0
There are 2 independent parts, one for each index of `groups`. A program takes and returns all parts, laid end to end along the dimension named above; each array names one. Nothing has to cross between parts.
All inputs are finite; a program needn't handle non-finite values.
Results may differ from a plain program's by a relative error of at most 0.0003.
Values may be sent and summed in bfloat16 or wider, within the bound.
No kernel may reach another device: no remote copies, remote signals or barrier semaphores. Data moves between devices by JAX's collectives and lax.ppermute only.
A program may use at most 128 MiB of HBM per device.

v0:
```python
import jax
import jax.numpy as jnp
from jax import lax
from jax.sharding import PartitionSpec as P


def on_device(slab, factor):
    rows, species, cells = slab.shape
    flat = slab.reshape(rows, species * cells)
    total = species * cells
    blocks = lax.all_to_all(flat, "gx", split_axis=1, concat_axis=0, tiled=True)
    part = blocks
    gram = lax.psum_scatter(
        lax.dot_general(part, blocks, (((1,), (1,)), ((), ())), preferred_element_type=jnp.float32),
        "gx",
        scatter_dimension=0,
        tiled=True,
    ) / jnp.float32(total)
    part = flat
    core = lax.psum_scatter(
        lax.dot_general(part, factor, (((0,), (0,)), ((), ())), preferred_element_type=jnp.float32),
        "gx",
        scatter_dimension=0,
        tiled=True,
    )
    return (gram, core)


def solution(mesh):
    return jax.shard_map(
        on_device,
        mesh=mesh,
        in_specs=(P(("groups", "gx"), None, None), P(("groups", "gx"), None)),
        out_specs=(P(("groups", "gx"), None), P(("groups", "gx"), None)),
        check_vma=False,
    )
```

profile of v0, /device:TPU:0, one launch (start us, length us, event | category | flops | bytes accessed | tf_op | source)
XLA Modules:
  0.0 430.5 jit_solution(12377917081765247950)
XLA Ops:
  7.2 0.0 copy-start
  7.2 0.0 reduce-scatter.3.cloned.1.call-start
  7.2 6.9 %copy.4 = bf16[128,64,256]{0,2,1:T(8,128)(2,1)} copy(bf16[128,64,256]{2,1,0:T(8,128)(2,1)} %param.2) | data formatting | bytes 8388608 | tf_op args[0]
  14.1 99.7 %all_to_all.19 = bf16[128,16,1024]{0,2,1:T(8,128)(2,1)} all-to-all(bf16[128,16,1024]{0,2,1:T(8,128)(2,1)} %bitcast.12), channel_id=1, replica_groups=mesh['groups'=2,'gx'=16] {'gx'}, dimensions={1} | all-to-all | bytes 8388608 | tf_op jit(solution)/shard_map/all_to_all | solution.py:11
  113.9 6.4 %copy.5 = bf16[16,128,1024]{2,1,0:T(8,128)(2,1)} copy(bf16[16,128,1024]{1,2,0:T(8,128)(2,1)} %bitcast.11) | data formatting | bytes 8388608 | tf_op jit(solution)/shard_map/all_to_all | solution.py:11
  120.3 15.7 %fusion = f32[2048,2048]{1,0:T(8,128)} fusion(bf16[2048,1024]{1,0:T(8,128)(2,1)} %bitcast.13), kind=kOutput, calls=%fused_computation.1 | convolution fusion | flops 8589934592 | bytes 20971520 | tf_op jit(solution)/shard_map/dot_general | solution.py:14
  136.0 0.0 reduce-scatter.3.cloned.1.call-update
  136.0 0.0 reduce-scatter.5.cloned.1.call-start
  136.0 5.1 %copy.6 = bf16[16,8,64,256]{3,1,2,0:T(8,128)(2,1)S(1)} copy(bf16[16,8,64,256]{3,2,1,0:T(8,128)(2,1)} %bitcast.10) | data formatting | bytes 8388608
  141.1 0.0 copy-done
  141.1 5.3 %fusion.1 = f32[16384,128]{1,0:T(8,128)} fusion(bf16[128,16384]{1,0:T(8,128)(2,1)S(1)} %bitcast.9, bf16[128,128]{1,0:T(8,128)(2,1)S(1)} %copy-done), kind=kOutput, calls=%fused_computation.2 | convolution fusion | flops 536870912 | bytes 12615680 | tf_op jit(solution)/shard_map/dot_general | solution.py:21
  146.4 0.0 reduce-scatter.5.cloned.1.call-update
  146.4 169.0 %reduce-scatter.3.cloned.1.call-done = f32[128,2048]{1,0:T(8,128)} async-done(((f32[2048,2048]{1,0:T(8,128)}), f32[128,2048]{1,0:T(8,128)}) %reduce-scatter.3.cloned.1.call-update) | async-done | bytes 1048592 | tf_op jit(solution)/shard_map/reduce_scatter | solution.py:13
  315.4 2.3 broadcast_multiply_fusion
  317.7 106.0 %reduce-scatter.5.cloned.1.call-done = f32[1024,128]{1,0:T(8,128)} async-done(((f32[16384,128]{1,0:T(8,128)}), f32[1024,128]{1,0:T(8,128)}) %reduce-scatter.5.cloned.1.call-update) | async-done | bytes 524304 | tf_op jit(solution)/shard_map/reduce_scatter | solution.py:20
Async XLA Ops:
  7.2 133.9 %copy-start = (bf16[128,128]{1,0:T(8,128)(2,1)S(1)}, bf16[128,128]{1,0:T(8,128)(2,1)}, u32[]{:S(2)}) copy-start(bf16[128,128]{1,0:T(8,128)(2,1)} %param.3) | copy-start | bytes 98308
  7.2 308.2 %reduce-scatter.3.cloned.1.call-start = ((), (), s32[]{:S(2)}) async-start(), calls=%async_computation.3 | async-start | bytes 17825792 | tf_op jit(solution)/shard_map/reduce_scatter | solution.py:13
  136.0 287.6 %reduce-scatter.5.cloned.1.call-start = ((), (), s32[]{:S(2)}) async-start(), calls=%async_computation.4 | async-start | bytes 8912896 | tf_op jit(solution)/shard_map/reduce_scatter | solution.py:20
Sparse Core Ops, SparseCore 0:
  136.1 179.2 reduce-scatter.2
  320.0 103.5 reduce-scatter.4
where the time goes:
time: 431 us; the launch traced here: 430 us
  waiting for transfers between devices  275 us (64%)
  blocking collectives  99.7 us (23%)
  matrix products  21 us (5%)
  local copies, waits for them, and re-layouts  18.4 us (4%)
  between operations  14.1 us (3%)
    reduce_scatter x1, waiting for transfers between devices, on_device(): lax.psum_scatter(lax.dot_general(part, blocks, (((1,), (1,)), ((), ())),...  169 us
    reduce_scatter x1, waiting for transfers between devices, on_device(): lax.psum_scatter(lax.dot_general(part, factor, (((0,), (0,)), ((), ())),...  106 us
    all_to_all x1, blocking collectives, on_device(): blocks = lax.all_to_all(flat, 'gx', split_axis=1, concat_axis=0, tiled=True)  99.7 us
    dot_general x1, matrix products, on_device(): lax.dot_general(part, blocks, (((1,), (1,)), ((), ())), preferred_element...  15.7 us
    unnamed x4, local copies, waits for them, and re-layouts  12 us
  transfers between devices with their start and end apart: 2, of which 2 were waited for; matrix products, arithmetic and copies ran while one was open for 3% of the time, Pallas kernels for 0%

commit v1 on v0

v1 whole, which is shorter than its diff:
```python
import jax
import jax.numpy as jnp
import numpy as np
from jax import lax
from jax.sharding import Mesh
from jax.sharding import PartitionSpec as P

AXES = ("groups", "z", "y", "c")
CHUNKS = 4


def nt_dot(a, b):
    return lax.dot_general(a, b, (((1,), (1,)), ((), ())), preferred_element_type=jnp.float32)


def on_device(planes, slab, factor):
    rows, species, cells = slab.shape
    total = species * cells
    z, y, c = (lax.axis_index(name) for name in ("z", "y", "c"))
    width = total // (planes * CHUNKS)
    full_factor = lax.all_gather(factor, ("z", "y", "c"), axis=0, tiled=True)
    sent = [slab.reshape(rows, planes, CHUNKS, width)[:, :, j].transpose(1, 0, 2) for j in range(CHUNKS)]
    swap = [(0, 1), (1, 0)]
    sums = [jnp.float32(0)] * 4
    core = jnp.zeros((width, factor.shape[1]), jnp.float32)
    for j in range(CHUNKS):
        stack = sent[j]
        for shift in range(1, planes):
            piece = lax.dynamic_index_in_dim(sent[j], (z + shift) % planes, 0, keepdims=True)
            came = lax.ppermute(piece, "z", [(i, (i + shift) % planes) for i in range(planes)])
            stack = lax.dynamic_update_slice(stack, came, ((z - shift) % planes, 0, 0))
        across = lax.ppermute(stack, "y", swap)
        blocks = [stack, lax.ppermute(stack, "c", swap), across, lax.ppermute(across, "c", swap)]
        flat = [b.reshape(planes * rows, width) for b in blocks]
        for k in range(4):
            sums[k] = sums[k] + nt_dot(flat[0], flat[k])
        mine = y * 2 + c == j
        factors = full_factor.reshape(planes, 2, 2, rows, -1)
        part = jnp.float32(0)
        for k in range(4):
            f = lax.dynamic_index_in_dim(factors, y ^ (k // 2), 1, keepdims=False)
            f = lax.dynamic_index_in_dim(f, c ^ (k % 2), 1, keepdims=False)
            part = part + lax.dot_general(
                flat[k], f.reshape(planes * rows, -1), (((0,), (0,)), ((), ())), preferred_element_type=jnp.float32
            )
        core = jnp.where(mine, part, core)
    gram = jnp.concatenate(sums, axis=1)
    gram = lax.psum_scatter(gram, "z", scatter_dimension=0, tiled=True)
    gram = gram.reshape(rows, 2, 2, planes, rows)
    gram = jnp.where(y == 1, gram[:, ::-1], gram)
    gram = jnp.where(c == 1, gram[:, :, ::-1], gram)
    gram = gram.transpose(0, 3, 1, 2, 4).reshape(rows, -1) / jnp.float32(total)
    return (gram, core)


def solution(mesh):
    groups, n = mesh.devices.shape
    planes = n // 4
    fine = Mesh(np.reshape(mesh.devices, (groups, planes, 2, 2)), AXES)
    spec = P(AXES)
    return jax.shard_map(
        lambda slab, factor: on_device(planes, slab, factor),
        mesh=fine,
        in_specs=(spec, spec),
        out_specs=(spec, spec),
        check_vma=False,
    )
```

time: 431 us -> 298 us (0.69)
  waiting for transfers between devices: 275 us -> 138 us
  blocking collectives: 99.7 us -> 24 us
  starting transfers between devices: 0.08 us -> 39.4 us
  local copies, waits for them, and re-layouts: 18.4 us -> 52 us
    reduce_scatter x2 -> x1, waiting for transfers between devices: 275 us -> 43.9 us  [on_device(): gram = lax.psum_scatter(gram, 'z', scatter_dimension=0, tiled=True)]
    all_to_all x1 -> x0, blocking collectives: 99.7 us -> none  [on_device(): blocks = lax.all_to_all(flat, 'gx', split_axis=1, concat_axis=0, tiled=True)]
    ppermute x0 -> x24, waiting for transfers between devices: none -> 94.1 us  [the longest x4 66 us: on_device(): across = lax.ppermute(stack, 'y', swap)]
    ppermute x0 -> x24, starting transfers between devices: none -> 39.4 us  [the longest x12 32.3 us: on_device(): lax.ppermute(piece, 'z', [(i, (i + shift) % planes) for i in range(planes)])]
    all_gather x0 -> x1, blocking collectives: none -> 24 us  [on_device(): full_factor = lax.all_gather(factor, ('z', 'y', 'c'), axis=0, tiled=True)]
    another operation x0 -> x14, local copies, waits for them, and re-layouts: none -> 23.6 us
    slice x0 -> x5, local copies, waits for them, and re-layouts: none -> 9.07 us  [on_device(): slab.reshape(rows, planes, CHUNKS, width)[:, :, j].transpose(1, 0, 2)]
    dynamic_update_slice x0 -> x12, local copies, waits for them, and re-layouts: none -> 7.07 us  [on_device(): stack = lax.dynamic_update_slice(stack, came, ((z - shift) % planes, 0, 0))]
  transfers between devices with their start and end apart: 2 -> 25, of which waited for: 2 -> 7; matrix products, arithmetic and copies ran while one was open for 3% -> 19% of each run, Pallas kernels for 0% -> 0%
where the time goes in v1:
time: 298 us; the launch traced here: 297 us
  waiting for transfers between devices  138 us (46%)
  local copies, waits for them, and re-layouts  52 us (17%)
  starting transfers between devices  39.4 us (13%)
  matrix products  24.4 us (8%)
  blocking collectives  24 us (8%)
  between operations  14.8 us (5%)
  other arithmetic  4.18 us (1%)
    ppermute x4, waiting for transfers between devices, on_device(): across = lax.ppermute(stack, 'y', swap)  66 us
    reduce_scatter x1, waiting for transfers between devices, on_device(): gram = lax.psum_scatter(gram, 'z', scatter_dimension=0, tiled=True)  43.9 us
    ppermute x12, starting transfers between devices, on_device(): lax.ppermute(piece, 'z', [(i, (i + shift) % planes) for i in range(planes)])  32.3 us
    ppermute x12, waiting for transfers between devices, on_device(): lax.ppermute(piece, 'z', [(i, (i + shift) % planes) for i in range(planes)])  28.1 us
    all_gather x1, blocking collectives, on_device(): full_factor = lax.all_gather(factor, ('z', 'y', 'c'), axis=0, tiled=True)  24 us
    another operation x14, local copies, waits for them, and re-layouts  23.6 us
    dot_general x16, matrix products, nt_dot(): lax.dot_general(a, b, (((1,), (1,)), ((), ())), preferred_element_type=jn...  13.4 us
    dot_general x16, matrix products, on_device(): lax.dot_general(flat[k], f.reshape(planes * rows, -1), (((0,), (0,)), (()...  10.9 us
  transfers between devices with their start and end apart: 25, of which 7 were waited for; matrix products, arithmetic and copies ran while one was open for 19% of the time, Pallas kernels for 0%

profile of v1, /device:TPU:0, one launch (start us, length us, event | category | flops | bytes accessed | tf_op | source)
XLA Modules:
  0.0 296.8 jit_solution(17924172591393791387)
XLA Ops:
  7.2 6.9 %copy.12 = bf16[128,64,256]{0,2,1:T(8,128)(2,1)} copy(bf16[128,64,256]{2,1,0:T(8,128)(2,1)} %param.2) | data formatting | bytes 8388608 | tf_op args[0]
  14.1 3.5 %fusion.18 = (bf16[128,4,1,1024]{0,3,2,1:T(8,128)(2,1)}, bf16[128,4,1,1024]{0,3,2,1:T(8,128)(2,1)S(1)}, bf16[128,4,1,1024]{0,3,2,1:T(8,128)(2,1)S(1)}, bf16[128,4,1,1024]{0,3,2,1:T(8,128)(2,1)S(1)}) fusion(bf16[128,4,4,1024]{0,3,2,1:T(8,128)(2,1)} %bitcast.119), kind=kLoop, calls=%fused_computation.61 | loop fusion | bytes 8388608 | tf_op jit(solution)/shard_map/slice | solution.py:22
  17.6 2.5 constant_dynamic-slice_fusion.10
  20.2 1.8 copy.14
  22.0 3.0 %collective-permute-start = (bf16[1,128,1024]{2,1,0:T(8,128)(2,1)}, bf16[1,128,1024]{2,1,0:T(8,128)(2,1)}, u32[]{:S(2)}, u32[]{:S(2)}) collective-permute-start(bf16[1,128,1024]{2,1,0:T(8,128)(2,1)} %bitcast.182), channel_id=1, source_target_pairs={{0,4},{4,8},{8,12},{12,0},{1,5},{5,9},{9,13},{13,1},{2,6},{6,10},{... | collective-permute-start | bytes 786440 | tf_op jit(solution)/shard_map/ppermute | solution.py:30
  32.8 1.8 copy.16
  34.6 2.2 collective-permute-start.2
  36.9 1.8 copy.15
  40.2 2.3 copy.17
  44.3 1.9 copy.20
  47.0 1.8 copy.28
  48.8 1.8 copy.27
  50.6 1.8 copy.22
  52.4 1.8 copy.23
  55.2 3.0 %collective-permute-start.4 = (bf16[1,128,1024]{2,1,0:T(8,128)(2,1)}, bf16[1,128,1024]{2,1,0:T(8,128)(2,1)S(1)}, u32[]{:S(2)}, u32[]{:S(2)}) collective-permute-start(bf16[1,128,1024]{2,1,0:T(8,128)(2,1)} %bitcast.190), channel_id=1, source_target_pairs={{0,8},{4,12},{8,0},{12,4},{1,9},{5,13},{9,1},{13,5},{2,10},{6,14},... | collective-permute-start | bytes 786440 | tf_op jit(solution)/shard_map/ppermute | solution.py:30
  61.0 2.1 collective-permute-start.5
  64.1 14.5 %collective-permute-done.4 = bf16[1,128,1024]{2,1,0:T(8,128)(2,1)S(1)} collective-permute-done((bf16[1,128,1024]{2,1,0:T(8,128)(2,1)}, bf16[1,128,1024]{2,1,0:T(8,128)(2,1)S(1)}, u32[]{:S(2)}, u32[]{:S(2)}) %collective-permute-start.4) | collective-permute-done | bytes 262176 | tf_op jit(solution)/shard_map/ppermute | solution.py:30
  78.6 8.3 %collective-permute-start.11 = (bf16[1,128,1024]{2,1,0:T(8,128)(2,1)}, bf16[1,128,1024]{2,1,0:T(8,128)(2,1)S(1)}, u32[]{:S(2)}, u32[]{:S(2)}) collective-permute-start(bf16[1,128,1024]{2,1,0:T(8,128)(2,1)} %bitcast.187), channel_id=1, source_target_pairs={{0,12},{4,0},{8,4},{12,8},{1,13},{5,1},{9,5},{13,9},{2,14},{6,2},{... | collective-permute-start | bytes 786440 | tf_op jit(solution)/shard_map/ppermute | solution.py:30
  87.6 7.1 %collective-permute-start.6 = (bf16[1,128,1024]{2,1,0:T(8,128)(2,1)}, bf16[1,128,1024]{2,1,0:T(8,128)(2,1)S(1)}, u32[]{:S(2)}, u32[]{:S(2)}) collective-permute-start(bf16[1,128,1024]{2,1,0:T(8,128)(2,1)} %bitcast.186), channel_id=1, source_target_pairs={{0,4},{4,8},{8,12},{12,0},{1,5},{5,9},{9,13},{13,1},{2,6},{6,10},{... | collective-permute-start | bytes 786440 | tf_op jit(solution)/shard_map/ppermute | solution.py:30
  94.7 3.3 %collective-permute-start.7 = (bf16[1,128,1024]{2,1,0:T(8,128)(2,1)}, bf16[1,128,1024]{2,1,0:T(8,128)(2,1)S(1)}, u32[]{:S(2)}, u32[]{:S(2)}) collective-permute-start(bf16[1,128,1024]{2,1,0:T(8,128)(2,1)} %bitcast.185), channel_id=1, source_target_pairs={{0,8},{4,12},{8,0},{12,4},{1,9},{5,13},{9,1},{13,5},{2,10},{6,14},... | collective-permute-start | bytes 786440 | tf_op jit(solution)/shard_map/ppermute | solution.py:30
  98.8 6.1 %collective-permute-done.6 = bf16[1,128,1024]{2,1,0:T(8,128)(2,1)S(1)} collective-permute-done((bf16[1,128,1024]{2,1,0:T(8,128)(2,1)}, bf16[1,128,1024]{2,1,0:T(8,128)(2,1)S(1)}, u32[]{:S(2)}, u32[]{:S(2)}) %collective-permute-start.6) | collective-permute-done | bytes 262176 | tf_op jit(solution)/shard_map/ppermute | solution.py:30
  106.4 7.5 %collective-permute-done.7 = bf16[1,128,1024]{2,1,0:T(8,128)(2,1)S(1)} collective-permute-done((bf16[1,128,1024]{2,1,0:T(8,128)(2,1)}, bf16[1,128,1024]{2,1,0:T(8,128)(2,1)S(1)}, u32[]{:S(2)}, u32[]{:S(2)}) %collective-permute-start.7) | collective-permute-done | bytes 262176 | tf_op jit(solution)/shard_map/ppermute | solution.py:30
  115.6 2.3 fusion.19
  124.3 6.7 %collective-permute-done.19 = bf16[4,128,1024]{2,1,0:T(8,128)(2,1)S(1)} collective-permute-done((bf16[4,128,1024]{2,1,0:T(8,128)(2,1)S(1)}, bf16[4,128,1024]{2,1,0:T(8,128)(2,1)S(1)}, u32[]{:S(2)}, u32[]{:S(2)}) %collective-permute-start.19) | collective-permute-done | bytes 1048608 | tf_op jit(solution)/shard_map/ppermute | solution.py:32
  131.7 44.2 %collective-permute-done.18 = bf16[4,128,1024]{2,1,0:T(8,128)(2,1)S(1)} collective-permute-done((bf16[4,128,1024]{2,1,0:T(8,128)(2,1)S(1)}, bf16[4,128,1024]{2,1,0:T(8,128)(2,1)S(1)}, u32[]{:S(2)}, u32[]{:S(2)}) %collective-permute-start.18) | collective-permute-done | bytes 1048608 | tf_op jit(solution)/shard_map/ppermute | solution.py:32
  178.0 15.1 %collective-permute-done.16 = bf16[4,128,1024]{2,1,0:T(8,128)(2,1)S(1)} collective-permute-done((bf16[4,128,1024]{2,1,0:T(8,128)(2,1)S(1)}, bf16[4,128,1024]{2,1,0:T(8,128)(2,1)S(1)}, u32[]{:S(2)}, u32[]{:S(2)}) %collective-permute-start.16) | collective-permute-done | bytes 1048608 | tf_op jit(solution)/shard_map/ppermute | solution.py:32
  203.3 2.4 pad_maximum_fusion
  206.4 24.0 %all_gather.3 = bf16[2048,128]{1,0:T(8,128)(2,1)S(1)} all-gather(bf16[128,128]{1,0:T(8,128)(2,1)S(1)} %copy-done.26), channel_id=1, replica_groups=mesh['groups'=2,'z'=4,'y'=2,'c'=2] {'z','y','c'}, dimensions={0}, use_global_device_ids=true | all-gather | bytes 557056 | tf_op jit(solution)/shard_map/all_gather | solution.py:21
  230.5 1.8 fusion.32
  232.3 1.8 fusion.34
  241.6 43.9 %reduce-scatter.2.cloned.1.call-done = f32[128,2048]{0,1:T(8,128)} async-done(((f32[512,2048]{0,1:T(8,128)}), f32[128,2048]{0,1:T(8,128)}) %reduce-scatter.2.cloned.1.call-update) | async-done | bytes 1048592 | tf_op jit(solution)/shard_map/reduce_scatter | solution.py:48
  288.1 1.8 div.13
  (144 shorter events, 51.3 us)
Async XLA Ops:
  7.2 278.4 %reduce-scatter.2.cloned.1.call-start = ((), (), s32[]{:S(2)}) async-start(), calls=%async_computation.1 | async-start | bytes 5242880 | tf_op jit(solution)/shard_map/reduce_scatter | solution.py:48
  22.0 33.3 %collective-permute-start = (bf16[1,128,1024]{2,1,0:T(8,128)(2,1)}, bf16[1,128,1024]{2,1,0:T(8,128)(2,1)}, u32[]{:S(2)}, u32[]{:S(2)}) collective-permute-start(bf16[1,128,1024]{2,1,0:T(8,128)(2,1)} %bitcast.182), channel_id=1, source_target_pairs={{0,4},{4,8},{8,12},{12,0},{1,5},{5,9},{9,13},{13,1},{2,6},{6,10},{... | collective-permute-start | bytes 786440 | tf_op jit(solution)/shard_map/ppermute | solution.py:30
  26.8 32.5 %collective-permute-start.3 = (bf16[1,128,1024]{2,1,0:T(8,128)(2,1)}, bf16[1,128,1024]{2,1,0:T(8,128)(2,1)}, u32[]{:S(2)}, u32[]{:S(2)}) collective-permute-start(bf16[1,128,1024]{2,1,0:T(8,128)(2,1)} %bitcast.181), channel_id=1, source_target_pairs={{0,4},{4,8},{8,12},{12,0},{1,5},{5,9},{9,13},{13,1},{2,6},{6,10},{... | collective-permute-start | bytes 786440 | tf_op jit(solution)/shard_map/ppermute | solution.py:30
  31.2 29.7 %collective-permute-start.9 = (bf16[1,128,1024]{2,1,0:T(8,128)(2,1)}, bf16[1,128,1024]{2,1,0:T(8,128)(2,1)}, u32[]{:S(2)}, u32[]{:S(2)}) collective-permute-start(bf16[1,128,1024]{2,1,0:T(8,128)(2,1)} %bitcast.183), channel_id=1, source_target_pairs={{0,4},{4,8},{8,12},{12,0},{1,5},{5,9},{9,13},{13,1},{2,6},{6,10},{... | collective-permute-start | bytes 786440 | tf_op jit(solution)/shard_map/ppermute | solution.py:30
  34.6 86.3 %collective-permute-start.2 = (bf16[1,128,1024]{2,1,0:T(8,128)(2,1)}, bf16[1,128,1024]{2,1,0:T(8,128)(2,1)}, u32[]{:S(2)}, u32[]{:S(2)}) collective-permute-start(bf16[1,128,1024]{2,1,0:T(8,128)(2,1)} %bitcast.180), channel_id=1, source_target_pairs={{0,12},{4,0},{8,4},{12,8},{1,13},{5,1},{9,5},{13,9},{2,14},{6,2},{... | collective-permute-start | bytes 786440 | tf_op jit(solution)/shard_map/ppermute | solution.py:30
  38.7 79.2 %collective-permute-start.1 = (bf16[1,128,1024]{2,1,0:T(8,128)(2,1)}, bf16[1,128,1024]{2,1,0:T(8,128)(2,1)}, u32[]{:S(2)}, u32[]{:S(2)}) collective-permute-start(bf16[1,128,1024]{2,1,0:T(8,128)(2,1)} %bitcast.4), channel_id=1, source_target_pairs={{0,8},{4,12},{8,0},{12,4},{1,9},{5,13},{9,1},{13,5},{2,10},{6,14},... | collective-permute-start | bytes 786440 | tf_op jit(solution)/shard_map/ppermute | solution.py:30
  44.3 18.8 %copy-start.1 = (bf16[128,4,1,1024]{3,0,2,1:T(8,128)(2,1)S(1)}, bf16[128,4,1,1024]{3,0,2,1:T(8,128)(2,1)}, u32[]{:S(2)}) copy-start(bf16[128,4,1,1024]{3,0,2,1:T(8,128)(2,1)} %copy.25) | copy-start | bytes 3145732
  55.2 23.3 %collective-permute-start.4 = (bf16[1,128,1024]{2,1,0:T(8,128)(2,1)}, bf16[1,128,1024]{2,1,0:T(8,128)(2,1)S(1)}, u32[]{:S(2)}, u32[]{:S(2)}) collective-permute-start(bf16[1,128,1024]{2,1,0:T(8,128)(2,1)} %bitcast.190), channel_id=1, source_target_pairs={{0,8},{4,12},{8,0},{12,4},{1,9},{5,13},{9,1},{13,5},{2,10},{6,14},... | collective-permute-start | bytes 786440 | tf_op jit(solution)/shard_map/ppermute | solution.py:30
  59.2 28.4 %collective-permute-start.10 = (bf16[1,128,1024]{2,1,0:T(8,128)(2,1)}, bf16[1,128,1024]{2,1,0:T(8,128)(2,1)S(1)}, u32[]{:S(2)}, u32[]{:S(2)}) collective-permute-start(bf16[1,128,1024]{2,1,0:T(8,128)(2,1)} %bitcast.189), channel_id=1, source_target_pairs={{0,8},{4,12},{8,0},{12,4},{1,9},{5,13},{9,1},{13,5},{2,10},{6,14},... | collective-permute-start | bytes 786440 | tf_op jit(solution)/shard_map/ppermute | solution.py:30
  61.0 33.7 %collective-permute-start.5 = (bf16[1,128,1024]{2,1,0:T(8,128)(2,1)}, bf16[1,128,1024]{2,1,0:T(8,128)(2,1)S(1)}, u32[]{:S(2)}, u32[]{:S(2)}) collective-permute-start(bf16[1,128,1024]{2,1,0:T(8,128)(2,1)} %bitcast.188), channel_id=1, source_target_pairs={{0,12},{4,0},{8,4},{12,8},{1,13},{5,1},{9,5},{13,9},{2,14},{6,2},{... | collective-permute-start | bytes 786440 | tf_op jit(solution)/shard_map/ppermute | solution.py:30
  78.6 20.2 %collective-permute-start.11 = (bf16[1,128,1024]{2,1,0:T(8,128)(2,1)}, bf16[1,128,1024]{2,1,0:T(8,128)(2,1)S(1)}, u32[]{:S(2)}, u32[]{:S(2)}) collective-permute-start(bf16[1,128,1024]{2,1,0:T(8,128)(2,1)} %bitcast.187), channel_id=1, source_target_pairs={{0,12},{4,0},{8,4},{12,8},{1,13},{5,1},{9,5},{13,9},{2,14},{6,2},{... | collective-permute-start | bytes 786440 | tf_op jit(solution)/shard_map/ppermute | solution.py:30
  87.6 17.3 %collective-permute-start.6 = (bf16[1,128,1024]{2,1,0:T(8,128)(2,1)}, bf16[1,128,1024]{2,1,0:T(8,128)(2,1)S(1)}, u32[]{:S(2)}, u32[]{:S(2)}) collective-permute-start(bf16[1,128,1024]{2,1,0:T(8,128)(2,1)} %bitcast.186), channel_id=1, source_target_pairs={{0,4},{4,8},{8,12},{12,0},{1,5},{5,9},{9,13},{13,1},{2,6},{6,10},{... | collective-permute-start | bytes 786440 | tf_op jit(solution)/shard_map/ppermute | solution.py:30
  94.7 19.2 %collective-permute-start.7 = (bf16[1,128,1024]{2,1,0:T(8,128)(2,1)}, bf16[1,128,1024]{2,1,0:T(8,128)(2,1)S(1)}, u32[]{:S(2)}, u32[]{:S(2)}) collective-permute-start(bf16[1,128,1024]{2,1,0:T(8,128)(2,1)} %bitcast.185), channel_id=1, source_target_pairs={{0,8},{4,12},{8,0},{12,4},{1,9},{5,13},{9,1},{13,5},{2,10},{6,14},... | collective-permute-start | bytes 786440 | tf_op jit(solution)/shard_map/ppermute | solution.py:30
  98.7 15.2 %collective-permute-start.8 = (bf16[1,128,1024]{2,1,0:T(8,128)(2,1)S(1)}, bf16[1,128,1024]{2,1,0:T(8,128)(2,1)S(1)}, u32[]{:S(2)}, u32[]{:S(2)}) collective-permute-start(bf16[1,128,1024]{2,1,0:T(8,128)(2,1)S(1)} %bitcast.184), channel_id=1, source_target_pairs={{0,12},{4,0},{8,4},{12,8},{1,13},{5,1},{9,5},{13,9},{2,14},{6,2},{... | collective-permute-start | bytes 786440 | tf_op jit(solution)/shard_map/ppermute | solution.py:30
  104.9 26.1 %collective-permute-start.19 = (bf16[4,128,1024]{2,1,0:T(8,128)(2,1)S(1)}, bf16[4,128,1024]{2,1,0:T(8,128)(2,1)S(1)}, u32[]{:S(2)}, u32[]{:S(2)}) collective-permute-start(bf16[4,128,1024]{2,1,0:T(8,128)(2,1)S(1)} %constant_dynamic-update-slice_fusion), channel_id=1, source_target_pairs={{0,2},{2,0},{1,3},{3,1},{4,6},{6,4},{5,7},{7,5},{8,10},{10,8},{9,1... | collective-permute-start | bytes 3145736 | tf_op jit(solution)/shard_map/ppermute | solution.py:32
  113.9 80.0 %collective-permute-start.15 = (bf16[4,128,1024]{2,1,0:T(8,128)(2,1)S(1)}, bf16[4,128,1024]{2,1,0:T(8,128)(2,1)S(1)}, u32[]{:S(2)}, u32[]{:S(2)}) collective-permute-start(bf16[4,128,1024]{2,1,0:T(8,128)(2,1)S(1)} %constant_dynamic-update-slice_fusion), channel_id=1, source_target_pairs={{0,1},{1,0},{2,3},{3,2},{4,5},{5,4},{6,7},{7,6},{8,9},{9,8},{10,11... | collective-permute-start | bytes 3145736 | tf_op jit(solution)/shard_map/ppermute | solution.py:33
  114.0 62.7 %collective-permute-start.17 = (bf16[4,128,1024]{2,1,0:T(8,128)(2,1)}, bf16[4,128,1024]{2,1,0:T(8,128)(2,1)S(1)}, u32[]{:S(2)}, u32[]{:S(2)}) collective-permute-start(bf16[4,128,1024]{2,1,0:T(8,128)(2,1)} %constant_dynamic-update-slice_fusion.6), channel_id=1, source_target_pairs={{0,2},{2,0},{1,3},{3,1},{4,6},{6,4},{5,7},{7,5},{8,10},{10,8},{9,1... | collective-permute-start | bytes 3145736 | tf_op jit(solution)/shard_map/ppermute | solution.py:32
  117.9 58.0 %collective-permute-start.18 = (bf16[4,128,1024]{2,1,0:T(8,128)(2,1)S(1)}, bf16[4,128,1024]{2,1,0:T(8,128)(2,1)S(1)}, u32[]{:S(2)}, u32[]{:S(2)}) collective-permute-start(bf16[4,128,1024]{2,1,0:T(8,128)(2,1)S(1)} %constant_dynamic-update-slice_fusion.3), channel_id=1, source_target_pairs={{0,2},{2,0},{1,3},{3,1},{4,6},{6,4},{5,7},{7,5},{8,10},{10,8},{9,1... | collective-permute-start | bytes 3145736 | tf_op jit(solution)/shard_map/ppermute | solution.py:32
  121.9 71.1 %collective-permute-start.16 = (bf16[4,128,1024]{2,1,0:T(8,128)(2,1)S(1)}, bf16[4,128,1024]{2,1,0:T(8,128)(2,1)S(1)}, u32[]{:S(2)}, u32[]{:S(2)}) collective-permute-start(bf16[4,128,1024]{2,1,0:T(8,128)(2,1)S(1)} %constant_dynamic-update-slice_fusion.9), channel_id=1, source_target_pairs={{0,2},{2,0},{1,3},{3,1},{4,6},{6,4},{5,7},{7,5},{8,10},{10,8},{9,1... | collective-permute-start | bytes 3145736 | tf_op jit(solution)/shard_map/ppermute | solution.py:32
  123.5 52.4 %copy-start.2 = (bf16[4,128,1024]{2,1,0:T(8,128)(2,1)S(1)}, bf16[4,128,1024]{2,1,0:T(8,128)(2,1)}, u32[]{:S(2)}) copy-start(bf16[4,128,1024]{2,1,0:T(8,128)(2,1)} %constant_dynamic-update-slice_fusion.6) | copy-start | bytes 3145732
  130.9 62.9 %copy-start.16 = (bf16[4,128,1024]{2,1,0:T(8,128)(2,1)}, bf16[4,128,1024]{2,1,0:T(8,128)(2,1)S(1)}, u32[]{:S(2)}) copy-start(bf16[4,128,1024]{2,1,0:T(8,128)(2,1)S(1)} %collective-permute-done.19) | copy-start | bytes 3145732
  130.9 64.3 %collective-permute-start.14 = (bf16[4,128,1024]{2,1,0:T(8,128)(2,1)S(1)}, bf16[4,128,1024]{2,1,0:T(8,128)(2,1)S(1)}, u32[]{:S(2)}, u32[]{:S(2)}) collective-permute-start(bf16[4,128,1024]{2,1,0:T(8,128)(2,1)S(1)} %constant_dynamic-update-slice_fusion.3), channel_id=1, source_target_pairs={{0,1},{1,0},{2,3},{3,2},{4,5},{5,4},{6,7},{7,6},{8,9},{9,8},{10,11... | collective-permute-start | bytes 3145736 | tf_op jit(solution)/shard_map/ppermute | solution.py:33
  175.9 21.2 %collective-permute-start.13 = (bf16[4,128,1024]{2,1,0:T(8,128)(2,1)S(1)}, bf16[4,128,1024]{2,1,0:T(8,128)(2,1)S(1)}, u32[]{:S(2)}, u32[]{:S(2)}) collective-permute-start(bf16[4,128,1024]{2,1,0:T(8,128)(2,1)S(1)} %copy-done.2), channel_id=1, source_target_pairs={{0,1},{1,0},{2,3},{3,2},{4,5},{5,4},{6,7},{7,6},{8,9},{9,8},{10,11... | collective-permute-start | bytes 3145736 | tf_op jit(solution)/shard_map/ppermute | solution.py:33
  176.7 20.3 %copy-start.19 = (bf16[4,128,1024]{2,1,0:T(8,128)(2,1)}, bf16[4,128,1024]{2,1,0:T(8,128)(2,1)S(1)}, u32[]{:S(2)}) copy-start(bf16[4,128,1024]{2,1,0:T(8,128)(2,1)S(1)} %collective-permute-done.17) | copy-start | bytes 3145732
  176.7 21.7 %collective-permute-start.12 = (bf16[4,128,1024]{2,1,0:T(8,128)(2,1)S(1)}, bf16[4,128,1024]{2,1,0:T(8,128)(2,1)S(1)}, u32[]{:S(2)}, u32[]{:S(2)}) collective-permute-start(bf16[4,128,1024]{2,1,0:T(8,128)(2,1)S(1)} %constant_dynamic-update-slice_fusion.9), channel_id=1, source_target_pairs={{0,1},{1,0},{2,3},{3,2},{4,5},{5,4},{6,7},{7,6},{8,9},{9,8},{10,11... | collective-permute-start | bytes 3145736 | tf_op jit(solution)/shard_map/ppermute | solution.py:33
  193.8 5.3 %collective-permute-start.23 = (bf16[4,128,1024]{2,1,0:T(8,128)(2,1)S(1)}, bf16[4,128,1024]{2,1,0:T(8,128)(2,1)S(1)}, u32[]{:S(2)}, u32[]{:S(2)}) collective-permute-start(bf16[4,128,1024]{2,1,0:T(8,128)(2,1)S(1)} %collective-permute-done.19), channel_id=1, source_target_pairs={{0,1},{1,0},{2,3},{3,2},{4,5},{5,4},{6,7},{7,6},{8,9},{9,8},{10,11... | collective-permute-start | bytes 3145736 | tf_op jit(solution)/shard_map/ppermute | solution.py:33
  194.7 5.3 %collective-permute-start.22 = (bf16[4,128,1024]{2,1,0:T(8,128)(2,1)S(1)}, bf16[4,128,1024]{2,1,0:T(8,128)(2,1)S(1)}, u32[]{:S(2)}, u32[]{:S(2)}) collective-permute-start(bf16[4,128,1024]{2,1,0:T(8,128)(2,1)S(1)} %collective-permute-done.18), channel_id=1, source_target_pairs={{0,1},{1,0},{2,3},{3,2},{4,5},{5,4},{6,7},{7,6},{8,9},{9,8},{10,11... | collective-permute-start | bytes 3145736 | tf_op jit(solution)/shard_map/ppermute | solution.py:33
  197.0 3.7 %collective-permute-start.21 = (bf16[4,128,1024]{2,1,0:T(8,128)(2,1)S(1)}, bf16[4,128,1024]{2,1,0:T(8,128)(2,1)S(1)}, u32[]{:S(2)}, u32[]{:S(2)}) collective-permute-start(bf16[4,128,1024]{2,1,0:T(8,128)(2,1)S(1)} %collective-permute-done.17), channel_id=1, source_target_pairs={{0,1},{1,0},{2,3},{3,2},{4,5},{5,4},{6,7},{7,6},{8,9},{9,8},{10,11... | collective-permute-start | bytes 3145736 | tf_op jit(solution)/shard_map/ppermute | solution.py:33
  197.9 3.6 %collective-permute-start.20 = (bf16[4,128,1024]{2,1,0:T(8,128)(2,1)S(1)}, bf16[4,128,1024]{2,1,0:T(8,128)(2,1)S(1)}, u32[]{:S(2)}, u32[]{:S(2)}) collective-permute-start(bf16[4,128,1024]{2,1,0:T(8,128)(2,1)S(1)} %collective-permute-done.16), channel_id=1, source_target_pairs={{0,1},{1,0},{2,3},{3,2},{4,5},{5,4},{6,7},{7,6},{8,9},{9,8},{10,11... | collective-permute-start | bytes 3145736 | tf_op jit(solution)/shard_map/ppermute | solution.py:33
  206.4 27.6 %copy-start.18 = (bf16[4,128,1024]{2,1,0:T(8,128)(2,1)S(1)}, bf16[4,128,1024]{2,1,0:T(8,128)(2,1)}, u32[]{:S(2)}) copy-start(bf16[4,128,1024]{2,1,0:T(8,128)(2,1)} %copy-done.17) | copy-start | bytes 3145732
  206.4 28.1 %copy-start.23 = (bf16[4,128,1024]{2,1,0:T(8,128)(2,1)S(1)}, bf16[4,128,1024]{2,1,0:T(8,128)(2,1)}, u32[]{:S(2)}) copy-start(bf16[4,128,1024]{2,1,0:T(8,128)(2,1)} %copy-done.22) | copy-start | bytes 3145732
  206.4 28.6 %copy-start.20 = (bf16[4,128,1024]{2,1,0:T(8,128)(2,1)S(1)}, bf16[4,128,1024]{2,1,0:T(8,128)(2,1)}, u32[]{:S(2)}) copy-start(bf16[4,128,1024]{2,1,0:T(8,128)(2,1)} %copy-done.19) | copy-start | bytes 3145732
  (20 other events, 74.0 us)
Sparse Core Ops, SparseCore 0:
  205.8 79.6 reduce-scatter.1

commit v2 on v1

v2 whole, which is shorter than its diff:
```python
import functools

import jax
import jax.numpy as jnp
import numpy as np
from jax import lax
from jax.experimental import pallas as pl
from jax.experimental.pallas import tpu as pltpu
from jax.sharding import Mesh
from jax.sharding import PartitionSpec as P

AXES = ("groups", "z", "y", "c")
BLOCK = 16
LANES = 128


def nt_dot(a, b):
    return lax.dot_general(a, b, (((1,), (1,)), ((), ())), preferred_element_type=jnp.float32)


def tn_dot(a, b):
    return lax.dot_general(a, b, (((0,), (0,)), ((), ())), preferred_element_type=jnp.float32)


def unfold_kernel(planes, per_plane, group, start, extra, z_ref, *refs):
    ins, outs, wide = refs[:planes], refs[planes + extra : -1], refs[-1]
    rows = ins[0].shape[0]
    for shift in range(planes):
        first = lax.rem(lax.rem(z_ref[0] + shift, planes) * per_plane + start, BLOCK)
        wide[...] = ins[shift][...].astype(jnp.float32).reshape(rows * BLOCK, LANES)
        for s in range(group):
            taken = wide[pl.ds(first + s, rows, stride=BLOCK), :]
            outs[shift][:, s * LANES : (s + 1) * LANES] = taken.astype(jnp.bfloat16)
        if extra:
            outs[shift][:, group * LANES :] = refs[planes][...]


def unfold(slab, factor, z, planes, group, start, lane_block):
    rows, species, cells = slab.shape
    per_plane = species // planes
    step = min(rows, 32)
    rank = factor.shape[1] if factor is not None else 0
    width = group * LANES + rank
    in_specs = [
        pl.BlockSpec(
            (step, BLOCK, LANES),
            lambda i, z_ref, shift=shift: (
                i, lax.div(lax.rem(z_ref[0] + shift, planes) * per_plane + start, BLOCK), lane_block
            ),
        )
        for shift in range(planes)
    ]
    operands = [slab] * planes
    if rank:
        in_specs.append(pl.BlockSpec((step, rank), lambda i, z_ref: (i, 0)))
        operands.append(factor)
    return pl.pallas_call(
        functools.partial(unfold_kernel, planes, per_plane, group, start, 1 if rank else 0),
        out_shape=[jax.ShapeDtypeStruct((rows, width), slab.dtype)] * planes,
        grid_spec=pltpu.PrefetchScalarGridSpec(
            num_scalar_prefetch=1,
            grid=(rows // step,),
            in_specs=in_specs,
            out_specs=[pl.BlockSpec((step, width), lambda i, z_ref: (i, 0))] * planes,
            scratch_shapes=[pltpu.VMEM((step * BLOCK, LANES), jnp.float32)],
        ),
        compiler_params=pltpu.CompilerParams(vmem_limit_bytes=16 * 2**20),
        cost_estimate=pl.CostEstimate(
            flops=0, bytes_accessed=planes * rows * (BLOCK * LANES + width) * 2, transcendentals=0
        ),
        name="unfold",
    )(z.reshape(1).astype(jnp.int32), *operands)


def on_device(planes, slab, factor):
    rows, species, cells = slab.shape
    rank = factor.shape[1]
    total = species * cells
    z, y, c = (lax.axis_index(name) for name in ("z", "y", "c"))
    per_plane = species // planes
    group = min(per_plane, 8)
    halves = cells // LANES
    chunks = [(o, h) for o in range(per_plane // group) for h in range(halves)]
    swap = [(0, 1), (1, 0)]
    sums = [jnp.float32(0)] * 4
    held, earlier = [], None
    width = group * LANES
    factors = None
    for j, (o, h) in enumerate(chunks):
        pieces = unfold(slab, factor if j == 1 else None, z, planes, group, o * group, h)
        came = []
        for shift in range(1, planes):
            piece = pieces[shift]
            if j:
                piece, _ = lax.optimization_barrier((piece, earlier[shift - 1]))
            came.append(lax.ppermute(piece, "z", [(i, (i + shift) % planes) for i in range(planes)]))
        earlier = came
        stack = jnp.zeros((planes,) + pieces[0].shape, slab.dtype)
        for shift in range(planes):
            piece = came[shift - 1] if shift else pieces[0]
            stack = lax.dynamic_update_slice(stack, piece[None], ((z - shift) % planes, 0, 0))
        across = lax.ppermute(stack, "y", swap)
        blocks = [stack, lax.ppermute(stack, "c", swap), across, lax.ppermute(across, "c", swap)]
        flat = [b.reshape(planes * rows, -1) for b in blocks]
        if j == 1:
            factors = [b[:, width:] for b in flat]
            flat = [b[:, :width] for b in flat]
        for k in range(4):
            sums[k] = sums[k] + nt_dot(flat[0], flat[k])
        held.append(flat)
    own = per_plane // 4
    at = (y * 2 + c) * own
    parts = []
    for h in range(halves):
        part = jnp.float32(0)
        for k in range(4):
            taken = None
            for j, (o, half) in enumerate(chunks):
                if half == h:
                    piece = lax.dynamic_slice_in_dim(held[j][k], (at % group) * LANES, own * LANES, 1)
                    taken = piece if taken is None else jnp.where(at // group == o, piece, taken)
            part = part + tn_dot(taken, factors[k])
        parts.append(part.reshape(own, 1, LANES, rank))
    core = jnp.concatenate(parts, axis=1).reshape(own * cells, rank)
    gram = jnp.concatenate(sums, axis=1)
    gram = lax.psum_scatter(gram, "z", scatter_dimension=0, tiled=True)
    gram = gram.reshape(rows, 2, 2, planes, rows)
    gram = jnp.where(y == 1, gram[:, ::-1], gram)
    gram = jnp.where(c == 1, gram[:, :, ::-1], gram)
    gram = gram.transpose(0, 3, 1, 2, 4).reshape(rows, -1) / jnp.float32(total)
    return (gram, core)


def solution(mesh):
    groups, n = mesh.devices.shape
    planes = n // 4
    fine = Mesh(np.reshape(mesh.devices, (groups, planes, 2, 2)), AXES)
    spec = P(AXES)
    return jax.shard_map(
        lambda slab, factor: on_device(planes, slab, factor),
        mesh=fine,
        in_specs=(spec, spec),
        out_specs=(spec, spec),
        check_vma=False,
    )
```

time: 298 us -> 261 us (0.88)
  blocking collectives: 24 us -> 0 us
  local copies, waits for them, and re-layouts: 52 us -> 35.1 us
  waiting for transfers between devices: 138 us -> 147 us
    ppermute x4, waiting for transfers between devices: 66 us -> 33.8 us  [on_device(): across = lax.ppermute(stack, 'y', swap)]
    all_gather x1 -> x0, blocking collectives: 24 us -> none  [on_device(): full_factor = lax.all_gather(factor, ('z', 'y', 'c'), axis=0, tiled=True)]
    another operation x14 -> x3, local copies, waits for them, and re-layouts: 23.6 us -> 1.33 us
    ppermute x12, waiting for transfers between devices: 28.1 us -> 49.1 us  [on_device(): lax.ppermute(piece, 'z', [(i, (i + shift) % planes) for i in range(planes)])]
    reduce_scatter x1, waiting for transfers between devices: 43.9 us -> 64.1 us  [on_device(): gram = lax.psum_scatter(gram, 'z', scatter_dimension=0, tiled=True)]
    pallas_call x0 -> x4, local copies, waits for them, and re-layouts: none -> 13.6 us  [unfold(): pl.pallas_call(functools.partial(unfold_kernel, planes, per_plane, group,...]
    slice x5 -> x4, local copies, waits for them, and re-layouts: 9.07 us -> 0.52 us  [on_device(): flat = [b[:, :width] for b in flat]]
    dot_general x16 -> x8, matrix products: 10.9 us -> 4.65 us  [tn_dot(): lax.dot_general(a, b, (((0,), (0,)), ((), ())), preferred_element_type=jn...]
  transfers between devices with their start and end apart: 25 -> 25, of which waited for: 7 -> 11; matrix products, arithmetic and copies ran while one was open for 19% -> 15% of each run, Pallas kernels for 0% -> 0%
where the time goes in v2:
time: 261 us
  waiting for transfers between devices  147 us (56%)
  starting transfers between devices  37.3 us (14%)
  local copies, waits for them, and re-layouts  35.1 us (13%)
  matrix products  22.5 us (9%)
  between operations  14.6 us (6%)
  other arithmetic  4.29 us (2%)
    reduce_scatter x1, waiting for transfers between devices, on_device(): gram = lax.psum_scatter(gram, 'z', scatter_dimension=0, tiled=True)  64.1 us
    ppermute x12, waiting for transfers between devices, on_device(): lax.ppermute(piece, 'z', [(i, (i + shift) % planes) for i in range(planes)])  49.1 us
    ppermute x4, waiting for transfers between devices, on_device(): across = lax.ppermute(stack, 'y', swap)  33.8 us
    ppermute x12, starting transfers between devices, on_device(): lax.ppermute(piece, 'z', [(i, (i + shift) % planes) for i in range(planes)])  31.1 us
    dot_general x16, matrix products, nt_dot(): lax.dot_general(a, b, (((1,), (1,)), ((), ())), preferred_element_type=jn...  17.8 us
    pallas_call x4, local copies, waits for them, and re-layouts, unfold(): pl.pallas_call(functools.partial(unfold_kernel, planes, per_plane, group,...  13.6 us
    unnamed x62, local copies, waits for them, and re-layouts  10.8 us
    dynamic_update_slice x12, local copies, waits for them, and re-layouts, on_device(): lax.dynamic_update_slice(stack, piece[None], ((z - shift) % planes, 0, 0))  5.28 us
  transfers between devices with their start and end apart: 25, of which 11 were waited for; matrix products, arithmetic and copies ran while one was open for 15% of the time, Pallas kernels for 0%

profile of v2, /device:TPU:0, one launch (start us, length us, event | category | flops | bytes accessed | tf_op | source)
XLA Modules:
  0.0 260.6 jit_solution(5778767157804751913)
XLA Ops:
  7.4 4.1 %unfold.7 = (bf16[4,128,1024]{2,1,0:T(8,128)(2,1)S(1)}, bf16[128,1024]{1,0:T(8,128)(2,1)}, bf16[128,1024]{1,0:T(8,128)(2,1)}, bf16[128,1024]{1,0:T(8,128)(2,1)}) fusion(bf16[4,128,1024]{2,1,0:T(8,128)(2,1)S(1)} %broadcast.14.clone.2, s32[]{:T(128)S(6)} %select_n.183, s32[1]{0:T(128)} %bitcast, bf16[128,64,256]{2,1,0:T(8,128)(2,1)} %param.2), kind=kCustom, calls=%fused_computation.73 | custom fusion | bytes 5242888 | tf_op jit(solution)/shard_map/unfold/pallas_call | solution.py:57
  11.5 3.0 %collective-permute-start = (bf16[128,1024]{1,0:T(8,128)(2,1)}, bf16[128,1024]{1,0:T(8,128)(2,1)}, u32[]{:S(2)}, u32[]{:S(2)}) collective-permute-start(bf16[128,1024]{1,0:T(8,128)(2,1)} %get-tuple-element.71), channel_id=1, source_target_pairs={{0,4},{4,8},{8,12},{12,0},{1,5},{5,9},{9,13},{13,1},{2,6},{6,10},{... | collective-permute-start | bytes 786440 | tf_op jit(solution)/shard_map/ppermute | solution.py:96
  14.5 2.6 collective-permute-start.1
  18.6 4.3 %unfold.6 = (bf16[4,128,1024]{2,1,0:T(8,128)(2,1)S(1)}, bf16[128,1024]{1,0:T(8,128)(2,1)}, bf16[128,1024]{1,0:T(8,128)(2,1)}, bf16[128,1024]{1,0:T(8,128)(2,1)}) fusion(bf16[4,128,1024]{2,1,0:T(8,128)(2,1)S(1)} %broadcast.14.clone.1, s32[]{:T(128)S(6)} %select_n.183, s32[1]{0:T(128)} %bitcast, bf16[128,64,256]{2,1,0:T(8,128)(2,1)} %param.2), kind=kCustom, calls=%fused_computation.69 | custom fusion | bytes 5242888 | tf_op jit(solution)/shard_map/unfold/pallas_call | solution.py:57
  24.0 2.6 unfold.5
  27.3 2.6 %unfold.4 = (bf16[4,128,1152]{2,1,0:T(8,128)(2,1)S(1)}, bf16[128,1152]{1,0:T(8,128)(2,1)}, bf16[128,1152]{1,0:T(8,128)(2,1)}, bf16[128,1152]{1,0:T(8,128)(2,1)}) fusion(bf16[4,128,1152]{2,1,0:T(8,128)(2,1)S(1)} %broadcast_in_dim.55, s32[]{:T(128)S(6)} %select_n.183, s32[1]{0:T(128)} %bitcast, bf16[128,64,256]{2,1,0:T(8,128)(2,1)S(1)} %copy-done, ...), kind=kCustom, calls=%fused_computation.61 | custom fusion | bytes 5406728 | tf_op jit(solution)/shard_map/unfold/pallas_call | solution.py:57
  29.9 4.0 %collective-permute-start.3 = (bf16[128,1152]{1,0:T(8,128)(2,1)}, bf16[128,1152]{1,0:T(8,128)(2,1)S(1)}, u32[]{:S(2)}, u32[]{:S(2)}) collective-permute-start(bf16[128,1152]{1,0:T(8,128)(2,1)} %get-tuple-element.33), channel_id=1, source_target_pairs={{0,4},{4,8},{8,12},{12,0},{1,5},{5,9},{9,13},{13,1},{2,6},{6,10},{... | collective-permute-start | bytes 884744 | tf_op jit(solution)/shard_map/ppermute | solution.py:96
  36.3 9.4 %collective-permute-start.5 = (bf16[128,1152]{1,0:T(8,128)(2,1)}, bf16[128,1152]{1,0:T(8,128)(2,1)S(1)}, u32[]{:S(2)}, u32[]{:S(2)}) collective-permute-start(bf16[128,1152]{1,0:T(8,128)(2,1)} %get-tuple-element.37), channel_id=1, source_target_pairs={{0,12},{4,0},{8,4},{12,8},{1,13},{5,1},{9,5},{13,9},{2,14},{6,2},{... | collective-permute-start | bytes 884744 | tf_op jit(solution)/shard_map/ppermute | solution.py:96
  48.7 1.6 collective-permute-start.16
  50.3 8.7 %collective-permute-done.4 = bf16[128,1152]{1,0:T(8,128)(2,1)S(1)} collective-permute-done((bf16[128,1152]{1,0:T(8,128)(2,1)}, bf16[128,1152]{1,0:T(8,128)(2,1)S(1)}, u32[]{:S(2)}, u32[]{:S(2)}) %collective-permute-start.4) | collective-permute-done | bytes 294944 | tf_op jit(solution)/shard_map/ppermute | solution.py:96
  59.0 6.1 %collective-permute-done.5 = bf16[128,1152]{1,0:T(8,128)(2,1)S(1)} collective-permute-done((bf16[128,1152]{1,0:T(8,128)(2,1)}, bf16[128,1152]{1,0:T(8,128)(2,1)S(1)}, u32[]{:S(2)}, u32[]{:S(2)}) %collective-permute-start.5) | collective-permute-done | bytes 294944 | tf_op jit(solution)/shard_map/ppermute | solution.py:96
  65.3 1.6 collective-permute-start.17
  67.5 1.6 collective-permute-start.7
  69.9 8.1 %collective-permute-done.6 = bf16[128,1024]{1,0:T(8,128)(2,1)S(1)} collective-permute-done((bf16[128,1024]{1,0:T(8,128)(2,1)S(1)}, bf16[128,1024]{1,0:T(8,128)(2,1)S(1)}, u32[]{:S(2)}, u32[]{:S(2)}) %collective-permute-start.6) | collective-permute-done | bytes 262176 | tf_op jit(solution)/shard_map/ppermute | solution.py:96
  78.0 10.5 %collective-permute-done.7 = bf16[128,1024]{1,0:T(8,128)(2,1)S(1)} collective-permute-done((bf16[128,1024]{1,0:T(8,128)(2,1)S(1)}, bf16[128,1024]{1,0:T(8,128)(2,1)S(1)}, u32[]{:S(2)}, u32[]{:S(2)}) %collective-permute-start.7) | collective-permute-done | bytes 262176 | tf_op jit(solution)/shard_map/ppermute | solution.py:96
  88.5 2.1 collective-permute-start.9
  90.6 3.4 %collective-permute-start.10 = (bf16[128,1024]{1,0:T(8,128)(2,1)S(1)}, bf16[128,1024]{1,0:T(8,128)(2,1)S(1)}, u32[]{:S(2)}, u32[]{:S(2)}) collective-permute-start(bf16[128,1024]{1,0:T(8,128)(2,1)S(1)} %copy-done.21), channel_id=1, source_target_pairs={{0,8},{4,12},{8,0},{12,4},{1,9},{5,13},{9,1},{13,5},{2,10},{6,14},... | collective-permute-start | bytes 786440 | tf_op jit(solution)/shard_map/ppermute | solution.py:96
  94.8 5.8 %collective-permute-done.9 = bf16[128,1024]{1,0:T(8,128)(2,1)S(1)} collective-permute-done((bf16[128,1024]{1,0:T(8,128)(2,1)S(1)}, bf16[128,1024]{1,0:T(8,128)(2,1)S(1)}, u32[]{:S(2)}, u32[]{:S(2)}) %collective-permute-start.9) | collective-permute-done | bytes 262176 | tf_op jit(solution)/shard_map/ppermute | solution.py:96
  100.6 1.9 collective-permute-start.11
  103.2 7.6 %collective-permute-done.10 = bf16[128,1024]{1,0:T(8,128)(2,1)S(1)} collective-permute-done((bf16[128,1024]{1,0:T(8,128)(2,1)S(1)}, bf16[128,1024]{1,0:T(8,128)(2,1)S(1)}, u32[]{:S(2)}, u32[]{:S(2)}) %collective-permute-start.10) | collective-permute-done | bytes 262176 | tf_op jit(solution)/shard_map/ppermute | solution.py:96
  113.7 2.3 fusion.92
  119.0 1.6 collective-permute-start.19
  121.6 17.0 %collective-permute-done.18 = bf16[4,128,1024]{2,1,0:T(8,128)(2,1)S(1)} collective-permute-done((bf16[4,128,1024]{2,1,0:T(8,128)(2,1)S(1)}, bf16[4,128,1024]{2,1,0:T(8,128)(2,1)S(1)}, u32[]{:S(2)}, u32[]{:S(2)}) %collective-permute-start.18) | collective-permute-done | bytes 1048608 | tf_op jit(solution)/shard_map/ppermute | solution.py:102
  139.9 2.0 fusion.94
  142.9 16.7 %collective-permute-done.19 = bf16[4,128,1024]{2,1,0:T(8,128)(2,1)S(1)} collective-permute-done((bf16[4,128,1024]{2,1,0:T(8,128)(2,1)}, bf16[4,128,1024]{2,1,0:T(8,128)(2,1)S(1)}, u32[]{:S(2)}, u32[]{:S(2)}) %collective-permute-start.19) | collective-permute-done | bytes 1048608 | tf_op jit(solution)/shard_map/ppermute | solution.py:102
  159.6 2.3 fusion.96
  164.9 2.3 fusion.98
  168.2 2.4 pad_maximum_fusion
  178.1 1.6 convolution_add_fusion.6
  185.2 64.1 %reduce-scatter.2.cloned.1.call-done = f32[128,2048]{0,1:T(8,128)} async-done(((f32[512,2048]{0,1:T(8,128)}), f32[128,2048]{0,1:T(8,128)}) %reduce-scatter.2.cloned.1.call-update) | async-done | bytes 1048592 | tf_op jit(solution)/shard_map/reduce_scatter | solution.py:126
  249.3 1.7 reverse_select_fusion.1
  252.0 1.8 div.28
  (136 shorter events, 38.4 us)
Async XLA Ops:
  7.2 242.1 %reduce-scatter.2.cloned.1.call-start = ((), (), s32[]{:S(2)}) async-start(), calls=%async_computation.1 | async-start | bytes 5242880 | tf_op jit(solution)/shard_map/reduce_scatter | solution.py:126
  11.5 18.5 %collective-permute-start = (bf16[128,1024]{1,0:T(8,128)(2,1)}, bf16[128,1024]{1,0:T(8,128)(2,1)}, u32[]{:S(2)}, u32[]{:S(2)}) collective-permute-start(bf16[128,1024]{1,0:T(8,128)(2,1)} %get-tuple-element.71), channel_id=1, source_target_pairs={{0,4},{4,8},{8,12},{12,0},{1,5},{5,9},{9,13},{13,1},{2,6},{6,10},{... | collective-permute-start | bytes 786440 | tf_op jit(solution)/shard_map/ppermute | solution.py:96
  14.5 20.8 %collective-permute-start.1 = (bf16[128,1024]{1,0:T(8,128)(2,1)}, bf16[128,1024]{1,0:T(8,128)(2,1)}, u32[]{:S(2)}, u32[]{:S(2)}) collective-permute-start(bf16[128,1024]{1,0:T(8,128)(2,1)} %get-tuple-element.73), channel_id=1, source_target_pairs={{0,8},{4,12},{8,0},{12,4},{1,9},{5,13},{9,1},{13,5},{2,10},{6,14},... | collective-permute-start | bytes 786440 | tf_op jit(solution)/shard_map/ppermute | solution.py:96
  17.1 19.2 %collective-permute-start.2 = (bf16[128,1024]{1,0:T(8,128)(2,1)}, bf16[128,1024]{1,0:T(8,128)(2,1)}, u32[]{:S(2)}, u32[]{:S(2)}) collective-permute-start(bf16[128,1024]{1,0:T(8,128)(2,1)} %get-tuple-element.75), channel_id=1, source_target_pairs={{0,12},{4,0},{8,4},{12,8},{1,13},{5,1},{9,5},{13,9},{2,14},{6,2},{... | collective-permute-start | bytes 786440 | tf_op jit(solution)/shard_map/ppermute | solution.py:96
  29.9 20.3 %collective-permute-start.3 = (bf16[128,1152]{1,0:T(8,128)(2,1)}, bf16[128,1152]{1,0:T(8,128)(2,1)S(1)}, u32[]{:S(2)}, u32[]{:S(2)}) collective-permute-start(bf16[128,1152]{1,0:T(8,128)(2,1)} %get-tuple-element.33), channel_id=1, source_target_pairs={{0,4},{4,8},{8,12},{12,0},{1,5},{5,9},{9,13},{13,1},{2,6},{6,10},{... | collective-permute-start | bytes 884744 | tf_op jit(solution)/shard_map/ppermute | solution.py:96
  35.2 23.8 %collective-permute-start.4 = (bf16[128,1152]{1,0:T(8,128)(2,1)}, bf16[128,1152]{1,0:T(8,128)(2,1)S(1)}, u32[]{:S(2)}, u32[]{:S(2)}) collective-permute-start(bf16[128,1152]{1,0:T(8,128)(2,1)} %get-tuple-element.35), channel_id=1, source_target_pairs={{0,8},{4,12},{8,0},{12,4},{1,9},{5,13},{9,1},{13,5},{2,10},{6,14},... | collective-permute-start | bytes 884744 | tf_op jit(solution)/shard_map/ppermute | solution.py:96
  36.3 28.9 %collective-permute-start.5 = (bf16[128,1152]{1,0:T(8,128)(2,1)}, bf16[128,1152]{1,0:T(8,128)(2,1)S(1)}, u32[]{:S(2)}, u32[]{:S(2)}) collective-permute-start(bf16[128,1152]{1,0:T(8,128)(2,1)} %get-tuple-element.37), channel_id=1, source_target_pairs={{0,12},{4,0},{8,4},{12,8},{1,13},{5,1},{9,5},{13,9},{2,14},{6,2},{... | collective-permute-start | bytes 884744 | tf_op jit(solution)/shard_map/ppermute | solution.py:96
  47.6 19.3 %copy-start.25 = (bf16[128,1024]{1,0:T(8,128)(2,1)S(1)}, bf16[128,1024]{1,0:T(8,128)(2,1)}, u32[]{:S(2)}) copy-start(bf16[128,1024]{1,0:T(8,128)(2,1)} %get-tuple-element.40) | copy-start | bytes 786436
  47.6 19.9 %copy-start.24 = (bf16[128,1024]{1,0:T(8,128)(2,1)S(1)}, bf16[128,1024]{1,0:T(8,128)(2,1)}, u32[]{:S(2)}) copy-start(bf16[128,1024]{1,0:T(8,128)(2,1)} %get-tuple-element.42) | copy-start | bytes 786436
  48.7 70.3 %collective-permute-start.16 = (bf16[4,128,1024]{2,1,0:T(8,128)(2,1)S(1)}, bf16[4,128,1024]{2,1,0:T(8,128)(2,1)S(1)}, u32[]{:S(2)}, u32[]{:S(2)}) collective-permute-start(bf16[4,128,1024]{2,1,0:T(8,128)(2,1)S(1)} %bitcast_dynamic-update-slice_fusion.12), channel_id=1, source_target_pairs={{0,2},{2,0},{1,3},{3,1},{4,6},{6,4},{5,7},{7,5},{8,10},{10,8},{9,1... | collective-permute-start | bytes 3145736 | tf_op jit(solution)/shard_map/ppermute | solution.py:102
  65.2 51.6 %collective-permute-start.13 = (bf16[4,128,1152]{2,1,0:T(8,128)(2,1)S(1)}, bf16[4,128,1152]{2,1,0:T(8,128)(2,1)S(1)}, u32[]{:S(2)}, u32[]{:S(2)}) collective-permute-start(bf16[4,128,1152]{2,1,0:T(8,128)(2,1)S(1)} %bitcast_dynamic-update-slice_fusion), channel_id=1, source_target_pairs={{0,1},{1,0},{2,3},{3,2},{4,5},{5,4},{6,7},{7,6},{8,9},{9,8},{10,11... | collective-permute-start | bytes 3538952 | tf_op jit(solution)/shard_map/ppermute | solution.py:103
  65.3 52.5 %collective-permute-start.17 = (bf16[4,128,1152]{2,1,0:T(8,128)(2,1)S(1)}, bf16[4,128,1152]{2,1,0:T(8,128)(2,1)S(1)}, u32[]{:S(2)}, u32[]{:S(2)}) collective-permute-start(bf16[4,128,1152]{2,1,0:T(8,128)(2,1)S(1)} %bitcast_dynamic-update-slice_fusion), channel_id=1, source_target_pairs={{0,2},{2,0},{1,3},{3,1},{4,6},{6,4},{5,7},{7,5},{8,10},{10,8},{9,1... | collective-permute-start | bytes 3538952 | tf_op jit(solution)/shard_map/ppermute | solution.py:102
  66.9 11.0 %collective-permute-start.6 = (bf16[128,1024]{1,0:T(8,128)(2,1)S(1)}, bf16[128,1024]{1,0:T(8,128)(2,1)S(1)}, u32[]{:S(2)}, u32[]{:S(2)}) collective-permute-start(bf16[128,1024]{1,0:T(8,128)(2,1)S(1)} %copy-done.25), channel_id=1, source_target_pairs={{0,4},{4,8},{8,12},{12,0},{1,5},{5,9},{9,13},{13,1},{2,6},{6,10},{... | collective-permute-start | bytes 786440 | tf_op jit(solution)/shard_map/ppermute | solution.py:96
  67.5 21.0 %collective-permute-start.7 = (bf16[128,1024]{1,0:T(8,128)(2,1)S(1)}, bf16[128,1024]{1,0:T(8,128)(2,1)S(1)}, u32[]{:S(2)}, u32[]{:S(2)}) collective-permute-start(bf16[128,1024]{1,0:T(8,128)(2,1)S(1)} %copy-done.24), channel_id=1, source_target_pairs={{0,8},{4,12},{8,0},{12,4},{1,9},{5,13},{9,1},{13,5},{2,10},{6,14},... | collective-permute-start | bytes 786440 | tf_op jit(solution)/shard_map/ppermute | solution.py:96
  69.1 8.8 %copy-start.23 = (bf16[128,1024]{1,0:T(8,128)(2,1)S(1)}, bf16[128,1024]{1,0:T(8,128)(2,1)}, u32[]{:S(2)}) copy-start(bf16[128,1024]{1,0:T(8,128)(2,1)} %get-tuple-element.44) | copy-start | bytes 786436
  69.1 19.3 %copy-start.22 = (bf16[128,1024]{1,0:T(8,128)(2,1)S(1)}, bf16[128,1024]{1,0:T(8,128)(2,1)}, u32[]{:S(2)}) copy-start(bf16[128,1024]{1,0:T(8,128)(2,1)} %get-tuple-element.47) | copy-start | bytes 786436
  69.1 21.4 %copy-start.21 = (bf16[128,1024]{1,0:T(8,128)(2,1)S(1)}, bf16[128,1024]{1,0:T(8,128)(2,1)}, u32[]{:S(2)}) copy-start(bf16[128,1024]{1,0:T(8,128)(2,1)} %get-tuple-element.49) | copy-start | bytes 786436
  77.9 12.6 %collective-permute-start.8 = (bf16[128,1024]{1,0:T(8,128)(2,1)S(1)}, bf16[128,1024]{1,0:T(8,128)(2,1)S(1)}, u32[]{:S(2)}, u32[]{:S(2)}) collective-permute-start(bf16[128,1024]{1,0:T(8,128)(2,1)S(1)} %copy-done.23), channel_id=1, source_target_pairs={{0,12},{4,0},{8,4},{12,8},{1,13},{5,1},{9,5},{13,9},{2,14},{6,2},{... | collective-permute-start | bytes 786440 | tf_op jit(solution)/shard_map/ppermute | solution.py:96
  88.5 12.1 %collective-permute-start.9 = (bf16[128,1024]{1,0:T(8,128)(2,1)S(1)}, bf16[128,1024]{1,0:T(8,128)(2,1)S(1)}, u32[]{:S(2)}, u32[]{:S(2)}) collective-permute-start(bf16[128,1024]{1,0:T(8,128)(2,1)S(1)} %copy-done.22), channel_id=1, source_target_pairs={{0,4},{4,8},{8,12},{12,0},{1,5},{5,9},{9,13},{13,1},{2,6},{6,10},{... | collective-permute-start | bytes 786440 | tf_op jit(solution)/shard_map/ppermute | solution.py:96
  90.6 20.3 %collective-permute-start.10 = (bf16[128,1024]{1,0:T(8,128)(2,1)S(1)}, bf16[128,1024]{1,0:T(8,128)(2,1)S(1)}, u32[]{:S(2)}, u32[]{:S(2)}) collective-permute-start(bf16[128,1024]{1,0:T(8,128)(2,1)S(1)} %copy-done.21), channel_id=1, source_target_pairs={{0,8},{4,12},{8,0},{12,4},{1,9},{5,13},{9,1},{13,5},{2,10},{6,14},... | collective-permute-start | bytes 786440 | tf_op jit(solution)/shard_map/ppermute | solution.py:96
  100.6 11.9 %collective-permute-start.11 = (bf16[128,1024]{1,0:T(8,128)(2,1)S(1)}, bf16[128,1024]{1,0:T(8,128)(2,1)S(1)}, u32[]{:S(2)}, u32[]{:S(2)}) collective-permute-start(bf16[128,1024]{1,0:T(8,128)(2,1)S(1)} %get-tuple-element.51), channel_id=1, source_target_pairs={{0,12},{4,0},{8,4},{12,8},{1,13},{5,1},{9,5},{13,9},{2,14},{6,2},{... | collective-permute-start | bytes 786440 | tf_op jit(solution)/shard_map/ppermute | solution.py:96
  110.9 9.7 %collective-permute-start.14 = (bf16[4,128,1024]{2,1,0:T(8,128)(2,1)S(1)}, bf16[4,128,1024]{2,1,0:T(8,128)(2,1)S(1)}, u32[]{:S(2)}, u32[]{:S(2)}) collective-permute-start(bf16[4,128,1024]{2,1,0:T(8,128)(2,1)S(1)} %bitcast_dynamic-update-slice_fusion.8), channel_id=1, source_target_pairs={{0,1},{1,0},{2,3},{3,2},{4,5},{5,4},{6,7},{7,6},{8,9},{9,8},{10,11... | collective-permute-start | bytes 3145736 | tf_op jit(solution)/shard_map/ppermute | solution.py:103
  112.5 26.1 %collective-permute-start.18 = (bf16[4,128,1024]{2,1,0:T(8,128)(2,1)S(1)}, bf16[4,128,1024]{2,1,0:T(8,128)(2,1)S(1)}, u32[]{:S(2)}, u32[]{:S(2)}) collective-permute-start(bf16[4,128,1024]{2,1,0:T(8,128)(2,1)S(1)} %bitcast_dynamic-update-slice_fusion.8), channel_id=1, source_target_pairs={{0,2},{2,0},{1,3},{3,1},{4,6},{6,4},{5,7},{7,5},{8,10},{10,8},{9,1... | collective-permute-start | bytes 3145736 | tf_op jit(solution)/shard_map/ppermute | solution.py:102
  116.8 22.5 %collective-permute-start.15 = (bf16[4,128,1024]{2,1,0:T(8,128)(2,1)}, bf16[4,128,1024]{2,1,0:T(8,128)(2,1)S(1)}, u32[]{:S(2)}, u32[]{:S(2)}) collective-permute-start(bf16[4,128,1024]{2,1,0:T(8,128)(2,1)} %bitcast_dynamic-update-slice_fusion.4), channel_id=1, source_target_pairs={{0,1},{1,0},{2,3},{3,2},{4,5},{5,4},{6,7},{7,6},{8,9},{9,8},{10,11... | collective-permute-start | bytes 3145736 | tf_op jit(solution)/shard_map/ppermute | solution.py:103
  117.8 20.8 %copy-start.7 = (bf16[4,128,1152]{2,1,0:T(8,128)(2,1)}, bf16[4,128,1152]{2,1,0:T(8,128)(2,1)S(1)}, u32[]{:S(2)}) copy-start(bf16[4,128,1152]{2,1,0:T(8,128)(2,1)S(1)} %collective-permute-done.17) | copy-start | bytes 3538948
  117.8 24.1 %collective-permute-start.12 = (bf16[4,128,1024]{2,1,0:T(8,128)(2,1)S(1)}, bf16[4,128,1024]{2,1,0:T(8,128)(2,1)S(1)}, u32[]{:S(2)}, u32[]{:S(2)}) collective-permute-start(bf16[4,128,1024]{2,1,0:T(8,128)(2,1)S(1)} %bitcast_dynamic-update-slice_fusion.12), channel_id=1, source_target_pairs={{0,1},{1,0},{2,3},{3,2},{4,5},{5,4},{6,7},{7,6},{8,9},{9,8},{10,11... | collective-permute-start | bytes 3145736 | tf_op jit(solution)/shard_map/ppermute | solution.py:103
  119.0 43.0 %copy-start.1 = (bf16[4,128,1024]{2,1,0:T(8,128)(2,1)}, bf16[4,128,1024]{2,1,0:T(8,128)(2,1)S(1)}, u32[]{:S(2)}) copy-start(bf16[4,128,1024]{2,1,0:T(8,128)(2,1)S(1)} %collective-permute-done.16) | copy-start | bytes 3145732
  119.0 40.7 %collective-permute-start.19 = (bf16[4,128,1024]{2,1,0:T(8,128)(2,1)}, bf16[4,128,1024]{2,1,0:T(8,128)(2,1)S(1)}, u32[]{:S(2)}, u32[]{:S(2)}) collective-permute-start(bf16[4,128,1024]{2,1,0:T(8,128)(2,1)} %bitcast_dynamic-update-slice_fusion.4), channel_id=1, source_target_pairs={{0,2},{2,0},{1,3},{3,1},{4,6},{6,4},{5,7},{7,5},{8,10},{10,8},{9,1... | collective-permute-start | bytes 3145736 | tf_op jit(solution)/shard_map/ppermute | solution.py:102
  120.6 46.7 %collective-permute-start.20 = (bf16[4,128,1024]{2,1,0:T(8,128)(2,1)S(1)}, bf16[4,128,1024]{2,1,0:T(8,128)(2,1)S(1)}, u32[]{:S(2)}, u32[]{:S(2)}) collective-permute-start(bf16[4,128,1024]{2,1,0:T(8,128)(2,1)S(1)} %collective-permute-done.16), channel_id=1, source_target_pairs={{0,1},{1,0},{2,3},{3,2},{4,5},{5,4},{6,7},{7,6},{8,9},{9,8},{10,11... | collective-permute-start | bytes 3145736 | tf_op jit(solution)/shard_map/ppermute | solution.py:103
  138.6 24.2 %collective-permute-start.21 = (bf16[4,128,1152]{2,1,0:T(8,128)(2,1)S(1)}, bf16[4,128,1152]{2,1,0:T(8,128)(2,1)S(1)}, u32[]{:S(2)}, u32[]{:S(2)}) collective-permute-start(bf16[4,128,1152]{2,1,0:T(8,128)(2,1)S(1)} %collective-permute-done.17), channel_id=1, source_target_pairs={{0,1},{1,0},{2,3},{3,2},{4,5},{5,4},{6,7},{7,6},{8,9},{9,8},{10,11... | collective-permute-start | bytes 3538952 | tf_op jit(solution)/shard_map/ppermute | solution.py:103
  139.6 24.3 %collective-permute-start.22 = (bf16[4,128,1024]{2,1,0:T(8,128)(2,1)S(1)}, bf16[4,128,1024]{2,1,0:T(8,128)(2,1)S(1)}, u32[]{:S(2)}, u32[]{:S(2)}) collective-permute-start(bf16[4,128,1024]{2,1,0:T(8,128)(2,1)S(1)} %collective-permute-done.18), channel_id=1, source_target_pairs={{0,1},{1,0},{2,3},{3,2},{4,5},{5,4},{6,7},{7,6},{8,9},{9,8},{10,11... | collective-permute-start | bytes 3145736 | tf_op jit(solution)/shard_map/ppermute | solution.py:103
  159.6 5.2 %collective-permute-start.23 = (bf16[4,128,1024]{2,1,0:T(8,128)(2,1)S(1)}, bf16[4,128,1024]{2,1,0:T(8,128)(2,1)S(1)}, u32[]{:S(2)}, u32[]{:S(2)}) collective-permute-start(bf16[4,128,1024]{2,1,0:T(8,128)(2,1)S(1)} %collective-permute-done.19), channel_id=1, source_target_pairs={{0,1},{1,0},{2,3},{3,2},{4,5},{5,4},{6,7},{7,6},{8,9},{9,8},{10,11... | collective-permute-start | bytes 3145736 | tf_op jit(solution)/shard_map/ppermute | solution.py:103
  (24 other events, 36.4 us)
Sparse Core Ops, SparseCore 0:
  170.8 78.4 reduce-scatter.1

commit v3 on v1

v3 whole, which is shorter than its diff:
```python
import functools

import jax
import jax.numpy as jnp
import numpy as np
from jax import lax
from jax.experimental import pallas as pl
from jax.experimental.pallas import tpu as pltpu
from jax.sharding import Mesh
from jax.sharding import PartitionSpec as P

AXES = ("groups", "z", "y", "c")
BLOCK = 16
LANES = 128
DEPTH = 512
SWAP = [(0, 1), (1, 0)]


def parts_of(rows):
    sizes = [rows // 4] * 3 + [rows // 8] * 2 if rows >= 8 * BLOCK else [BLOCK] * (rows // BLOCK)
    return [(sum(sizes[:i]), size) for i, size in enumerate(sizes)]


def nt_dot(a, b):
    return lax.dot_general(a, b, (((1,), (1,)), ((), ())), preferred_element_type=jnp.float32)


def tn_dot(a, b):
    return lax.dot_general(a, b, (((0,), (0,)), ((), ())), preferred_element_type=jnp.float32)


def unfold_kernel(planes, per_plane, z_ref, *refs):
    ins, factor, outs, wide = refs[:planes], refs[planes], refs[planes + 1 : -1], refs[-1]
    rows, _, cells = ins[0].shape
    for shift in range(planes):
        first = lax.rem(lax.rem(z_ref[0] + shift, planes) * per_plane, BLOCK)
        for h in range(0, cells, LANES):
            wide[...] = ins[shift][:, :, h : h + LANES].astype(jnp.float32).reshape(rows * BLOCK, LANES)
            for s in range(per_plane):
                at = s * cells + h
                outs[shift][:, at : at + LANES] = wide[pl.ds(first + s, rows, stride=BLOCK), :].astype(jnp.bfloat16)
        outs[shift][:, per_plane * cells :] = factor[...]


def unfold(slab, factor, z, planes, start, size):
    _, species, cells = slab.shape
    rank = factor.shape[1]
    per_plane = species // planes
    width = per_plane * cells + rank
    first = start // BLOCK
    in_specs = [
        pl.BlockSpec(
            (BLOCK, BLOCK, cells),
            lambda i, z_ref, shift=shift: (
                i + first, lax.div(lax.rem(z_ref[0] + shift, planes) * per_plane, BLOCK), 0
            ),
        )
        for shift in range(planes)
    ]
    in_specs.append(pl.BlockSpec((BLOCK, rank), lambda i, z_ref: (i + first, 0)))
    return pl.pallas_call(
        functools.partial(unfold_kernel, planes, per_plane),
        out_shape=[jax.ShapeDtypeStruct((size, width), slab.dtype)] * planes,
        grid_spec=pltpu.PrefetchScalarGridSpec(
            num_scalar_prefetch=1,
            grid=(size // BLOCK,),
            in_specs=in_specs,
            out_specs=[pl.BlockSpec((BLOCK, width), lambda i, z_ref: (i, 0))] * planes,
            scratch_shapes=[pltpu.VMEM((BLOCK * BLOCK, LANES), jnp.float32)],
        ),
        compiler_params=pltpu.CompilerParams(vmem_limit_bytes=16 * 2**20),
        cost_estimate=pl.CostEstimate(
            flops=0, bytes_accessed=planes * size * (BLOCK * cells + width) * 2, transcendentals=0
        ),
        name="unfold",
    )(z.reshape(1).astype(jnp.int32), *([slab] * planes), factor)


def products_kernel(planes, sizes, *refs):
    last = len(sizes) - 1
    size = sizes[last]
    blocks = [[refs[4 * j + k][...] for k in range(4)] for j in range(last + 1)]
    out = refs[-1]
    first = pl.program_id(0) == 0

    @pl.when(first)
    def _():
        out[...] = jnp.zeros_like(out)

    every = jnp.concatenate([b for part in blocks for b in part], axis=0)
    step = 4 * planes * size
    for n in range(every.shape[0] // step):
        got = nt_dot(blocks[last][0], every[n * step : (n + 1) * step])
        out[:, n * size : (n + 1) * size, :] += got.reshape(planes, size, step)
    start = sum(sizes)
    new = every[every.shape[0] - step :]
    for j in range(last):
        got = nt_dot(blocks[j][0], new)
        out[:, start : start + sizes[j], :] += got.reshape(planes, sizes[j], step)
        start += sizes[j]


def products(planes, sizes, blocks, depth):
    total = sum(sizes)
    shape = (planes, 2 * total - sizes[-1], 4 * planes * sizes[-1])
    tile = min(depth, DEPTH)
    return pl.pallas_call(
        functools.partial(products_kernel, planes, sizes),
        out_shape=jax.ShapeDtypeStruct(shape, jnp.float32),
        grid=(depth // tile,),
        in_specs=[pl.BlockSpec((b.shape[0], tile), lambda i: (0, i)) for part in blocks for b in part],
        out_specs=pl.BlockSpec(shape, lambda i: (0, 0, 0)),
        compiler_params=pltpu.CompilerParams(vmem_limit_bytes=40 * 2**20),
        cost_estimate=pl.CostEstimate(
            flops=2 * shape[0] * shape[1] * shape[2] * depth,
            bytes_accessed=4 * planes * total * depth * 2 + 4 * shape[0] * shape[1] * shape[2],
            transcendentals=0,
        ),
        name="products",
    )(*[b for part in blocks for b in part])


def order_kernel(planes, parts, scale, place_ref, *refs):
    sums, out = refs[:-1], refs[-1]
    rows = out.shape[0]

    def block(i, j, k, z):
        (start_i, size_i), (start_j, size_j) = parts[i], parts[j]
        if j <= i:
            step = 4 * planes * size_i
            at = 4 * planes * start_j + (k * planes + z) * size_j
            n, lane = at // step, at % step
            return sums[i][n * size_i : (n + 1) * size_i, lane : lane + size_j]
        start = start_j + size_j + start_i
        lane = (k * planes + z) * size_j
        return sums[j][start : start + size_i, lane : lane + size_j]

    for place in range(4):

        @pl.when(place_ref[0] == place)
        def _():
            for i, (start, size) in enumerate(parts):
                for at in range(0, 4 * planes * rows, LANES):
                    pieces = []
                    for column in range(at // rows, (at + LANES - 1) // rows + 1):
                        z, other = column // 4, column % 4
                        for j in range(len(parts)):
                            pieces.append(block(i, j, place ^ other, z))
                    taken = jnp.concatenate(pieces, axis=1)
                    out[start : start + size, at : at + LANES] = taken * scale


def order(planes, parts, total, place, sums):
    rows = parts[-1][0] + parts[-1][1]
    return pl.pallas_call(
        functools.partial(order_kernel, planes, parts, 1.0 / total),
        out_shape=jax.ShapeDtypeStruct((rows, 4 * planes * rows), jnp.float32),
        in_specs=[pl.BlockSpec(memory_space=pltpu.SMEM)] + [pl.BlockSpec(memory_space=pltpu.VMEM)] * len(sums),
        out_specs=pl.BlockSpec(memory_space=pltpu.VMEM),
        compiler_params=pltpu.CompilerParams(vmem_limit_bytes=16 * 2**20),
        name="order",
    )(place.reshape(1).astype(jnp.int32), *sums)


def after(value, *others):
    return lax.optimization_barrier((value, others))[0]


def on_device(planes, slab, factor):
    rows, species, cells = slab.shape
    rank = factor.shape[1]
    total = species * cells
    depth = total // planes
    z, y, c = (lax.axis_index(name) for name in ("z", "y", "c"))
    parts = parts_of(rows)
    came, waits, held, made, sums = [], [], [], [], []
    for i, (start, size) in enumerate(parts):
        pieces = unfold(slab, factor, z, planes, start, size)
        arrived = []
        for shift in range(1, planes):
            piece = pieces[shift]
            if i:
                piece = after(piece, came[i - 1][shift - 1], *(waits[i - 2] if i > 1 else ()), *made[: max(i - 2, 0)])
            arrived.append(lax.ppermute(piece, "z", [(s, (s + shift) % planes) for s in range(planes)]))
        came.append(arrived)
        stack = jnp.zeros((planes,) + pieces[0].shape, slab.dtype)
        for shift in range(planes):
            piece = arrived[shift - 1] if shift else pieces[0]
            stack = lax.dynamic_update_slice(stack, piece[None], ((z - shift) % planes, 0, 0))
        stack = stack.reshape(planes * size, -1)
        across = lax.ppermute(stack, "y", SWAP)
        beside = lax.ppermute(stack, "c", SWAP)
        waits.append((across, beside))
        held.append([stack, beside, across, lax.ppermute(across, "c", SWAP)])
        part = products(planes, [size for _, size in parts[: i + 1]], held, depth)
        if i:
            part = after(part, made[-1])
        made.append(part)
        sums.append(lax.psum_scatter(part, "z", scatter_dimension=0, tiled=False))
    gram = order(planes, parts, total, y * 2 + c, sums)
    own = depth // 4
    core = jnp.float32(0)
    for part in held:
        for b in part:
            b = after(b, made[-1])
            taken = lax.dynamic_slice_in_dim(b[:, :depth], (y * 2 + c) * own, own, 1)
            core = core + tn_dot(taken, b[:, depth:])
    return (gram, core)


def solution(mesh):
    groups, n = mesh.devices.shape
    planes = n // 4
    fine = Mesh(np.reshape(mesh.devices, (groups, planes, 2, 2)), AXES)
    spec = P(AXES)
    return jax.shard_map(
        lambda slab, factor: on_device(planes, slab, factor),
        mesh=fine,
        in_specs=(spec, spec),
        out_specs=(spec, spec),
        check_vma=False,
    )
```

time: 298 us -> 298 us (level)
  Pallas kernels: 0 us -> 53.7 us
  waiting for transfers between devices: 138 us -> 87.8 us
  blocking collectives: 24 us -> 0 us
  starting transfers between devices: 39.4 us -> 60.3 us
  local copies, waits for them, and re-layouts: 52 us -> 66.9 us
  matrix products: 24.4 us -> 13 us
  other arithmetic: 4.18 us -> 0 us
    pallas_call x0 -> x6, Pallas kernels: none -> 53.7 us  [the longest x5 51.6 us: products(): pl.pallas_call(functools.partial(products_kernel, planes, sizes), out_sha...]
    ppermute x24 -> x30, waiting for transfers between devices: 94.1 us -> 59 us  [the longest x15 29.8 us: on_device(): lax.ppermute(piece, 'z', [(s, (s + shift) % planes) for s in range(planes)])]
    all_gather x1 -> x0, blocking collectives: 24 us -> none  [on_device(): full_factor = lax.all_gather(factor, ('z', 'y', 'c'), axis=0, tiled=True)]
    unnamed x55 -> x86, local copies, waits for them, and re-layouts: 9.65 us -> 33.5 us
    another operation x14 -> x5, local copies, waits for them, and re-layouts: 23.6 us -> 1.11 us
    ppermute x24 -> x30, starting transfers between devices: 39.4 us -> 59.9 us  [the longest x15 53.7 us: on_device(): lax.ppermute(piece, 'z', [(s, (s + shift) % planes) for s in range(planes)])]
    reduce_scatter x1 -> x5, waiting for transfers between devices: 43.9 us -> 28.2 us  [on_device(): sums.append(lax.psum_scatter(part, 'z', scatter_dimension=0, tiled=False))]
    dot_general x32 -> x20, matrix products: 24.4 us -> 13 us  [tn_dot(): lax.dot_general(a, b, (((0,), (0,)), ((), ())), preferred_element_type=jn...]
  transfers between devices with their start and end apart: 25 -> 35, of which waited for: 7 -> 13; matrix products, arithmetic and copies ran while one was open for 19% -> 15% of each run, Pallas kernels for 0% -> 17%
where the time goes in v3:
time: 298 us; the launch traced here: 296 us
  waiting for transfers between devices  87.8 us (29%)
  local copies, waits for them, and re-layouts  66.9 us (22%)
  starting transfers between devices  60.3 us (20%)
  Pallas kernels  53.7 us (18%)
  between operations  14.3 us (5%)
  matrix products  13 us (4%)
    ppermute x15, starting transfers between devices, on_device(): lax.ppermute(piece, 'z', [(s, (s + shift) % planes) for s in range(planes)])  53.7 us
    pallas_call x5, Pallas kernels, products(): pl.pallas_call(functools.partial(products_kernel, planes, sizes), out_sha...  51.6 us
    unnamed x86, local copies, waits for them, and re-layouts  33.5 us
    ppermute x15, waiting for transfers between devices, on_device(): lax.ppermute(piece, 'z', [(s, (s + shift) % planes) for s in range(planes)])  29.8 us
    reduce_scatter x5, waiting for transfers between devices, on_device(): sums.append(lax.psum_scatter(part, 'z', scatter_dimension=0, tiled=False))  28.2 us
    ppermute x5, waiting for transfers between devices, on_device(): across = lax.ppermute(stack, 'y', SWAP)  27.2 us
    dot_general x20, matrix products, tn_dot(): lax.dot_general(a, b, (((0,), (0,)), ((), ())), preferred_element_type=jn...  13 us
    slice x25, local copies, waits for them, and re-layouts, on_device(): taken = lax.dynamic_slice_in_dim(b[:, :depth], (y * 2 + c) * own, own, 1)  12.5 us
  transfers between devices with their start and end apart: 35, of which 13 were waited for; matrix products, arithmetic and copies ran while one was open for 15% of the time, Pallas kernels for 17%

profile of v3, /device:TPU:0, one launch (start us, length us, event | category | flops | bytes accessed | tf_op | source)
XLA Modules:
  0.0 296.1 jit_solution(9083185801470063068)
XLA Ops:
  7.9 2.1 unfold.7
  10.0 3.1 %collective-permute-start = (bf16[32,4224]{1,0:T(8,128)(2,1)S(1)}, bf16[32,4224]{1,0:T(8,128)(2,1)S(1)}, u32[]{:S(2)}, u32[]{:S(2)}) collective-permute-start(bf16[32,4224]{1,0:T(8,128)(2,1)S(1)} %get-tuple-element.133), channel_id=1, source_target_pairs={{0,4},{4,8},{8,12},{12,0},{1,5},{5,9},{9,13},{13,1},{2,6},{6,10},{... | collective-permute-start | bytes 811016 | tf_op jit(solution)/shard_map/ppermute | solution.py:184
  13.1 2.6 collective-permute-start.1
  17.1 3.0 %unfold.6 = (bf16[4,32,4224]{2,1,0:T(8,128)(2,1)S(1)}, bf16[32,4224]{1,0:T(8,128)(2,1)}, bf16[32,4224]{1,0:T(8,128)(2,1)}, bf16[32,4224]{1,0:T(8,128)(2,1)}) fusion(bf16[4,32,4224]{2,1,0:T(8,128)(2,1)S(1)} %broadcast.10.clone.1, s32[]{:T(128)S(6)} %select_n.102, s32[1]{0:T(128)} %bitcast.1, bf16[128,64,256]{2,1,0:T(8,128)(2,1)} %param.2, ...), kind=kCustom, calls=%fused_computation.26 | custom fusion | bytes 5308424 | tf_op jit(solution)/shard_map/unfold/pallas_call | solution.py:61
  20.2 1.9 unfold.5
  27.3 5.5 %collective-permute-start.6 = (bf16[32,4224]{1,0:T(8,128)(2,1)}, bf16[32,4224]{1,0:T(8,128)(2,1)S(1)}, u32[]{:S(2)}, u32[]{:S(2)}) collective-permute-start(bf16[32,4224]{1,0:T(8,128)(2,1)} %get-tuple-element.64), channel_id=1, source_target_pairs={{0,4},{4,8},{8,12},{12,0},{1,5},{5,9},{9,13},{13,1},{2,6},{6,10},{... | collective-permute-start | bytes 811016 | tf_op jit(solution)/shard_map/ppermute | solution.py:184
  34.3 1.8 collective-permute-start.4
  36.2 9.9 %collective-permute-start.7 = (bf16[32,4224]{1,0:T(8,128)(2,1)}, bf16[32,4224]{1,0:T(8,128)(2,1)S(1)}, u32[]{:S(2)}, u32[]{:S(2)}) collective-permute-start(bf16[32,4224]{1,0:T(8,128)(2,1)} %get-tuple-element.66), channel_id=1, source_target_pairs={{0,8},{4,12},{8,0},{12,4},{1,9},{5,13},{9,1},{13,5},{2,10},{6,14},... | collective-permute-start | bytes 811016 | tf_op jit(solution)/shard_map/ppermute | solution.py:184
  46.1 3.4 %collective-permute-start.8 = (bf16[32,4224]{1,0:T(8,128)(2,1)}, bf16[32,4224]{1,0:T(8,128)(2,1)S(1)}, u32[]{:S(2)}, u32[]{:S(2)}) collective-permute-start(bf16[32,4224]{1,0:T(8,128)(2,1)} %get-tuple-element.68), channel_id=1, source_target_pairs={{0,12},{4,0},{8,4},{12,8},{1,13},{5,1},{9,5},{13,9},{2,14},{6,2},{... | collective-permute-start | bytes 811016 | tf_op jit(solution)/shard_map/ppermute | solution.py:184
  50.2 9.2 %collective-permute-done.7 = bf16[32,4224]{1,0:T(8,128)(2,1)S(1)} collective-permute-done((bf16[32,4224]{1,0:T(8,128)(2,1)}, bf16[32,4224]{1,0:T(8,128)(2,1)S(1)}, u32[]{:S(2)}, u32[]{:S(2)}) %collective-permute-start.7) | collective-permute-done | bytes 270368 | tf_op jit(solution)/shard_map/ppermute | solution.py:184
  60.6 11.2 %collective-permute-start.12 = (bf16[32,4224]{1,0:T(8,128)(2,1)S(1)}, bf16[32,4224]{1,0:T(8,128)(2,1)S(1)}, u32[]{:S(2)}, u32[]{:S(2)}) collective-permute-start(bf16[32,4224]{1,0:T(8,128)(2,1)S(1)} %copy-done.42), channel_id=1, source_target_pairs={{0,4},{4,8},{8,12},{12,0},{1,5},{5,9},{9,13},{13,1},{2,6},{6,10},{... | collective-permute-start | bytes 811016 | tf_op jit(solution)/shard_map/ppermute | solution.py:184
  74.0 2.4 collective-permute-start.14
  76.4 2.3 collective-permute-done.12
  79.4 9.4 %collective-permute-done.13 = bf16[32,4224]{1,0:T(8,128)(2,1)S(1)} collective-permute-done((bf16[32,4224]{1,0:T(8,128)(2,1)S(1)}, bf16[32,4224]{1,0:T(8,128)(2,1)S(1)}, u32[]{:S(2)}, u32[]{:S(2)}) %collective-permute-start.13) | collective-permute-done | bytes 270368 | tf_op jit(solution)/shard_map/ppermute | solution.py:184
  89.6 4.7 %products.5 = f32[4,32,512]{2,1,0:T(8,128)} custom-call(bf16[128,4224]{1,0:T(8,128)(2,1)S(1)} %bitcast.54, bf16[128,4224]{1,0:T(8,128)(2,1)S(1)} %collective-permute-done.3.refs_1_, bf16[128,4224]{1,0:T(8,128)(2,1)S(1)} %collective-permute-done.4.refs_2_, bf16[128,4224]{1,0:T(8,128)(2,1)S(1)} %collective-permute-done.5.refs_3_), custom_call_target="tpu_custom_call" | custom-call | flops 536870912 | bytes 4456448 | tf_op jit(solution)/shard_map/products/pallas_call | solution.py:107
  95.2 3.9 %collective-permute-done.10.refs_6_ = bf16[128,4224]{1,0:T(8,128)(2,1)} collective-permute-done((bf16[128,4224]{1,0:T(8,128)(2,1)}, bf16[128,4224]{1,0:T(8,128)(2,1)}, u32[]{:S(2)}, u32[]{:S(2)}) %collective-permute-start.10) | collective-permute-done | bytes 1081376 | tf_op jit(solution)/shard_map/ppermute | solution.py:191
  99.1 2.3 collective-permute-start.18
  101.4 1.7 bitcast_dynamic-update-slice_fusion
  104.9 3.4 %collective-permute-start.19 = (bf16[16,4224]{1,0:T(8,128)(2,1)}, bf16[16,4224]{1,0:T(8,128)(2,1)S(1)}, u32[]{:S(2)}, u32[]{:S(2)}) collective-permute-start(bf16[16,4224]{1,0:T(8,128)(2,1)} %get-tuple-element.82), channel_id=1, source_target_pairs={{0,8},{4,12},{8,0},{12,4},{1,9},{5,13},{9,1},{13,5},{2,10},{6,14},... | collective-permute-start | bytes 405512 | tf_op jit(solution)/shard_map/ppermute | solution.py:184
  111.1 5.3 %collective-permute-done.19 = bf16[16,4224]{1,0:T(8,128)(2,1)S(1)} collective-permute-done((bf16[16,4224]{1,0:T(8,128)(2,1)}, bf16[16,4224]{1,0:T(8,128)(2,1)S(1)}, u32[]{:S(2)}, u32[]{:S(2)}) %collective-permute-start.19) | collective-permute-done | bytes 135200 | tf_op jit(solution)/shard_map/ppermute | solution.py:184
  119.6 8.7 %products.6 = f32[4,96,512]{2,1,0:T(8,128)S(1)} custom-call(bf16[128,4224]{1,0:T(8,128)(2,1)S(1)} %bitcast.55, bf16[128,4224]{1,0:T(8,128)(2,1)S(1)} %collective-permute-done.3.refs_1_, bf16[128,4224]{1,0:T(8,128)(2,1)S(1)} %collective-permute-done.4.refs_2_, bf16[128,4224]{1,0:T(8,128)(2,1)S(1)} %copy-done.3, bf16[128,4224]{1,0:T(8,128)(2,1)S(1)} %bitcast.63, ...), custom_call_target="tpu_custom_call" | custom-call | flops 1610612736 | bytes 9175040 | tf_op jit(solution)/shard_map/products/pallas_call | solution.py:107
  129.7 4.0 %collective-permute-start.24 = (bf16[16,4224]{1,0:T(8,128)(2,1)}, bf16[16,4224]{1,0:T(8,128)(2,1)S(1)}, u32[]{:S(2)}, u32[]{:S(2)}) collective-permute-start(bf16[16,4224]{1,0:T(8,128)(2,1)} %get-tuple-element.88), channel_id=1, source_target_pairs={{0,4},{4,8},{8,12},{12,0},{1,5},{5,9},{9,13},{13,1},{2,6},{6,10},{... | collective-permute-start | bytes 405512 | tf_op jit(solution)/shard_map/ppermute | solution.py:184
  134.8 3.4 %collective-permute-start.25 = (bf16[16,4224]{1,0:T(8,128)(2,1)}, bf16[16,4224]{1,0:T(8,128)(2,1)S(1)}, u32[]{:S(2)}, u32[]{:S(2)}) collective-permute-start(bf16[16,4224]{1,0:T(8,128)(2,1)} %get-tuple-element.90), channel_id=1, source_target_pairs={{0,8},{4,12},{8,0},{12,4},{1,9},{5,13},{9,1},{13,5},{2,10},{6,14},... | collective-permute-start | bytes 405512 | tf_op jit(solution)/shard_map/ppermute | solution.py:184
  138.3 2.2 collective-permute-done.24
  141.2 8.2 %collective-permute-done.22.refs_14_ = bf16[64,4224]{1,0:T(8,128)(2,1)} collective-permute-done((bf16[64,4224]{1,0:T(8,128)(2,1)}, bf16[64,4224]{1,0:T(8,128)(2,1)}, u32[]{:S(2)}, u32[]{:S(2)}) %collective-permute-start.22) | collective-permute-done | bytes 540704 | tf_op jit(solution)/shard_map/ppermute | solution.py:191
  153.8 12.0 %products.7 = f32[4,160,512]{2,1,0:T(8,128)S(1)} custom-call(bf16[128,4224]{1,0:T(8,128)(2,1)S(1)} %bitcast.56, bf16[128,4224]{1,0:T(8,128)(2,1)S(1)} %collective-permute-done.3.refs_1_, bf16[128,4224]{1,0:T(8,128)(2,1)S(1)} %collective-permute-done.4.refs_2_, bf16[128,4224]{1,0:T(8,128)(2,1)S(1)} %copy-done.4, bf16[128,4224]{1,0:T(8,128)(2,1)S(1)} %bitcast.64, ...), custom_call_target="tpu_custom_call" | custom-call | flops 2684354560 | bytes 13893632 | tf_op jit(solution)/shard_map/products/pallas_call | solution.py:107
  172.5 12.1 %products.8 = f32[4,208,256]{2,1,0:T(8,128)S(1)} custom-call(bf16[128,4224]{1,0:T(8,128)(2,1)S(1)} %bitcast.57, bf16[128,4224]{1,0:T(8,128)(2,1)S(1)} %collective-permute-done.3.refs_1_, bf16[128,4224]{1,0:T(8,128)(2,1)S(1)} %collective-permute-done.4.refs_2_, bf16[128,4224]{1,0:T(8,128)(2,1)S(1)} %copy-done.5, bf16[128,4224]{1,0:T(8,128)(2,1)S(1)} %bitcast.65, ...), custom_call_target="tpu_custom_call" | custom-call | flops 1744830464 | bytes 15532032 | tf_op jit(solution)/shard_map/products/pallas_call | solution.py:107
  187.1 14.2 %collective-permute-done.28.refs_18_ = bf16[64,4224]{1,0:T(8,128)(2,1)S(1)} collective-permute-done((bf16[64,4224]{1,0:T(8,128)(2,1)}, bf16[64,4224]{1,0:T(8,128)(2,1)S(1)}, u32[]{:S(2)}, u32[]{:S(2)}) %collective-permute-start.28) | collective-permute-done | bytes 540704 | tf_op jit(solution)/shard_map/ppermute | solution.py:191
  201.4 1.9 collective-permute-done.29.refs_19_
  206.8 14.1 %products.9 = f32[4,240,256]{2,1,0:T(8,128)S(1)} custom-call(bf16[128,4224]{1,0:T(8,128)(2,1)S(1)} %bitcast.58, bf16[128,4224]{1,0:T(8,128)(2,1)S(1)} %collective-permute-done.3.refs_1_, bf16[128,4224]{1,0:T(8,128)(2,1)S(1)} %collective-permute-done.4.refs_2_, bf16[128,4224]{1,0:T(8,128)(2,1)S(1)} %copy-done.6, bf16[128,4224]{1,0:T(8,128)(2,1)S(1)} %bitcast.66, ...), custom_call_target="tpu_custom_call" | custom-call | flops 2013265920 | bytes 17760256 | tf_op jit(solution)/shard_map/products/pallas_call | solution.py:107
  254.6 28.2 %reduce-scatter.10.cloned.1.call-done = f32[1,160,512]{2,1,0:T(8,128)} async-done(((f32[4,160,512]{2,1,0:T(8,128)}), f32[1,160,512]{2,1,0:T(8,128)}) %reduce-scatter.10.cloned.1.call-update) | async-done | bytes 327696 | tf_op jit(solution)/shard_map/reduce_scatter | solution.py:199
  287.4 2.1 order.1
  (205 shorter events, 81.7 us)
Async XLA Ops:
  7.2 247.4 %reduce-scatter.6.cloned.1.call-start = ((), (), s32[]{:S(2)}) async-start(), calls=%async_computation.5 | async-start | bytes 327680 | tf_op jit(solution)/shard_map/reduce_scatter | solution.py:199
  10.0 17.3 %collective-permute-start = (bf16[32,4224]{1,0:T(8,128)(2,1)S(1)}, bf16[32,4224]{1,0:T(8,128)(2,1)S(1)}, u32[]{:S(2)}, u32[]{:S(2)}) collective-permute-start(bf16[32,4224]{1,0:T(8,128)(2,1)S(1)} %get-tuple-element.133), channel_id=1, source_target_pairs={{0,4},{4,8},{8,12},{12,0},{1,5},{5,9},{9,13},{13,1},{2,6},{6,10},{... | collective-permute-start | bytes 811016 | tf_op jit(solution)/shard_map/ppermute | solution.py:184
  13.1 21.1 %collective-permute-start.1 = (bf16[32,4224]{1,0:T(8,128)(2,1)S(1)}, bf16[32,4224]{1,0:T(8,128)(2,1)S(1)}, u32[]{:S(2)}, u32[]{:S(2)}) collective-permute-start(bf16[32,4224]{1,0:T(8,128)(2,1)S(1)} %get-tuple-element.135), channel_id=1, source_target_pairs={{0,8},{4,12},{8,0},{12,4},{1,9},{5,13},{9,1},{13,5},{2,10},{6,14},... | collective-permute-start | bytes 811016 | tf_op jit(solution)/shard_map/ppermute | solution.py:184
  15.7 18.5 %collective-permute-start.2 = (bf16[32,4224]{1,0:T(8,128)(2,1)S(1)}, bf16[32,4224]{1,0:T(8,128)(2,1)S(1)}, u32[]{:S(2)}, u32[]{:S(2)}) collective-permute-start(bf16[32,4224]{1,0:T(8,128)(2,1)S(1)} %get-tuple-element.137), channel_id=1, source_target_pairs={{0,12},{4,0},{8,4},{12,8},{1,13},{5,1},{9,5},{13,9},{2,14},{6,2},{... | collective-permute-start | bytes 811016 | tf_op jit(solution)/shard_map/ppermute | solution.py:184
  27.3 22.2 %collective-permute-start.6 = (bf16[32,4224]{1,0:T(8,128)(2,1)}, bf16[32,4224]{1,0:T(8,128)(2,1)S(1)}, u32[]{:S(2)}, u32[]{:S(2)}) collective-permute-start(bf16[32,4224]{1,0:T(8,128)(2,1)} %get-tuple-element.64), channel_id=1, source_target_pairs={{0,4},{4,8},{8,12},{12,0},{1,5},{5,9},{9,13},{13,1},{2,6},{6,10},{... | collective-permute-start | bytes 811016 | tf_op jit(solution)/shard_map/ppermute | solution.py:184
  34.2 25.8 %collective-permute-start.3 = (bf16[128,4224]{1,0:T(8,128)(2,1)S(1)}, bf16[128,4224]{1,0:T(8,128)(2,1)S(1)}, u32[]{:S(2)}, u32[]{:S(2)}) collective-permute-start(bf16[128,4224]{1,0:T(8,128)(2,1)S(1)} %bitcast.52), channel_id=1, source_target_pairs={{0,1},{1,0},{2,3},{3,2},{4,5},{5,4},{6,7},{7,6},{8,9},{9,8},{10,11... | collective-permute-start | bytes 3244040 | tf_op jit(solution)/shard_map/ppermute | solution.py:192
  34.3 26.3 %collective-permute-start.4 = (bf16[128,4224]{1,0:T(8,128)(2,1)S(1)}, bf16[128,4224]{1,0:T(8,128)(2,1)S(1)}, u32[]{:S(2)}, u32[]{:S(2)}) collective-permute-start(bf16[128,4224]{1,0:T(8,128)(2,1)S(1)} %bitcast.53), channel_id=1, source_target_pairs={{0,2},{2,0},{1,3},{3,1},{4,6},{6,4},{5,7},{7,5},{8,10},{10,8},{9,1... | collective-permute-start | bytes 3244040 | tf_op jit(solution)/shard_map/ppermute | solution.py:191
  36.2 23.2 %collective-permute-start.7 = (bf16[32,4224]{1,0:T(8,128)(2,1)}, bf16[32,4224]{1,0:T(8,128)(2,1)S(1)}, u32[]{:S(2)}, u32[]{:S(2)}) collective-permute-start(bf16[32,4224]{1,0:T(8,128)(2,1)} %get-tuple-element.66), channel_id=1, source_target_pairs={{0,8},{4,12},{8,0},{12,4},{1,9},{5,13},{9,1},{13,5},{2,10},{6,14},... | collective-permute-start | bytes 811016 | tf_op jit(solution)/shard_map/ppermute | solution.py:184
  46.1 25.7 %collective-permute-start.8 = (bf16[32,4224]{1,0:T(8,128)(2,1)}, bf16[32,4224]{1,0:T(8,128)(2,1)S(1)}, u32[]{:S(2)}, u32[]{:S(2)}) collective-permute-start(bf16[32,4224]{1,0:T(8,128)(2,1)} %get-tuple-element.68), channel_id=1, source_target_pairs={{0,12},{4,0},{8,4},{12,8},{1,13},{5,1},{9,5},{13,9},{2,14},{6,2},{... | collective-permute-start | bytes 811016 | tf_op jit(solution)/shard_map/ppermute | solution.py:184
  60.6 18.1 %collective-permute-start.12 = (bf16[32,4224]{1,0:T(8,128)(2,1)S(1)}, bf16[32,4224]{1,0:T(8,128)(2,1)S(1)}, u32[]{:S(2)}, u32[]{:S(2)}) collective-permute-start(bf16[32,4224]{1,0:T(8,128)(2,1)S(1)} %copy-done.42), channel_id=1, source_target_pairs={{0,4},{4,8},{8,12},{12,0},{1,5},{5,9},{9,13},{13,1},{2,6},{6,10},{... | collective-permute-start | bytes 811016 | tf_op jit(solution)/shard_map/ppermute | solution.py:184
  72.5 22.7 %collective-permute-start.9 = (bf16[128,4224]{1,0:T(8,128)(2,1)}, bf16[128,4224]{1,0:T(8,128)(2,1)}, u32[]{:S(2)}, u32[]{:S(2)}) collective-permute-start(bf16[128,4224]{1,0:T(8,128)(2,1)} %bitcast.61), channel_id=1, source_target_pairs={{0,1},{1,0},{2,3},{3,2},{4,5},{5,4},{6,7},{7,6},{8,9},{9,8},{10,11... | collective-permute-start | bytes 3244040 | tf_op jit(solution)/shard_map/ppermute | solution.py:192
  72.5 26.6 %collective-permute-start.10 = (bf16[128,4224]{1,0:T(8,128)(2,1)}, bf16[128,4224]{1,0:T(8,128)(2,1)}, u32[]{:S(2)}, u32[]{:S(2)}) collective-permute-start(bf16[128,4224]{1,0:T(8,128)(2,1)} %bitcast.62), channel_id=1, source_target_pairs={{0,2},{2,0},{1,3},{3,1},{4,6},{6,4},{5,7},{7,5},{8,10},{10,8},{9,1... | collective-permute-start | bytes 3244040 | tf_op jit(solution)/shard_map/ppermute | solution.py:191
  74.0 14.8 %collective-permute-start.13 = (bf16[32,4224]{1,0:T(8,128)(2,1)S(1)}, bf16[32,4224]{1,0:T(8,128)(2,1)S(1)}, u32[]{:S(2)}, u32[]{:S(2)}) collective-permute-start(bf16[32,4224]{1,0:T(8,128)(2,1)S(1)} %copy-done.41), channel_id=1, source_target_pairs={{0,8},{4,12},{8,0},{12,4},{1,9},{5,13},{9,1},{13,5},{2,10},{6,14},... | collective-permute-start | bytes 811016 | tf_op jit(solution)/shard_map/ppermute | solution.py:184
  74.0 27.4 %collective-permute-start.14 = (bf16[32,4224]{1,0:T(8,128)(2,1)S(1)}, bf16[32,4224]{1,0:T(8,128)(2,1)}, u32[]{:S(2)}, u32[]{:S(2)}) collective-permute-start(bf16[32,4224]{1,0:T(8,128)(2,1)S(1)} %get-tuple-element.76), channel_id=1, source_target_pairs={{0,12},{4,0},{8,4},{12,8},{1,13},{5,1},{9,5},{13,9},{2,14},{6,2},{... | collective-permute-start | bytes 811016 | tf_op jit(solution)/shard_map/ppermute | solution.py:184
  78.7 10.9 %collective-permute-start.5 = (bf16[128,4224]{1,0:T(8,128)(2,1)S(1)}, bf16[128,4224]{1,0:T(8,128)(2,1)S(1)}, u32[]{:S(2)}, u32[]{:S(2)}) collective-permute-start(bf16[128,4224]{1,0:T(8,128)(2,1)S(1)} %collective-permute-done.4.refs_2_), channel_id=1, source_target_pairs={{0,1},{1,0},{2,3},{3,2},{4,5},{5,4},{6,7},{7,6},{8,9},{9,8},{10,11... | collective-permute-start | bytes 3244040 | tf_op jit(solution)/shard_map/ppermute | solution.py:194
  103.1 26.2 %collective-permute-start.15 = (bf16[128,4224]{1,0:T(8,128)(2,1)}, bf16[128,4224]{1,0:T(8,128)(2,1)}, u32[]{:S(2)}, u32[]{:S(2)}) collective-permute-start(bf16[128,4224]{1,0:T(8,128)(2,1)} %bitcast.69), channel_id=1, source_target_pairs={{0,1},{1,0},{2,3},{3,2},{4,5},{5,4},{6,7},{7,6},{8,9},{9,8},{10,11... | collective-permute-start | bytes 3244040 | tf_op jit(solution)/shard_map/ppermute | solution.py:192
  103.1 26.6 %collective-permute-start.16 = (bf16[128,4224]{1,0:T(8,128)(2,1)}, bf16[128,4224]{1,0:T(8,128)(2,1)}, u32[]{:S(2)}, u32[]{:S(2)}) collective-permute-start(bf16[128,4224]{1,0:T(8,128)(2,1)} %bitcast.70), channel_id=1, source_target_pairs={{0,2},{2,0},{1,3},{3,1},{4,6},{6,4},{5,7},{7,5},{8,10},{10,8},{9,1... | collective-permute-start | bytes 3244040 | tf_op jit(solution)/shard_map/ppermute | solution.py:191
  104.6 12.5 %collective-permute-start.11 = (bf16[128,4224]{1,0:T(8,128)(2,1)}, bf16[128,4224]{1,0:T(8,128)(2,1)}, u32[]{:S(2)}, u32[]{:S(2)}) collective-permute-start(bf16[128,4224]{1,0:T(8,128)(2,1)} %collective-permute-done.10.refs_6_), channel_id=1, source_target_pairs={{0,1},{1,0},{2,3},{3,2},{4,5},{5,4},{6,7},{7,6},{8,9},{9,8},{10,11... | collective-permute-start | bytes 3244040 | tf_op jit(solution)/shard_map/ppermute | solution.py:194
  104.8 149.7 %reduce-scatter.8.cloned.1.call-start = ((), (), s32[]{:S(2)}) async-start(), calls=%async_computation.6 | async-start | bytes 983040 | tf_op jit(solution)/shard_map/reduce_scatter | solution.py:199
  104.9 11.5 %collective-permute-start.19 = (bf16[16,4224]{1,0:T(8,128)(2,1)}, bf16[16,4224]{1,0:T(8,128)(2,1)S(1)}, u32[]{:S(2)}, u32[]{:S(2)}) collective-permute-start(bf16[16,4224]{1,0:T(8,128)(2,1)} %get-tuple-element.82), channel_id=1, source_target_pairs={{0,8},{4,12},{8,0},{12,4},{1,9},{5,13},{9,1},{13,5},{2,10},{6,14},... | collective-permute-start | bytes 405512 | tf_op jit(solution)/shard_map/ppermute | solution.py:184
  108.3 25.3 %collective-permute-start.20 = (bf16[16,4224]{1,0:T(8,128)(2,1)}, bf16[16,4224]{1,0:T(8,128)(2,1)S(1)}, u32[]{:S(2)}, u32[]{:S(2)}) collective-permute-start(bf16[16,4224]{1,0:T(8,128)(2,1)} %get-tuple-element.84), channel_id=1, source_target_pairs={{0,12},{4,0},{8,4},{12,8},{1,13},{5,1},{9,5},{13,9},{2,14},{6,2},{... | collective-permute-start | bytes 405512 | tf_op jit(solution)/shard_map/ppermute | solution.py:184
  129.7 10.8 %collective-permute-start.24 = (bf16[16,4224]{1,0:T(8,128)(2,1)}, bf16[16,4224]{1,0:T(8,128)(2,1)S(1)}, u32[]{:S(2)}, u32[]{:S(2)}) collective-permute-start(bf16[16,4224]{1,0:T(8,128)(2,1)} %get-tuple-element.88), channel_id=1, source_target_pairs={{0,4},{4,8},{8,12},{12,0},{1,5},{5,9},{9,13},{13,1},{2,6},{6,10},{... | collective-permute-start | bytes 405512 | tf_op jit(solution)/shard_map/ppermute | solution.py:184
  134.3 33.4 %collective-permute-start.21 = (bf16[64,4224]{1,0:T(8,128)(2,1)}, bf16[64,4224]{1,0:T(8,128)(2,1)}, u32[]{:S(2)}, u32[]{:S(2)}) collective-permute-start(bf16[64,4224]{1,0:T(8,128)(2,1)} %bitcast.76), channel_id=1, source_target_pairs={{0,1},{1,0},{2,3},{3,2},{4,5},{5,4},{6,7},{7,6},{8,9},{9,8},{10,11... | collective-permute-start | bytes 1622024 | tf_op jit(solution)/shard_map/ppermute | solution.py:192
  134.3 15.0 %collective-permute-start.22 = (bf16[64,4224]{1,0:T(8,128)(2,1)}, bf16[64,4224]{1,0:T(8,128)(2,1)}, u32[]{:S(2)}, u32[]{:S(2)}) collective-permute-start(bf16[64,4224]{1,0:T(8,128)(2,1)} %bitcast.77), channel_id=1, source_target_pairs={{0,2},{2,0},{1,3},{3,1},{4,6},{6,4},{5,7},{7,5},{8,10},{10,8},{9,1... | collective-permute-start | bytes 1622024 | tf_op jit(solution)/shard_map/ppermute | solution.py:191
  134.8 119.8 %reduce-scatter.12.cloned.1.call-start = ((), (), s32[]{:S(2)}) async-start(), calls=%async_computation.8 | async-start | bytes 1064960 | tf_op jit(solution)/shard_map/reduce_scatter | solution.py:199
  134.8 14.5 %collective-permute-start.25 = (bf16[16,4224]{1,0:T(8,128)(2,1)}, bf16[16,4224]{1,0:T(8,128)(2,1)S(1)}, u32[]{:S(2)}, u32[]{:S(2)}) collective-permute-start(bf16[16,4224]{1,0:T(8,128)(2,1)} %get-tuple-element.90), channel_id=1, source_target_pairs={{0,8},{4,12},{8,0},{12,4},{1,9},{5,13},{9,1},{13,5},{2,10},{6,14},... | collective-permute-start | bytes 405512 | tf_op jit(solution)/shard_map/ppermute | solution.py:184
  138.2 47.6 %collective-permute-start.26 = (bf16[16,4224]{1,0:T(8,128)(2,1)}, bf16[16,4224]{1,0:T(8,128)(2,1)S(1)}, u32[]{:S(2)}, u32[]{:S(2)}) collective-permute-start(bf16[16,4224]{1,0:T(8,128)(2,1)} %get-tuple-element.92), channel_id=1, source_target_pairs={{0,12},{4,0},{8,4},{12,8},{1,13},{5,1},{9,5},{13,9},{2,14},{6,2},{... | collective-permute-start | bytes 405512 | tf_op jit(solution)/shard_map/ppermute | solution.py:184
  149.3 18.4 %collective-permute-start.23 = (bf16[64,4224]{1,0:T(8,128)(2,1)}, bf16[64,4224]{1,0:T(8,128)(2,1)}, u32[]{:S(2)}, u32[]{:S(2)}) collective-permute-start(bf16[64,4224]{1,0:T(8,128)(2,1)} %collective-permute-done.22.refs_14_), channel_id=1, source_target_pairs={{0,1},{1,0},{2,3},{3,2},{4,5},{5,4},{6,7},{7,6},{8,9},{9,8},{10,11... | collective-permute-start | bytes 1622024 | tf_op jit(solution)/shard_map/ppermute | solution.py:194
  185.6 69.0 %reduce-scatter.14.cloned.1.call-start = ((), (), s32[]{:S(2)}) async-start(), calls=%async_computation.9 | async-start | bytes 1228800 | tf_op jit(solution)/shard_map/reduce_scatter | solution.py:199
  186.5 14.9 %collective-permute-start.28 = (bf16[64,4224]{1,0:T(8,128)(2,1)}, bf16[64,4224]{1,0:T(8,128)(2,1)S(1)}, u32[]{:S(2)}, u32[]{:S(2)}) collective-permute-start(bf16[64,4224]{1,0:T(8,128)(2,1)} %bitcast.30.refs_16_), channel_id=1, source_target_pairs={{0,2},{2,0},{1,3},{3,1},{4,6},{6,4},{5,7},{7,5},{8,10},{10,8},{9,1... | collective-permute-start | bytes 1622024 | tf_op jit(solution)/shard_map/ppermute | solution.py:191
  186.9 14.5 %collective-permute-start.27 = (bf16[64,4224]{1,0:T(8,128)(2,1)}, bf16[64,4224]{1,0:T(8,128)(2,1)S(1)}, u32[]{:S(2)}, u32[]{:S(2)}) collective-permute-start(bf16[64,4224]{1,0:T(8,128)(2,1)} %bitcast.30.refs_16_), channel_id=1, source_target_pairs={{0,1},{1,0},{2,3},{3,2},{4,5},{5,4},{6,7},{7,6},{8,9},{9,8},{10,11... | collective-permute-start | bytes 1622024 | tf_op jit(solution)/shard_map/ppermute | solution.py:192
  224.3 58.5 %reduce-scatter.10.cloned.1.call-start = ((), (), s32[]{:S(2)}) async-start(), calls=%async_computation.7 | async-start | bytes 1638400 | tf_op jit(solution)/shard_map/reduce_scatter | solution.py:199
  (51 other events, 309.1 us)
Sparse Core Ops, SparseCore 0:
  105.0 21.7 reduce-scatter.5
  134.9 27.8 reduce-scatter.7
  185.7 27.9 reduce-scatter.11
  224.4 26.2 reduce-scatter.13
  253.0 29.7 reduce-scatter.9

commit v4 on v1

v4 whole, which is shorter than its diff:
```python
import functools

import jax
import jax.numpy as jnp
import numpy as np
from jax import lax
from jax.experimental import pallas as pl
from jax.experimental.pallas import tpu as pltpu
from jax.sharding import Mesh
from jax.sharding import PartitionSpec as P

AXES = ("groups", "z", "y", "c")
BLOCK = 16
LANES = 128
SWAP = [(0, 1), (1, 0)]


def chunks_of(per_plane):
    unit = per_plane // 4
    sizes = [unit] * 3 + ([unit // 2] * 2 if unit % 2 == 0 else [unit])
    return [(sum(sizes[:i]), size) for i, size in enumerate(sizes)]


def nt_dot(a, b):
    return lax.dot_general(a, b, (((1,), (1,)), ((), ())), preferred_element_type=jnp.float32)


def tn_dot(a, b):
    return lax.dot_general(a, b, (((0,), (0,)), ((), ())), preferred_element_type=jnp.float32)


def after(value, *others):
    return lax.optimization_barrier((value, others))[0]


def unfold_kernel(planes, per_plane, chunks, extra, z_ref, *refs):
    ins, factor, outs, wide = refs[:planes], refs[planes], refs[planes + 1 : -1], refs[-1]
    rows, _, cells = ins[0].shape
    for shift in range(planes):
        first = lax.rem(lax.rem(z_ref[0] + shift, planes) * per_plane, BLOCK)
        for h in range(0, cells, LANES):
            wide[...] = ins[shift][:, :, h : h + LANES].astype(jnp.float32).reshape(rows * BLOCK, LANES)
            for n, (start, size) in enumerate(chunks):
                out = outs[n * planes + shift]
                for s in range(size):
                    taken = wide[pl.ds(first + start + s, rows, stride=BLOCK), :]
                    out[:, s * cells + h : s * cells + h + LANES] = taken.astype(jnp.bfloat16)
        if extra is not None:
            outs[extra * planes + shift][:, chunks[extra][1] * cells :] = factor[...]


def unfold(slab, factor, z, planes, chunks, extra):
    rows, species, cells = slab.shape
    rank = factor.shape[1]
    per_plane = species // planes
    step = min(rows, 32)
    widths = [size * cells + (rank if n == extra else 0) for n, (_, size) in enumerate(chunks)]
    in_specs = [
        pl.BlockSpec(
            (step, BLOCK, cells),
            lambda i, z_ref, shift=shift: (i, lax.div(lax.rem(z_ref[0] + shift, planes) * per_plane, BLOCK), 0),
        )
        for shift in range(planes)
    ]
    in_specs.append(pl.BlockSpec((step, rank), lambda i, z_ref: (i, 0)))
    out = pl.pallas_call(
        functools.partial(unfold_kernel, planes, per_plane, chunks, extra),
        out_shape=[jax.ShapeDtypeStruct((rows, width), slab.dtype) for width in widths for _ in range(planes)],
        grid_spec=pltpu.PrefetchScalarGridSpec(
            num_scalar_prefetch=1,
            grid=(rows // step,),
            in_specs=in_specs,
            out_specs=[pl.BlockSpec((step, width), lambda i, z_ref: (i, 0)) for width in widths for _ in range(planes)],
            scratch_shapes=[pltpu.VMEM((step * BLOCK, LANES), jnp.float32)],
        ),
        compiler_params=pltpu.CompilerParams(vmem_limit_bytes=24 * 2**20),
        cost_estimate=pl.CostEstimate(
            flops=0, bytes_accessed=planes * rows * (BLOCK * cells + sum(widths)) * 2, transcendentals=0
        ),
        name="unfold",
    )(z.reshape(1).astype(jnp.int32), *([slab] * planes), factor)
    return [out[n * planes : (n + 1) * planes] for n in range(len(chunks))]


def finish_kernel(planes, scale, place_ref, *refs):
    out = refs[-1]
    rows = out.shape[0]
    sums = []
    for pair in range(2):
        own, below, above = refs[3 * pair : 3 * pair + 3]
        sums.append((own[...] + below[...] + above[...]) * scale)

    def block(k, z):
        at = ((k % 2) * planes + z) * rows
        return sums[k // 2][:, at : at + rows]

    for place in range(4):

        @pl.when(place_ref[0] == place)
        def _():
            for z in range(planes):
                pieces = [block(place ^ other, z) for other in range(4)]
                out[:, z * 4 * rows : (z + 1) * 4 * rows] = jnp.concatenate(pieces, axis=1)


def finish(planes, total, place, parts):
    rows = parts[0].shape[0]
    return pl.pallas_call(
        functools.partial(finish_kernel, planes, 1.0 / total),
        out_shape=jax.ShapeDtypeStruct((rows, 4 * planes * rows), jnp.float32),
        in_specs=[pl.BlockSpec(memory_space=pltpu.SMEM)] + [pl.BlockSpec(memory_space=pltpu.VMEM)] * len(parts),
        out_specs=pl.BlockSpec(memory_space=pltpu.VMEM),
        compiler_params=pltpu.CompilerParams(vmem_limit_bytes=24 * 2**20),
        name="finish",
    )(place.reshape(1).astype(jnp.int32), *parts)


def chain(planes, z, sums, up):
    rows = sums.shape[0] // planes
    got = None
    for step in range(1, planes):
        plane = planes - step + z if up else z - planes + step
        sent = lax.dynamic_slice_in_dim(sums, jnp.clip(plane, 0, planes - 1) * rows, rows, 0)
        if got is not None:
            sent = sent + got
        pairs = [(i, i + 1) for i in range(step)] if up else [(planes - 1 - i, planes - 2 - i) for i in range(step)]
        got = lax.ppermute(sent, "z", pairs)
    return got


def on_device(planes, slab, factor):
    rows, species, cells = slab.shape
    rank = factor.shape[1]
    total = species * cells
    z, y, c = (lax.axis_index(name) for name in ("z", "y", "c"))
    place = y * 2 + c
    per_plane = species // planes
    chunks = chunks_of(per_plane)
    last = len(chunks) - 1
    pieces = unfold(slab, factor, z, planes, chunks[:1], None) + unfold(slab, factor, z, planes, chunks[1:], 0)

    def stacked(parts):
        stack = jnp.zeros((planes,) + parts[0].shape, slab.dtype)
        for shift in range(planes):
            stack = lax.dynamic_update_slice(stack, parts[shift][None], ((z - shift) % planes, 0, 0))
        return stack.reshape(planes * rows, -1)

    came, waits, held = [], [], []
    for j in range(last + 1):
        arrived = [pieces[j][0]]
        for shift in range(1, planes):
            piece = pieces[j][shift]
            if j:
                piece = after(piece, came[j - 1][shift], *(waits[j - 2] if j > 1 else ()))
            arrived.append(lax.ppermute(piece, "z", [(s, (s + shift) % planes) for s in range(planes)]))
        came.append(arrived)
        stack = stacked(arrived)
        across = lax.ppermute(stack, "y", SWAP)
        beside = lax.ppermute(stack, "c", SWAP)
        waits.append((across, beside))
        held.append([stack, beside, across, lax.ppermute(across, "c", SWAP)])
    flat = [[b[:, : size * cells] for b in held[j]] for j, (_, size) in enumerate(chunks)]
    factors = [b[:, chunks[1][1] * cells :] for b in held[1]]
    sums = [sum(nt_dot(flat[j][0], flat[j][k]) for j in range(last + 1)) for k in range(4)]
    parts = []
    for pair in range(2):
        both = jnp.concatenate(sums[2 * pair : 2 * pair + 2], axis=1)
        parts.append(lax.dynamic_slice_in_dim(both, z * rows, rows, 0))
        parts.append(chain(planes, z, both, True))
        parts.append(chain(planes, z, both, False))
    gram = finish(planes, total, place, parts)
    own = per_plane // 4
    whole = [sum(tn_dot(flat[j][k], factors[k]) for k in range(4)) for j in range(last + 1)]
    whole = jnp.concatenate(whole, axis=0)
    core = lax.dynamic_slice_in_dim(whole, place * own * cells, own * cells, 0)
    return (gram, core)


def solution(mesh):
    groups, n = mesh.devices.shape
    planes = n // 4
    fine = Mesh(np.reshape(mesh.devices, (groups, planes, 2, 2)), AXES)
    spec = P(AXES)
    return jax.shard_map(
        lambda slab, factor: on_device(planes, slab, factor),
        mesh=fine,
        in_specs=(spec, spec),
        out_specs=(spec, spec),
        check_vma=False,
    )
```

time: 298 us -> 225 us (0.76)
  local copies, waits for them, and re-layouts: 52 us -> 15 us
  starting transfers between devices: 39.4 us -> 68.6 us
  blocking collectives: 24 us -> 0 us
  waiting for transfers between devices: 138 us -> 116 us
  between operations: 14.8 us -> 1.49 us
  other arithmetic: 4.18 us -> 0.93 us
  matrix products: 24.4 us -> 21.2 us
    reduce_scatter x1 -> x0, waiting for transfers between devices: 43.9 us -> none  [on_device(): gram = lax.psum_scatter(gram, 'z', scatter_dimension=0, tiled=True)]
    ppermute x24 -> x42, starting transfers between devices: 39.4 us -> 68.6 us  [the longest x15 38.2 us: on_device(): lax.ppermute(piece, 'z', [(s, (s + shift) % planes) for s in range(planes)])]
    all_gather x1 -> x0, blocking collectives: 24 us -> none  [on_device(): full_factor = lax.all_gather(factor, ('z', 'y', 'c'), axis=0, tiled=True)]
    another operation x14 -> x4, local copies, waits for them, and re-layouts: 23.6 us -> 0.31 us
    ppermute x24 -> x42, waiting for transfers between devices: 94.1 us -> 116 us  [the longest x15 57 us: on_device(): lax.ppermute(piece, 'z', [(s, (s + shift) % planes) for s in range(planes)])]
    pallas_call x0 -> x2, local copies, waits for them, and re-layouts: none -> 9.08 us  [unfold(): pl.pallas_call(functools.partial(unfold_kernel, planes, per_plane, chunks...]
    slice x5 -> x0, local copies, waits for them, and re-layouts: 9.07 us -> none  [on_device(): slab.reshape(rows, planes, CHUNKS, width)[:, :, j].transpose(1, 0, 2)]
    unnamed x55 -> x28, local copies, waits for them, and re-layouts: 9.65 us -> 1.47 us
  transfers between devices with their start and end apart: 25 -> 42, of which waited for: 7 -> 17; matrix products, arithmetic and copies ran while one was open for 19% -> 14% of each run, Pallas kernels for 0% -> 0%
where the time goes in v4:
time: 225 us
  waiting for transfers between devices  116 us (52%)
  starting transfers between devices  68.6 us (30%)
  matrix products  21.2 us (9%)
  local copies, waits for them, and re-layouts  15 us (7%)
    ppermute x15, waiting for transfers between devices, on_device(): lax.ppermute(piece, 'z', [(s, (s + shift) % planes) for s in range(planes)])  57 us
    ppermute x15, starting transfers between devices, on_device(): lax.ppermute(piece, 'z', [(s, (s + shift) % planes) for s in range(planes)])  38.2 us
    ppermute x12, waiting for transfers between devices, chain(): got = lax.ppermute(sent, 'z', pairs)  33.2 us
    ppermute x5, waiting for transfers between devices, on_device(): across = lax.ppermute(stack, 'y', SWAP)  25.7 us
    ppermute x12, starting transfers between devices, chain(): got = lax.ppermute(sent, 'z', pairs)  24.1 us
    dot_general x20, matrix products, nt_dot(): lax.dot_general(a, b, (((1,), (1,)), ((), ())), preferred_element_type=jn...  12.8 us
    pallas_call x2, local copies, waits for them, and re-layouts, unfold(): pl.pallas_call(functools.partial(unfold_kernel, planes, per_plane, chunks...  9.08 us
    dot_general x20, matrix products, tn_dot(): lax.dot_general(a, b, (((0,), (0,)), ((), ())), preferred_element_type=jn...  8.38 us
  transfers between devices with their start and end apart: 42, of which 17 were waited for; matrix products, arithmetic and copies ran while one was open for 14% of the time, Pallas kernels for 0%

profile of v4, /device:TPU:0, one launch (start us, length us, event | category | flops | bytes accessed | tf_op | source)
XLA Modules:
  0.0 224.5 jit_solution(6418286545482772794)
XLA Ops:
  0.8 4.7 %unfold.3 = (bf16[4,128,1024]{2,1,0:T(8,128)(2,1)S(1)}, bf16[128,1024]{1,0:T(8,128)(2,1)}, bf16[128,1024]{1,0:T(8,128)(2,1)}, bf16[128,1024]{1,0:T(8,128)(2,1)}) fusion(bf16[4,128,1024]{2,1,0:T(8,128)(2,1)S(1)} %broadcast.10.clone, s32[]{:T(128)S(6)} %select_n.111, s32[1]{0:T(128)} %bitcast.1, bf16[128,64,256]{2,1,0:T(8,128)(2,1)} %param.2, ...), kind=kCustom, calls=%fused_computation.113 | custom fusion | bytes 5275656 | tf_op jit(solution)/shard_map/unfold/pallas_call | solution.py:66
  5.5 3.1 %collective-permute-start = (bf16[128,1024]{1,0:T(8,128)(2,1)}, bf16[128,1024]{1,0:T(8,128)(2,1)}, u32[]{:S(2)}, u32[]{:S(2)}) collective-permute-start(bf16[128,1024]{1,0:T(8,128)(2,1)} %get-tuple-element.69), channel_id=1, source_target_pairs={{0,4},{4,8},{8,12},{12,0},{1,5},{5,9},{9,13},{13,1},{2,6},{6,10},{... | collective-permute-start | bytes 786440 | tf_op jit(solution)/shard_map/ppermute | solution.py:155
  8.6 2.6 %collective-permute-start.1 = (bf16[128,1024]{1,0:T(8,128)(2,1)}, bf16[128,1024]{1,0:T(8,128)(2,1)}, u32[]{:S(2)}, u32[]{:S(2)}) collective-permute-start(bf16[128,1024]{1,0:T(8,128)(2,1)} %get-tuple-element.71), channel_id=1, source_target_pairs={{0,8},{4,12},{8,0},{12,4},{1,9},{5,13},{9,1},{13,5},{2,10},{6,14},... | collective-permute-start | bytes 786440 | tf_op jit(solution)/shard_map/ppermute | solution.py:155
  12.6 4.4 %unfold.2 = (bf16[4,128,1152]{2,1,0:T(8,128)(2,1)S(1)}, bf16[128,1152]{1,0:T(8,128)(2,1)}, bf16[128,1152]{1,0:T(8,128)(2,1)}, bf16[128,1152]{1,0:T(8,128)(2,1)},...) fusion(bf16[4,128,1152]{2,1,0:T(8,128)(2,1)S(1)} %broadcast_in_, ...), kind=kCustom, calls=%fused_computation.105 | custom fusion | bytes 7503880 | tf_op jit(solution)/shard_map/unfold/pallas_call | solution.py:66
  18.4 9.6 %collective-permute-start.3 = (bf16[128,1152]{1,0:T(8,128)(2,1)}, bf16[128,1152]{1,0:T(8,128)(2,1)S(1)}, u32[]{:S(2)}, u32[]{:S(2)}) collective-permute-start(bf16[128,1152]{1,0:T(8,128)(2,1)} %get-tuple-element.40), channel_id=1, source_target_pairs={{0,4},{4,8},{8,12},{12,0},{1,5},{5,9},{9,13},{13,1},{2,6},{6,10},{... | collective-permute-start | bytes 884744 | tf_op jit(solution)/shard_map/ppermute | solution.py:155
  31.4 1.8 collective-permute-start.6
  33.3 7.2 %collective-permute-start.5 = (bf16[128,1152]{1,0:T(8,128)(2,1)S(1)}, bf16[128,1152]{1,0:T(8,128)(2,1)S(1)}, u32[]{:S(2)}, u32[]{:S(2)}) collective-permute-start(bf16[128,1152]{1,0:T(8,128)(2,1)S(1)} %copy-done.3), channel_id=1, source_target_pairs={{0,12},{4,0},{8,4},{12,8},{1,13},{5,1},{9,5},{13,9},{2,14},{6,2},{... | collective-permute-start | bytes 884744 | tf_op jit(solution)/shard_map/ppermute | solution.py:155
  40.4 4.6 %collective-permute-start.4 = (bf16[128,1152]{1,0:T(8,128)(2,1)S(1)}, bf16[128,1152]{1,0:T(8,128)(2,1)S(1)}, u32[]{:S(2)}, u32[]{:S(2)}) collective-permute-start(bf16[128,1152]{1,0:T(8,128)(2,1)S(1)} %copy-done.4), channel_id=1, source_target_pairs={{0,8},{4,12},{8,0},{12,4},{1,9},{5,13},{9,1},{13,5},{2,10},{6,14},... | collective-permute-start | bytes 884744 | tf_op jit(solution)/shard_map/ppermute | solution.py:155
  45.0 20.0 %collective-permute-done.4 = bf16[128,1152]{1,0:T(8,128)(2,1)S(1)} collective-permute-done((bf16[128,1152]{1,0:T(8,128)(2,1)S(1)}, bf16[128,1152]{1,0:T(8,128)(2,1)S(1)}, u32[]{:S(2)}, u32[]{:S(2)}) %collective-permute-start.4) | collective-permute-done | bytes 294944 | tf_op jit(solution)/shard_map/ppermute | solution.py:155
  66.1 2.0 collective-permute-start.8
  68.9 2.3 %collective-permute-start.10 = (bf16[128,1024]{1,0:T(8,128)(2,1)S(1)}, bf16[128,1024]{1,0:T(8,128)(2,1)S(1)}, u32[]{:S(2)}, u32[]{:S(2)}) collective-permute-start(bf16[128,1024]{1,0:T(8,128)(2,1)S(1)} %get-tuple-element.51), channel_id=1, source_target_pairs={{0,12},{4,0},{8,4},{12,8},{1,13},{5,1},{9,5},{13,9},{2,14},{6,2},{... | collective-permute-start | bytes 786440 | tf_op jit(solution)/shard_map/ppermute | solution.py:155
  71.2 12.1 %collective-permute-done.8 = bf16[128,1024]{1,0:T(8,128)(2,1)S(1)} collective-permute-done((bf16[128,1024]{1,0:T(8,128)(2,1)S(1)}, bf16[128,1024]{1,0:T(8,128)(2,1)S(1)}, u32[]{:S(2)}, u32[]{:S(2)}) %collective-permute-start.8) | collective-permute-done | bytes 262176 | tf_op jit(solution)/shard_map/ppermute | solution.py:155
  83.3 2.8 %collective-permute-done.9 = bf16[128,1024]{1,0:T(8,128)(2,1)S(1)} collective-permute-done((bf16[128,1024]{1,0:T(8,128)(2,1)S(1)}, bf16[128,1024]{1,0:T(8,128)(2,1)S(1)}, u32[]{:S(2)}, u32[]{:S(2)}) %collective-permute-start.9) | collective-permute-done | bytes 262176 | tf_op jit(solution)/shard_map/ppermute | solution.py:155
  87.7 1.6 collective-permute-start.16
  90.0 4.1 %collective-permute-done.11 = bf16[512,1152]{1,0:T(8,128)(2,1)S(1)} collective-permute-done((bf16[512,1152]{1,0:T(8,128)(2,1)S(1)}, bf16[512,1152]{1,0:T(8,128)(2,1)S(1)}, u32[]{:S(2)}, u32[]{:S(2)}) %collective-permute-start.11) | collective-permute-done | bytes 1179680 | tf_op jit(solution)/shard_map/ppermute | solution.py:158
  94.1 2.0 collective-permute-start.13
  100.0 2.0 collective-permute-done.13
  102.9 6.7 %collective-permute-done.14 = bf16[128,512]{1,0:T(8,128)(2,1)S(1)} collective-permute-done((bf16[128,512]{1,0:T(8,128)(2,1)S(1)}, bf16[128,512]{1,0:T(8,128)(2,1)S(1)}, u32[]{:S(2)}, u32[]{:S(2)}) %collective-permute-start.14) | collective-permute-done | bytes 131104 | tf_op jit(solution)/shard_map/ppermute | solution.py:155
  111.2 15.3 %collective-permute-done.29 = bf16[512,512]{1,0:T(8,128)(2,1)S(1)} collective-permute-done((bf16[512,512]{1,0:T(8,128)(2,1)S(1)}, bf16[512,512]{1,0:T(8,128)(2,1)S(1)}, u32[]{:S(2)}, u32[]{:S(2)}) %collective-permute-start.29) | collective-permute-done | bytes 524320 | tf_op jit(solution)/shard_map/ppermute | solution.py:158
  129.5 2.3 %collective-permute-start.18 = (bf16[128,512]{1,0:T(8,128)(2,1)S(1)}, bf16[128,512]{1,0:T(8,128)(2,1)S(1)}, u32[]{:S(2)}, u32[]{:S(2)}) collective-permute-start(bf16[128,512]{1,0:T(8,128)(2,1)S(1)} %copy-done.9), channel_id=1, source_target_pairs={{0,4},{4,8},{8,12},{12,0},{1,5},{5,9},{9,13},{13,1},{2,6},{6,10},{... | collective-permute-start | bytes 393224 | tf_op jit(solution)/shard_map/ppermute | solution.py:155
  134.7 4.1 %collective-permute-done.18 = bf16[128,512]{1,0:T(8,128)(2,1)S(1)} collective-permute-done((bf16[128,512]{1,0:T(8,128)(2,1)S(1)}, bf16[128,512]{1,0:T(8,128)(2,1)S(1)}, u32[]{:S(2)}, u32[]{:S(2)}) %collective-permute-start.18) | collective-permute-done | bytes 131104 | tf_op jit(solution)/shard_map/ppermute | solution.py:155
  139.0 7.3 %collective-permute-done.19 = bf16[128,512]{1,0:T(8,128)(2,1)S(1)} collective-permute-done((bf16[128,512]{1,0:T(8,128)(2,1)S(1)}, bf16[128,512]{1,0:T(8,128)(2,1)S(1)}, u32[]{:S(2)}, u32[]{:S(2)}) %collective-permute-start.19) | collective-permute-done | bytes 131104 | tf_op jit(solution)/shard_map/ppermute | solution.py:155
  154.3 6.4 %collective-permute-done.30 = bf16[512,512]{1,0:T(8,128)(2,1)S(1)} collective-permute-done((bf16[512,512]{1,0:T(8,128)(2,1)S(1)}, bf16[512,512]{1,0:T(8,128)(2,1)S(1)}, u32[]{:S(2)}, u32[]{:S(2)}) %collective-permute-start.30) | collective-permute-done | bytes 524320 | tf_op jit(solution)/shard_map/ppermute | solution.py:158
  167.5 2.4 %collective-permute-start.24 = (f32[128,1024]{1,0:T(8,128)S(1)}, f32[128,1024]{1,0:T(8,128)S(1)}, u32[]{:S(2)}, u32[]{:S(2)}) collective-permute-start(f32[128,1024]{1,0:T(8,128)S(1)} %get-tuple-element.117), channel_id=1, source_target_pairs={{0,4},{4,8},{1,5},{5,9},{2,6},{6,10},{3,7},{7,11},{16,20},{20,24},... | collective-permute-start | bytes 1572872 | tf_op jit(solution)/shard_map/ppermute | solution.py:127
  170.6 7.9 %collective-permute-done.36 = f32[128,1024]{1,0:T(8,128)S(1)} collective-permute-done((f32[128,1024]{1,0:T(8,128)S(1)}, f32[128,1024]{1,0:T(8,128)S(1)}, u32[]{:S(2)}, u32[]{:S(2)}) %collective-permute-start.36) | collective-permute-done | bytes 524320 | tf_op jit(solution)/shard_map/ppermute | solution.py:127
  178.6 4.4 %collective-permute-start.37 = (f32[128,1024]{1,0:T(8,128)S(1)}, f32[128,1024]{1,0:T(8,128)S(1)}, u32[]{:S(2)}, u32[]{:S(2)}) collective-permute-start(f32[128,1024]{1,0:T(8,128)S(1)} %get-tuple-element.110), channel_id=1, source_target_pairs={{0,4},{4,8},{1,5},{5,9},{2,6},{6,10},{3,7},{7,11},{16,20},{20,24},... | collective-permute-start | bytes 1572872 | tf_op jit(solution)/shard_map/ppermute | solution.py:127
  184.5 5.2 %collective-permute-done.24 = f32[128,1024]{1,0:T(8,128)S(1)} collective-permute-done((f32[128,1024]{1,0:T(8,128)S(1)}, f32[128,1024]{1,0:T(8,128)S(1)}, u32[]{:S(2)}, u32[]{:S(2)}) %collective-permute-start.24) | collective-permute-done | bytes 524320 | tf_op jit(solution)/shard_map/ppermute | solution.py:127
  190.0 4.4 %collective-permute-start.25 = (f32[128,1024]{1,0:T(8,128)S(1)}, f32[128,1024]{1,0:T(8,128)S(1)}, u32[]{:S(2)}, u32[]{:S(2)}) collective-permute-start(f32[128,1024]{1,0:T(8,128)S(1)} %get-tuple-element.115), channel_id=1, source_target_pairs={{0,4},{4,8},{8,12},{1,5},{5,9},{9,13},{2,6},{6,10},{10,14},{3,7},{... | collective-permute-start | bytes 1572872 | tf_op jit(solution)/shard_map/ppermute | solution.py:127
  195.7 5.3 %collective-permute-done.37 = f32[128,1024]{1,0:T(8,128)S(1)} collective-permute-done((f32[128,1024]{1,0:T(8,128)S(1)}, f32[128,1024]{1,0:T(8,128)S(1)}, u32[]{:S(2)}, u32[]{:S(2)}) %collective-permute-start.37) | collective-permute-done | bytes 524320 | tf_op jit(solution)/shard_map/ppermute | solution.py:127
  201.2 4.4 %collective-permute-start.38 = (f32[128,1024]{1,0:T(8,128)S(1)}, f32[128,1024]{1,0:T(8,128)S(1)}, u32[]{:S(2)}, u32[]{:S(2)}) collective-permute-start(f32[128,1024]{1,0:T(8,128)S(1)} %get-tuple-element.108), channel_id=1, source_target_pairs={{0,4},{4,8},{8,12},{1,5},{5,9},{9,13},{2,6},{6,10},{10,14},{3,7},{... | collective-permute-start | bytes 1572872 | tf_op jit(solution)/shard_map/ppermute | solution.py:127
  208.5 3.7 %collective-permute-done.25.refs_1_ = f32[128,1024]{1,0:T(8,128)S(1)} collective-permute-done((f32[128,1024]{1,0:T(8,128)S(1)}, f32[128,1024]{1,0:T(8,128)S(1)}, u32[]{:S(2)}, u32[]{:S(2)}) %collective-permute-start.25) | collective-permute-done | bytes 524320 | tf_op jit(solution)/shard_map/ppermute | solution.py:127
  212.2 11.0 %collective-permute-done.38.refs_4_ = f32[128,1024]{1,0:T(8,128)S(1)} collective-permute-done((f32[128,1024]{1,0:T(8,128)S(1)}, f32[128,1024]{1,0:T(8,128)S(1)}, u32[]{:S(2)}, u32[]{:S(2)}) %collective-permute-start.38) | collective-permute-done | bytes 524320 | tf_op jit(solution)/shard_map/ppermute | solution.py:127
  (153 shorter events, 45.2 us)
Async XLA Ops:
  8.6 20.9 %collective-permute-start.1 = (bf16[128,1024]{1,0:T(8,128)(2,1)}, bf16[128,1024]{1,0:T(8,128)(2,1)}, u32[]{:S(2)}, u32[]{:S(2)}) collective-permute-start(bf16[128,1024]{1,0:T(8,128)(2,1)} %get-tuple-element.71), channel_id=1, source_target_pairs={{0,8},{4,12},{8,0},{12,4},{1,9},{5,13},{9,1},{13,5},{2,10},{6,14},... | collective-permute-start | bytes 786440 | tf_op jit(solution)/shard_map/ppermute | solution.py:155
  11.1 19.3 %collective-permute-start.2 = (bf16[128,1024]{1,0:T(8,128)(2,1)}, bf16[128,1024]{1,0:T(8,128)(2,1)}, u32[]{:S(2)}, u32[]{:S(2)}) collective-permute-start(bf16[128,1024]{1,0:T(8,128)(2,1)} %get-tuple-element.73), channel_id=1, source_target_pairs={{0,12},{4,0},{8,4},{12,8},{1,13},{5,1},{9,5},{13,9},{2,14},{6,2},{... | collective-permute-start | bytes 786440 | tf_op jit(solution)/shard_map/ppermute | solution.py:155
  18.4 26.7 %collective-permute-start.3 = (bf16[128,1152]{1,0:T(8,128)(2,1)}, bf16[128,1152]{1,0:T(8,128)(2,1)S(1)}, u32[]{:S(2)}, u32[]{:S(2)}) collective-permute-start(bf16[128,1152]{1,0:T(8,128)(2,1)} %get-tuple-element.40), channel_id=1, source_target_pairs={{0,4},{4,8},{8,12},{12,0},{1,5},{5,9},{9,13},{13,1},{2,6},{6,10},{... | collective-permute-start | bytes 884744 | tf_op jit(solution)/shard_map/ppermute | solution.py:155
  31.4 34.3 %collective-permute-start.6 = (bf16[512,1024]{1,0:T(8,128)(2,1)S(1)}, bf16[512,1024]{1,0:T(8,128)(2,1)S(1)}, u32[]{:S(2)}, u32[]{:S(2)}) collective-permute-start(bf16[512,1024]{1,0:T(8,128)(2,1)S(1)} %bitcast.95), channel_id=1, source_target_pairs={{0,2},{2,0},{1,3},{3,1},{4,6},{6,4},{5,7},{7,5},{8,10},{10,8},{9,1... | collective-permute-start | bytes 3145736 | tf_op jit(solution)/shard_map/ppermute | solution.py:158
  33.3 32.4 %collective-permute-start.7 = (bf16[512,1024]{1,0:T(8,128)(2,1)S(1)}, bf16[512,1024]{1,0:T(8,128)(2,1)S(1)}, u32[]{:S(2)}, u32[]{:S(2)}) collective-permute-start(bf16[512,1024]{1,0:T(8,128)(2,1)S(1)} %bitcast.96), channel_id=1, source_target_pairs={{0,1},{1,0},{2,3},{3,2},{4,5},{5,4},{6,7},{7,6},{8,9},{9,8},{10,11... | collective-permute-start | bytes 3145736 | tf_op jit(solution)/shard_map/ppermute | solution.py:159
  33.3 31.8 %collective-permute-start.5 = (bf16[128,1152]{1,0:T(8,128)(2,1)S(1)}, bf16[128,1152]{1,0:T(8,128)(2,1)S(1)}, u32[]{:S(2)}, u32[]{:S(2)}) collective-permute-start(bf16[128,1152]{1,0:T(8,128)(2,1)S(1)} %copy-done.3), channel_id=1, source_target_pairs={{0,12},{4,0},{8,4},{12,8},{1,13},{5,1},{9,5},{13,9},{2,14},{6,2},{... | collective-permute-start | bytes 884744 | tf_op jit(solution)/shard_map/ppermute | solution.py:155
  40.4 24.6 %collective-permute-start.4 = (bf16[128,1152]{1,0:T(8,128)(2,1)S(1)}, bf16[128,1152]{1,0:T(8,128)(2,1)S(1)}, u32[]{:S(2)}, u32[]{:S(2)}) collective-permute-start(bf16[128,1152]{1,0:T(8,128)(2,1)S(1)} %copy-done.4), channel_id=1, source_target_pairs={{0,8},{4,12},{8,0},{12,4},{1,9},{5,13},{9,1},{13,5},{2,10},{6,14},... | collective-permute-start | bytes 884744 | tf_op jit(solution)/shard_map/ppermute | solution.py:155
  65.1 28.9 %collective-permute-start.11 = (bf16[512,1152]{1,0:T(8,128)(2,1)S(1)}, bf16[512,1152]{1,0:T(8,128)(2,1)S(1)}, u32[]{:S(2)}, u32[]{:S(2)}) collective-permute-start(bf16[512,1152]{1,0:T(8,128)(2,1)S(1)} %bitcast.116), channel_id=1, source_target_pairs={{0,2},{2,0},{1,3},{3,1},{4,6},{6,4},{5,7},{7,5},{8,10},{10,8},{9,1... | collective-permute-start | bytes 3538952 | tf_op jit(solution)/shard_map/ppermute | solution.py:158
  65.7 28.4 %collective-permute-start.12 = (bf16[512,1152]{1,0:T(8,128)(2,1)S(1)}, bf16[512,1152]{1,0:T(8,128)(2,1)S(1)}, u32[]{:S(2)}, u32[]{:S(2)}) collective-permute-start(bf16[512,1152]{1,0:T(8,128)(2,1)S(1)} %bitcast.117), channel_id=1, source_target_pairs={{0,1},{1,0},{2,3},{3,2},{4,5},{5,4},{6,7},{7,6},{8,9},{9,8},{10,11... | collective-permute-start | bytes 3538952 | tf_op jit(solution)/shard_map/ppermute | solution.py:159
  65.7 20.4 %collective-permute-start.9 = (bf16[128,1024]{1,0:T(8,128)(2,1)S(1)}, bf16[128,1024]{1,0:T(8,128)(2,1)S(1)}, u32[]{:S(2)}, u32[]{:S(2)}) collective-permute-start(bf16[128,1024]{1,0:T(8,128)(2,1)S(1)} %copy-done.5), channel_id=1, source_target_pairs={{0,8},{4,12},{8,0},{12,4},{1,9},{5,13},{9,1},{13,5},{2,10},{6,14},... | collective-permute-start | bytes 786440 | tf_op jit(solution)/shard_map/ppermute | solution.py:155
  66.1 17.2 %collective-permute-start.8 = (bf16[128,1024]{1,0:T(8,128)(2,1)S(1)}, bf16[128,1024]{1,0:T(8,128)(2,1)S(1)}, u32[]{:S(2)}, u32[]{:S(2)}) collective-permute-start(bf16[128,1024]{1,0:T(8,128)(2,1)S(1)} %copy-done.6), channel_id=1, source_target_pairs={{0,4},{4,8},{8,12},{12,0},{1,5},{5,9},{9,13},{13,1},{2,6},{6,10},{... | collective-permute-start | bytes 786440 | tf_op jit(solution)/shard_map/ppermute | solution.py:155
  68.9 18.8 %collective-permute-start.10 = (bf16[128,1024]{1,0:T(8,128)(2,1)S(1)}, bf16[128,1024]{1,0:T(8,128)(2,1)S(1)}, u32[]{:S(2)}, u32[]{:S(2)}) collective-permute-start(bf16[128,1024]{1,0:T(8,128)(2,1)S(1)} %get-tuple-element.51), channel_id=1, source_target_pairs={{0,12},{4,0},{8,4},{12,8},{1,13},{5,1},{9,5},{13,9},{2,14},{6,2},{... | collective-permute-start | bytes 786440 | tf_op jit(solution)/shard_map/ppermute | solution.py:155
  83.3 64.9 %collective-permute-start.31 = (bf16[512,1024]{1,0:T(8,128)(2,1)S(1)}, bf16[512,1024]{1,0:T(8,128)(2,1)S(1)}, u32[]{:S(2)}, u32[]{:S(2)}) collective-permute-start(bf16[512,1024]{1,0:T(8,128)(2,1)S(1)} %collective-permute-done.6), channel_id=1, source_target_pairs={{0,1},{1,0},{2,3},{3,2},{4,5},{5,4},{6,7},{7,6},{8,9},{9,8},{10,11... | collective-permute-start | bytes 3145736 | tf_op jit(solution)/shard_map/ppermute | solution.py:161
  87.7 41.4 %collective-permute-start.16 = (bf16[512,1024]{1,0:T(8,128)(2,1)S(1)}, bf16[512,1024]{1,0:T(8,128)(2,1)S(1)}, u32[]{:S(2)}, u32[]{:S(2)}) collective-permute-start(bf16[512,1024]{1,0:T(8,128)(2,1)S(1)} %bitcast.127), channel_id=1, source_target_pairs={{0,2},{2,0},{1,3},{3,1},{4,6},{6,4},{5,7},{7,5},{8,10},{10,8},{9,1... | collective-permute-start | bytes 3145736 | tf_op jit(solution)/shard_map/ppermute | solution.py:158
  89.2 39.8 %collective-permute-start.17 = (bf16[512,1024]{1,0:T(8,128)(2,1)S(1)}, bf16[512,1024]{1,0:T(8,128)(2,1)S(1)}, u32[]{:S(2)}, u32[]{:S(2)}) collective-permute-start(bf16[512,1024]{1,0:T(8,128)(2,1)S(1)} %bitcast.128), channel_id=1, source_target_pairs={{0,1},{1,0},{2,3},{3,2},{4,5},{5,4},{6,7},{7,6},{8,9},{9,8},{10,11... | collective-permute-start | bytes 3145736 | tf_op jit(solution)/shard_map/ppermute | solution.py:159
  94.1 15.5 %collective-permute-start.15 = (bf16[128,512]{1,0:T(8,128)(2,1)S(1)}, bf16[128,512]{1,0:T(8,128)(2,1)S(1)}, u32[]{:S(2)}, u32[]{:S(2)}) collective-permute-start(bf16[128,512]{1,0:T(8,128)(2,1)S(1)} %copy-done.10), channel_id=1, source_target_pairs={{0,12},{4,0},{8,4},{12,8},{1,13},{5,1},{9,5},{13,9},{2,14},{6,2},{... | collective-permute-start | bytes 393224 | tf_op jit(solution)/shard_map/ppermute | solution.py:155
  109.6 16.9 %collective-permute-start.29 = (bf16[512,512]{1,0:T(8,128)(2,1)S(1)}, bf16[512,512]{1,0:T(8,128)(2,1)S(1)}, u32[]{:S(2)}, u32[]{:S(2)}) collective-permute-start(bf16[512,512]{1,0:T(8,128)(2,1)S(1)} %bitcast.102), channel_id=1, source_target_pairs={{0,2},{2,0},{1,3},{3,1},{4,6},{6,4},{5,7},{7,5},{8,10},{10,8},{9,1... | collective-permute-start | bytes 1572872 | tf_op jit(solution)/shard_map/ppermute | solution.py:158
  110.7 16.2 %collective-permute-start.21 = (bf16[512,512]{1,0:T(8,128)(2,1)S(1)}, bf16[512,512]{1,0:T(8,128)(2,1)S(1)}, u32[]{:S(2)}, u32[]{:S(2)}) collective-permute-start(bf16[512,512]{1,0:T(8,128)(2,1)S(1)} %bitcast.103), channel_id=1, source_target_pairs={{0,1},{1,0},{2,3},{3,2},{4,5},{5,4},{6,7},{7,6},{8,9},{9,8},{10,11... | collective-permute-start | bytes 1572872 | tf_op jit(solution)/shard_map/ppermute | solution.py:159
  126.5 22.1 %collective-permute-start.32 = (bf16[512,1152]{1,0:T(8,128)(2,1)S(1)}, bf16[512,1152]{1,0:T(8,128)(2,1)S(1)}, u32[]{:S(2)}, u32[]{:S(2)}) collective-permute-start(bf16[512,1152]{1,0:T(8,128)(2,1)S(1)} %collective-permute-done.11), channel_id=1, source_target_pairs={{0,1},{1,0},{2,3},{3,2},{4,5},{5,4},{6,7},{7,6},{8,9},{9,8},{10,11... | collective-permute-start | bytes 3538952 | tf_op jit(solution)/shard_map/ppermute | solution.py:161
  126.8 22.7 %collective-permute-start.34 = (bf16[512,512]{1,0:T(8,128)(2,1)S(1)}, bf16[512,512]{1,0:T(8,128)(2,1)S(1)}, u32[]{:S(2)}, u32[]{:S(2)}) collective-permute-start(bf16[512,512]{1,0:T(8,128)(2,1)S(1)} %collective-permute-done.29), channel_id=1, source_target_pairs={{0,1},{1,0},{2,3},{3,2},{4,5},{5,4},{6,7},{7,6},{8,9},{9,8},{10,11... | collective-permute-start | bytes 1572872 | tf_op jit(solution)/shard_map/ppermute | solution.py:161
  129.5 16.8 %collective-permute-start.20 = (bf16[128,512]{1,0:T(8,128)(2,1)S(1)}, bf16[128,512]{1,0:T(8,128)(2,1)S(1)}, u32[]{:S(2)}, u32[]{:S(2)}) collective-permute-start(bf16[128,512]{1,0:T(8,128)(2,1)S(1)} %copy-done.7), channel_id=1, source_target_pairs={{0,12},{4,0},{8,4},{12,8},{1,13},{5,1},{9,5},{13,9},{2,14},{6,2},{... | collective-permute-start | bytes 393224 | tf_op jit(solution)/shard_map/ppermute | solution.py:155
  146.3 16.5 %collective-permute-start.33 = (bf16[512,1024]{1,0:T(8,128)(2,1)S(1)}, bf16[512,1024]{1,0:T(8,128)(2,1)S(1)}, u32[]{:S(2)}, u32[]{:S(2)}) collective-permute-start(bf16[512,1024]{1,0:T(8,128)(2,1)S(1)} %collective-permute-done.16), channel_id=1, source_target_pairs={{0,1},{1,0},{2,3},{3,2},{4,5},{5,4},{6,7},{7,6},{8,9},{9,8},{10,11... | collective-permute-start | bytes 3145736 | tf_op jit(solution)/shard_map/ppermute | solution.py:161
  146.3 14.4 %collective-permute-start.30 = (bf16[512,512]{1,0:T(8,128)(2,1)S(1)}, bf16[512,512]{1,0:T(8,128)(2,1)S(1)}, u32[]{:S(2)}, u32[]{:S(2)}) collective-permute-start(bf16[512,512]{1,0:T(8,128)(2,1)S(1)} %bitcast.109), channel_id=1, source_target_pairs={{0,2},{2,0},{1,3},{3,1},{4,6},{6,4},{5,7},{7,5},{8,10},{10,8},{9,1... | collective-permute-start | bytes 1572872 | tf_op jit(solution)/shard_map/ppermute | solution.py:158
  152.1 15.2 %collective-permute-start.23 = (f32[128,1024]{1,0:T(8,128)S(1)}, f32[128,1024]{1,0:T(8,128)S(1)}, u32[]{:S(2)}, u32[]{:S(2)}) collective-permute-start(f32[128,1024]{1,0:T(8,128)S(1)} %get-tuple-element.119), channel_id=1, source_target_pairs={{0,4},{1,5},{2,6},{3,7},{16,20},{17,21},{18,22},{19,23}} | collective-permute-start | bytes 1572872 | tf_op jit(solution)/shard_map/ppermute | solution.py:127
  167.5 22.3 %collective-permute-start.24 = (f32[128,1024]{1,0:T(8,128)S(1)}, f32[128,1024]{1,0:T(8,128)S(1)}, u32[]{:S(2)}, u32[]{:S(2)}) collective-permute-start(f32[128,1024]{1,0:T(8,128)S(1)} %get-tuple-element.117), channel_id=1, source_target_pairs={{0,4},{4,8},{1,5},{5,9},{2,6},{6,10},{3,7},{7,11},{16,20},{20,24},... | collective-permute-start | bytes 1572872 | tf_op jit(solution)/shard_map/ppermute | solution.py:127
  169.9 19.8 %collective-permute-start.27 = (f32[128,1024]{1,0:T(8,128)S(1)}, f32[128,1024]{1,0:T(8,128)S(1)}, u32[]{:S(2)}, u32[]{:S(2)}) collective-permute-start(f32[128,1024]{1,0:T(8,128)S(1)} %get-tuple-element.116), channel_id=1, source_target_pairs={{12,8},{8,4},{13,9},{9,5},{14,10},{10,6},{15,11},{11,7},{28,24},{2... | collective-permute-start | bytes 1572872 | tf_op jit(solution)/shard_map/ppermute | solution.py:127
  178.6 22.3 %collective-permute-start.37 = (f32[128,1024]{1,0:T(8,128)S(1)}, f32[128,1024]{1,0:T(8,128)S(1)}, u32[]{:S(2)}, u32[]{:S(2)}) collective-permute-start(f32[128,1024]{1,0:T(8,128)S(1)} %get-tuple-element.110), channel_id=1, source_target_pairs={{0,4},{4,8},{1,5},{5,9},{2,6},{6,10},{3,7},{7,11},{16,20},{20,24},... | collective-permute-start | bytes 1572872 | tf_op jit(solution)/shard_map/ppermute | solution.py:127
  183.1 17.9 %collective-permute-start.40 = (f32[128,1024]{1,0:T(8,128)S(1)}, f32[128,1024]{1,0:T(8,128)S(1)}, u32[]{:S(2)}, u32[]{:S(2)}) collective-permute-start(f32[128,1024]{1,0:T(8,128)S(1)} %get-tuple-element.109), channel_id=1, source_target_pairs={{12,8},{8,4},{13,9},{9,5},{14,10},{10,6},{15,11},{11,7},{28,24},{2... | collective-permute-start | bytes 1572872 | tf_op jit(solution)/shard_map/ppermute | solution.py:127
  190.0 22.2 %collective-permute-start.25 = (f32[128,1024]{1,0:T(8,128)S(1)}, f32[128,1024]{1,0:T(8,128)S(1)}, u32[]{:S(2)}, u32[]{:S(2)}) collective-permute-start(f32[128,1024]{1,0:T(8,128)S(1)} %get-tuple-element.115), channel_id=1, source_target_pairs={{0,4},{4,8},{8,12},{1,5},{5,9},{9,13},{2,6},{6,10},{10,14},{3,7},{... | collective-permute-start | bytes 1572872 | tf_op jit(solution)/shard_map/ppermute | solution.py:127
  194.4 17.8 %collective-permute-start.28 = (f32[128,1024]{1,0:T(8,128)S(1)}, f32[128,1024]{1,0:T(8,128)S(1)}, u32[]{:S(2)}, u32[]{:S(2)}) collective-permute-start(f32[128,1024]{1,0:T(8,128)S(1)} %get-tuple-element.113), channel_id=1, source_target_pairs={{12,8},{8,4},{4,0},{13,9},{9,5},{5,1},{14,10},{10,6},{6,2},{15,11}... | collective-permute-start | bytes 1572872 | tf_op jit(solution)/shard_map/ppermute | solution.py:127
  201.2 22.1 %collective-permute-start.38 = (f32[128,1024]{1,0:T(8,128)S(1)}, f32[128,1024]{1,0:T(8,128)S(1)}, u32[]{:S(2)}, u32[]{:S(2)}) collective-permute-start(f32[128,1024]{1,0:T(8,128)S(1)} %get-tuple-element.108), channel_id=1, source_target_pairs={{0,4},{4,8},{8,12},{1,5},{5,9},{9,13},{2,6},{6,10},{10,14},{3,7},{... | collective-permute-start | bytes 1572872 | tf_op jit(solution)/shard_map/ppermute | solution.py:127
  205.6 17.6 %collective-permute-start.41 = (f32[128,1024]{1,0:T(8,128)S(1)}, f32[128,1024]{1,0:T(8,128)S(1)}, u32[]{:S(2)}, u32[]{:S(2)}) collective-permute-start(f32[128,1024]{1,0:T(8,128)S(1)} %get-tuple-element.106), channel_id=1, source_target_pairs={{12,8},{8,4},{4,0},{13,9},{9,5},{5,1},{14,10},{10,6},{6,2},{15,11}... | collective-permute-start | bytes 1572872 | tf_op jit(solution)/shard_map/ppermute | solution.py:127
  (24 other events, 256.6 us)

commit v5 on v4

--- a/solution.py
+++ b/solution.py
@@ -37,7 +37,7 @@
     ins, factor, outs, wide = refs[:planes], refs[planes], refs[planes + 1 : -1], refs[-1]
     rows, _, cells = ins[0].shape
     for shift in range(planes):
-        first = lax.rem(lax.rem(z_ref[0] + shift, planes) * per_plane, BLOCK)
+        first = lax.rem((z_ref[0] ^ shift) * per_plane, BLOCK)
         for h in range(0, cells, LANES):
             wide[...] = ins[shift][:, :, h : h + LANES].astype(jnp.float32).reshape(rows * BLOCK, LANES)
             for n, (start, size) in enumerate(chunks):
@@ -58,7 +58,7 @@
     in_specs = [
         pl.BlockSpec(
             (step, BLOCK, cells),
-            lambda i, z_ref, shift=shift: (i, lax.div(lax.rem(z_ref[0] + shift, planes) * per_plane, BLOCK), 0),
+            lambda i, z_ref, shift=shift: (i, lax.div((z_ref[0] ^ shift) * per_plane, BLOCK), 0),
         )
         for shift in range(planes)
     ]
@@ -142,23 +142,24 @@
     def stacked(parts):
         stack = jnp.zeros((planes,) + parts[0].shape, slab.dtype)
         for shift in range(planes):
-            stack = lax.dynamic_update_slice(stack, parts[shift][None], ((z - shift) % planes, 0, 0))
+            stack = lax.dynamic_update_slice(stack, parts[shift][None], (z ^ shift, 0, 0))
         return stack.reshape(planes * rows, -1)
 
-    came, waits, held = [], [], []
+    came, held = [], []
+    across = pair = None
     for j in range(last + 1):
         arrived = [pieces[j][0]]
         for shift in range(1, planes):
             piece = pieces[j][shift]
             if j:
-                piece = after(piece, came[j - 1][shift], *(waits[j - 2] if j > 1 else ()))
-            arrived.append(lax.ppermute(piece, "z", [(s, (s + shift) % planes) for s in range(planes)]))
+                piece = after(piece, came[j - 1][shift], *([held[j - 2][2]] if j > 1 and shift == 1 else []))
+            arrived.append(lax.ppermute(piece, "z", [(s, s ^ shift) for s in range(planes)]))
         came.append(arrived)
         stack = stacked(arrived)
-        across = lax.ppermute(stack, "y", SWAP)
-        beside = lax.ppermute(stack, "c", SWAP)
-        waits.append((across, beside))
-        held.append([stack, beside, across, lax.ppermute(across, "c", SWAP)])
+        across = lax.ppermute(stack if across is None else after(stack, across), "y", SWAP)
+        beside = lax.ppermute(stack if pair is None else after(stack, pair), "c", SWAP)
+        pair = lax.ppermute(after(across, beside), "c", SWAP)
+        held.append([stack, beside, across, pair])
     flat = [[b[:, : size * cells] for b in held[j]] for j, (_, size) in enumerate(chunks)]
     factors = [b[:, chunks[1][1] * cells :] for b in held[1]]
     sums = [sum(nt_dot(flat[j][0], flat[j][k]) for j in range(last + 1)) for k in range(4)]

time: 225 us -> 257 us (1.14)
  waiting for transfers between devices: 116 us -> 149 us
    ppermute x30, waiting for transfers between devices: 82.8 us -> 112 us  [the longest x15 58.4 us: on_device(): lax.ppermute(piece, 'z', [(s, s ^ shift) for s in range(planes)])]
    ppermute x30, starting transfers between devices: 44.5 us -> 38.7 us  [the longest x15 29.6 us: on_device(): lax.ppermute(piece, 'z', [(s, s ^ shift) for s in range(planes)])]
    ppermute x12, starting transfers between devices: 24.1 us -> 29.8 us  [chain(): got = lax.ppermute(sent, 'z', pairs)]
    ppermute x12, waiting for transfers between devices: 33.2 us -> 37.1 us  [chain(): got = lax.ppermute(sent, 'z', pairs)]
  transfers between devices with their start and end apart: 42 -> 42, of which waited for: 17 -> 20; matrix products, arithmetic and copies ran while one was open for 14% -> 12% of each run, Pallas kernels for 0% -> 0%
where the time goes in v5:
time: 257 us; the launch traced here: 256 us
  waiting for transfers between devices  149 us (58%)
  starting transfers between devices  68.5 us (27%)
  matrix products  21.9 us (9%)
  local copies, waits for them, and re-layouts  13.6 us (5%)
    ppermute x15, waiting for transfers between devices, on_device(): lax.ppermute(piece, 'z', [(s, s ^ shift) for s in range(planes)])  58.4 us
    ppermute x5, waiting for transfers between devices, on_device(): lax.ppermute(stack if across is None else after(stack, across), 'y', SWAP)  50.4 us
    ppermute x12, waiting for transfers between devices, chain(): got = lax.ppermute(sent, 'z', pairs)  37.1 us
    ppermute x12, starting transfers between devices, chain(): got = lax.ppermute(sent, 'z', pairs)  29.8 us
    ppermute x15, starting transfers between devices, on_device(): lax.ppermute(piece, 'z', [(s, s ^ shift) for s in range(planes)])  29.6 us
    dot_general x20, matrix products, nt_dot(): lax.dot_general(a, b, (((1,), (1,)), ((), ())), preferred_element_type=jn...  13.5 us
    pallas_call x2, local copies, waits for them, and re-layouts, unfold(): pl.pallas_call(functools.partial(unfold_kernel, planes, per_plane, chunks...  9.04 us
    dot_general x20, matrix products, tn_dot(): lax.dot_general(a, b, (((0,), (0,)), ((), ())), preferred_element_type=jn...  8.44 us
  transfers between devices with their start and end apart: 42, of which 20 were waited for; matrix products, arithmetic and copies ran while one was open for 12% of the time, Pallas kernels for 0%

profile of v5, /device:TPU:0, one launch (start us, length us, event | category | flops | bytes accessed | tf_op | source)
XLA Modules:
  0.0 256.5 jit_solution(740282009546702533)
XLA Ops:
  0.8 4.7 %unfold.3 = (bf16[4,128,1024]{2,1,0:T(8,128)(2,1)S(1)}, bf16[128,1024]{1,0:T(8,128)(2,1)}, bf16[128,1024]{1,0:T(8,128)(2,1)}, bf16[128,1024]{1,0:T(8,128)(2,1)}) fusion(bf16[4,128,1024]{2,1,0:T(8,128)(2,1)S(1)} %broadcast.6.clone, s32[]{:T(128)S(6)} %select_n.24, s32[1]{0:T(128)} %bitcast.1, bf16[128,64,256]{2,1,0:T(8,128)(2,1)} %param.2, ...), kind=kCustom, calls=%fused_computation.114 | custom fusion | bytes 5275656 | tf_op jit(solution)/shard_map/unfold/pallas_call | solution.py:66
  5.5 3.1 %collective-permute-start = (bf16[128,1024]{1,0:T(8,128)(2,1)}, bf16[128,1024]{1,0:T(8,128)(2,1)}, u32[]{:S(2)}, u32[]{:S(2)}) collective-permute-start(bf16[128,1024]{1,0:T(8,128)(2,1)} %get-tuple-element.95), channel_id=1, source_target_pairs={{0,4},{4,0},{8,12},{12,8},{1,5},{5,1},{9,13},{13,9},{2,6},{6,2},{1... | collective-permute-start | bytes 786440 | tf_op jit(solution)/shard_map/ppermute | solution.py:156
  8.5 2.6 %collective-permute-start.1 = (bf16[128,1024]{1,0:T(8,128)(2,1)}, bf16[128,1024]{1,0:T(8,128)(2,1)}, u32[]{:S(2)}, u32[]{:S(2)}) collective-permute-start(bf16[128,1024]{1,0:T(8,128)(2,1)} %get-tuple-element.97), channel_id=1, source_target_pairs={{0,8},{4,12},{8,0},{12,4},{1,9},{5,13},{9,1},{13,5},{2,10},{6,14},... | collective-permute-start | bytes 786440 | tf_op jit(solution)/shard_map/ppermute | solution.py:156
  11.2 4.3 %unfold.2 = (bf16[4,128,1152]{2,1,0:T(8,128)(2,1)S(1)}, bf16[128,1152]{1,0:T(8,128)(2,1)}, bf16[128,1152]{1,0:T(8,128)(2,1)}, bf16[128,1152]{1,0:T(8,128)(2,1)},...) fusion(bf16[4,128,1152]{2,1,0:T(8,128)(2,1)S(1)} %broadcast_in_, ...), kind=kCustom, calls=%fused_computation.106 | custom fusion | bytes 7503880 | tf_op jit(solution)/shard_map/unfold/pallas_call | solution.py:66
  16.0 4.0 %collective-permute-done = bf16[128,1024]{1,0:T(8,128)(2,1)} collective-permute-done((bf16[128,1024]{1,0:T(8,128)(2,1)}, bf16[128,1024]{1,0:T(8,128)(2,1)}, u32[]{:S(2)}, u32[]{:S(2)}) %collective-permute-start) | collective-permute-done | bytes 262176 | tf_op jit(solution)/shard_map/ppermute | solution.py:156
  20.0 10.2 %collective-permute-done.1 = bf16[128,1024]{1,0:T(8,128)(2,1)} collective-permute-done((bf16[128,1024]{1,0:T(8,128)(2,1)}, bf16[128,1024]{1,0:T(8,128)(2,1)}, u32[]{:S(2)}, u32[]{:S(2)}) %collective-permute-start.1) | collective-permute-done | bytes 262176 | tf_op jit(solution)/shard_map/ppermute | solution.py:156
  30.2 2.5 collective-permute-start.5
  32.7 10.1 %collective-permute-start.4 = (bf16[128,1152]{1,0:T(8,128)(2,1)S(1)}, bf16[128,1152]{1,0:T(8,128)(2,1)S(1)}, u32[]{:S(2)}, u32[]{:S(2)}) collective-permute-start(bf16[128,1152]{1,0:T(8,128)(2,1)S(1)} %copy-done.2), channel_id=1, source_target_pairs={{0,8},{4,12},{8,0},{12,4},{1,9},{5,13},{9,1},{13,5},{2,10},{6,14},... | collective-permute-start | bytes 884744 | tf_op jit(solution)/shard_map/ppermute | solution.py:156
  46.0 1.6 collective-permute-start.6
  47.6 2.3 collective-permute-start.9
  49.9 23.2 %collective-permute-done.4 = bf16[128,1152]{1,0:T(8,128)(2,1)S(1)} collective-permute-done((bf16[128,1152]{1,0:T(8,128)(2,1)S(1)}, bf16[128,1152]{1,0:T(8,128)(2,1)S(1)}, u32[]{:S(2)}, u32[]{:S(2)}) %collective-permute-start.4) | collective-permute-done | bytes 294944 | tf_op jit(solution)/shard_map/ppermute | solution.py:156
  74.7 13.0 %collective-permute-done.8 = bf16[128,1024]{1,0:T(8,128)(2,1)S(1)} collective-permute-done((bf16[128,1024]{1,0:T(8,128)(2,1)S(1)}, bf16[128,1024]{1,0:T(8,128)(2,1)S(1)}, u32[]{:S(2)}, u32[]{:S(2)}) %collective-permute-start.8) | collective-permute-done | bytes 262176 | tf_op jit(solution)/shard_map/ppermute | solution.py:156
  87.9 4.2 %collective-permute-start.7 = (bf16[128,1024]{1,0:T(8,128)(2,1)S(1)}, bf16[128,1024]{1,0:T(8,128)(2,1)S(1)}, u32[]{:S(2)}, u32[]{:S(2)}) collective-permute-start(bf16[128,1024]{1,0:T(8,128)(2,1)S(1)} %copy-done.4), channel_id=1, source_target_pairs={{0,4},{4,0},{8,12},{12,8},{1,5},{5,1},{9,13},{13,9},{2,6},{6,2},{1... | collective-permute-start | bytes 786440 | tf_op jit(solution)/shard_map/ppermute | solution.py:156
  96.0 6.1 %collective-permute-done.7 = bf16[128,1024]{1,0:T(8,128)(2,1)S(1)} collective-permute-done((bf16[128,1024]{1,0:T(8,128)(2,1)S(1)}, bf16[128,1024]{1,0:T(8,128)(2,1)S(1)}, u32[]{:S(2)}, u32[]{:S(2)}) %collective-permute-start.7) | collective-permute-done | bytes 262176 | tf_op jit(solution)/shard_map/ppermute | solution.py:156
  103.0 17.1 %collective-permute-done.10 = bf16[512,1152]{1,0:T(8,128)(2,1)S(1)} collective-permute-done((bf16[512,1152]{1,0:T(8,128)(2,1)S(1)}, bf16[512,1152]{1,0:T(8,128)(2,1)S(1)}, u32[]{:S(2)}, u32[]{:S(2)}) %collective-permute-start.10) | collective-permute-done | bytes 1179680 | tf_op jit(solution)/shard_map/ppermute | solution.py:159
  120.4 1.5 collective-permute-start.14
  123.2 1.9 collective-permute-done.11
  125.6 19.3 %collective-permute-done.14 = bf16[512,1024]{1,0:T(8,128)(2,1)S(1)} collective-permute-done((bf16[512,1024]{1,0:T(8,128)(2,1)S(1)}, bf16[512,1024]{1,0:T(8,128)(2,1)S(1)}, u32[]{:S(2)}, u32[]{:S(2)}) %collective-permute-start.14) | collective-permute-done | bytes 1048608 | tf_op jit(solution)/shard_map/ppermute | solution.py:159
  152.7 5.6 %collective-permute-done.25 = bf16[512,512]{1,0:T(8,128)(2,1)S(1)} collective-permute-done((bf16[512,512]{1,0:T(8,128)(2,1)S(1)}, bf16[512,512]{1,0:T(8,128)(2,1)S(1)}, u32[]{:S(2)}, u32[]{:S(2)}) %collective-permute-start.25) | collective-permute-done | bytes 524320 | tf_op jit(solution)/shard_map/ppermute | solution.py:159
  160.6 8.5 %collective-permute-done.34 = bf16[512,512]{1,0:T(8,128)(2,1)S(1)} collective-permute-done((bf16[512,512]{1,0:T(8,128)(2,1)S(1)}, bf16[512,512]{1,0:T(8,128)(2,1)S(1)}, u32[]{:S(2)}, u32[]{:S(2)}) %collective-permute-start.34) | collective-permute-done | bytes 524320 | tf_op jit(solution)/shard_map/ppermute | solution.py:159
  184.4 2.9 %collective-permute-start.28 = (f32[128,1024]{1,0:T(8,128)S(1)}, f32[128,1024]{1,0:T(8,128)S(1)}, u32[]{:S(2)}, u32[]{:S(2)}) collective-permute-start(f32[128,1024]{1,0:T(8,128)S(1)} %get-tuple-element.145), channel_id=1, source_target_pairs={{0,4},{1,5},{2,6},{3,7},{16,20},{17,21},{18,22},{19,23}} | collective-permute-start | bytes 1572872 | tf_op jit(solution)/shard_map/ppermute | solution.py:127
  191.2 8.3 %collective-permute-done.28 = f32[128,1024]{1,0:T(8,128)S(1)} collective-permute-done((f32[128,1024]{1,0:T(8,128)S(1)}, f32[128,1024]{1,0:T(8,128)S(1)}, u32[]{:S(2)}, u32[]{:S(2)}) %collective-permute-start.28) | collective-permute-done | bytes 524320 | tf_op jit(solution)/shard_map/ppermute | solution.py:127
  200.4 5.0 %collective-permute-start.29 = (f32[128,1024]{1,0:T(8,128)S(1)}, f32[128,1024]{1,0:T(8,128)S(1)}, u32[]{:S(2)}, u32[]{:S(2)}) collective-permute-start(f32[128,1024]{1,0:T(8,128)S(1)} %get-tuple-element.143), channel_id=1, source_target_pairs={{0,4},{4,8},{1,5},{5,9},{2,6},{6,10},{3,7},{7,11},{16,20},{20,24},... | collective-permute-start | bytes 1572872 | tf_op jit(solution)/shard_map/ppermute | solution.py:127
  205.5 5.3 %collective-permute-done.36 = f32[128,1024]{1,0:T(8,128)S(1)} collective-permute-done((f32[128,1024]{1,0:T(8,128)S(1)}, f32[128,1024]{1,0:T(8,128)S(1)}, u32[]{:S(2)}, u32[]{:S(2)}) %collective-permute-start.36) | collective-permute-done | bytes 524320 | tf_op jit(solution)/shard_map/ppermute | solution.py:127
  211.7 5.0 %collective-permute-start.37 = (f32[128,1024]{1,0:T(8,128)S(1)}, f32[128,1024]{1,0:T(8,128)S(1)}, u32[]{:S(2)}, u32[]{:S(2)}) collective-permute-start(f32[128,1024]{1,0:T(8,128)S(1)} %get-tuple-element.136), channel_id=1, source_target_pairs={{0,4},{4,8},{1,5},{5,9},{2,6},{6,10},{3,7},{7,11},{16,20},{20,24},... | collective-permute-start | bytes 1572872 | tf_op jit(solution)/shard_map/ppermute | solution.py:127
  217.1 5.0 %collective-permute-done.29 = f32[128,1024]{1,0:T(8,128)S(1)} collective-permute-done((f32[128,1024]{1,0:T(8,128)S(1)}, f32[128,1024]{1,0:T(8,128)S(1)}, u32[]{:S(2)}, u32[]{:S(2)}) %collective-permute-start.29) | collective-permute-done | bytes 524320 | tf_op jit(solution)/shard_map/ppermute | solution.py:127
  223.6 5.0 %collective-permute-start.30 = (f32[128,1024]{1,0:T(8,128)S(1)}, f32[128,1024]{1,0:T(8,128)S(1)}, u32[]{:S(2)}, u32[]{:S(2)}) collective-permute-start(f32[128,1024]{1,0:T(8,128)S(1)} %get-tuple-element.141), channel_id=1, source_target_pairs={{0,4},{4,8},{8,12},{1,5},{5,9},{9,13},{2,6},{6,10},{10,14},{3,7},{... | collective-permute-start | bytes 1572872 | tf_op jit(solution)/shard_map/ppermute | solution.py:127
  228.6 4.7 %collective-permute-done.37 = f32[128,1024]{1,0:T(8,128)S(1)} collective-permute-done((f32[128,1024]{1,0:T(8,128)S(1)}, f32[128,1024]{1,0:T(8,128)S(1)}, u32[]{:S(2)}, u32[]{:S(2)}) %collective-permute-start.37) | collective-permute-done | bytes 524320 | tf_op jit(solution)/shard_map/ppermute | solution.py:127
  234.8 5.0 %collective-permute-start.38 = (f32[128,1024]{1,0:T(8,128)S(1)}, f32[128,1024]{1,0:T(8,128)S(1)}, u32[]{:S(2)}, u32[]{:S(2)}) collective-permute-start(f32[128,1024]{1,0:T(8,128)S(1)} %get-tuple-element.134), channel_id=1, source_target_pairs={{0,4},{4,8},{8,12},{1,5},{5,9},{9,13},{2,6},{6,10},{10,14},{3,7},{... | collective-permute-start | bytes 1572872 | tf_op jit(solution)/shard_map/ppermute | solution.py:127
  241.4 3.1 %collective-permute-done.30.refs_1_ = f32[128,1024]{1,0:T(8,128)S(1)} collective-permute-done((f32[128,1024]{1,0:T(8,128)S(1)}, f32[128,1024]{1,0:T(8,128)S(1)}, u32[]{:S(2)}, u32[]{:S(2)}) %collective-permute-start.30) | collective-permute-done | bytes 524320 | tf_op jit(solution)/shard_map/ppermute | solution.py:127
  244.5 4.5 %collective-permute-done.41.refs_5_ = f32[128,1024]{1,0:T(8,128)S(1)} collective-permute-done((f32[128,1024]{1,0:T(8,128)S(1)}, f32[128,1024]{1,0:T(8,128)S(1)}, u32[]{:S(2)}, u32[]{:S(2)}) %collective-permute-start.41) | collective-permute-done | bytes 524320 | tf_op jit(solution)/shard_map/ppermute | solution.py:127
  249.0 6.2 %collective-permute-done.38.refs_4_ = f32[128,1024]{1,0:T(8,128)S(1)} collective-permute-done((f32[128,1024]{1,0:T(8,128)S(1)}, f32[128,1024]{1,0:T(8,128)S(1)}, u32[]{:S(2)}, u32[]{:S(2)}) %collective-permute-start.38) | collective-permute-done | bytes 524320 | tf_op jit(solution)/shard_map/ppermute | solution.py:127
  (153 shorter events, 49.2 us)
Async XLA Ops:
  5.5 14.5 %collective-permute-start = (bf16[128,1024]{1,0:T(8,128)(2,1)}, bf16[128,1024]{1,0:T(8,128)(2,1)}, u32[]{:S(2)}, u32[]{:S(2)}) collective-permute-start(bf16[128,1024]{1,0:T(8,128)(2,1)} %get-tuple-element.95), channel_id=1, source_target_pairs={{0,4},{4,0},{8,12},{12,8},{1,5},{5,1},{9,13},{13,9},{2,6},{6,2},{1... | collective-permute-start | bytes 786440 | tf_op jit(solution)/shard_map/ppermute | solution.py:156
  8.5 21.7 %collective-permute-start.1 = (bf16[128,1024]{1,0:T(8,128)(2,1)}, bf16[128,1024]{1,0:T(8,128)(2,1)}, u32[]{:S(2)}, u32[]{:S(2)}) collective-permute-start(bf16[128,1024]{1,0:T(8,128)(2,1)} %get-tuple-element.97), channel_id=1, source_target_pairs={{0,8},{4,12},{8,0},{12,4},{1,9},{5,13},{9,1},{13,5},{2,10},{6,14},... | collective-permute-start | bytes 786440 | tf_op jit(solution)/shard_map/ppermute | solution.py:156
  11.1 19.1 %collective-permute-start.2 = (bf16[128,1024]{1,0:T(8,128)(2,1)}, bf16[128,1024]{1,0:T(8,128)(2,1)}, u32[]{:S(2)}, u32[]{:S(2)}) collective-permute-start(bf16[128,1024]{1,0:T(8,128)(2,1)} %get-tuple-element.99), channel_id=1, source_target_pairs={{0,12},{4,8},{8,4},{12,0},{1,13},{5,9},{9,5},{13,1},{2,14},{6,10},... | collective-permute-start | bytes 786440 | tf_op jit(solution)/shard_map/ppermute | solution.py:156
  30.2 17.4 %collective-permute-start.5 = (bf16[128,1152]{1,0:T(8,128)(2,1)S(1)}, bf16[128,1152]{1,0:T(8,128)(2,1)S(1)}, u32[]{:S(2)}, u32[]{:S(2)}) collective-permute-start(bf16[128,1152]{1,0:T(8,128)(2,1)S(1)} %copy-done.3), channel_id=1, source_target_pairs={{0,12},{4,8},{8,4},{12,0},{1,13},{5,9},{9,5},{13,1},{2,14},{6,10},... | collective-permute-start | bytes 884744 | tf_op jit(solution)/shard_map/ppermute | solution.py:156
  32.7 40.4 %collective-permute-start.4 = (bf16[128,1152]{1,0:T(8,128)(2,1)S(1)}, bf16[128,1152]{1,0:T(8,128)(2,1)S(1)}, u32[]{:S(2)}, u32[]{:S(2)}) collective-permute-start(bf16[128,1152]{1,0:T(8,128)(2,1)S(1)} %copy-done.2), channel_id=1, source_target_pairs={{0,8},{4,12},{8,0},{12,4},{1,9},{5,13},{9,1},{13,5},{2,10},{6,14},... | collective-permute-start | bytes 884744 | tf_op jit(solution)/shard_map/ppermute | solution.py:156
  42.8 30.4 %collective-permute-start.3 = (bf16[128,1152]{1,0:T(8,128)(2,1)S(1)}, bf16[128,1152]{1,0:T(8,128)(2,1)S(1)}, u32[]{:S(2)}, u32[]{:S(2)}) collective-permute-start(bf16[128,1152]{1,0:T(8,128)(2,1)S(1)} %copy-done.1), channel_id=1, source_target_pairs={{0,4},{4,0},{8,12},{12,8},{1,5},{5,1},{9,13},{13,9},{2,6},{6,2},{1... | collective-permute-start | bytes 884744 | tf_op jit(solution)/shard_map/ppermute | solution.py:156
  46.0 41.8 %collective-permute-start.18 = (bf16[512,1024]{1,0:T(8,128)(2,1)S(1)}, bf16[512,1024]{1,0:T(8,128)(2,1)S(1)}, u32[]{:S(2)}, u32[]{:S(2)}) collective-permute-start(bf16[512,1024]{1,0:T(8,128)(2,1)S(1)} %bitcast.95), channel_id=1, source_target_pairs={{0,1},{1,0},{2,3},{3,2},{4,5},{5,4},{6,7},{7,6},{8,9},{9,8},{10,11... | collective-permute-start | bytes 3145736 | tf_op jit(solution)/shard_map/ppermute | solution.py:160
  46.0 41.7 %collective-permute-start.6 = (bf16[512,1024]{1,0:T(8,128)(2,1)S(1)}, bf16[512,1024]{1,0:T(8,128)(2,1)S(1)}, u32[]{:S(2)}, u32[]{:S(2)}) collective-permute-start(bf16[512,1024]{1,0:T(8,128)(2,1)S(1)} %bitcast.96), channel_id=1, source_target_pairs={{0,2},{2,0},{1,3},{3,1},{4,6},{6,4},{5,7},{7,5},{8,10},{10,8},{9,1... | collective-permute-start | bytes 3145736 | tf_op jit(solution)/shard_map/ppermute | solution.py:159
  47.6 25.7 %collective-permute-start.9 = (bf16[128,1024]{1,0:T(8,128)(2,1)S(1)}, bf16[128,1024]{1,0:T(8,128)(2,1)S(1)}, u32[]{:S(2)}, u32[]{:S(2)}) collective-permute-start(bf16[128,1024]{1,0:T(8,128)(2,1)S(1)} %copy-done.6), channel_id=1, source_target_pairs={{0,12},{4,8},{8,4},{12,0},{1,13},{5,9},{9,5},{13,1},{2,14},{6,10},... | collective-permute-start | bytes 786440 | tf_op jit(solution)/shard_map/ppermute | solution.py:156
  73.2 14.6 %collective-permute-start.8 = (bf16[128,1024]{1,0:T(8,128)(2,1)S(1)}, bf16[128,1024]{1,0:T(8,128)(2,1)S(1)}, u32[]{:S(2)}, u32[]{:S(2)}) collective-permute-start(bf16[128,1024]{1,0:T(8,128)(2,1)S(1)} %copy-done.5), channel_id=1, source_target_pairs={{0,8},{4,12},{8,0},{12,4},{1,9},{5,13},{9,1},{13,5},{2,10},{6,14},... | collective-permute-start | bytes 786440 | tf_op jit(solution)/shard_map/ppermute | solution.py:156
  73.3 21.0 %collective-permute-start.13 = (bf16[128,512]{1,0:T(8,128)(2,1)S(1)}, bf16[128,512]{1,0:T(8,128)(2,1)S(1)}, u32[]{:S(2)}, u32[]{:S(2)}) collective-permute-start(bf16[128,512]{1,0:T(8,128)(2,1)S(1)} %copy-done.12), channel_id=1, source_target_pairs={{0,12},{4,8},{8,4},{12,0},{1,13},{5,9},{9,5},{13,1},{2,14},{6,10},... | collective-permute-start | bytes 393224 | tf_op jit(solution)/shard_map/ppermute | solution.py:156
  87.8 15.2 %collective-permute-start.19 = (bf16[512,1024]{1,0:T(8,128)(2,1)S(1)}, bf16[512,1024]{1,0:T(8,128)(2,1)S(1)}, u32[]{:S(2)}, u32[]{:S(2)}) collective-permute-start(bf16[512,1024]{1,0:T(8,128)(2,1)S(1)} %collective-permute-done.6), channel_id=1, source_target_pairs={{0,1},{1,0},{2,3},{3,2},{4,5},{5,4},{6,7},{7,6},{8,9},{9,8},{10,11... | collective-permute-start | bytes 3145736 | tf_op jit(solution)/shard_map/ppermute | solution.py:161
  87.9 14.2 %collective-permute-start.7 = (bf16[128,1024]{1,0:T(8,128)(2,1)S(1)}, bf16[128,1024]{1,0:T(8,128)(2,1)S(1)}, u32[]{:S(2)}, u32[]{:S(2)}) collective-permute-start(bf16[128,1024]{1,0:T(8,128)(2,1)S(1)} %copy-done.4), channel_id=1, source_target_pairs={{0,4},{4,0},{8,12},{12,8},{1,5},{5,1},{9,13},{13,9},{2,6},{6,2},{1... | collective-permute-start | bytes 786440 | tf_op jit(solution)/shard_map/ppermute | solution.py:156
  92.1 28.0 %collective-permute-start.10 = (bf16[512,1152]{1,0:T(8,128)(2,1)S(1)}, bf16[512,1152]{1,0:T(8,128)(2,1)S(1)}, u32[]{:S(2)}, u32[]{:S(2)}) collective-permute-start(bf16[512,1152]{1,0:T(8,128)(2,1)S(1)} %bitcast.116), channel_id=1, source_target_pairs={{0,2},{2,0},{1,3},{3,1},{4,6},{6,4},{5,7},{7,5},{8,10},{10,8},{9,1... | collective-permute-start | bytes 3538952 | tf_op jit(solution)/shard_map/ppermute | solution.py:159
  94.3 57.0 %collective-permute-start.17 = (bf16[128,512]{1,0:T(8,128)(2,1)S(1)}, bf16[128,512]{1,0:T(8,128)(2,1)S(1)}, u32[]{:S(2)}, u32[]{:S(2)}) collective-permute-start(bf16[128,512]{1,0:T(8,128)(2,1)S(1)} %copy-done.7), channel_id=1, source_target_pairs={{0,12},{4,8},{8,4},{12,0},{1,13},{5,9},{9,5},{13,1},{2,14},{6,10},... | collective-permute-start | bytes 393224 | tf_op jit(solution)/shard_map/ppermute | solution.py:156
  94.6 56.7 %collective-permute-start.16 = (bf16[128,512]{1,0:T(8,128)(2,1)S(1)}, bf16[128,512]{1,0:T(8,128)(2,1)S(1)}, u32[]{:S(2)}, u32[]{:S(2)}) collective-permute-start(bf16[128,512]{1,0:T(8,128)(2,1)S(1)} %copy-done.8), channel_id=1, source_target_pairs={{0,8},{4,12},{8,0},{12,4},{1,9},{5,13},{9,1},{13,5},{2,10},{6,14},... | collective-permute-start | bytes 393224 | tf_op jit(solution)/shard_map/ppermute | solution.py:156
  102.9 44.8 %collective-permute-start.20 = (bf16[512,1152]{1,0:T(8,128)(2,1)S(1)}, bf16[512,1152]{1,0:T(8,128)(2,1)S(1)}, u32[]{:S(2)}, u32[]{:S(2)}) collective-permute-start(bf16[512,1152]{1,0:T(8,128)(2,1)S(1)} %bitcast.118), channel_id=1, source_target_pairs={{0,1},{1,0},{2,3},{3,2},{4,5},{5,4},{6,7},{7,6},{8,9},{9,8},{10,11... | collective-permute-start | bytes 3538952 | tf_op jit(solution)/shard_map/ppermute | solution.py:160
  120.4 24.4 %collective-permute-start.14 = (bf16[512,1024]{1,0:T(8,128)(2,1)S(1)}, bf16[512,1024]{1,0:T(8,128)(2,1)S(1)}, u32[]{:S(2)}, u32[]{:S(2)}) collective-permute-start(bf16[512,1024]{1,0:T(8,128)(2,1)S(1)} %bitcast.128), channel_id=1, source_target_pairs={{0,2},{2,0},{1,3},{3,1},{4,6},{6,4},{5,7},{7,5},{8,10},{10,8},{9,1... | collective-permute-start | bytes 3145736 | tf_op jit(solution)/shard_map/ppermute | solution.py:159
  146.2 12.1 %collective-permute-start.25 = (bf16[512,512]{1,0:T(8,128)(2,1)S(1)}, bf16[512,512]{1,0:T(8,128)(2,1)S(1)}, u32[]{:S(2)}, u32[]{:S(2)}) collective-permute-start(bf16[512,512]{1,0:T(8,128)(2,1)S(1)} %bitcast.110), channel_id=1, source_target_pairs={{0,2},{2,0},{1,3},{3,1},{4,6},{6,4},{5,7},{7,5},{8,10},{10,8},{9,1... | collective-permute-start | bytes 1572872 | tf_op jit(solution)/shard_map/ppermute | solution.py:159
  148.7 21.8 %collective-permute-start.21 = (bf16[512,1152]{1,0:T(8,128)(2,1)S(1)}, bf16[512,1152]{1,0:T(8,128)(2,1)S(1)}, u32[]{:S(2)}, u32[]{:S(2)}) collective-permute-start(bf16[512,1152]{1,0:T(8,128)(2,1)S(1)} %collective-permute-done.10), channel_id=1, source_target_pairs={{0,1},{1,0},{2,3},{3,2},{4,5},{5,4},{6,7},{7,6},{8,9},{9,8},{10,11... | collective-permute-start | bytes 3538952 | tf_op jit(solution)/shard_map/ppermute | solution.py:161
  158.3 10.8 %collective-permute-start.34 = (bf16[512,512]{1,0:T(8,128)(2,1)S(1)}, bf16[512,512]{1,0:T(8,128)(2,1)S(1)}, u32[]{:S(2)}, u32[]{:S(2)}) collective-permute-start(bf16[512,512]{1,0:T(8,128)(2,1)S(1)} %bitcast.103), channel_id=1, source_target_pairs={{0,2},{2,0},{1,3},{3,1},{4,6},{6,4},{5,7},{7,5},{8,10},{10,8},{9,1... | collective-permute-start | bytes 1572872 | tf_op jit(solution)/shard_map/ppermute | solution.py:159
  184.4 15.2 %collective-permute-start.28 = (f32[128,1024]{1,0:T(8,128)S(1)}, f32[128,1024]{1,0:T(8,128)S(1)}, u32[]{:S(2)}, u32[]{:S(2)}) collective-permute-start(f32[128,1024]{1,0:T(8,128)S(1)} %get-tuple-element.145), channel_id=1, source_target_pairs={{0,4},{1,5},{2,6},{3,7},{16,20},{17,21},{18,22},{19,23}} | collective-permute-start | bytes 1572872 | tf_op jit(solution)/shard_map/ppermute | solution.py:127
  188.8 16.6 %collective-permute-start.39 = (f32[128,1024]{1,0:T(8,128)S(1)}, f32[128,1024]{1,0:T(8,128)S(1)}, u32[]{:S(2)}, u32[]{:S(2)}) collective-permute-start(f32[128,1024]{1,0:T(8,128)S(1)} %get-tuple-element.137), channel_id=1, source_target_pairs={{12,8},{13,9},{14,10},{15,11},{28,24},{29,25},{30,26},{31,27}} | collective-permute-start | bytes 1572872 | tf_op jit(solution)/shard_map/ppermute | solution.py:127
  189.5 21.3 %collective-permute-start.36 = (f32[128,1024]{1,0:T(8,128)S(1)}, f32[128,1024]{1,0:T(8,128)S(1)}, u32[]{:S(2)}, u32[]{:S(2)}) collective-permute-start(f32[128,1024]{1,0:T(8,128)S(1)} %get-tuple-element.138), channel_id=1, source_target_pairs={{0,4},{1,5},{2,6},{3,7},{16,20},{17,21},{18,22},{19,23}} | collective-permute-start | bytes 1572872 | tf_op jit(solution)/shard_map/ppermute | solution.py:127
  199.7 17.3 %collective-permute-start.32 = (f32[128,1024]{1,0:T(8,128)S(1)}, f32[128,1024]{1,0:T(8,128)S(1)}, u32[]{:S(2)}, u32[]{:S(2)}) collective-permute-start(f32[128,1024]{1,0:T(8,128)S(1)} %get-tuple-element.142), channel_id=1, source_target_pairs={{12,8},{8,4},{13,9},{9,5},{14,10},{10,6},{15,11},{11,7},{28,24},{2... | collective-permute-start | bytes 1572872 | tf_op jit(solution)/shard_map/ppermute | solution.py:127
  200.4 21.6 %collective-permute-start.29 = (f32[128,1024]{1,0:T(8,128)S(1)}, f32[128,1024]{1,0:T(8,128)S(1)}, u32[]{:S(2)}, u32[]{:S(2)}) collective-permute-start(f32[128,1024]{1,0:T(8,128)S(1)} %get-tuple-element.143), channel_id=1, source_target_pairs={{0,4},{4,8},{1,5},{5,9},{2,6},{6,10},{3,7},{7,11},{16,20},{20,24},... | collective-permute-start | bytes 1572872 | tf_op jit(solution)/shard_map/ppermute | solution.py:127
  211.0 17.6 %collective-permute-start.40 = (f32[128,1024]{1,0:T(8,128)S(1)}, f32[128,1024]{1,0:T(8,128)S(1)}, u32[]{:S(2)}, u32[]{:S(2)}) collective-permute-start(f32[128,1024]{1,0:T(8,128)S(1)} %get-tuple-element.135), channel_id=1, source_target_pairs={{12,8},{8,4},{13,9},{9,5},{14,10},{10,6},{15,11},{11,7},{28,24},{2... | collective-permute-start | bytes 1572872 | tf_op jit(solution)/shard_map/ppermute | solution.py:127
  211.7 21.6 %collective-permute-start.37 = (f32[128,1024]{1,0:T(8,128)S(1)}, f32[128,1024]{1,0:T(8,128)S(1)}, u32[]{:S(2)}, u32[]{:S(2)}) collective-permute-start(f32[128,1024]{1,0:T(8,128)S(1)} %get-tuple-element.136), channel_id=1, source_target_pairs={{0,4},{4,8},{1,5},{5,9},{2,6},{6,10},{3,7},{7,11},{16,20},{20,24},... | collective-permute-start | bytes 1572872 | tf_op jit(solution)/shard_map/ppermute | solution.py:127
  222.3 19.1 %collective-permute-start.33 = (f32[128,1024]{1,0:T(8,128)S(1)}, f32[128,1024]{1,0:T(8,128)S(1)}, u32[]{:S(2)}, u32[]{:S(2)}) collective-permute-start(f32[128,1024]{1,0:T(8,128)S(1)} %get-tuple-element.139), channel_id=1, source_target_pairs={{12,8},{8,4},{4,0},{13,9},{9,5},{5,1},{14,10},{10,6},{6,2},{15,11}... | collective-permute-start | bytes 1572872 | tf_op jit(solution)/shard_map/ppermute | solution.py:127
  223.6 21.0 %collective-permute-start.30 = (f32[128,1024]{1,0:T(8,128)S(1)}, f32[128,1024]{1,0:T(8,128)S(1)}, u32[]{:S(2)}, u32[]{:S(2)}) collective-permute-start(f32[128,1024]{1,0:T(8,128)S(1)} %get-tuple-element.141), channel_id=1, source_target_pairs={{0,4},{4,8},{8,12},{1,5},{5,9},{9,13},{2,6},{6,10},{10,14},{3,7},{... | collective-permute-start | bytes 1572872 | tf_op jit(solution)/shard_map/ppermute | solution.py:127
  233.5 15.5 %collective-permute-start.41 = (f32[128,1024]{1,0:T(8,128)S(1)}, f32[128,1024]{1,0:T(8,128)S(1)}, u32[]{:S(2)}, u32[]{:S(2)}) collective-permute-start(f32[128,1024]{1,0:T(8,128)S(1)} %get-tuple-element.132), channel_id=1, source_target_pairs={{12,8},{8,4},{4,0},{13,9},{9,5},{5,1},{14,10},{10,6},{6,2},{15,11}... | collective-permute-start | bytes 1572872 | tf_op jit(solution)/shard_map/ppermute | solution.py:127
  234.8 20.4 %collective-permute-start.38 = (f32[128,1024]{1,0:T(8,128)S(1)}, f32[128,1024]{1,0:T(8,128)S(1)}, u32[]{:S(2)}, u32[]{:S(2)}) collective-permute-start(f32[128,1024]{1,0:T(8,128)S(1)} %get-tuple-element.134), channel_id=1, source_target_pairs={{0,4},{4,8},{8,12},{1,5},{5,9},{9,13},{2,6},{6,10},{10,14},{3,7},{... | collective-permute-start | bytes 1572872 | tf_op jit(solution)/shard_map/ppermute | solution.py:127
  (24 other events, 371.2 us)

commit v6 on v4

--- a/solution.py
+++ b/solution.py
@@ -12,12 +12,13 @@
 AXES = ("groups", "z", "y", "c")
 BLOCK = 16
 LANES = 128
+WINDOW = 4
 SWAP = [(0, 1), (1, 0)]
 
 
 def chunks_of(per_plane):
-    unit = per_plane // 4
-    sizes = [unit] * 3 + ([unit // 2] * 2 if unit % 2 == 0 else [unit])
+    unit = per_plane // 16
+    sizes = [5 * unit, 5 * unit, 4 * unit, 2 * unit] if unit else [1] * per_plane
     return [(sum(sizes[:i]), size) for i, size in enumerate(sizes)]
 
 
@@ -145,15 +146,15 @@
             stack = lax.dynamic_update_slice(stack, parts[shift][None], ((z - shift) % planes, 0, 0))
         return stack.reshape(planes * rows, -1)
 
-    came, waits, held = [], [], []
+    sent, waits, held = [], [], []
     for j in range(last + 1):
         arrived = [pieces[j][0]]
         for shift in range(1, planes):
             piece = pieces[j][shift]
-            if j:
-                piece = after(piece, came[j - 1][shift], *(waits[j - 2] if j > 1 else ()))
-            arrived.append(lax.ppermute(piece, "z", [(s, (s + shift) % planes) for s in range(planes)]))
-        came.append(arrived)
+            if len(sent) >= WINDOW:
+                piece = after(piece, sent[-WINDOW], *(waits[min(j, last - 1) - 2] if j > 1 else ()))
+            sent.append(lax.ppermute(piece, "z", [(s, (s + shift) % planes) for s in range(planes)]))
+            arrived.append(sent[-1])
         stack = stacked(arrived)
         across = lax.ppermute(stack, "y", SWAP)
         beside = lax.ppermute(stack, "c", SWAP)

time: 225 us -> 224 us (level); the launches traced: 225 us -> 221 us
  starting transfers between devices: 68.6 us -> 66.1 us
    ppermute x15 -> x12, starting transfers between devices: 38.2 us -> 29.3 us  [on_device(): lax.ppermute(piece, 'z', [(s, (s + shift) % planes) for s in range(planes)])]
    ppermute x15 -> x12, waiting for transfers between devices: 57 us -> 63.8 us  [on_device(): lax.ppermute(piece, 'z', [(s, (s + shift) % planes) for s in range(planes)])]
    ppermute x12, starting transfers between devices: 24.1 us -> 30.6 us  [chain(): got = lax.ppermute(sent, 'z', pairs)]
    ppermute x5 -> x4, waiting for transfers between devices: 25.7 us -> 20.2 us  [on_device(): across = lax.ppermute(stack, 'y', SWAP)]
    dot_general x20 -> x16, matrix products: 12.8 us -> 12 us  [nt_dot(): lax.dot_general(a, b, (((1,), (1,)), ((), ())), preferred_element_type=jn...]
    dot_general x20 -> x16, matrix products: 8.38 us -> 7.59 us  [tn_dot(): lax.dot_general(a, b, (((0,), (0,)), ((), ())), preferred_element_type=jn...]
    ppermute x5 -> x4, starting transfers between devices: 5.2 us -> 5.31 us  [on_device(): across = lax.ppermute(stack, 'y', SWAP)]
  transfers between devices with their start and end apart: 42 -> 36, of which waited for: 17 -> 16; matrix products, arithmetic and copies ran while one was open for 14% -> 13% of each run, Pallas kernels for 0% -> 0%
where the time goes in v6:
time: 224 us; the launch traced here: 221 us
  waiting for transfers between devices  116 us (52%)
  starting transfers between devices  66.1 us (30%)
  matrix products  19.6 us (9%)
  local copies, waits for them, and re-layouts  14.1 us (6%)
  other arithmetic  2.46 us (1%)
    ppermute x12, waiting for transfers between devices, on_device(): lax.ppermute(piece, 'z', [(s, (s + shift) % planes) for s in range(planes)])  63.8 us
    ppermute x12, waiting for transfers between devices, chain(): got = lax.ppermute(sent, 'z', pairs)  32.2 us
    ppermute x12, starting transfers between devices, chain(): got = lax.ppermute(sent, 'z', pairs)  30.6 us
    ppermute x12, starting transfers between devices, on_device(): lax.ppermute(piece, 'z', [(s, (s + shift) % planes) for s in range(planes)])  29.3 us
    ppermute x4, waiting for transfers between devices, on_device(): across = lax.ppermute(stack, 'y', SWAP)  20.2 us
    dot_general x16, matrix products, nt_dot(): lax.dot_general(a, b, (((1,), (1,)), ((), ())), preferred_element_type=jn...  12 us
    pallas_call x2, local copies, waits for them, and re-layouts, unfold(): pl.pallas_call(functools.partial(unfold_kernel, planes, per_plane, chunks...  8.83 us
    dot_general x16, matrix products, tn_dot(): lax.dot_general(a, b, (((0,), (0,)), ((), ())), preferred_element_type=jn...  7.59 us
  transfers between devices with their start and end apart: 36, of which 16 were waited for; matrix products, arithmetic and copies ran while one was open for 13% of the time, Pallas kernels for 0%

profile of v6, /device:TPU:0, one launch (start us, length us, event | category | flops | bytes accessed | tf_op | source)
XLA Modules:
  0.0 221.1 jit_solution(13754148553640349063)
XLA Ops:
  1.4 5.8 %unfold.2 = (bf16[4,128,1408]{2,1,0:T(8,128)(2,1)S(1)}, bf16[128,1408]{1,0:T(8,128)(2,1)}, bf16[128,1408]{1,0:T(8,128)(2,1)}, bf16[128,1408]{1,0:T(8,128)(2,1)},...) fusion(bf16[4,128,1408]{2,1,0:T(8,128)(2,1)S(1)} %broadcast_in_, ...), kind=kCustom, calls=%fused_computation.100 | custom fusion | bytes 7241736 | tf_op jit(solution)/shard_map/unfold/pallas_call | solution.py:67
  7.2 3.1 %collective-permute-start.3 = (bf16[128,1408]{1,0:T(8,128)(2,1)}, bf16[128,1408]{1,0:T(8,128)(2,1)}, u32[]{:S(2)}, u32[]{:S(2)}) collective-permute-start(bf16[128,1408]{1,0:T(8,128)(2,1)} %get-tuple-element.61), channel_id=1, source_target_pairs={{0,4},{4,8},{8,12},{12,0},{1,5},{5,9},{9,13},{13,1},{2,6},{6,10},{... | collective-permute-start | bytes 1081352 | tf_op jit(solution)/shard_map/ppermute | solution.py:156
  10.4 3.0 %unfold.3 = (bf16[4,128,1280]{2,1,0:T(8,128)(2,1)S(1)}, bf16[128,1280]{1,0:T(8,128)(2,1)}, bf16[128,1280]{1,0:T(8,128)(2,1)}, bf16[128,1280]{1,0:T(8,128)(2,1)}) fusion(bf16[4,128,1280]{2,1,0:T(8,128)(2,1)S(1)} %broadcast_in_dim.60, s32[]{:T(128)S(6)} %select_n.99, s32[1]{0:T(128)} %bitcast.1, bf16[128,64,256]{2,1,0:T(8,128)(2,1)S(1)} %copy-done, ...), kind=kCustom, calls=%fused_computation.104 | custom fusion | bytes 5537800 | tf_op jit(solution)/shard_map/unfold/pallas_call | solution.py:67
  13.4 1.6 collective-permute-start
  16.0 2.9 %collective-permute-start.2 = (bf16[128,1280]{1,0:T(8,128)(2,1)}, bf16[128,1280]{1,0:T(8,128)(2,1)}, u32[]{:S(2)}, u32[]{:S(2)}) collective-permute-start(bf16[128,1280]{1,0:T(8,128)(2,1)} %get-tuple-element.57), channel_id=1, source_target_pairs={{0,12},{4,0},{8,4},{12,8},{1,13},{5,1},{9,5},{13,9},{2,14},{6,2},{... | collective-permute-start | bytes 983048 | tf_op jit(solution)/shard_map/ppermute | solution.py:156
  19.2 9.8 %collective-permute-done = bf16[128,1280]{1,0:T(8,128)(2,1)} collective-permute-done((bf16[128,1280]{1,0:T(8,128)(2,1)}, bf16[128,1280]{1,0:T(8,128)(2,1)}, u32[]{:S(2)}, u32[]{:S(2)}) %collective-permute-start) | collective-permute-done | bytes 327712 | tf_op jit(solution)/shard_map/ppermute | solution.py:156
  30.0 12.2 %collective-permute-done.1 = bf16[128,1280]{1,0:T(8,128)(2,1)} collective-permute-done((bf16[128,1280]{1,0:T(8,128)(2,1)}, bf16[128,1280]{1,0:T(8,128)(2,1)}, u32[]{:S(2)}, u32[]{:S(2)}) %collective-permute-start.1) | collective-permute-done | bytes 327712 | tf_op jit(solution)/shard_map/ppermute | solution.py:156
  44.3 1.6 collective-permute-start.6
  45.9 5.4 %collective-permute-start.4 = (bf16[128,1408]{1,0:T(8,128)(2,1)S(1)}, bf16[128,1408]{1,0:T(8,128)(2,1)S(1)}, u32[]{:S(2)}, u32[]{:S(2)}) collective-permute-start(bf16[128,1408]{1,0:T(8,128)(2,1)S(1)} %copy-done.2), channel_id=1, source_target_pairs={{0,8},{4,12},{8,0},{12,4},{1,9},{5,13},{9,1},{13,5},{2,10},{6,14},... | collective-permute-start | bytes 1081352 | tf_op jit(solution)/shard_map/ppermute | solution.py:156
  51.3 3.4 %collective-permute-start.5 = (bf16[128,1408]{1,0:T(8,128)(2,1)S(1)}, bf16[128,1408]{1,0:T(8,128)(2,1)S(1)}, u32[]{:S(2)}, u32[]{:S(2)}) collective-permute-start(bf16[128,1408]{1,0:T(8,128)(2,1)S(1)} %copy-done.1), channel_id=1, source_target_pairs={{0,12},{4,0},{8,4},{12,8},{1,13},{5,1},{9,5},{13,9},{2,14},{6,2},{... | collective-permute-start | bytes 1081352 | tf_op jit(solution)/shard_map/ppermute | solution.py:156
  55.7 12.6 %collective-permute-done.4 = bf16[128,1408]{1,0:T(8,128)(2,1)S(1)} collective-permute-done((bf16[128,1408]{1,0:T(8,128)(2,1)S(1)}, bf16[128,1408]{1,0:T(8,128)(2,1)S(1)}, u32[]{:S(2)}, u32[]{:S(2)}) %collective-permute-start.4) | collective-permute-done | bytes 360480 | tf_op jit(solution)/shard_map/ppermute | solution.py:156
  69.0 7.0 %collective-permute-done.6 = bf16[512,1280]{1,0:T(8,128)(2,1)S(1)} collective-permute-done((bf16[512,1280]{1,0:T(8,128)(2,1)S(1)}, bf16[512,1280]{1,0:T(8,128)(2,1)S(1)}, u32[]{:S(2)}, u32[]{:S(2)}) %collective-permute-start.6) | collective-permute-done | bytes 1310752 | tf_op jit(solution)/shard_map/ppermute | solution.py:159
  76.0 6.4 %collective-permute-start.8 = (bf16[128,1024]{1,0:T(8,128)(2,1)S(1)}, bf16[128,1024]{1,0:T(8,128)(2,1)S(1)}, u32[]{:S(2)}, u32[]{:S(2)}) collective-permute-start(bf16[128,1024]{1,0:T(8,128)(2,1)S(1)} %copy-done.5), channel_id=1, source_target_pairs={{0,4},{4,8},{8,12},{12,0},{1,5},{5,9},{9,13},{13,1},{2,6},{6,10},{... | collective-permute-start | bytes 786440 | tf_op jit(solution)/shard_map/ppermute | solution.py:156
  84.5 8.1 %collective-permute-done.11 = bf16[128,512]{1,0:T(8,128)(2,1)S(1)} collective-permute-done((bf16[128,512]{1,0:T(8,128)(2,1)S(1)}, bf16[128,512]{1,0:T(8,128)(2,1)S(1)}, u32[]{:S(2)}, u32[]{:S(2)}) %collective-permute-start.11) | collective-permute-done | bytes 131104 | tf_op jit(solution)/shard_map/ppermute | solution.py:156
  92.7 8.6 %collective-permute-done.9 = bf16[128,1024]{1,0:T(8,128)(2,1)S(1)} collective-permute-done((bf16[128,1024]{1,0:T(8,128)(2,1)S(1)}, bf16[128,1024]{1,0:T(8,128)(2,1)S(1)}, u32[]{:S(2)}, u32[]{:S(2)}) %collective-permute-start.9) | collective-permute-done | bytes 262176 | tf_op jit(solution)/shard_map/ppermute | solution.py:156
  101.3 4.0 %collective-permute-start.12 = (bf16[128,512]{1,0:T(8,128)(2,1)S(1)}, bf16[128,512]{1,0:T(8,128)(2,1)S(1)}, u32[]{:S(2)}, u32[]{:S(2)}) collective-permute-start(bf16[128,512]{1,0:T(8,128)(2,1)S(1)} %copy-done.7), channel_id=1, source_target_pairs={{0,8},{4,12},{8,0},{12,4},{1,9},{5,13},{9,1},{13,5},{2,10},{6,14},... | collective-permute-start | bytes 393224 | tf_op jit(solution)/shard_map/ppermute | solution.py:156
  105.4 3.0 %collective-permute-done.10 = bf16[128,1024]{1,0:T(8,128)(2,1)S(1)} collective-permute-done((bf16[128,1024]{1,0:T(8,128)(2,1)S(1)}, bf16[128,1024]{1,0:T(8,128)(2,1)S(1)}, u32[]{:S(2)}, u32[]{:S(2)}) %collective-permute-start.10) | collective-permute-done | bytes 262176 | tf_op jit(solution)/shard_map/ppermute | solution.py:156
  108.4 1.6 collective-permute-start.24
  110.7 4.9 %collective-permute-done.12 = bf16[128,512]{1,0:T(8,128)(2,1)S(1)} collective-permute-done((bf16[128,512]{1,0:T(8,128)(2,1)S(1)}, bf16[128,512]{1,0:T(8,128)(2,1)S(1)}, u32[]{:S(2)}, u32[]{:S(2)}) %collective-permute-start.12) | collective-permute-done | bytes 131104 | tf_op jit(solution)/shard_map/ppermute | solution.py:156
  115.9 4.7 %collective-permute-done.13 = bf16[128,512]{1,0:T(8,128)(2,1)S(1)} collective-permute-done((bf16[128,512]{1,0:T(8,128)(2,1)S(1)}, bf16[128,512]{1,0:T(8,128)(2,1)S(1)}, u32[]{:S(2)}, u32[]{:S(2)}) %collective-permute-start.13) | collective-permute-done | bytes 131104 | tf_op jit(solution)/shard_map/ppermute | solution.py:156
  128.9 13.2 %collective-permute-done.25 = bf16[512,512]{1,0:T(8,128)(2,1)S(1)} collective-permute-done((bf16[512,512]{1,0:T(8,128)(2,1)S(1)}, bf16[512,512]{1,0:T(8,128)(2,1)S(1)}, u32[]{:S(2)}, u32[]{:S(2)}) %collective-permute-start.25) | collective-permute-done | bytes 524320 | tf_op jit(solution)/shard_map/ppermute | solution.py:159
  146.4 6.0 %collective-permute-start.17 = (f32[128,1024]{1,0:T(8,128)S(1)}, f32[128,1024]{1,0:T(8,128)S(1)}, u32[]{:S(2)}, u32[]{:S(2)}) collective-permute-start(f32[128,1024]{1,0:T(8,128)S(1)} %get-tuple-element.95), channel_id=1, source_target_pairs={{0,4},{1,5},{2,6},{3,7},{16,20},{17,21},{18,22},{19,23}} | collective-permute-start | bytes 1572872 | tf_op jit(solution)/shard_map/ppermute | solution.py:128
  161.7 2.9 %collective-permute-done.17 = f32[128,1024]{1,0:T(8,128)S(1)} collective-permute-done((f32[128,1024]{1,0:T(8,128)S(1)}, f32[128,1024]{1,0:T(8,128)S(1)}, u32[]{:S(2)}, u32[]{:S(2)}) %collective-permute-start.17) | collective-permute-done | bytes 524320 | tf_op jit(solution)/shard_map/ppermute | solution.py:128
  164.8 4.4 %collective-permute-start.18 = (f32[128,1024]{1,0:T(8,128)S(1)}, f32[128,1024]{1,0:T(8,128)S(1)}, u32[]{:S(2)}, u32[]{:S(2)}) collective-permute-start(f32[128,1024]{1,0:T(8,128)S(1)} %get-tuple-element.93), channel_id=1, source_target_pairs={{0,4},{4,8},{1,5},{5,9},{2,6},{6,10},{3,7},{7,11},{16,20},{20,24},... | collective-permute-start | bytes 1572872 | tf_op jit(solution)/shard_map/ppermute | solution.py:128
  170.5 5.4 %collective-permute-done.30 = f32[128,1024]{1,0:T(8,128)S(1)} collective-permute-done((f32[128,1024]{1,0:T(8,128)S(1)}, f32[128,1024]{1,0:T(8,128)S(1)}, u32[]{:S(2)}, u32[]{:S(2)}) %collective-permute-start.30) | collective-permute-done | bytes 524320 | tf_op jit(solution)/shard_map/ppermute | solution.py:128
  176.0 4.4 %collective-permute-start.31 = (f32[128,1024]{1,0:T(8,128)S(1)}, f32[128,1024]{1,0:T(8,128)S(1)}, u32[]{:S(2)}, u32[]{:S(2)}) collective-permute-start(f32[128,1024]{1,0:T(8,128)S(1)} %get-tuple-element.86), channel_id=1, source_target_pairs={{0,4},{4,8},{1,5},{5,9},{2,6},{6,10},{3,7},{7,11},{16,20},{20,24},... | collective-permute-start | bytes 1572872 | tf_op jit(solution)/shard_map/ppermute | solution.py:128
  181.7 5.4 %collective-permute-done.18 = f32[128,1024]{1,0:T(8,128)S(1)} collective-permute-done((f32[128,1024]{1,0:T(8,128)S(1)}, f32[128,1024]{1,0:T(8,128)S(1)}, u32[]{:S(2)}, u32[]{:S(2)}) %collective-permute-start.18) | collective-permute-done | bytes 524320 | tf_op jit(solution)/shard_map/ppermute | solution.py:128
  187.3 4.4 %collective-permute-start.19 = (f32[128,1024]{1,0:T(8,128)S(1)}, f32[128,1024]{1,0:T(8,128)S(1)}, u32[]{:S(2)}, u32[]{:S(2)}) collective-permute-start(f32[128,1024]{1,0:T(8,128)S(1)} %get-tuple-element.91), channel_id=1, source_target_pairs={{0,4},{4,8},{8,12},{1,5},{5,9},{9,13},{2,6},{6,10},{10,14},{3,7},{... | collective-permute-start | bytes 1572872 | tf_op jit(solution)/shard_map/ppermute | solution.py:128
  193.0 5.3 %collective-permute-done.31 = f32[128,1024]{1,0:T(8,128)S(1)} collective-permute-done((f32[128,1024]{1,0:T(8,128)S(1)}, f32[128,1024]{1,0:T(8,128)S(1)}, u32[]{:S(2)}, u32[]{:S(2)}) %collective-permute-start.31) | collective-permute-done | bytes 524320 | tf_op jit(solution)/shard_map/ppermute | solution.py:128
  198.6 4.4 %collective-permute-start.32 = (f32[128,1024]{1,0:T(8,128)S(1)}, f32[128,1024]{1,0:T(8,128)S(1)}, u32[]{:S(2)}, u32[]{:S(2)}) collective-permute-start(f32[128,1024]{1,0:T(8,128)S(1)} %get-tuple-element.84), channel_id=1, source_target_pairs={{0,4},{4,8},{8,12},{1,5},{5,9},{9,13},{2,6},{6,10},{10,14},{3,7},{... | collective-permute-start | bytes 1572872 | tf_op jit(solution)/shard_map/ppermute | solution.py:128
  206.6 2.9 %collective-permute-done.19.refs_1_ = f32[128,1024]{1,0:T(8,128)S(1)} collective-permute-done((f32[128,1024]{1,0:T(8,128)S(1)}, f32[128,1024]{1,0:T(8,128)S(1)}, u32[]{:S(2)}, u32[]{:S(2)}) %collective-permute-start.19) | collective-permute-done | bytes 524320 | tf_op jit(solution)/shard_map/ppermute | solution.py:128
  209.6 10.3 %collective-permute-done.32.refs_4_ = f32[128,1024]{1,0:T(8,128)S(1)} collective-permute-done((f32[128,1024]{1,0:T(8,128)S(1)}, f32[128,1024]{1,0:T(8,128)S(1)}, u32[]{:S(2)}, u32[]{:S(2)}) %collective-permute-start.32) | collective-permute-done | bytes 524320 | tf_op jit(solution)/shard_map/ppermute | solution.py:128
  (120 shorter events, 41.2 us)
Async XLA Ops:
  7.2 47.5 %collective-permute-start.3 = (bf16[128,1408]{1,0:T(8,128)(2,1)}, bf16[128,1408]{1,0:T(8,128)(2,1)}, u32[]{:S(2)}, u32[]{:S(2)}) collective-permute-start(bf16[128,1408]{1,0:T(8,128)(2,1)} %get-tuple-element.61), channel_id=1, source_target_pairs={{0,4},{4,8},{8,12},{12,0},{1,5},{5,9},{9,13},{13,1},{2,6},{6,10},{... | collective-permute-start | bytes 1081352 | tf_op jit(solution)/shard_map/ppermute | solution.py:156
  13.4 15.6 %collective-permute-start = (bf16[128,1280]{1,0:T(8,128)(2,1)}, bf16[128,1280]{1,0:T(8,128)(2,1)}, u32[]{:S(2)}, u32[]{:S(2)}) collective-permute-start(bf16[128,1280]{1,0:T(8,128)(2,1)} %get-tuple-element.53), channel_id=1, source_target_pairs={{0,4},{4,8},{8,12},{12,0},{1,5},{5,9},{9,13},{13,1},{2,6},{6,10},{... | collective-permute-start | bytes 983048 | tf_op jit(solution)/shard_map/ppermute | solution.py:156
  15.0 27.2 %collective-permute-start.1 = (bf16[128,1280]{1,0:T(8,128)(2,1)}, bf16[128,1280]{1,0:T(8,128)(2,1)}, u32[]{:S(2)}, u32[]{:S(2)}) collective-permute-start(bf16[128,1280]{1,0:T(8,128)(2,1)} %get-tuple-element.55), channel_id=1, source_target_pairs={{0,8},{4,12},{8,0},{12,4},{1,9},{5,13},{9,1},{13,5},{2,10},{6,14},... | collective-permute-start | bytes 983048 | tf_op jit(solution)/shard_map/ppermute | solution.py:156
  16.0 27.2 %collective-permute-start.2 = (bf16[128,1280]{1,0:T(8,128)(2,1)}, bf16[128,1280]{1,0:T(8,128)(2,1)}, u32[]{:S(2)}, u32[]{:S(2)}) collective-permute-start(bf16[128,1280]{1,0:T(8,128)(2,1)} %get-tuple-element.57), channel_id=1, source_target_pairs={{0,12},{4,0},{8,4},{12,8},{1,13},{5,1},{9,5},{13,9},{2,14},{6,2},{... | collective-permute-start | bytes 983048 | tf_op jit(solution)/shard_map/ppermute | solution.py:156
  44.3 31.7 %collective-permute-start.6 = (bf16[512,1280]{1,0:T(8,128)(2,1)S(1)}, bf16[512,1280]{1,0:T(8,128)(2,1)S(1)}, u32[]{:S(2)}, u32[]{:S(2)}) collective-permute-start(bf16[512,1280]{1,0:T(8,128)(2,1)S(1)} %bitcast.74), channel_id=1, source_target_pairs={{0,2},{2,0},{1,3},{3,1},{4,6},{6,4},{5,7},{7,5},{8,10},{10,8},{9,1... | collective-permute-start | bytes 3932168 | tf_op jit(solution)/shard_map/ppermute | solution.py:159
  45.9 30.1 %collective-permute-start.7 = (bf16[512,1280]{1,0:T(8,128)(2,1)S(1)}, bf16[512,1280]{1,0:T(8,128)(2,1)S(1)}, u32[]{:S(2)}, u32[]{:S(2)}) collective-permute-start(bf16[512,1280]{1,0:T(8,128)(2,1)S(1)} %bitcast.75), channel_id=1, source_target_pairs={{0,1},{1,0},{2,3},{3,2},{4,5},{5,4},{6,7},{7,6},{8,9},{9,8},{10,11... | collective-permute-start | bytes 3932168 | tf_op jit(solution)/shard_map/ppermute | solution.py:160
  45.9 22.4 %collective-permute-start.4 = (bf16[128,1408]{1,0:T(8,128)(2,1)S(1)}, bf16[128,1408]{1,0:T(8,128)(2,1)S(1)}, u32[]{:S(2)}, u32[]{:S(2)}) collective-permute-start(bf16[128,1408]{1,0:T(8,128)(2,1)S(1)} %copy-done.2), channel_id=1, source_target_pairs={{0,8},{4,12},{8,0},{12,4},{1,9},{5,13},{9,1},{13,5},{2,10},{6,14},... | collective-permute-start | bytes 1081352 | tf_op jit(solution)/shard_map/ppermute | solution.py:156
  51.3 17.1 %collective-permute-start.5 = (bf16[128,1408]{1,0:T(8,128)(2,1)S(1)}, bf16[128,1408]{1,0:T(8,128)(2,1)S(1)}, u32[]{:S(2)}, u32[]{:S(2)}) collective-permute-start(bf16[128,1408]{1,0:T(8,128)(2,1)S(1)} %copy-done.1), channel_id=1, source_target_pairs={{0,12},{4,0},{8,4},{12,8},{1,13},{5,1},{9,5},{13,9},{2,14},{6,2},{... | collective-permute-start | bytes 1081352 | tf_op jit(solution)/shard_map/ppermute | solution.py:156
  68.4 53.5 %collective-permute-start.23 = (bf16[512,1408]{1,0:T(8,128)(2,1)S(1)}, bf16[512,1408]{1,0:T(8,128)(2,1)S(1)}, u32[]{:S(2)}, u32[]{:S(2)}) collective-permute-start(bf16[512,1408]{1,0:T(8,128)(2,1)S(1)} %bitcast.88), channel_id=1, source_target_pairs={{0,2},{2,0},{1,3},{3,1},{4,6},{6,4},{5,7},{7,5},{8,10},{10,8},{9,1... | collective-permute-start | bytes 4325384 | tf_op jit(solution)/shard_map/ppermute | solution.py:159
  69.0 55.1 %collective-permute-start.14 = (bf16[512,1408]{1,0:T(8,128)(2,1)S(1)}, bf16[512,1408]{1,0:T(8,128)(2,1)S(1)}, u32[]{:S(2)}, u32[]{:S(2)}) collective-permute-start(bf16[512,1408]{1,0:T(8,128)(2,1)S(1)} %bitcast.89), channel_id=1, source_target_pairs={{0,1},{1,0},{2,3},{3,2},{4,5},{5,4},{6,7},{7,6},{8,9},{9,8},{10,11... | collective-permute-start | bytes 4325384 | tf_op jit(solution)/shard_map/ppermute | solution.py:160
  76.0 16.6 %collective-permute-start.8 = (bf16[128,1024]{1,0:T(8,128)(2,1)S(1)}, bf16[128,1024]{1,0:T(8,128)(2,1)S(1)}, u32[]{:S(2)}, u32[]{:S(2)}) collective-permute-start(bf16[128,1024]{1,0:T(8,128)(2,1)S(1)} %copy-done.5), channel_id=1, source_target_pairs={{0,4},{4,8},{8,12},{12,0},{1,5},{5,9},{9,13},{13,1},{2,6},{6,10},{... | collective-permute-start | bytes 786440 | tf_op jit(solution)/shard_map/ppermute | solution.py:156
  83.4 17.9 %collective-permute-start.9 = (bf16[128,1024]{1,0:T(8,128)(2,1)S(1)}, bf16[128,1024]{1,0:T(8,128)(2,1)S(1)}, u32[]{:S(2)}, u32[]{:S(2)}) collective-permute-start(bf16[128,1024]{1,0:T(8,128)(2,1)S(1)} %copy-done.4), channel_id=1, source_target_pairs={{0,8},{4,12},{8,0},{12,4},{1,9},{5,13},{9,1},{13,5},{2,10},{6,14},... | collective-permute-start | bytes 786440 | tf_op jit(solution)/shard_map/ppermute | solution.py:156
  92.6 15.8 %collective-permute-start.10 = (bf16[128,1024]{1,0:T(8,128)(2,1)S(1)}, bf16[128,1024]{1,0:T(8,128)(2,1)S(1)}, u32[]{:S(2)}, u32[]{:S(2)}) collective-permute-start(bf16[128,1024]{1,0:T(8,128)(2,1)S(1)} %copy-done.3), channel_id=1, source_target_pairs={{0,12},{4,0},{8,4},{12,8},{1,13},{5,1},{9,5},{13,9},{2,14},{6,2},{... | collective-permute-start | bytes 786440 | tf_op jit(solution)/shard_map/ppermute | solution.py:156
  92.6 66.1 %collective-permute-start.26 = (bf16[512,1280]{1,0:T(8,128)(2,1)S(1)}, bf16[512,1280]{1,0:T(8,128)(2,1)S(1)}, u32[]{:S(2)}, u32[]{:S(2)}) collective-permute-start(bf16[512,1280]{1,0:T(8,128)(2,1)S(1)} %collective-permute-done.6), channel_id=1, source_target_pairs={{0,1},{1,0},{2,3},{3,2},{4,5},{5,4},{6,7},{7,6},{8,9},{9,8},{10,11... | collective-permute-start | bytes 3932168 | tf_op jit(solution)/shard_map/ppermute | solution.py:162
  101.3 14.2 %collective-permute-start.12 = (bf16[128,512]{1,0:T(8,128)(2,1)S(1)}, bf16[128,512]{1,0:T(8,128)(2,1)S(1)}, u32[]{:S(2)}, u32[]{:S(2)}) collective-permute-start(bf16[128,512]{1,0:T(8,128)(2,1)S(1)} %copy-done.7), channel_id=1, source_target_pairs={{0,8},{4,12},{8,0},{12,4},{1,9},{5,13},{9,1},{13,5},{2,10},{6,14},... | collective-permute-start | bytes 393224 | tf_op jit(solution)/shard_map/ppermute | solution.py:156
  108.4 44.0 %collective-permute-start.24 = (bf16[512,1024]{1,0:T(8,128)(2,1)S(1)}, bf16[512,1024]{1,0:T(8,128)(2,1)S(1)}, u32[]{:S(2)}, u32[]{:S(2)}) collective-permute-start(bf16[512,1024]{1,0:T(8,128)(2,1)S(1)} %bitcast.98), channel_id=1, source_target_pairs={{0,2},{2,0},{1,3},{3,1},{4,6},{6,4},{5,7},{7,5},{8,10},{10,8},{9,1... | collective-permute-start | bytes 3145736 | tf_op jit(solution)/shard_map/ppermute | solution.py:159
  120.6 24.0 %collective-permute-start.15 = (bf16[512,1024]{1,0:T(8,128)(2,1)S(1)}, bf16[512,1024]{1,0:T(8,128)(2,1)S(1)}, u32[]{:S(2)}, u32[]{:S(2)}) collective-permute-start(bf16[512,1024]{1,0:T(8,128)(2,1)S(1)} %bitcast.100), channel_id=1, source_target_pairs={{0,1},{1,0},{2,3},{3,2},{4,5},{5,4},{6,7},{7,6},{8,9},{9,8},{10,11... | collective-permute-start | bytes 3145736 | tf_op jit(solution)/shard_map/ppermute | solution.py:160
  122.0 20.1 %collective-permute-start.25 = (bf16[512,512]{1,0:T(8,128)(2,1)S(1)}, bf16[512,512]{1,0:T(8,128)(2,1)S(1)}, u32[]{:S(2)}, u32[]{:S(2)}) collective-permute-start(bf16[512,512]{1,0:T(8,128)(2,1)S(1)} %bitcast.82), channel_id=1, source_target_pairs={{0,2},{2,0},{1,3},{3,1},{4,6},{6,4},{5,7},{7,5},{8,10},{10,8},{9,1... | collective-permute-start | bytes 1572872 | tf_op jit(solution)/shard_map/ppermute | solution.py:159
  124.1 18.3 %collective-permute-start.16 = (bf16[512,512]{1,0:T(8,128)(2,1)S(1)}, bf16[512,512]{1,0:T(8,128)(2,1)S(1)}, u32[]{:S(2)}, u32[]{:S(2)}) collective-permute-start(bf16[512,512]{1,0:T(8,128)(2,1)S(1)} %bitcast.83), channel_id=1, source_target_pairs={{0,1},{1,0},{2,3},{3,2},{4,5},{5,4},{6,7},{7,6},{8,9},{9,8},{10,11... | collective-permute-start | bytes 1572872 | tf_op jit(solution)/shard_map/ppermute | solution.py:160
  142.0 14.9 %collective-permute-start.27 = (bf16[512,1408]{1,0:T(8,128)(2,1)S(1)}, bf16[512,1408]{1,0:T(8,128)(2,1)S(1)}, u32[]{:S(2)}, u32[]{:S(2)}) collective-permute-start(bf16[512,1408]{1,0:T(8,128)(2,1)S(1)} %collective-permute-done.23), channel_id=1, source_target_pairs={{0,1},{1,0},{2,3},{3,2},{4,5},{5,4},{6,7},{7,6},{8,9},{9,8},{10,11... | collective-permute-start | bytes 4325384 | tf_op jit(solution)/shard_map/ppermute | solution.py:162
  142.4 13.2 %collective-permute-start.29 = (bf16[512,512]{1,0:T(8,128)(2,1)S(1)}, bf16[512,512]{1,0:T(8,128)(2,1)S(1)}, u32[]{:S(2)}, u32[]{:S(2)}) collective-permute-start(bf16[512,512]{1,0:T(8,128)(2,1)S(1)} %collective-permute-done.25), channel_id=1, source_target_pairs={{0,1},{1,0},{2,3},{3,2},{4,5},{5,4},{6,7},{7,6},{8,9},{9,8},{10,11... | collective-permute-start | bytes 1572872 | tf_op jit(solution)/shard_map/ppermute | solution.py:162
  146.4 18.3 %collective-permute-start.17 = (f32[128,1024]{1,0:T(8,128)S(1)}, f32[128,1024]{1,0:T(8,128)S(1)}, u32[]{:S(2)}, u32[]{:S(2)}) collective-permute-start(f32[128,1024]{1,0:T(8,128)S(1)} %get-tuple-element.95), channel_id=1, source_target_pairs={{0,4},{1,5},{2,6},{3,7},{16,20},{17,21},{18,22},{19,23}} | collective-permute-start | bytes 1572872 | tf_op jit(solution)/shard_map/ppermute | solution.py:128
  159.6 16.2 %collective-permute-start.30 = (f32[128,1024]{1,0:T(8,128)S(1)}, f32[128,1024]{1,0:T(8,128)S(1)}, u32[]{:S(2)}, u32[]{:S(2)}) collective-permute-start(f32[128,1024]{1,0:T(8,128)S(1)} %get-tuple-element.88), channel_id=1, source_target_pairs={{0,4},{1,5},{2,6},{3,7},{16,20},{17,21},{18,22},{19,23}} | collective-permute-start | bytes 1572872 | tf_op jit(solution)/shard_map/ppermute | solution.py:128
  161.0 14.9 %collective-permute-start.33 = (f32[128,1024]{1,0:T(8,128)S(1)}, f32[128,1024]{1,0:T(8,128)S(1)}, u32[]{:S(2)}, u32[]{:S(2)}) collective-permute-start(f32[128,1024]{1,0:T(8,128)S(1)} %get-tuple-element.87), channel_id=1, source_target_pairs={{12,8},{13,9},{14,10},{15,11},{28,24},{29,25},{30,26},{31,27}} | collective-permute-start | bytes 1572872 | tf_op jit(solution)/shard_map/ppermute | solution.py:128
  164.8 22.3 %collective-permute-start.18 = (f32[128,1024]{1,0:T(8,128)S(1)}, f32[128,1024]{1,0:T(8,128)S(1)}, u32[]{:S(2)}, u32[]{:S(2)}) collective-permute-start(f32[128,1024]{1,0:T(8,128)S(1)} %get-tuple-element.93), channel_id=1, source_target_pairs={{0,4},{4,8},{1,5},{5,9},{2,6},{6,10},{3,7},{7,11},{16,20},{20,24},... | collective-permute-start | bytes 1572872 | tf_op jit(solution)/shard_map/ppermute | solution.py:128
  169.2 17.9 %collective-permute-start.21 = (f32[128,1024]{1,0:T(8,128)S(1)}, f32[128,1024]{1,0:T(8,128)S(1)}, u32[]{:S(2)}, u32[]{:S(2)}) collective-permute-start(f32[128,1024]{1,0:T(8,128)S(1)} %get-tuple-element.92), channel_id=1, source_target_pairs={{12,8},{8,4},{13,9},{9,5},{14,10},{10,6},{15,11},{11,7},{28,24},{2... | collective-permute-start | bytes 1572872 | tf_op jit(solution)/shard_map/ppermute | solution.py:128
  176.0 22.3 %collective-permute-start.31 = (f32[128,1024]{1,0:T(8,128)S(1)}, f32[128,1024]{1,0:T(8,128)S(1)}, u32[]{:S(2)}, u32[]{:S(2)}) collective-permute-start(f32[128,1024]{1,0:T(8,128)S(1)} %get-tuple-element.86), channel_id=1, source_target_pairs={{0,4},{4,8},{1,5},{5,9},{2,6},{6,10},{3,7},{7,11},{16,20},{20,24},... | collective-permute-start | bytes 1572872 | tf_op jit(solution)/shard_map/ppermute | solution.py:128
  180.4 17.9 %collective-permute-start.34 = (f32[128,1024]{1,0:T(8,128)S(1)}, f32[128,1024]{1,0:T(8,128)S(1)}, u32[]{:S(2)}, u32[]{:S(2)}) collective-permute-start(f32[128,1024]{1,0:T(8,128)S(1)} %get-tuple-element.85), channel_id=1, source_target_pairs={{12,8},{8,4},{13,9},{9,5},{14,10},{10,6},{15,11},{11,7},{28,24},{2... | collective-permute-start | bytes 1572872 | tf_op jit(solution)/shard_map/ppermute | solution.py:128
  187.3 22.2 %collective-permute-start.19 = (f32[128,1024]{1,0:T(8,128)S(1)}, f32[128,1024]{1,0:T(8,128)S(1)}, u32[]{:S(2)}, u32[]{:S(2)}) collective-permute-start(f32[128,1024]{1,0:T(8,128)S(1)} %get-tuple-element.91), channel_id=1, source_target_pairs={{0,4},{4,8},{8,12},{1,5},{5,9},{9,13},{2,6},{6,10},{10,14},{3,7},{... | collective-permute-start | bytes 1572872 | tf_op jit(solution)/shard_map/ppermute | solution.py:128
  191.7 17.8 %collective-permute-start.22 = (f32[128,1024]{1,0:T(8,128)S(1)}, f32[128,1024]{1,0:T(8,128)S(1)}, u32[]{:S(2)}, u32[]{:S(2)}) collective-permute-start(f32[128,1024]{1,0:T(8,128)S(1)} %get-tuple-element.89), channel_id=1, source_target_pairs={{12,8},{8,4},{4,0},{13,9},{9,5},{5,1},{14,10},{10,6},{6,2},{15,11}... | collective-permute-start | bytes 1572872 | tf_op jit(solution)/shard_map/ppermute | solution.py:128
  198.6 21.3 %collective-permute-start.32 = (f32[128,1024]{1,0:T(8,128)S(1)}, f32[128,1024]{1,0:T(8,128)S(1)}, u32[]{:S(2)}, u32[]{:S(2)}) collective-permute-start(f32[128,1024]{1,0:T(8,128)S(1)} %get-tuple-element.84), channel_id=1, source_target_pairs={{0,4},{4,8},{8,12},{1,5},{5,9},{9,13},{2,6},{6,10},{10,14},{3,7},{... | collective-permute-start | bytes 1572872 | tf_op jit(solution)/shard_map/ppermute | solution.py:128
  203.0 16.9 %collective-permute-start.35 = (f32[128,1024]{1,0:T(8,128)S(1)}, f32[128,1024]{1,0:T(8,128)S(1)}, u32[]{:S(2)}, u32[]{:S(2)}) collective-permute-start(f32[128,1024]{1,0:T(8,128)S(1)} %get-tuple-element.82), channel_id=1, source_target_pairs={{12,8},{8,4},{4,0},{13,9},{9,5},{5,1},{14,10},{10,6},{6,2},{15,11}... | collective-permute-start | bytes 1572872 | tf_op jit(solution)/shard_map/ppermute | solution.py:128
  (14 other events, 206.9 us)

commit v7 on v6

--- a/solution.py
+++ b/solution.py
@@ -18,7 +18,7 @@
 
 def chunks_of(per_plane):
     unit = per_plane // 16
-    sizes = [5 * unit, 5 * unit, 4 * unit, 2 * unit] if unit else [1] * per_plane
+    sizes = [4 * unit, 5 * unit, 5 * unit, 2 * unit] if unit else [1] * per_plane
     return [(sum(sizes[:i]), size) for i, size in enumerate(sizes)]
 
 
@@ -118,7 +118,7 @@
 
 def chain(planes, z, sums, up):
     rows = sums.shape[0] // planes
-    got = None
+    got = first = None
     for step in range(1, planes):
         plane = planes - step + z if up else z - planes + step
         sent = lax.dynamic_slice_in_dim(sums, jnp.clip(plane, 0, planes - 1) * rows, rows, 0)
@@ -126,7 +126,8 @@
             sent = sent + got
         pairs = [(i, i + 1) for i in range(step)] if up else [(planes - 1 - i, planes - 2 - i) for i in range(step)]
         got = lax.ppermute(sent, "z", pairs)
-    return got
+        first = got if first is None else first
+    return got, first
 
 
 def on_device(planes, slab, factor):
@@ -138,7 +139,8 @@
     per_plane = species // planes
     chunks = chunks_of(per_plane)
     last = len(chunks) - 1
-    pieces = unfold(slab, factor, z, planes, chunks[:1], None) + unfold(slab, factor, z, planes, chunks[1:], 0)
+    pieces = unfold(slab, factor, z, planes, chunks[:1], None)
+    pieces += unfold(slab, after(factor, pieces[0]), z, planes, chunks[1:], 0)
 
     def stacked(parts):
         stack = jnp.zeros((planes,) + parts[0].shape, slab.dtype)
@@ -159,16 +161,23 @@
         across = lax.ppermute(stack, "y", SWAP)
         beside = lax.ppermute(stack, "c", SWAP)
         waits.append((across, beside))
-        held.append([stack, beside, across, lax.ppermute(across, "c", SWAP)])
-    flat = [[b[:, : size * cells] for b in held[j]] for j, (_, size) in enumerate(chunks)]
-    factors = [b[:, chunks[1][1] * cells :] for b in held[1]]
-    sums = [sum(nt_dot(flat[j][0], flat[j][k]) for j in range(last + 1)) for k in range(4)]
-    parts = []
-    for pair in range(2):
-        both = jnp.concatenate(sums[2 * pair : 2 * pair + 2], axis=1)
-        parts.append(lax.dynamic_slice_in_dim(both, z * rows, rows, 0))
-        parts.append(chain(planes, z, both, True))
-        parts.append(chain(planes, z, both, False))
+        held.append([stack, beside, across])
+    flat = [[b[:, : size * cells] for b in held[j][:2]] for j, (_, size) in enumerate(chunks)]
+    sums = [sum(nt_dot(flat[j][0], flat[j][k]) for j in range(last + 1)) for k in range(2)]
+    parts, gate = [], None
+    for half in range(2):
+        if half:
+            for j in range(last + 1):
+                across = after(held[j][2], *gate) if j >= last - 1 else held[j][2]
+                held[j].append(lax.ppermute(across, "c", SWAP))
+                flat[j] += [b[:, : chunks[j][1] * cells] for b in held[j][2:]]
+            sums = [sum(nt_dot(flat[j][0], flat[j][k]) for j in range(last + 1)) for k in range(2, 4)]
+        both = jnp.concatenate(sums, axis=1)
+        up, first_up = chain(planes, z, both, True)
+        down, first_down = chain(planes, z, both, False)
+        gate = (first_up, first_down)
+        parts += [lax.dynamic_slice_in_dim(both, z * rows, rows, 0), up, down]
+    factors = after([b[:, chunks[1][1] * cells :] for b in held[1]], *gate)
     gram = finish(planes, total, place, parts)
     own = per_plane // 4
     whole = [sum(tn_dot(flat[j][k], factors[k]) for k in range(4)) for j in range(last + 1)]

time: 224 us -> 224 us (level)
  waiting for transfers between devices: 116 us -> 106 us
  local copies, waits for them, and re-layouts: 14.1 us -> 23.5 us
  other arithmetic: 2.46 us -> 7.43 us
  starting transfers between devices: 66.1 us -> 61.5 us
    ppermute x12, waiting for transfers between devices: 32.2 us -> 13.8 us  [chain(): got = lax.ppermute(sent, 'z', pairs)]
    unnamed x20 -> x86, local copies, waits for them, and re-layouts: 0.66 us -> 9.51 us
    ppermute x4, waiting for transfers between devices: 20.2 us -> 25.8 us  [on_device(): across = lax.ppermute(stack, 'y', SWAP)]
    add x4, other arithmetic: 0.77 us -> 4.66 us  [chain(): sent = sent + got]
    slice x0 -> x4, local copies, waits for them, and re-layouts: none -> 3.66 us  [on_device(): factors = after([b[:, chunks[1][1] * cells:] for b in held[1]], *gate)]
    pallas_call x2 -> x1, local copies, waits for them, and re-layouts: 8.83 us -> 5.65 us  [unfold(): pl.pallas_call(functools.partial(unfold_kernel, planes, per_plane, chunks...]
    ppermute x12, waiting for transfers between devices: 63.8 us -> 66.3 us  [on_device(): lax.ppermute(piece, 'z', [(s, (s + shift) % planes) for s in range(planes)])]
  transfers between devices with their start and end apart: 36 -> 36, of which waited for: 16 -> 11; matrix products, arithmetic and copies ran while one was open for 13% -> 18% of each run, Pallas kernels for 0% -> 0%
where the time goes in v7:
time: 224 us; the launch traced here: 223 us
  waiting for transfers between devices  106 us (47%)
  starting transfers between devices  61.5 us (27%)
  local copies, waits for them, and re-layouts  23.5 us (10%)
  matrix products  19.7 us (9%)
  other arithmetic  7.43 us (3%)
  Pallas kernels  3.21 us (1%)
    ppermute x12, waiting for transfers between devices, on_device(): lax.ppermute(piece, 'z', [(s, (s + shift) % planes) for s in range(planes)])  66.3 us
    ppermute x12, starting transfers between devices, chain(): got = lax.ppermute(sent, 'z', pairs)  28.8 us
    ppermute x12, starting transfers between devices, on_device(): lax.ppermute(piece, 'z', [(s, (s + shift) % planes) for s in range(planes)])  28 us
    ppermute x4, waiting for transfers between devices, on_device(): across = lax.ppermute(stack, 'y', SWAP)  25.8 us
    ppermute x12, waiting for transfers between devices, chain(): got = lax.ppermute(sent, 'z', pairs)  13.8 us
    dot_general x16, matrix products, nt_dot(): lax.dot_general(a, b, (((1,), (1,)), ((), ())), preferred_element_type=jn...  12.1 us
    unnamed x86, local copies, waits for them, and re-layouts  9.51 us
    dot_general x16, matrix products, tn_dot(): lax.dot_general(a, b, (((0,), (0,)), ((), ())), preferred_element_type=jn...  7.62 us
  transfers between devices with their start and end apart: 36, of which 11 were waited for; matrix products, arithmetic and copies ran while one was open for 18% of the time, Pallas kernels for 0%

profile of v7, /device:TPU:0, one launch (start us, length us, event | category | flops | bytes accessed | tf_op | source)
XLA Modules:
  0.0 222.9 jit_solution(2746451136036466258)
XLA Ops:
  0.6 2.2 copy-done
  3.6 2.0 unfold.2
  5.6 3.1 %collective-permute-start = (bf16[128,1024]{1,0:T(8,128)(2,1)S(1)}, bf16[128,1024]{1,0:T(8,128)(2,1)}, u32[]{:S(2)}, u32[]{:S(2)}) collective-permute-start(bf16[128,1024]{1,0:T(8,128)(2,1)S(1)} %get-tuple-element.34), channel_id=1, source_target_pairs={{0,4},{4,8},{8,12},{12,0},{1,5},{5,9},{9,13},{13,1},{2,6},{6,10},{... | collective-permute-start | bytes 786440 | tf_op jit(solution)/shard_map/ppermute | solution.py:158
  8.6 2.6 %collective-permute-start.1 = (bf16[128,1024]{1,0:T(8,128)(2,1)S(1)}, bf16[128,1024]{1,0:T(8,128)(2,1)}, u32[]{:S(2)}, u32[]{:S(2)}) collective-permute-start(bf16[128,1024]{1,0:T(8,128)(2,1)S(1)} %get-tuple-element.35), channel_id=1, source_target_pairs={{0,8},{4,12},{8,0},{12,4},{1,9},{5,13},{9,1},{13,5},{2,10},{6,14},... | collective-permute-start | bytes 786440 | tf_op jit(solution)/shard_map/ppermute | solution.py:158
  11.2 1.3 collective-permute-start.2
  12.7 5.6 %unfold.3 = (bf16[4,128,1408]{2,1,0:T(8,128)(2,1)S(1)}, bf16[128,1408]{1,0:T(8,128)(2,1)S(1)}, bf16[128,1408]{1,0:T(8,128)(2,1)S(1)}, bf16[128,1408]{1,0:T(8,128...) fusion(bf16[4,128,1408]{2,1,0:T(8,128)(2,1)S(1)} %broadcast_in_, ...), kind=kCustom, calls=%fused_computation.101 | custom fusion | bytes 7503880 | tf_op jit(solution)/shard_map/unfold/pallas_call | solution.py:67
  21.5 7.8 %collective-permute-done.1 = bf16[128,1024]{1,0:T(8,128)(2,1)} collective-permute-done((bf16[128,1024]{1,0:T(8,128)(2,1)S(1)}, bf16[128,1024]{1,0:T(8,128)(2,1)}, u32[]{:S(2)}, u32[]{:S(2)}) %collective-permute-start.1) | collective-permute-done | bytes 262176 | tf_op jit(solution)/shard_map/ppermute | solution.py:158
  31.4 1.8 collective-permute-start.6
  33.2 7.2 %collective-permute-start.5 = (bf16[128,1408]{1,0:T(8,128)(2,1)S(1)}, bf16[128,1408]{1,0:T(8,128)(2,1)S(1)}, u32[]{:S(2)}, u32[]{:S(2)}) collective-permute-start(bf16[128,1408]{1,0:T(8,128)(2,1)S(1)} %get-tuple-element.43), channel_id=1, source_target_pairs={{0,12},{4,0},{8,4},{12,8},{1,13},{5,1},{9,5},{13,9},{2,14},{6,2},{... | collective-permute-start | bytes 1081352 | tf_op jit(solution)/shard_map/ppermute | solution.py:158
  40.4 5.9 %collective-permute-start.4 = (bf16[128,1408]{1,0:T(8,128)(2,1)S(1)}, bf16[128,1408]{1,0:T(8,128)(2,1)S(1)}, u32[]{:S(2)}, u32[]{:S(2)}) collective-permute-start(bf16[128,1408]{1,0:T(8,128)(2,1)S(1)} %get-tuple-element.41), channel_id=1, source_target_pairs={{0,8},{4,12},{8,0},{12,4},{1,9},{5,13},{9,1},{13,5},{2,10},{6,14},... | collective-permute-start | bytes 1081352 | tf_op jit(solution)/shard_map/ppermute | solution.py:158
  47.4 22.9 %collective-permute-done.4 = bf16[128,1408]{1,0:T(8,128)(2,1)S(1)} collective-permute-done((bf16[128,1408]{1,0:T(8,128)(2,1)S(1)}, bf16[128,1408]{1,0:T(8,128)(2,1)S(1)}, u32[]{:S(2)}, u32[]{:S(2)}) %collective-permute-start.4) | collective-permute-done | bytes 360480 | tf_op jit(solution)/shard_map/ppermute | solution.py:158
  72.1 3.8 %collective-permute-start.10 = (bf16[128,1280]{1,0:T(8,128)(2,1)S(1)}, bf16[128,1280]{1,0:T(8,128)(2,1)S(1)}, u32[]{:S(2)}, u32[]{:S(2)}) collective-permute-start(bf16[128,1280]{1,0:T(8,128)(2,1)S(1)} %copy-done.37), channel_id=1, source_target_pairs={{0,12},{4,0},{8,4},{12,8},{1,13},{5,1},{9,5},{13,9},{2,14},{6,2},{... | collective-permute-start | bytes 983048 | tf_op jit(solution)/shard_map/ppermute | solution.py:158
  75.8 10.0 %collective-permute-done.11 = bf16[128,512]{1,0:T(8,128)(2,1)S(1)} collective-permute-done((bf16[128,512]{1,0:T(8,128)(2,1)S(1)}, bf16[128,512]{1,0:T(8,128)(2,1)S(1)}, u32[]{:S(2)}, u32[]{:S(2)}) %collective-permute-start.11) | collective-permute-done | bytes 131104 | tf_op jit(solution)/shard_map/ppermute | solution.py:158
  85.9 3.0 %collective-permute-start.12 = (bf16[128,512]{1,0:T(8,128)(2,1)S(1)}, bf16[128,512]{1,0:T(8,128)(2,1)S(1)}, u32[]{:S(2)}, u32[]{:S(2)}) collective-permute-start(bf16[128,512]{1,0:T(8,128)(2,1)S(1)} %copy-done.41), channel_id=1, source_target_pairs={{0,8},{4,12},{8,0},{12,4},{1,9},{5,13},{9,1},{13,5},{2,10},{6,14},... | collective-permute-start | bytes 393224 | tf_op jit(solution)/shard_map/ppermute | solution.py:158
  88.9 19.1 %collective-permute-done.9 = bf16[128,1280]{1,0:T(8,128)(2,1)S(1)} collective-permute-done((bf16[128,1280]{1,0:T(8,128)(2,1)S(1)}, bf16[128,1280]{1,0:T(8,128)(2,1)S(1)}, u32[]{:S(2)}, u32[]{:S(2)}) %collective-permute-start.9) | collective-permute-done | bytes 327712 | tf_op jit(solution)/shard_map/ppermute | solution.py:158
  111.0 5.3 %collective-permute-done.13 = bf16[128,512]{1,0:T(8,128)(2,1)S(1)} collective-permute-done((bf16[128,512]{1,0:T(8,128)(2,1)S(1)}, bf16[128,512]{1,0:T(8,128)(2,1)S(1)}, u32[]{:S(2)}, u32[]{:S(2)}) %collective-permute-start.13) | collective-permute-done | bytes 131104 | tf_op jit(solution)/shard_map/ppermute | solution.py:158
  122.9 1.5 collective-permute-start.17
  125.3 25.7 %collective-permute-done.25 = bf16[512,512]{1,0:T(8,128)(2,1)S(1)} collective-permute-done((bf16[512,512]{1,0:T(8,128)(2,1)S(1)}, bf16[512,512]{1,0:T(8,128)(2,1)S(1)}, u32[]{:S(2)}, u32[]{:S(2)}) %collective-permute-start.25) | collective-permute-done | bytes 524320 | tf_op jit(solution)/shard_map/ppermute | solution.py:161
  155.1 1.5 collective-permute-start.21
  156.5 2.1 collective-permute-start.18
  163.3 1.5 collective-permute-start.33
  164.8 3.3 %collective-permute-start.30 = (f32[128,1024]{1,0:T(8,128)}, f32[128,1024]{1,0:T(8,128)}, u32[]{:S(2)}, u32[]{:S(2)}) collective-permute-start(f32[128,1024]{1,0:T(8,128)} %get-tuple-element.94), channel_id=1, source_target_pairs={{0,4},{1,5},{2,6},{3,7},{16,20},{17,21},{18,22},{19,23}} | collective-permute-start | bytes 1572872 | tf_op jit(solution)/shard_map/ppermute | solution.py:128
  171.8 2.0 fusion.53
  175.1 4.7 %collective-permute-start.19 = (f32[128,1024]{1,0:T(8,128)S(1)}, f32[128,1024]{1,0:T(8,128)S(1)}, u32[]{:S(2)}, u32[]{:S(2)}) collective-permute-start(f32[128,1024]{1,0:T(8,128)S(1)} %get-tuple-element.97), channel_id=1, source_target_pairs={{0,4},{4,8},{8,12},{1,5},{5,9},{9,13},{2,6},{6,10},{10,14},{3,7},{... | collective-permute-start | bytes 1572872 | tf_op jit(solution)/shard_map/ppermute | solution.py:128
  179.8 1.8 collective-permute-done.30
  181.7 1.3 fusion.44
  183.9 5.0 %collective-permute-start.31 = (f32[128,1024]{1,0:T(8,128)S(1)}, f32[128,1024]{1,0:T(8,128)S(1)}, u32[]{:S(2)}, u32[]{:S(2)}) collective-permute-start(f32[128,1024]{1,0:T(8,128)S(1)} %get-tuple-element.92), channel_id=1, source_target_pairs={{0,4},{4,8},{1,5},{5,9},{2,6},{6,10},{3,7},{7,11},{16,20},{20,24},... | collective-permute-start | bytes 1572872 | tf_op jit(solution)/shard_map/ppermute | solution.py:128
  200.5 3.3 %collective-permute-done.31 = f32[128,1024]{1,0:T(8,128)S(1)} collective-permute-done((f32[128,1024]{1,0:T(8,128)S(1)}, f32[128,1024]{1,0:T(8,128)S(1)}, u32[]{:S(2)}, u32[]{:S(2)}) %collective-permute-start.31) | collective-permute-done | bytes 524320 | tf_op jit(solution)/shard_map/ppermute | solution.py:128
  204.0 1.4 collective-permute-start.35
  205.4 5.0 %collective-permute-start.32 = (f32[128,1024]{1,0:T(8,128)S(1)}, f32[128,1024]{1,0:T(8,128)S(1)}, u32[]{:S(2)}, u32[]{:S(2)}) collective-permute-start(f32[128,1024]{1,0:T(8,128)S(1)} %get-tuple-element.90), channel_id=1, source_target_pairs={{0,4},{4,8},{8,12},{1,5},{5,9},{9,13},{2,6},{6,10},{10,14},{3,7},{... | collective-permute-start | bytes 1572872 | tf_op jit(solution)/shard_map/ppermute | solution.py:128
  211.4 1.5 fusion.33
  212.9 7.5 %collective-permute-done.35.refs_5_ = f32[128,1024]{1,0:T(8,128)S(1)} collective-permute-done((f32[128,1024]{1,0:T(8,128)S(1)}, f32[128,1024]{1,0:T(8,128)S(1)}, u32[]{:S(2)}, u32[]{:S(2)}) %collective-permute-start.35) | collective-permute-done | bytes 524320 | tf_op jit(solution)/shard_map/ppermute | solution.py:128
  (191 shorter events, 48.5 us)
Async XLA Ops:
  5.6 14.9 %collective-permute-start = (bf16[128,1024]{1,0:T(8,128)(2,1)S(1)}, bf16[128,1024]{1,0:T(8,128)(2,1)}, u32[]{:S(2)}, u32[]{:S(2)}) collective-permute-start(bf16[128,1024]{1,0:T(8,128)(2,1)S(1)} %get-tuple-element.34), channel_id=1, source_target_pairs={{0,4},{4,8},{8,12},{12,0},{1,5},{5,9},{9,13},{13,1},{2,6},{6,10},{... | collective-permute-start | bytes 786440 | tf_op jit(solution)/shard_map/ppermute | solution.py:158
  8.6 20.6 %collective-permute-start.1 = (bf16[128,1024]{1,0:T(8,128)(2,1)S(1)}, bf16[128,1024]{1,0:T(8,128)(2,1)}, u32[]{:S(2)}, u32[]{:S(2)}) collective-permute-start(bf16[128,1024]{1,0:T(8,128)(2,1)S(1)} %get-tuple-element.35), channel_id=1, source_target_pairs={{0,8},{4,12},{8,0},{12,4},{1,9},{5,13},{9,1},{13,5},{2,10},{6,14},... | collective-permute-start | bytes 786440 | tf_op jit(solution)/shard_map/ppermute | solution.py:158
  11.2 19.1 %collective-permute-start.2 = (bf16[128,1024]{1,0:T(8,128)(2,1)S(1)}, bf16[128,1024]{1,0:T(8,128)(2,1)}, u32[]{:S(2)}, u32[]{:S(2)}) collective-permute-start(bf16[128,1024]{1,0:T(8,128)(2,1)S(1)} %get-tuple-element.36), channel_id=1, source_target_pairs={{0,12},{4,0},{8,4},{12,8},{1,13},{5,1},{9,5},{13,9},{2,14},{6,2},{... | collective-permute-start | bytes 786440 | tf_op jit(solution)/shard_map/ppermute | solution.py:158
  18.4 28.0 %collective-permute-start.3 = (bf16[128,1408]{1,0:T(8,128)(2,1)S(1)}, bf16[128,1408]{1,0:T(8,128)(2,1)}, u32[]{:S(2)}, u32[]{:S(2)}) collective-permute-start(bf16[128,1408]{1,0:T(8,128)(2,1)S(1)} %get-tuple-element.67), channel_id=1, source_target_pairs={{0,4},{4,8},{8,12},{12,0},{1,5},{5,9},{9,13},{13,1},{2,6},{6,10},{... | collective-permute-start | bytes 1081352 | tf_op jit(solution)/shard_map/ppermute | solution.py:158
  31.3 39.1 %collective-permute-start.7 = (bf16[512,1024]{1,0:T(8,128)(2,1)S(1)}, bf16[512,1024]{1,0:T(8,128)(2,1)S(1)}, u32[]{:S(2)}, u32[]{:S(2)}) collective-permute-start(bf16[512,1024]{1,0:T(8,128)(2,1)S(1)} %bitcast.90), channel_id=1, source_target_pairs={{0,1},{1,0},{2,3},{3,2},{4,5},{5,4},{6,7},{7,6},{8,9},{9,8},{10,11... | collective-permute-start | bytes 3145736 | tf_op jit(solution)/shard_map/ppermute | solution.py:162
  31.4 39.0 %collective-permute-start.6 = (bf16[512,1024]{1,0:T(8,128)(2,1)S(1)}, bf16[512,1024]{1,0:T(8,128)(2,1)S(1)}, u32[]{:S(2)}, u32[]{:S(2)}) collective-permute-start(bf16[512,1024]{1,0:T(8,128)(2,1)S(1)} %bitcast.91), channel_id=1, source_target_pairs={{0,2},{2,0},{1,3},{3,1},{4,6},{6,4},{5,7},{7,5},{8,10},{10,8},{9,1... | collective-permute-start | bytes 3145736 | tf_op jit(solution)/shard_map/ppermute | solution.py:161
  33.2 37.1 %collective-permute-start.5 = (bf16[128,1408]{1,0:T(8,128)(2,1)S(1)}, bf16[128,1408]{1,0:T(8,128)(2,1)S(1)}, u32[]{:S(2)}, u32[]{:S(2)}) collective-permute-start(bf16[128,1408]{1,0:T(8,128)(2,1)S(1)} %get-tuple-element.43), channel_id=1, source_target_pairs={{0,12},{4,0},{8,4},{12,8},{1,13},{5,1},{9,5},{13,9},{2,14},{6,2},{... | collective-permute-start | bytes 1081352 | tf_op jit(solution)/shard_map/ppermute | solution.py:158
  40.4 29.8 %collective-permute-start.4 = (bf16[128,1408]{1,0:T(8,128)(2,1)S(1)}, bf16[128,1408]{1,0:T(8,128)(2,1)S(1)}, u32[]{:S(2)}, u32[]{:S(2)}) collective-permute-start(bf16[128,1408]{1,0:T(8,128)(2,1)S(1)} %get-tuple-element.41), channel_id=1, source_target_pairs={{0,8},{4,12},{8,0},{12,4},{1,9},{5,13},{9,1},{13,5},{2,10},{6,14},... | collective-permute-start | bytes 1081352 | tf_op jit(solution)/shard_map/ppermute | solution.py:158
  70.4 15.4 %collective-permute-start.8 = (bf16[128,1280]{1,0:T(8,128)(2,1)S(1)}, bf16[128,1280]{1,0:T(8,128)(2,1)S(1)}, u32[]{:S(2)}, u32[]{:S(2)}) collective-permute-start(bf16[128,1280]{1,0:T(8,128)(2,1)S(1)} %copy-done.39), channel_id=1, source_target_pairs={{0,4},{4,8},{8,12},{12,0},{1,5},{5,9},{9,13},{13,1},{2,6},{6,10},{... | collective-permute-start | bytes 983048 | tf_op jit(solution)/shard_map/ppermute | solution.py:158
  70.5 15.3 %collective-permute-start.11 = (bf16[128,512]{1,0:T(8,128)(2,1)S(1)}, bf16[128,512]{1,0:T(8,128)(2,1)S(1)}, u32[]{:S(2)}, u32[]{:S(2)}) collective-permute-start(bf16[128,512]{1,0:T(8,128)(2,1)S(1)} %copy-done.42), channel_id=1, source_target_pairs={{0,4},{4,8},{8,12},{12,0},{1,5},{5,9},{9,13},{13,1},{2,6},{6,10},{... | collective-permute-start | bytes 393224 | tf_op jit(solution)/shard_map/ppermute | solution.py:158
  71.5 46.2 %collective-permute-start.23 = (bf16[512,1408]{1,0:T(8,128)(2,1)S(1)}, bf16[512,1408]{1,0:T(8,128)(2,1)S(1)}, u32[]{:S(2)}, u32[]{:S(2)}) collective-permute-start(bf16[512,1408]{1,0:T(8,128)(2,1)S(1)} %bitcast.105), channel_id=1, source_target_pairs={{0,2},{2,0},{1,3},{3,1},{4,6},{6,4},{5,7},{7,5},{8,10},{10,8},{9,1... | collective-permute-start | bytes 4325384 | tf_op jit(solution)/shard_map/ppermute | solution.py:161
  72.0 46.4 %collective-permute-start.14 = (bf16[512,1408]{1,0:T(8,128)(2,1)S(1)}, bf16[512,1408]{1,0:T(8,128)(2,1)S(1)}, u32[]{:S(2)}, u32[]{:S(2)}) collective-permute-start(bf16[512,1408]{1,0:T(8,128)(2,1)S(1)} %bitcast.106), channel_id=1, source_target_pairs={{0,1},{1,0},{2,3},{3,2},{4,5},{5,4},{6,7},{7,6},{8,9},{9,8},{10,11... | collective-permute-start | bytes 4325384 | tf_op jit(solution)/shard_map/ppermute | solution.py:162
  72.1 35.9 %collective-permute-start.10 = (bf16[128,1280]{1,0:T(8,128)(2,1)S(1)}, bf16[128,1280]{1,0:T(8,128)(2,1)S(1)}, u32[]{:S(2)}, u32[]{:S(2)}) collective-permute-start(bf16[128,1280]{1,0:T(8,128)(2,1)S(1)} %copy-done.37), channel_id=1, source_target_pairs={{0,12},{4,0},{8,4},{12,8},{1,13},{5,1},{9,5},{13,9},{2,14},{6,2},{... | collective-permute-start | bytes 983048 | tf_op jit(solution)/shard_map/ppermute | solution.py:158
  85.8 22.1 %collective-permute-start.9 = (bf16[128,1280]{1,0:T(8,128)(2,1)S(1)}, bf16[128,1280]{1,0:T(8,128)(2,1)S(1)}, u32[]{:S(2)}, u32[]{:S(2)}) collective-permute-start(bf16[128,1280]{1,0:T(8,128)(2,1)S(1)} %copy-done.38), channel_id=1, source_target_pairs={{0,8},{4,12},{8,0},{12,4},{1,9},{5,13},{9,1},{13,5},{2,10},{6,14},... | collective-permute-start | bytes 983048 | tf_op jit(solution)/shard_map/ppermute | solution.py:158
  85.9 24.9 %collective-permute-start.12 = (bf16[128,512]{1,0:T(8,128)(2,1)S(1)}, bf16[128,512]{1,0:T(8,128)(2,1)S(1)}, u32[]{:S(2)}, u32[]{:S(2)}) collective-permute-start(bf16[128,512]{1,0:T(8,128)(2,1)S(1)} %copy-done.41), channel_id=1, source_target_pairs={{0,8},{4,12},{8,0},{12,4},{1,9},{5,13},{9,1},{13,5},{2,10},{6,14},... | collective-permute-start | bytes 393224 | tf_op jit(solution)/shard_map/ppermute | solution.py:158
  108.9 42.6 %collective-permute-start.24 = (bf16[512,1280]{1,0:T(8,128)(2,1)S(1)}, bf16[512,1280]{1,0:T(8,128)(2,1)S(1)}, u32[]{:S(2)}, u32[]{:S(2)}) collective-permute-start(bf16[512,1280]{1,0:T(8,128)(2,1)S(1)} %bitcast.113), channel_id=1, source_target_pairs={{0,2},{2,0},{1,3},{3,1},{4,6},{6,4},{5,7},{7,5},{8,10},{10,8},{9,1... | collective-permute-start | bytes 3932168 | tf_op jit(solution)/shard_map/ppermute | solution.py:161
  109.5 10.6 %collective-permute-start.15 = (bf16[512,1280]{1,0:T(8,128)(2,1)S(1)}, bf16[512,1280]{1,0:T(8,128)(2,1)S(1)}, u32[]{:S(2)}, u32[]{:S(2)}) collective-permute-start(bf16[512,1280]{1,0:T(8,128)(2,1)S(1)} %bitcast.114), channel_id=1, source_target_pairs={{0,1},{1,0},{2,3},{3,2},{4,5},{5,4},{6,7},{7,6},{8,9},{9,8},{10,11... | collective-permute-start | bytes 3932168 | tf_op jit(solution)/shard_map/ppermute | solution.py:162
  117.7 33.3 %collective-permute-start.25 = (bf16[512,512]{1,0:T(8,128)(2,1)S(1)}, bf16[512,512]{1,0:T(8,128)(2,1)S(1)}, u32[]{:S(2)}, u32[]{:S(2)}) collective-permute-start(bf16[512,512]{1,0:T(8,128)(2,1)S(1)} %bitcast.99), channel_id=1, source_target_pairs={{0,2},{2,0},{1,3},{3,1},{4,6},{6,4},{5,7},{7,5},{8,10},{10,8},{9,1... | collective-permute-start | bytes 1572872 | tf_op jit(solution)/shard_map/ppermute | solution.py:161
  118.4 38.1 %collective-permute-start.27 = (bf16[512,1408]{1,0:T(8,128)(2,1)S(1)}, bf16[512,1408]{1,0:T(8,128)(2,1)S(1)}, u32[]{:S(2)}, u32[]{:S(2)}) collective-permute-start(bf16[512,1408]{1,0:T(8,128)(2,1)S(1)} %collective-permute-done.23), channel_id=1, source_target_pairs={{0,1},{1,0},{2,3},{3,2},{4,5},{5,4},{6,7},{7,6},{8,9},{9,8},{10,11... | collective-permute-start | bytes 4325384 | tf_op jit(solution)/shard_map/ppermute | solution.py:172
  122.2 29.3 %collective-permute-start.20 = (f32[128,1024]{1,0:T(8,128)S(1)}, f32[128,1024]{1,0:T(8,128)S(1)}, u32[]{:S(2)}, u32[]{:S(2)}) collective-permute-start(f32[128,1024]{1,0:T(8,128)S(1)} %get-tuple-element.100), channel_id=1, source_target_pairs={{12,8},{13,9},{14,10},{15,11},{28,24},{29,25},{30,26},{31,27}} | collective-permute-start | bytes 1572872 | tf_op jit(solution)/shard_map/ppermute | solution.py:128
  122.9 28.6 %collective-permute-start.17 = (f32[128,1024]{1,0:T(8,128)S(1)}, f32[128,1024]{1,0:T(8,128)S(1)}, u32[]{:S(2)}, u32[]{:S(2)}) collective-permute-start(f32[128,1024]{1,0:T(8,128)S(1)} %get-tuple-element.101), channel_id=1, source_target_pairs={{0,4},{1,5},{2,6},{3,7},{16,20},{17,21},{18,22},{19,23}} | collective-permute-start | bytes 1572872 | tf_op jit(solution)/shard_map/ppermute | solution.py:128
  151.0 10.1 %collective-permute-start.26 = (bf16[512,1024]{1,0:T(8,128)(2,1)S(1)}, bf16[512,1024]{1,0:T(8,128)(2,1)S(1)}, u32[]{:S(2)}, u32[]{:S(2)}) collective-permute-start(bf16[512,1024]{1,0:T(8,128)(2,1)S(1)} %collective-permute-done.6), channel_id=1, source_target_pairs={{0,1},{1,0},{2,3},{3,2},{4,5},{5,4},{6,7},{7,6},{8,9},{9,8},{10,11... | collective-permute-start | bytes 3145736 | tf_op jit(solution)/shard_map/ppermute | solution.py:172
  155.1 16.7 %collective-permute-start.21 = (f32[128,1024]{1,0:T(8,128)}, f32[128,1024]{1,0:T(8,128)}, u32[]{:S(2)}, u32[]{:S(2)}) collective-permute-start(f32[128,1024]{1,0:T(8,128)} %get-tuple-element.98), channel_id=1, source_target_pairs={{12,8},{8,4},{13,9},{9,5},{14,10},{10,6},{15,11},{11,7},{28,24},{2... | collective-permute-start | bytes 1572872 | tf_op jit(solution)/shard_map/ppermute | solution.py:128
  156.5 15.3 %collective-permute-start.18 = (f32[128,1024]{1,0:T(8,128)}, f32[128,1024]{1,0:T(8,128)}, u32[]{:S(2)}, u32[]{:S(2)}) collective-permute-start(f32[128,1024]{1,0:T(8,128)} %get-tuple-element.99), channel_id=1, source_target_pairs={{0,4},{4,8},{1,5},{5,9},{2,6},{6,10},{3,7},{7,11},{16,20},{20,24},... | collective-permute-start | bytes 1572872 | tf_op jit(solution)/shard_map/ppermute | solution.py:128
  163.3 16.5 %collective-permute-start.33 = (f32[128,1024]{1,0:T(8,128)}, f32[128,1024]{1,0:T(8,128)}, u32[]{:S(2)}, u32[]{:S(2)}) collective-permute-start(f32[128,1024]{1,0:T(8,128)} %get-tuple-element.93), channel_id=1, source_target_pairs={{12,8},{13,9},{14,10},{15,11},{28,24},{29,25},{30,26},{31,27}} | collective-permute-start | bytes 1572872 | tf_op jit(solution)/shard_map/ppermute | solution.py:128
  164.8 16.9 %collective-permute-start.30 = (f32[128,1024]{1,0:T(8,128)}, f32[128,1024]{1,0:T(8,128)}, u32[]{:S(2)}, u32[]{:S(2)}) collective-permute-start(f32[128,1024]{1,0:T(8,128)} %get-tuple-element.94), channel_id=1, source_target_pairs={{0,4},{1,5},{2,6},{3,7},{16,20},{17,21},{18,22},{19,23}} | collective-permute-start | bytes 1572872 | tf_op jit(solution)/shard_map/ppermute | solution.py:128
  173.8 39.1 %collective-permute-start.22 = (f32[128,1024]{1,0:T(8,128)S(1)}, f32[128,1024]{1,0:T(8,128)S(1)}, u32[]{:S(2)}, u32[]{:S(2)}) collective-permute-start(f32[128,1024]{1,0:T(8,128)S(1)} %get-tuple-element.95), channel_id=1, source_target_pairs={{12,8},{8,4},{4,0},{13,9},{9,5},{5,1},{14,10},{10,6},{6,2},{15,11}... | collective-permute-start | bytes 1572872 | tf_op jit(solution)/shard_map/ppermute | solution.py:128
  175.1 37.8 %collective-permute-start.19 = (f32[128,1024]{1,0:T(8,128)S(1)}, f32[128,1024]{1,0:T(8,128)S(1)}, u32[]{:S(2)}, u32[]{:S(2)}) collective-permute-start(f32[128,1024]{1,0:T(8,128)S(1)} %get-tuple-element.97), channel_id=1, source_target_pairs={{0,4},{4,8},{8,12},{1,5},{5,9},{9,13},{2,6},{6,10},{10,14},{3,7},{... | collective-permute-start | bytes 1572872 | tf_op jit(solution)/shard_map/ppermute | solution.py:128
  183.0 17.4 %collective-permute-start.34 = (f32[128,1024]{1,0:T(8,128)S(1)}, f32[128,1024]{1,0:T(8,128)S(1)}, u32[]{:S(2)}, u32[]{:S(2)}) collective-permute-start(f32[128,1024]{1,0:T(8,128)S(1)} %get-tuple-element.91), channel_id=1, source_target_pairs={{12,8},{8,4},{13,9},{9,5},{14,10},{10,6},{15,11},{11,7},{28,24},{2... | collective-permute-start | bytes 1572872 | tf_op jit(solution)/shard_map/ppermute | solution.py:128
  183.9 19.9 %collective-permute-start.31 = (f32[128,1024]{1,0:T(8,128)S(1)}, f32[128,1024]{1,0:T(8,128)S(1)}, u32[]{:S(2)}, u32[]{:S(2)}) collective-permute-start(f32[128,1024]{1,0:T(8,128)S(1)} %get-tuple-element.92), channel_id=1, source_target_pairs={{0,4},{4,8},{1,5},{5,9},{2,6},{6,10},{3,7},{7,11},{16,20},{20,24},... | collective-permute-start | bytes 1572872 | tf_op jit(solution)/shard_map/ppermute | solution.py:128
  204.0 16.4 %collective-permute-start.35 = (f32[128,1024]{1,0:T(8,128)S(1)}, f32[128,1024]{1,0:T(8,128)S(1)}, u32[]{:S(2)}, u32[]{:S(2)}) collective-permute-start(f32[128,1024]{1,0:T(8,128)S(1)} %get-tuple-element.88), channel_id=1, source_target_pairs={{12,8},{8,4},{4,0},{13,9},{9,5},{5,1},{14,10},{10,6},{6,2},{15,11}... | collective-permute-start | bytes 1572872 | tf_op jit(solution)/shard_map/ppermute | solution.py:128
  205.4 16.2 %collective-permute-start.32 = (f32[128,1024]{1,0:T(8,128)S(1)}, f32[128,1024]{1,0:T(8,128)S(1)}, u32[]{:S(2)}, u32[]{:S(2)}) collective-permute-start(f32[128,1024]{1,0:T(8,128)S(1)} %get-tuple-element.90), channel_id=1, source_target_pairs={{0,4},{4,8},{8,12},{1,5},{5,9},{9,13},{2,6},{6,10},{10,14},{3,7},{... | collective-permute-start | bytes 1572872 | tf_op jit(solution)/shard_map/ppermute | solution.py:128
  (47 other events, 606.8 us)

commit v8 on v7

--- a/solution.py
+++ b/solution.py
@@ -18,7 +18,7 @@
 
 def chunks_of(per_plane):
     unit = per_plane // 16
-    sizes = [4 * unit, 5 * unit, 5 * unit, 2 * unit] if unit else [1] * per_plane
+    sizes = [4 * unit, 4 * unit, 4 * unit, 2 * unit, 2 * unit] if unit else [1] * per_plane
     return [(sum(sizes[:i]), size) for i, size in enumerate(sizes)]
 
 
@@ -83,51 +83,106 @@
     return [out[n * planes : (n + 1) * planes] for n in range(len(chunks))]
 
 
-def finish_kernel(planes, scale, place_ref, *refs):
+def finish_kernel(planes, scale, at_ref, *refs):
     out = refs[-1]
     rows = out.shape[0]
-    sums = []
-    for pair in range(2):
-        own, below, above = refs[3 * pair : 3 * pair + 3]
-        sums.append((own[...] + below[...] + above[...]) * scale)
-
-    def block(k, z):
-        at = ((k % 2) * planes + z) * rows
-        return sums[k // 2][:, at : at + rows]
-
-    for place in range(4):
-
-        @pl.when(place_ref[0] == place)
-        def _():
-            for z in range(planes):
-                pieces = [block(place ^ other, z) for other in range(4)]
-                out[:, z * 4 * rows : (z + 1) * 4 * rows] = jnp.concatenate(pieces, axis=1)
-
-
-def finish(planes, total, place, parts):
+    half = planes // 2
+    each = 2 * half
+    z, place = at_ref[0], at_ref[1]
+
+    def put(k, plane, value):
+        at = (lax.rem(plane, planes) * 4 + (place ^ k)) * rows
+        out[:, pl.ds(pl.multiple_of(at, LANES), rows)] = value * scale
+
+    for h in range(2):
+        own, others = refs[each * h], refs[each * h + 1 : each * (h + 1)]
+        for n in range(2):
+            k = 2 * h + n
+            for e in range(half):
+                at = (n * half + e) * rows
+                put(k, z + e, own[:, at : at + rows])
+                if e:
+                    put(k, z + planes - e, others[n * (half - 1) + e - 1][...].T)
+        lower = (z < half).astype(jnp.int32)
+        put(2 * h + 1 - lower, z + half, own[:, 2 * half * rows :])
+        put(2 * h + lower, z + half, others[-1][...].T)
+
+
+def finish(planes, total, z, place, parts):
     rows = parts[0].shape[0]
-    return pl.pallas_call(
-        functools.partial(finish_kernel, planes, 1.0 / total),
-        out_shape=jax.ShapeDtypeStruct((rows, 4 * planes * rows), jnp.float32),
-        in_specs=[pl.BlockSpec(memory_space=pltpu.SMEM)] + [pl.BlockSpec(memory_space=pltpu.VMEM)] * len(parts),
-        out_specs=pl.BlockSpec(memory_space=pltpu.VMEM),
-        compiler_params=pltpu.CompilerParams(vmem_limit_bytes=24 * 2**20),
-        name="finish",
-    )(place.reshape(1).astype(jnp.int32), *parts)
+    half = planes // 2
+    if rows % LANES == 0:
+        return pl.pallas_call(
+            functools.partial(finish_kernel, planes, 1.0 / total),
+            out_shape=jax.ShapeDtypeStruct((rows, 4 * planes * rows), jnp.float32),
+            in_specs=[pl.BlockSpec(memory_space=pltpu.SMEM)] + [pl.BlockSpec(memory_space=pltpu.VMEM)] * len(parts),
+            out_specs=pl.BlockSpec(memory_space=pltpu.VMEM),
+            compiler_params=pltpu.CompilerParams(vmem_limit_bytes=24 * 2**20),
+            name="finish",
+        )(jnp.stack([z, place]).astype(jnp.int32), *parts)
+    each = 2 * half
+    blocks = {}
+    for h in range(2):
+        own, others = parts[each * h], parts[each * h + 1 : each * (h + 1)]
+        for n in range(2):
+            for e in range(half):
+                at = (n * half + e) * rows
+                blocks[e, 2 * h + n] = own[:, at : at + rows]
+                if e:
+                    blocks[planes - e, 2 * h + n] = others[n * (half - 1) + e - 1].T
+        last, got = own[:, 2 * half * rows :], others[-1].T
+        blocks[half, 2 * h] = jnp.where(z < half, last, got)
+        blocks[half, 2 * h + 1] = jnp.where(z < half, got, last)
+    near = jnp.stack([blocks[e, k] for e in range(planes) for k in range(4)])
+    column = jnp.arange(4 * planes)
+    near = jnp.take(near, (column // 4 - z) % planes * 4 + (column % 4 ^ place), axis=0)
+    return near.transpose(1, 0, 2).reshape(rows, -1) * (1.0 / total)
+
+
+def halves(planes, pair):
+    rows = pair[0].shape[0] // planes
+    half = planes // 2
+    out = []
+    for plane in range(planes):
+        own = [p[plane * rows : (plane + 1) * rows] for p in pair]
+        pieces = []
+        for p in own:
+            if plane + half <= planes:
+                pieces.append(p[:, plane * rows : (plane + half) * rows])
+            else:
+                pieces += [p[:, plane * rows :], p[:, : (plane + half - planes) * rows]]
+        far = (plane + half) % planes * rows
+        pieces.append(own[plane // half][:, far : far + rows])
+        out.append(jnp.concatenate(pieces, axis=1))
+    return jnp.stack(out)
+
+
+def mirror(planes, h, sums):
+    rows = sums.shape[0]
+    half = planes // 2
+    axes = ("z", "y", "c")
+    got = []
+    for n in range(2):
+        for e in range(1, half):
+            at = (n * half + e) * rows
+            pairs = [(4 * i + a, (i + e) % planes * 4 + (a ^ (2 * h + n))) for i in range(planes) for a in range(4)]
+            got.append(lax.ppermute(sums[:, at : at + rows], axes, pairs))
+    pairs = [(4 * i + a, (i + half) % planes * 4 + (a ^ (2 * h + i // half))) for i in range(planes) for a in range(4)]
+    got.append(lax.ppermute(sums[:, 2 * half * rows :], axes, pairs))
+    return got
 
 
 def chain(planes, z, sums, up):
-    rows = sums.shape[0] // planes
-    got = first = None
+    got = early = None
     for step in range(1, planes):
         plane = planes - step + z if up else z - planes + step
-        sent = lax.dynamic_slice_in_dim(sums, jnp.clip(plane, 0, planes - 1) * rows, rows, 0)
+        sent = lax.dynamic_index_in_dim(sums, jnp.clip(plane, 0, planes - 1), 0, keepdims=False)
         if got is not None:
             sent = sent + got
         pairs = [(i, i + 1) for i in range(step)] if up else [(planes - 1 - i, planes - 2 - i) for i in range(step)]
         got = lax.ppermute(sent, "z", pairs)
-        first = got if first is None else first
-    return got, first
+        early = got if step < 3 else early
+    return got, early
 
 
 def on_device(planes, slab, factor):
@@ -154,7 +209,12 @@
         for shift in range(1, planes):
             piece = pieces[j][shift]
             if len(sent) >= WINDOW:
-                piece = after(piece, sent[-WINDOW], *(waits[min(j, last - 1) - 2] if j > 1 else ()))
+                piece = after(
+                    piece,
+                    sent[-WINDOW],
+                    *(waits[min(j, last - 1) - 2] if j > 1 else ()),
+                    *(held[j - 3][3:] if j > 2 else ()),
+                )
             sent.append(lax.ppermute(piece, "z", [(s, (s + shift) % planes) for s in range(planes)]))
             arrived.append(sent[-1])
         stack = stacked(arrived)
@@ -162,23 +222,27 @@
         beside = lax.ppermute(stack, "c", SWAP)
         waits.append((across, beside))
         held.append([stack, beside, across])
+        if j < last - 2:
+            held[j].append(lax.ppermute(across, "c", SWAP))
     flat = [[b[:, : size * cells] for b in held[j][:2]] for j, (_, size) in enumerate(chunks)]
     sums = [sum(nt_dot(flat[j][0], flat[j][k]) for j in range(last + 1)) for k in range(2)]
     parts, gate = [], None
     for half in range(2):
         if half:
             for j in range(last + 1):
-                across = after(held[j][2], *gate) if j >= last - 1 else held[j][2]
-                held[j].append(lax.ppermute(across, "c", SWAP))
+                if j >= last - 2:
+                    held[j][2] = after(held[j][2], *gate)
+                    held[j].append(lax.ppermute(held[j][2], "c", SWAP))
                 flat[j] += [b[:, : chunks[j][1] * cells] for b in held[j][2:]]
             sums = [sum(nt_dot(flat[j][0], flat[j][k]) for j in range(last + 1)) for k in range(2, 4)]
-        both = jnp.concatenate(sums, axis=1)
-        up, first_up = chain(planes, z, both, True)
-        down, first_down = chain(planes, z, both, False)
-        gate = (first_up, first_down)
-        parts += [lax.dynamic_slice_in_dim(both, z * rows, rows, 0), up, down]
-    factors = after([b[:, chunks[1][1] * cells :] for b in held[1]], *gate)
-    gram = finish(planes, total, place, parts)
+        both = halves(planes, sums)
+        up, early_up = chain(planes, z, both, True)
+        down, early_down = chain(planes, z, both, False)
+        gate = (early_up, early_down)
+        whole = lax.dynamic_index_in_dim(both, z, 0, keepdims=False) + up + down
+        parts += [whole, *mirror(planes, half, whole)]
+    factors = [b[:, chunks[1][1] * cells :] for b in held[1]]
+    gram = finish(planes, total, z, place, parts)
     own = per_plane // 4
     whole = [sum(tn_dot(flat[j][k], factors[k]) for k in range(4)) for j in range(last + 1)]
     whole = jnp.concatenate(whole, axis=0)

time: 224 us -> 272 us (1.21)
  waiting for transfers between devices: 106 us -> 67.6 us
  matrix products: 19.7 us -> 55.9 us
  starting transfers between devices: 61.5 us -> 85.4 us
  local copies, waits for them, and re-layouts: 23.5 us -> 41.3 us
  other arithmetic: 7.43 us -> 14.5 us
    dot_general x16 -> x20, matrix products: 7.62 us -> 33 us  [tn_dot(): lax.dot_general(a, b, (((0,), (0,)), ((), ())), preferred_element_type=jn...]
    ppermute x4 -> x5, waiting for transfers between devices: 25.8 us -> 2.25 us  [on_device(): across = lax.ppermute(stack, 'y', SWAP)]
    dynamic_slice x0 -> x17, local copies, waits for them, and re-layouts: none -> 21.8 us  [the longest x12 16.2 us: chain(): lax.dynamic_index_in_dim(sums, jnp.clip(plane, 0, planes - 1), 0, keepdim...]
    ppermute x12 -> x15, waiting for transfers between devices: 66.3 us -> 49.2 us  [on_device(): lax.ppermute(piece, 'z', [(s, (s + shift) % planes) for s in range(planes)])]
    ppermute x12 -> x15, starting transfers between devices: 28 us -> 42.6 us  [on_device(): lax.ppermute(piece, 'z', [(s, (s + shift) % planes) for s in range(planes)])]
    dot_general x16 -> x20, matrix products: 12.1 us -> 22.9 us  [nt_dot(): lax.dot_general(a, b, (((1,), (1,)), ((), ())), preferred_element_type=jn...]
    add x4 -> x8, other arithmetic: 4.66 us -> 12.8 us  [chain(): sent = sent + got]
    ppermute x0 -> x9, starting transfers between devices: none -> 7.84 us  [the longest x4 4.49 us: mirror(): got.append(lax.ppermute(sums[:, at:at + rows], axes, pairs))]
  transfers between devices with their start and end apart: 36 -> 48, of which waited for: 11 -> 15; matrix products, arithmetic and copies ran while one was open for 18% -> 40% of each run, Pallas kernels for 0% -> 0%
where the time goes in v8:
time: 272 us; the launch traced here: 270 us
  starting transfers between devices  85.4 us (31%)
  waiting for transfers between devices  67.6 us (25%)
  matrix products  55.9 us (21%)
  local copies, waits for them, and re-layouts  41.3 us (15%)
  other arithmetic  14.5 us (5%)
  Pallas kernels  3.72 us (1%)
    ppermute x15, waiting for transfers between devices, on_device(): lax.ppermute(piece, 'z', [(s, (s + shift) % planes) for s in range(planes)])  49.2 us
    ppermute x15, starting transfers between devices, on_device(): lax.ppermute(piece, 'z', [(s, (s + shift) % planes) for s in range(planes)])  42.6 us
    dot_general x20, matrix products, tn_dot(): lax.dot_general(a, b, (((0,), (0,)), ((), ())), preferred_element_type=jn...  33 us
    ppermute x12, starting transfers between devices, chain(): got = lax.ppermute(sent, 'z', pairs)  28.5 us
    dot_general x20, matrix products, nt_dot(): lax.dot_general(a, b, (((1,), (1,)), ((), ())), preferred_element_type=jn...  22.9 us
    dynamic_slice x12, local copies, waits for them, and re-layouts, chain(): lax.dynamic_index_in_dim(sums, jnp.clip(plane, 0, planes - 1), 0, keepdim...  16.2 us
    add x8, other arithmetic, chain(): sent = sent + got  12.8 us
    ppermute x12, waiting for transfers between devices, chain(): got = lax.ppermute(sent, 'z', pairs)  9.14 us
  transfers between devices with their start and end apart: 48, of which 15 were waited for; matrix products, arithmetic and copies ran while one was open for 40% of the time, Pallas kernels for 0%

profile of v8, /device:TPU:0, one launch (start us, length us, event | category | flops | bytes accessed | tf_op | source)
XLA Modules:
  0.0 270.0 jit_solution(16253410443455792813)
XLA Ops:
  5.6 3.1 %collective-permute-start = (bf16[128,1024]{1,0:T(8,128)(2,1)S(1)}, bf16[128,1024]{1,0:T(8,128)(2,1)}, u32[]{:S(2)}, u32[]{:S(2)}) collective-permute-start(bf16[128,1024]{1,0:T(8,128)(2,1)S(1)} %get-tuple-element.38), channel_id=1, source_target_pairs={{0,4},{4,8},{8,12},{12,0},{1,5},{5,9},{9,13},{13,1},{2,6},{6,10},{... | collective-permute-start | bytes 786440 | tf_op jit(solution)/shard_map/ppermute | solution.py:218
  8.6 2.6 collective-permute-start.1
  12.7 5.9 %unfold.3 = (bf16[4,128,1152]{2,1,0:T(8,128)(2,1)S(1)}, bf16[128,1152]{1,0:T(8,128)(2,1)}, bf16[128,1152]{1,0:T(8,128)(2,1)}, bf16[128,1152]{1,0:T(8,128)(2,1)},...) fusion(bf16[4,128,1152]{2,1,0:T(8,128)(2,1)S(1)} %broadcast_in_, ...), kind=kCustom, calls=%fused_computation.77 | custom fusion | bytes 7503880 | tf_op jit(solution)/shard_map/unfold/pallas_call | solution.py:67
  23.6 5.7 %collective-permute-done.1 = bf16[128,1024]{1,0:T(8,128)(2,1)} collective-permute-done((bf16[128,1024]{1,0:T(8,128)(2,1)S(1)}, bf16[128,1024]{1,0:T(8,128)(2,1)}, u32[]{:S(2)}, u32[]{:S(2)}) %collective-permute-start.1) | collective-permute-done | bytes 262176 | tf_op jit(solution)/shard_map/ppermute | solution.py:218
  33.2 9.1 %collective-permute-start.4 = (bf16[128,1152]{1,0:T(8,128)(2,1)}, bf16[128,1152]{1,0:T(8,128)(2,1)S(1)}, u32[]{:S(2)}, u32[]{:S(2)}) collective-permute-start(bf16[128,1152]{1,0:T(8,128)(2,1)} %get-tuple-element.45), channel_id=1, source_target_pairs={{0,8},{4,12},{8,0},{12,4},{1,9},{5,13},{9,1},{13,5},{2,10},{6,14},... | collective-permute-start | bytes 884744 | tf_op jit(solution)/shard_map/ppermute | solution.py:218
  42.3 3.5 %collective-permute-start.5 = (bf16[128,1152]{1,0:T(8,128)(2,1)}, bf16[128,1152]{1,0:T(8,128)(2,1)S(1)}, u32[]{:S(2)}, u32[]{:S(2)}) collective-permute-start(bf16[128,1152]{1,0:T(8,128)(2,1)} %get-tuple-element.47), channel_id=1, source_target_pairs={{0,12},{4,0},{8,4},{12,8},{1,13},{5,1},{9,5},{13,9},{2,14},{6,2},{... | collective-permute-start | bytes 884744 | tf_op jit(solution)/shard_map/ppermute | solution.py:218
  46.8 9.9 %collective-permute-done.4 = bf16[128,1152]{1,0:T(8,128)(2,1)S(1)} collective-permute-done((bf16[128,1152]{1,0:T(8,128)(2,1)}, bf16[128,1152]{1,0:T(8,128)(2,1)S(1)}, u32[]{:S(2)}, u32[]{:S(2)}) %collective-permute-start.4) | collective-permute-done | bytes 294944 | tf_op jit(solution)/shard_map/ppermute | solution.py:218
  57.4 10.2 %collective-permute-start.8 = (bf16[128,1024]{1,0:T(8,128)(2,1)S(1)}, bf16[128,1024]{1,0:T(8,128)(2,1)S(1)}, u32[]{:S(2)}, u32[]{:S(2)}) collective-permute-start(bf16[128,1024]{1,0:T(8,128)(2,1)S(1)} %copy-done.38), channel_id=1, source_target_pairs={{0,4},{4,8},{8,12},{12,0},{1,5},{5,9},{9,13},{13,1},{2,6},{6,10},{... | collective-permute-start | bytes 786440 | tf_op jit(solution)/shard_map/ppermute | solution.py:218
  68.6 2.3 collective-permute-start.10
  70.9 3.5 %collective-permute-done.8 = bf16[128,1024]{1,0:T(8,128)(2,1)S(1)} collective-permute-done((bf16[128,1024]{1,0:T(8,128)(2,1)S(1)}, bf16[128,1024]{1,0:T(8,128)(2,1)S(1)}, u32[]{:S(2)}, u32[]{:S(2)}) %collective-permute-start.8) | collective-permute-done | bytes 262176 | tf_op jit(solution)/shard_map/ppermute | solution.py:218
  75.1 10.3 %collective-permute-done.9 = bf16[128,1024]{1,0:T(8,128)(2,1)S(1)} collective-permute-done((bf16[128,1024]{1,0:T(8,128)(2,1)S(1)}, bf16[128,1024]{1,0:T(8,128)(2,1)S(1)}, u32[]{:S(2)}, u32[]{:S(2)}) %collective-permute-start.9) | collective-permute-done | bytes 262176 | tf_op jit(solution)/shard_map/ppermute | solution.py:218
  88.4 2.3 fusion.100
  96.7 5.4 %collective-permute-start.14 = (bf16[128,512]{1,0:T(8,128)(2,1)S(1)}, bf16[128,512]{1,0:T(8,128)(2,1)S(1)}, u32[]{:S(2)}, u32[]{:S(2)}) collective-permute-start(bf16[128,512]{1,0:T(8,128)(2,1)S(1)} %copy-done.44), channel_id=1, source_target_pairs={{0,4},{4,8},{8,12},{12,0},{1,5},{5,9},{9,13},{13,1},{2,6},{6,10},{... | collective-permute-start | bytes 393224 | tf_op jit(solution)/shard_map/ppermute | solution.py:218
  104.6 2.7 %collective-permute-done.14 = bf16[128,512]{1,0:T(8,128)(2,1)S(1)} collective-permute-done((bf16[128,512]{1,0:T(8,128)(2,1)S(1)}, bf16[128,512]{1,0:T(8,128)(2,1)S(1)}, u32[]{:S(2)}, u32[]{:S(2)}) %collective-permute-start.14) | collective-permute-done | bytes 131104 | tf_op jit(solution)/shard_map/ppermute | solution.py:218
  107.6 8.4 %collective-permute-done.15 = bf16[128,512]{1,0:T(8,128)(2,1)S(1)} collective-permute-done((bf16[128,512]{1,0:T(8,128)(2,1)S(1)}, bf16[128,512]{1,0:T(8,128)(2,1)S(1)}, u32[]{:S(2)}, u32[]{:S(2)}) %collective-permute-start.15) | collective-permute-done | bytes 131104 | tf_op jit(solution)/shard_map/ppermute | solution.py:218
  125.6 6.4 %collective-permute-done.18 = bf16[128,512]{1,0:T(8,128)(2,1)S(1)} collective-permute-done((bf16[128,512]{1,0:T(8,128)(2,1)S(1)}, bf16[128,512]{1,0:T(8,128)(2,1)S(1)}, u32[]{:S(2)}, u32[]{:S(2)}) %collective-permute-start.18) | collective-permute-done | bytes 131104 | tf_op jit(solution)/shard_map/ppermute | solution.py:218
  132.1 2.2 collective-permute-done.19
  141.6 3.0 %collective-permute-start.24 = (f32[128,640]{1,0:T(8,128)}, f32[128,640]{1,0:T(8,128)}, u32[]{:S(2)}, u32[]{:S(2)}) collective-permute-start(f32[128,640]{1,0:T(8,128)} %bitcast.173), channel_id=1, source_target_pairs={{0,4},{1,5},{2,6},{3,7},{16,20},{17,21},{18,22},{19,23}} | collective-permute-start | bytes 983048 | tf_op jit(solution)/shard_map/ppermute | solution.py:183
  144.6 2.4 fusion.13
  150.4 2.7 %fusion.12 = f32[4096,128]{1,0:T(8,128)} fusion(f32[4096,128]{1,0:T(8,128)} %fusion.13, f32[1024,128]{1,0:T(8,128)} %convolution_add_fusion.6, bf16[512,1152]{1,0:T(8,128)(2,1)} %copy-done.10), kind=kOutput, calls=%fused_computation.20 | convolution fusion | flops 134348800 | bytes 2228224 | tf_op jit(solution)/shard_map/dot_general | solution.py:30
  173.4 2.3 fusion.106
  175.7 2.2 collective-permute-done.35
  180.5 2.9 %collective-permute-start.26 = (f32[128,640]{1,0:T(8,128)S(1)}, f32[128,640]{1,0:T(8,128)S(1)}, u32[]{:S(2)}, u32[]{:S(2)}) collective-permute-start(f32[128,640]{1,0:T(8,128)S(1)} %bitcast_add_fusion.8), channel_id=1, source_target_pairs={{0,4},{4,8},{8,12},{1,5},{5,9},{9,13},{2,6},{6,10},{10,14},{3,7},{... | collective-permute-start | bytes 983048 | tf_op jit(solution)/shard_map/ppermute | solution.py:183
  192.6 4.1 %collective-permute-done.29 = f32[128,640]{1,0:T(8,128)S(1)} collective-permute-done((f32[128,640]{1,0:T(8,128)S(1)}, f32[128,640]{1,0:T(8,128)S(1)}, u32[]{:S(2)}, u32[]{:S(2)}) %collective-permute-start.29) | collective-permute-done | bytes 327712 | tf_op jit(solution)/shard_map/ppermute | solution.py:183
  197.4 2.3 collective-permute-start.30
  204.2 2.4 fusion.109
  210.9 4.6 %collective-permute-start.39 = (f32[128,640]{1,0:T(8,128)}, f32[128,640]{1,0:T(8,128)}, u32[]{:S(2)}, u32[]{:S(2)}) collective-permute-start(f32[128,640]{1,0:T(8,128)} %bitcast.174), channel_id=1, source_target_pairs={{0,4},{1,5},{2,6},{3,7},{16,20},{17,21},{18,22},{19,23}} | collective-permute-start | bytes 983048 | tf_op jit(solution)/shard_map/ppermute | solution.py:183
  226.2 3.7 %collective-permute-start.40 = (f32[128,640]{1,0:T(8,128)}, f32[128,640]{1,0:T(8,128)}, u32[]{:S(2)}, u32[]{:S(2)}) collective-permute-start(f32[128,640]{1,0:T(8,128)} %bitcast_add_fusion.2), channel_id=1, source_target_pairs={{0,4},{4,8},{1,5},{5,9},{2,6},{6,10},{3,7},{7,11},{16,20},{20,24},... | collective-permute-start | bytes 983048 | tf_op jit(solution)/shard_map/ppermute | solution.py:183
  233.0 2.5 fusion.17
  239.7 3.7 %collective-permute-start.41 = (f32[128,640]{1,0:T(8,128)}, f32[128,640]{1,0:T(8,128)}, u32[]{:S(2)}, u32[]{:S(2)}) collective-permute-start(f32[128,640]{1,0:T(8,128)} %bitcast_add_fusion.3), channel_id=1, source_target_pairs={{0,4},{4,8},{8,12},{1,5},{5,9},{9,13},{2,6},{6,10},{10,14},{3,7},{... | collective-permute-start | bytes 983048 | tf_op jit(solution)/shard_map/ppermute | solution.py:183
  250.8 5.0 %collective-permute-done.44 = f32[128,640]{1,0:T(8,128)} collective-permute-done((f32[128,640]{1,0:T(8,128)}, f32[128,640]{1,0:T(8,128)}, u32[]{:S(2)}, u32[]{:S(2)}) %collective-permute-start.44) | collective-permute-done | bytes 327712 | tf_op jit(solution)/shard_map/ppermute | solution.py:183
  265.9 2.3 collective-permute-done.47.refs_7_
  (267 shorter events, 128.5 us)
Async XLA Ops:
  5.6 16.9 %collective-permute-start = (bf16[128,1024]{1,0:T(8,128)(2,1)S(1)}, bf16[128,1024]{1,0:T(8,128)(2,1)}, u32[]{:S(2)}, u32[]{:S(2)}) collective-permute-start(bf16[128,1024]{1,0:T(8,128)(2,1)S(1)} %get-tuple-element.38), channel_id=1, source_target_pairs={{0,4},{4,8},{8,12},{12,0},{1,5},{5,9},{9,13},{13,1},{2,6},{6,10},{... | collective-permute-start | bytes 786440 | tf_op jit(solution)/shard_map/ppermute | solution.py:218
  8.6 20.6 %collective-permute-start.1 = (bf16[128,1024]{1,0:T(8,128)(2,1)S(1)}, bf16[128,1024]{1,0:T(8,128)(2,1)}, u32[]{:S(2)}, u32[]{:S(2)}) collective-permute-start(bf16[128,1024]{1,0:T(8,128)(2,1)S(1)} %get-tuple-element.39), channel_id=1, source_target_pairs={{0,8},{4,12},{8,0},{12,4},{1,9},{5,13},{9,1},{13,5},{2,10},{6,14},... | collective-permute-start | bytes 786440 | tf_op jit(solution)/shard_map/ppermute | solution.py:218
  11.2 19.1 %collective-permute-start.2 = (bf16[128,1024]{1,0:T(8,128)(2,1)S(1)}, bf16[128,1024]{1,0:T(8,128)(2,1)}, u32[]{:S(2)}, u32[]{:S(2)}) collective-permute-start(bf16[128,1024]{1,0:T(8,128)(2,1)S(1)} %get-tuple-element.40), channel_id=1, source_target_pairs={{0,12},{4,0},{8,4},{12,8},{1,13},{5,1},{9,5},{13,9},{2,14},{6,2},{... | collective-permute-start | bytes 786440 | tf_op jit(solution)/shard_map/ppermute | solution.py:218
  19.6 26.2 %collective-permute-start.3 = (bf16[128,1152]{1,0:T(8,128)(2,1)}, bf16[128,1152]{1,0:T(8,128)(2,1)}, u32[]{:S(2)}, u32[]{:S(2)}) collective-permute-start(bf16[128,1152]{1,0:T(8,128)(2,1)} %get-tuple-element.75), channel_id=1, source_target_pairs={{0,4},{4,8},{8,12},{12,0},{1,5},{5,9},{9,13},{13,1},{2,6},{6,10},{... | collective-permute-start | bytes 884744 | tf_op jit(solution)/shard_map/ppermute | solution.py:218
  31.3 26.1 %collective-permute-start.6 = (bf16[512,1024]{1,0:T(8,128)(2,1)S(1)}, bf16[512,1024]{1,0:T(8,128)(2,1)S(1)}, u32[]{:S(2)}, u32[]{:S(2)}) collective-permute-start(bf16[512,1024]{1,0:T(8,128)(2,1)S(1)} %bitcast.139), channel_id=1, source_target_pairs={{0,2},{2,0},{1,3},{3,1},{4,6},{6,4},{5,7},{7,5},{8,10},{10,8},{9,1... | collective-permute-start | bytes 3145736 | tf_op jit(solution)/shard_map/ppermute | solution.py:221
  33.2 24.2 %collective-permute-start.7 = (bf16[512,1024]{1,0:T(8,128)(2,1)S(1)}, bf16[512,1024]{1,0:T(8,128)(2,1)S(1)}, u32[]{:S(2)}, u32[]{:S(2)}) collective-permute-start(bf16[512,1024]{1,0:T(8,128)(2,1)S(1)} %bitcast.140), channel_id=1, source_target_pairs={{0,1},{1,0},{2,3},{3,2},{4,5},{5,4},{6,7},{7,6},{8,9},{9,8},{10,11... | collective-permute-start | bytes 3145736 | tf_op jit(solution)/shard_map/ppermute | solution.py:222
  33.2 23.6 %collective-permute-start.4 = (bf16[128,1152]{1,0:T(8,128)(2,1)}, bf16[128,1152]{1,0:T(8,128)(2,1)S(1)}, u32[]{:S(2)}, u32[]{:S(2)}) collective-permute-start(bf16[128,1152]{1,0:T(8,128)(2,1)} %get-tuple-element.45), channel_id=1, source_target_pairs={{0,8},{4,12},{8,0},{12,4},{1,9},{5,13},{9,1},{13,5},{2,10},{6,14},... | collective-permute-start | bytes 884744 | tf_op jit(solution)/shard_map/ppermute | solution.py:218
  42.3 14.5 %collective-permute-start.5 = (bf16[128,1152]{1,0:T(8,128)(2,1)}, bf16[128,1152]{1,0:T(8,128)(2,1)S(1)}, u32[]{:S(2)}, u32[]{:S(2)}) collective-permute-start(bf16[128,1152]{1,0:T(8,128)(2,1)} %get-tuple-element.47), channel_id=1, source_target_pairs={{0,12},{4,0},{8,4},{12,8},{1,13},{5,1},{9,5},{13,9},{2,14},{6,2},{... | collective-permute-start | bytes 884744 | tf_op jit(solution)/shard_map/ppermute | solution.py:218
  56.8 34.8 %collective-permute-start.11 = (bf16[512,1152]{1,0:T(8,128)(2,1)S(1)}, bf16[512,1152]{1,0:T(8,128)(2,1)S(1)}, u32[]{:S(2)}, u32[]{:S(2)}) collective-permute-start(bf16[512,1152]{1,0:T(8,128)(2,1)S(1)} %bitcast.160), channel_id=1, source_target_pairs={{0,2},{2,0},{1,3},{3,1},{4,6},{6,4},{5,7},{7,5},{8,10},{10,8},{9,1... | collective-permute-start | bytes 3538952 | tf_op jit(solution)/shard_map/ppermute | solution.py:221
  57.4 33.3 %collective-permute-start.12 = (bf16[512,1152]{1,0:T(8,128)(2,1)S(1)}, bf16[512,1152]{1,0:T(8,128)(2,1)S(1)}, u32[]{:S(2)}, u32[]{:S(2)}) collective-permute-start(bf16[512,1152]{1,0:T(8,128)(2,1)S(1)} %bitcast.161), channel_id=1, source_target_pairs={{0,1},{1,0},{2,3},{3,2},{4,5},{5,4},{6,7},{7,6},{8,9},{9,8},{10,11... | collective-permute-start | bytes 3538952 | tf_op jit(solution)/shard_map/ppermute | solution.py:222
  57.4 17.0 %collective-permute-start.8 = (bf16[128,1024]{1,0:T(8,128)(2,1)S(1)}, bf16[128,1024]{1,0:T(8,128)(2,1)S(1)}, u32[]{:S(2)}, u32[]{:S(2)}) collective-permute-start(bf16[128,1024]{1,0:T(8,128)(2,1)S(1)} %copy-done.38), channel_id=1, source_target_pairs={{0,4},{4,8},{8,12},{12,0},{1,5},{5,9},{9,13},{13,1},{2,6},{6,10},{... | collective-permute-start | bytes 786440 | tf_op jit(solution)/shard_map/ppermute | solution.py:218
  67.6 17.8 %collective-permute-start.9 = (bf16[128,1024]{1,0:T(8,128)(2,1)S(1)}, bf16[128,1024]{1,0:T(8,128)(2,1)S(1)}, u32[]{:S(2)}, u32[]{:S(2)}) collective-permute-start(bf16[128,1024]{1,0:T(8,128)(2,1)S(1)} %copy-done.37), channel_id=1, source_target_pairs={{0,8},{4,12},{8,0},{12,4},{1,9},{5,13},{9,1},{13,5},{2,10},{6,14},... | collective-permute-start | bytes 786440 | tf_op jit(solution)/shard_map/ppermute | solution.py:218
  68.6 17.5 %collective-permute-start.10 = (bf16[128,1024]{1,0:T(8,128)(2,1)S(1)}, bf16[128,1024]{1,0:T(8,128)(2,1)S(1)}, u32[]{:S(2)}, u32[]{:S(2)}) collective-permute-start(bf16[128,1024]{1,0:T(8,128)(2,1)S(1)} %copy-done.36), channel_id=1, source_target_pairs={{0,12},{4,0},{8,4},{12,8},{1,13},{5,1},{9,5},{13,9},{2,14},{6,2},{... | collective-permute-start | bytes 786440 | tf_op jit(solution)/shard_map/ppermute | solution.py:218
  74.4 22.3 %collective-permute-start.13 = (bf16[512,1024]{1,0:T(8,128)(2,1)S(1)}, bf16[512,1024]{1,0:T(8,128)(2,1)S(1)}, u32[]{:S(2)}, u32[]{:S(2)}) collective-permute-start(bf16[512,1024]{1,0:T(8,128)(2,1)S(1)} %collective-permute-done.6), channel_id=1, source_target_pairs={{0,1},{1,0},{2,3},{3,2},{4,5},{5,4},{6,7},{7,6},{8,9},{9,8},{10,11... | collective-permute-start | bytes 3145736 | tf_op jit(solution)/shard_map/ppermute | solution.py:226
  86.8 30.3 %collective-permute-start.21 = (bf16[512,1024]{1,0:T(8,128)(2,1)}, bf16[512,1024]{1,0:T(8,128)(2,1)S(1)}, u32[]{:S(2)}, u32[]{:S(2)}) collective-permute-start(bf16[512,1024]{1,0:T(8,128)(2,1)} %bitcast.16), channel_id=1, source_target_pairs={{0,1},{1,0},{2,3},{3,2},{4,5},{5,4},{6,7},{7,6},{8,9},{9,8},{10,11... | collective-permute-start | bytes 3145736 | tf_op jit(solution)/shard_map/ppermute | solution.py:222
  86.8 84.4 %collective-permute-start.33 = (bf16[512,1024]{1,0:T(8,128)(2,1)}, bf16[512,1024]{1,0:T(8,128)(2,1)}, u32[]{:S(2)}, u32[]{:S(2)}) collective-permute-start(bf16[512,1024]{1,0:T(8,128)(2,1)} %bitcast.16), channel_id=1, source_target_pairs={{0,2},{2,0},{1,3},{3,1},{4,6},{6,4},{5,7},{7,5},{8,10},{10,8},{9,1... | collective-permute-start | bytes 3145736 | tf_op jit(solution)/shard_map/ppermute | solution.py:221
  92.1 28.3 %collective-permute-start.17 = (bf16[512,1152]{1,0:T(8,128)(2,1)S(1)}, bf16[512,1152]{1,0:T(8,128)(2,1)S(1)}, u32[]{:S(2)}, u32[]{:S(2)}) collective-permute-start(bf16[512,1152]{1,0:T(8,128)(2,1)S(1)} %collective-permute-done.11), channel_id=1, source_target_pairs={{0,1},{1,0},{2,3},{3,2},{4,5},{5,4},{6,7},{7,6},{8,9},{9,8},{10,11... | collective-permute-start | bytes 3538952 | tf_op jit(solution)/shard_map/ppermute | solution.py:226
  103.5 12.5 %collective-permute-start.16 = (bf16[128,512]{1,0:T(8,128)(2,1)S(1)}, bf16[128,512]{1,0:T(8,128)(2,1)S(1)}, u32[]{:S(2)}, u32[]{:S(2)}) collective-permute-start(bf16[128,512]{1,0:T(8,128)(2,1)S(1)} %copy-done.42), channel_id=1, source_target_pairs={{0,12},{4,0},{8,4},{12,8},{1,13},{5,1},{9,5},{13,9},{2,14},{6,2},{... | collective-permute-start | bytes 393224 | tf_op jit(solution)/shard_map/ppermute | solution.py:218
  116.1 55.2 %collective-permute-start.34 = (bf16[512,512]{1,0:T(8,128)(2,1)S(1)}, bf16[512,512]{1,0:T(8,128)(2,1)}, u32[]{:S(2)}, u32[]{:S(2)}) collective-permute-start(bf16[512,512]{1,0:T(8,128)(2,1)S(1)} %bitcast.154), channel_id=1, source_target_pairs={{0,2},{2,0},{1,3},{3,1},{4,6},{6,4},{5,7},{7,5},{8,10},{10,8},{9,1... | collective-permute-start | bytes 1572872 | tf_op jit(solution)/shard_map/ppermute | solution.py:221
  120.4 13.9 %collective-permute-start.20 = (bf16[128,512]{1,0:T(8,128)(2,1)S(1)}, bf16[128,512]{1,0:T(8,128)(2,1)S(1)}, u32[]{:S(2)}, u32[]{:S(2)}) collective-permute-start(bf16[128,512]{1,0:T(8,128)(2,1)S(1)} %get-tuple-element.68), channel_id=1, source_target_pairs={{0,12},{4,0},{8,4},{12,8},{1,13},{5,1},{9,5},{13,9},{2,14},{6,2},{... | collective-permute-start | bytes 393224 | tf_op jit(solution)/shard_map/ppermute | solution.py:218
  141.6 13.4 %collective-permute-start.24 = (f32[128,640]{1,0:T(8,128)}, f32[128,640]{1,0:T(8,128)}, u32[]{:S(2)}, u32[]{:S(2)}) collective-permute-start(f32[128,640]{1,0:T(8,128)} %bitcast.173), channel_id=1, source_target_pairs={{0,4},{1,5},{2,6},{3,7},{16,20},{17,21},{18,22},{19,23}} | collective-permute-start | bytes 983048 | tf_op jit(solution)/shard_map/ppermute | solution.py:183
  156.9 14.4 %collective-permute-start.25 = (f32[128,640]{1,0:T(8,128)}, f32[128,640]{1,0:T(8,128)}, u32[]{:S(2)}, u32[]{:S(2)}) collective-permute-start(f32[128,640]{1,0:T(8,128)} %bitcast_add_fusion.7), channel_id=1, source_target_pairs={{0,4},{4,8},{1,5},{5,9},{2,6},{6,10},{3,7},{7,11},{16,20},{20,24},... | collective-permute-start | bytes 983048 | tf_op jit(solution)/shard_map/ppermute | solution.py:183
  164.1 13.8 %collective-permute-start.35 = (bf16[512,512]{1,0:T(8,128)(2,1)S(1)}, bf16[512,512]{1,0:T(8,128)(2,1)}, u32[]{:S(2)}, u32[]{:S(2)}) collective-permute-start(bf16[512,512]{1,0:T(8,128)(2,1)S(1)} %bitcast.149), channel_id=1, source_target_pairs={{0,2},{2,0},{1,3},{3,1},{4,6},{6,4},{5,7},{7,5},{8,10},{10,8},{9,1... | collective-permute-start | bytes 1572872 | tf_op jit(solution)/shard_map/ppermute | solution.py:221
  171.3 32.9 %collective-permute-start.36 = (bf16[512,1024]{1,0:T(8,128)(2,1)}, bf16[512,1024]{1,0:T(8,128)(2,1)S(1)}, u32[]{:S(2)}, u32[]{:S(2)}) collective-permute-start(bf16[512,1024]{1,0:T(8,128)(2,1)} %collective-permute-done.33), channel_id=1, source_target_pairs={{0,1},{1,0},{2,3},{3,2},{4,5},{5,4},{6,7},{7,6},{8,9},{9,8},{10,11... | collective-permute-start | bytes 3145736 | tf_op jit(solution)/shard_map/ppermute | solution.py:235
  171.4 28.9 %collective-permute-start.37 = (bf16[512,512]{1,0:T(8,128)(2,1)}, bf16[512,512]{1,0:T(8,128)(2,1)S(1)}, u32[]{:S(2)}, u32[]{:S(2)}) collective-permute-start(bf16[512,512]{1,0:T(8,128)(2,1)} %collective-permute-done.34), channel_id=1, source_target_pairs={{0,1},{1,0},{2,3},{3,2},{4,5},{5,4},{6,7},{7,6},{8,9},{9,8},{10,11... | collective-permute-start | bytes 1572872 | tf_op jit(solution)/shard_map/ppermute | solution.py:235
  177.9 25.7 %collective-permute-start.38 = (bf16[512,512]{1,0:T(8,128)(2,1)}, bf16[512,512]{1,0:T(8,128)(2,1)S(1)}, u32[]{:S(2)}, u32[]{:S(2)}) collective-permute-start(bf16[512,512]{1,0:T(8,128)(2,1)} %collective-permute-done.35), channel_id=1, source_target_pairs={{0,1},{1,0},{2,3},{3,2},{4,5},{5,4},{6,7},{7,6},{8,9},{9,8},{10,11... | collective-permute-start | bytes 1572872 | tf_op jit(solution)/shard_map/ppermute | solution.py:235
  180.5 12.2 %collective-permute-start.26 = (f32[128,640]{1,0:T(8,128)S(1)}, f32[128,640]{1,0:T(8,128)S(1)}, u32[]{:S(2)}, u32[]{:S(2)}) collective-permute-start(f32[128,640]{1,0:T(8,128)S(1)} %bitcast_add_fusion.8), channel_id=1, source_target_pairs={{0,4},{4,8},{8,12},{1,5},{5,9},{9,13},{2,6},{6,10},{10,14},{3,7},{... | collective-permute-start | bytes 983048 | tf_op jit(solution)/shard_map/ppermute | solution.py:183
  184.4 12.3 %collective-permute-start.29 = (f32[128,640]{1,0:T(8,128)S(1)}, f32[128,640]{1,0:T(8,128)S(1)}, u32[]{:S(2)}, u32[]{:S(2)}) collective-permute-start(f32[128,640]{1,0:T(8,128)S(1)} %bitcast_add_fusion.6), channel_id=1, source_target_pairs={{12,8},{8,4},{4,0},{13,9},{9,5},{5,1},{14,10},{10,6},{6,2},{15,11}... | collective-permute-start | bytes 983048 | tf_op jit(solution)/shard_map/ppermute | solution.py:183
  197.4 61.3 %collective-permute-start.30 = (f32[128,128]{1,0:T(8,128)}, f32[128,128]{1,0:T(8,128)S(1)}, u32[]{:S(2)}, u32[]{:S(2)}) collective-permute-start(f32[128,128]{1,0:T(8,128)} %get-tuple-element.149), channel_id=1, source_target_pairs={{0,4},{1,5},{2,6},{3,7},{4,8},{5,9},{6,10},{7,11},{8,12},{9,13},{1... | collective-permute-start | bytes 196616 | tf_op jit(solution)/shard_map/ppermute | solution.py:169
  199.8 62.6 %collective-permute-start.31 = (f32[128,128]{1,0:T(8,128)}, f32[128,128]{1,0:T(8,128)S(1)}, u32[]{:S(2)}, u32[]{:S(2)}) collective-permute-start(f32[128,128]{1,0:T(8,128)} %get-tuple-element.148), channel_id=1, source_target_pairs={{0,5},{1,4},{2,7},{3,6},{4,9},{5,8},{6,11},{7,10},{8,13},{9,12},{1... | collective-permute-start | bytes 196616 | tf_op jit(solution)/shard_map/ppermute | solution.py:169
  200.2 62.2 %collective-permute-start.32 = (f32[128,128]{1,0:T(8,128)S(1)}, f32[128,128]{1,0:T(8,128)S(1)}, u32[]{:S(2)}, u32[]{:S(2)}) collective-permute-start(f32[128,128]{1,0:T(8,128)S(1)} %get-tuple-element.147), channel_id=1, source_target_pairs={{0,8},{1,9},{2,10},{3,11},{4,12},{5,13},{6,14},{7,15},{8,1},{9,0},... | collective-permute-start | bytes 196616 | tf_op jit(solution)/shard_map/ppermute | solution.py:171
  210.9 13.4 %collective-permute-start.39 = (f32[128,640]{1,0:T(8,128)}, f32[128,640]{1,0:T(8,128)}, u32[]{:S(2)}, u32[]{:S(2)}) collective-permute-start(f32[128,640]{1,0:T(8,128)} %bitcast.174), channel_id=1, source_target_pairs={{0,4},{1,5},{2,6},{3,7},{16,20},{17,21},{18,22},{19,23}} | collective-permute-start | bytes 983048 | tf_op jit(solution)/shard_map/ppermute | solution.py:183
  (61 other events, 610.5 us)

commit v9 on v7

--- a/solution.py
+++ b/solution.py
@@ -116,18 +116,18 @@
     )(place.reshape(1).astype(jnp.int32), *parts)
 
 
-def chain(planes, z, sums, up):
+def chain(planes, z, sums, up, ahead):
     rows = sums.shape[0] // planes
-    got = first = None
+    got = early = None
     for step in range(1, planes):
         plane = planes - step + z if up else z - planes + step
         sent = lax.dynamic_slice_in_dim(sums, jnp.clip(plane, 0, planes - 1) * rows, rows, 0)
         if got is not None:
-            sent = sent + got
+            sent = sent + (after(got, *ahead) if step == 2 else got)
         pairs = [(i, i + 1) for i in range(step)] if up else [(planes - 1 - i, planes - 2 - i) for i in range(step)]
+        early = sent if step < 4 else early
         got = lax.ppermute(sent, "z", pairs)
-        first = got if first is None else first
-    return got, first
+    return got, early
 
 
 def on_device(planes, slab, factor):
@@ -154,7 +154,12 @@
         for shift in range(1, planes):
             piece = pieces[j][shift]
             if len(sent) >= WINDOW:
-                piece = after(piece, sent[-WINDOW], *(waits[min(j, last - 1) - 2] if j > 1 else ()))
+                piece = after(
+                    piece,
+                    sent[-WINDOW],
+                    *(waits[min(j, last - 1) - 2] if j > 1 else ()),
+                    *(held[j - 3][3:] if j > 2 else ()),
+                )
             sent.append(lax.ppermute(piece, "z", [(s, (s + shift) % planes) for s in range(planes)]))
             arrived.append(sent[-1])
         stack = stacked(arrived)
@@ -162,22 +167,25 @@
         beside = lax.ppermute(stack, "c", SWAP)
         waits.append((across, beside))
         held.append([stack, beside, across])
+        if j < last - 1:
+            held[j].append(lax.ppermute(across, "c", SWAP))
     flat = [[b[:, : size * cells] for b in held[j][:2]] for j, (_, size) in enumerate(chunks)]
     sums = [sum(nt_dot(flat[j][0], flat[j][k]) for j in range(last + 1)) for k in range(2)]
     parts, gate = [], None
     for half in range(2):
         if half:
             for j in range(last + 1):
-                across = after(held[j][2], *gate) if j >= last - 1 else held[j][2]
-                held[j].append(lax.ppermute(across, "c", SWAP))
+                if j >= last - 1:
+                    held[j][2] = after(held[j][2], *gate)
+                    held[j].append(lax.ppermute(held[j][2], "c", SWAP))
                 flat[j] += [b[:, : chunks[j][1] * cells] for b in held[j][2:]]
             sums = [sum(nt_dot(flat[j][0], flat[j][k]) for j in range(last + 1)) for k in range(2, 4)]
         both = jnp.concatenate(sums, axis=1)
-        up, first_up = chain(planes, z, both, True)
-        down, first_down = chain(planes, z, both, False)
-        gate = (first_up, first_down)
+        up, early_up = chain(planes, z, both, True, parts[1:3])
+        down, early_down = chain(planes, z, both, False, parts[1:3])
+        gate = (early_up, early_down)
         parts += [lax.dynamic_slice_in_dim(both, z * rows, rows, 0), up, down]
-    factors = after([b[:, chunks[1][1] * cells :] for b in held[1]], *gate)
+    factors = [b[:, chunks[1][1] * cells :] for b in held[1]]
     gram = finish(planes, total, place, parts)
     own = per_plane // 4
     whole = [sum(tn_dot(flat[j][k], factors[k]) for k in range(4)) for j in range(last + 1)]

time: 224 us -> 233 us (1.040)
  starting transfers between devices: 61.5 us -> 80.1 us
  local copies, waits for them, and re-layouts: 23.5 us -> 14.5 us
  other arithmetic: 7.43 us -> 2.48 us
  matrix products: 19.7 us -> 24.4 us
    ppermute x12, waiting for transfers between devices: 13.8 us -> 48.7 us  [chain(): got = lax.ppermute(sent, 'z', pairs)]
    ppermute x4, waiting for transfers between devices: 25.8 us -> 0.73 us  [on_device(): across = lax.ppermute(stack, 'y', SWAP)]
    ppermute x12, starting transfers between devices: 28 us -> 41.9 us  [on_device(): lax.ppermute(piece, 'z', [(s, (s + shift) % planes) for s in range(planes)])]
    ppermute x12, waiting for transfers between devices: 66.3 us -> 56.5 us  [on_device(): lax.ppermute(piece, 'z', [(s, (s + shift) % planes) for s in range(planes)])]
    ppermute x12, starting transfers between devices: 28.8 us -> 34.6 us  [chain(): got = lax.ppermute(sent, 'z', pairs)]
    unnamed x86 -> x22, local copies, waits for them, and re-layouts: 9.51 us -> 4.09 us
    add x4, other arithmetic: 4.66 us -> 0.79 us  [chain(): sent = sent + (after(got, *ahead) if step == 2 else got)]
    slice x4 -> x0, local copies, waits for them, and re-layouts: 3.66 us -> none  [on_device(): factors = after([b[:, chunks[1][1] * cells:] for b in held[1]], *gate)]
  transfers between devices with their start and end apart: 36 -> 36, of which waited for: 11 -> 14; matrix products, arithmetic and copies ran while one was open for 18% -> 16% of each run, Pallas kernels for 0% -> 0%
where the time goes in v9:
time: 233 us; the launch traced here: 232 us
  waiting for transfers between devices  106 us (45%)
  starting transfers between devices  80.1 us (34%)
  matrix products  24.4 us (10%)
  local copies, waits for them, and re-layouts  14.5 us (6%)
  Pallas kernels  3.25 us (1%)
  other arithmetic  2.48 us (1%)
    ppermute x12, waiting for transfers between devices, on_device(): lax.ppermute(piece, 'z', [(s, (s + shift) % planes) for s in range(planes)])  56.5 us
    ppermute x12, waiting for transfers between devices, chain(): got = lax.ppermute(sent, 'z', pairs)  48.7 us
    ppermute x12, starting transfers between devices, on_device(): lax.ppermute(piece, 'z', [(s, (s + shift) % planes) for s in range(planes)])  41.9 us
    ppermute x12, starting transfers between devices, chain(): got = lax.ppermute(sent, 'z', pairs)  34.6 us
    dot_general x16, matrix products, nt_dot(): lax.dot_general(a, b, (((1,), (1,)), ((), ())), preferred_element_type=jn...  14.4 us
    dot_general x16, matrix products, tn_dot(): lax.dot_general(a, b, (((0,), (0,)), ((), ())), preferred_element_type=jn...  10 us
    pallas_call x1, local copies, waits for them, and re-layouts, unfold(): pl.pallas_call(functools.partial(unfold_kernel, planes, per_plane, chunks...  5.86 us
  transfers between devices with their start and end apart: 36, of which 14 were waited for; matrix products, arithmetic and copies ran while one was open for 16% of the time, Pallas kernels for 0%

profile of v9, /device:TPU:0, one launch (start us, length us, event | category | flops | bytes accessed | tf_op | source)
XLA Modules:
  0.0 232.2 jit_solution(11962647967503035322)
XLA Ops:
  0.6 2.2 copy-done
  3.6 2.0 unfold.2
  5.6 3.1 %collective-permute-start = (bf16[128,1024]{1,0:T(8,128)(2,1)S(1)}, bf16[128,1024]{1,0:T(8,128)(2,1)}, u32[]{:S(2)}, u32[]{:S(2)}) collective-permute-start(bf16[128,1024]{1,0:T(8,128)(2,1)S(1)} %get-tuple-element.32), channel_id=1, source_target_pairs={{0,4},{4,8},{8,12},{12,0},{1,5},{5,9},{9,13},{13,1},{2,6},{6,10},{... | collective-permute-start | bytes 786440 | tf_op jit(solution)/shard_map/ppermute | solution.py:163
  8.6 2.6 %collective-permute-start.1 = (bf16[128,1024]{1,0:T(8,128)(2,1)S(1)}, bf16[128,1024]{1,0:T(8,128)(2,1)}, u32[]{:S(2)}, u32[]{:S(2)}) collective-permute-start(bf16[128,1024]{1,0:T(8,128)(2,1)S(1)} %get-tuple-element.33), channel_id=1, source_target_pairs={{0,8},{4,12},{8,0},{12,4},{1,9},{5,13},{9,1},{13,5},{2,10},{6,14},... | collective-permute-start | bytes 786440 | tf_op jit(solution)/shard_map/ppermute | solution.py:163
  12.7 5.9 %unfold.3 = (bf16[4,128,1408]{2,1,0:T(8,128)(2,1)S(1)}, bf16[128,1408]{1,0:T(8,128)(2,1)}, bf16[128,1408]{1,0:T(8,128)(2,1)}, bf16[128,1408]{1,0:T(8,128)(2,1)},...) fusion(bf16[4,128,1408]{2,1,0:T(8,128)(2,1)S(1)} %broadcast_in_, ...), kind=kCustom, calls=%fused_computation.100 | custom fusion | bytes 7503880 | tf_op jit(solution)/shard_map/unfold/pallas_call | solution.py:67
  21.8 7.5 %collective-permute-done.1 = bf16[128,1024]{1,0:T(8,128)(2,1)} collective-permute-done((bf16[128,1024]{1,0:T(8,128)(2,1)S(1)}, bf16[128,1024]{1,0:T(8,128)(2,1)}, u32[]{:S(2)}, u32[]{:S(2)}) %collective-permute-start.1) | collective-permute-done | bytes 262176 | tf_op jit(solution)/shard_map/ppermute | solution.py:163
  31.2 1.8 collective-permute-start.6
  33.2 10.7 %collective-permute-start.4 = (bf16[128,1408]{1,0:T(8,128)(2,1)}, bf16[128,1408]{1,0:T(8,128)(2,1)S(1)}, u32[]{:S(2)}, u32[]{:S(2)}) collective-permute-start(bf16[128,1408]{1,0:T(8,128)(2,1)} %get-tuple-element.39), channel_id=1, source_target_pairs={{0,8},{4,12},{8,0},{12,4},{1,9},{5,13},{9,1},{13,5},{2,10},{6,14},... | collective-permute-start | bytes 1081352 | tf_op jit(solution)/shard_map/ppermute | solution.py:163
  43.9 3.5 %collective-permute-start.5 = (bf16[128,1408]{1,0:T(8,128)(2,1)}, bf16[128,1408]{1,0:T(8,128)(2,1)S(1)}, u32[]{:S(2)}, u32[]{:S(2)}) collective-permute-start(bf16[128,1408]{1,0:T(8,128)(2,1)} %get-tuple-element.41), channel_id=1, source_target_pairs={{0,12},{4,0},{8,4},{12,8},{1,13},{5,1},{9,5},{13,9},{2,14},{6,2},{... | collective-permute-start | bytes 1081352 | tf_op jit(solution)/shard_map/ppermute | solution.py:163
  48.4 12.7 %collective-permute-done.4 = bf16[128,1408]{1,0:T(8,128)(2,1)S(1)} collective-permute-done((bf16[128,1408]{1,0:T(8,128)(2,1)}, bf16[128,1408]{1,0:T(8,128)(2,1)S(1)}, u32[]{:S(2)}, u32[]{:S(2)}) %collective-permute-start.4) | collective-permute-done | bytes 360480 | tf_op jit(solution)/shard_map/ppermute | solution.py:163
  61.2 8.3 %collective-permute-start.8 = (bf16[128,1280]{1,0:T(8,128)(2,1)}, bf16[128,1280]{1,0:T(8,128)(2,1)S(1)}, u32[]{:S(2)}, u32[]{:S(2)}) collective-permute-start(bf16[128,1280]{1,0:T(8,128)(2,1)} %get-tuple-element.44), channel_id=1, source_target_pairs={{0,4},{4,8},{8,12},{12,0},{1,5},{5,9},{9,13},{13,1},{2,6},{6,10},{... | collective-permute-start | bytes 983048 | tf_op jit(solution)/shard_map/ppermute | solution.py:163
  71.1 2.8 %collective-permute-start.10 = (bf16[128,1280]{1,0:T(8,128)(2,1)S(1)}, bf16[128,1280]{1,0:T(8,128)(2,1)S(1)}, u32[]{:S(2)}, u32[]{:S(2)}) collective-permute-start(bf16[128,1280]{1,0:T(8,128)(2,1)S(1)} %copy-done.6), channel_id=1, source_target_pairs={{0,12},{4,0},{8,4},{12,8},{1,13},{5,1},{9,5},{13,9},{2,14},{6,2},{... | collective-permute-start | bytes 983048 | tf_op jit(solution)/shard_map/ppermute | solution.py:163
  74.5 6.5 %collective-permute-done.8 = bf16[128,1280]{1,0:T(8,128)(2,1)S(1)} collective-permute-done((bf16[128,1280]{1,0:T(8,128)(2,1)}, bf16[128,1280]{1,0:T(8,128)(2,1)S(1)}, u32[]{:S(2)}, u32[]{:S(2)}) %collective-permute-start.8) | collective-permute-done | bytes 327712 | tf_op jit(solution)/shard_map/ppermute | solution.py:163
  81.0 20.3 %collective-permute-done.9 = bf16[128,1280]{1,0:T(8,128)(2,1)S(1)} collective-permute-done((bf16[128,1280]{1,0:T(8,128)(2,1)S(1)}, bf16[128,1280]{1,0:T(8,128)(2,1)S(1)}, u32[]{:S(2)}, u32[]{:S(2)}) %collective-permute-start.9) | collective-permute-done | bytes 327712 | tf_op jit(solution)/shard_map/ppermute | solution.py:163
  111.0 3.4 %collective-permute-start.14 = (bf16[128,512]{1,0:T(8,128)(2,1)S(1)}, bf16[128,512]{1,0:T(8,128)(2,1)S(1)}, u32[]{:S(2)}, u32[]{:S(2)}) collective-permute-start(bf16[128,512]{1,0:T(8,128)(2,1)S(1)} %copy-done.8), channel_id=1, source_target_pairs={{0,12},{4,0},{8,4},{12,8},{1,13},{5,1},{9,5},{13,9},{2,14},{6,2},{... | collective-permute-start | bytes 393224 | tf_op jit(solution)/shard_map/ppermute | solution.py:163
  114.4 3.3 %collective-permute-done.12 = bf16[128,512]{1,0:T(8,128)(2,1)S(1)} collective-permute-done((bf16[128,512]{1,0:T(8,128)(2,1)S(1)}, bf16[128,512]{1,0:T(8,128)(2,1)S(1)}, u32[]{:S(2)}, u32[]{:S(2)}) %collective-permute-start.12) | collective-permute-done | bytes 131104 | tf_op jit(solution)/shard_map/ppermute | solution.py:163
  117.7 4.3 %collective-permute-start.13 = (bf16[128,512]{1,0:T(8,128)(2,1)S(1)}, bf16[128,512]{1,0:T(8,128)(2,1)S(1)}, u32[]{:S(2)}, u32[]{:S(2)}) collective-permute-start(bf16[128,512]{1,0:T(8,128)(2,1)S(1)} %copy-done.9), channel_id=1, source_target_pairs={{0,8},{4,12},{8,0},{12,4},{1,9},{5,13},{9,1},{13,5},{2,10},{6,14},... | collective-permute-start | bytes 393224 | tf_op jit(solution)/shard_map/ppermute | solution.py:163
  122.1 6.2 %collective-permute-done.13 = bf16[128,512]{1,0:T(8,128)(2,1)S(1)} collective-permute-done((bf16[128,512]{1,0:T(8,128)(2,1)S(1)}, bf16[128,512]{1,0:T(8,128)(2,1)S(1)}, u32[]{:S(2)}, u32[]{:S(2)}) %collective-permute-start.13) | collective-permute-done | bytes 131104 | tf_op jit(solution)/shard_map/ppermute | solution.py:163
  131.0 2.0 fusion.7
  136.4 10.0 %collective-permute-done.18 = f32[128,1024]{1,0:T(8,128)S(1)} collective-permute-done((f32[128,1024]{1,0:T(8,128)S(1)}, f32[128,1024]{1,0:T(8,128)S(1)}, u32[]{:S(2)}, u32[]{:S(2)}) %collective-permute-start.18) | collective-permute-done | bytes 524320 | tf_op jit(solution)/shard_map/ppermute | solution.py:129
  146.6 4.4 %collective-permute-start.19 = (f32[128,1024]{1,0:T(8,128)S(1)}, f32[128,1024]{1,0:T(8,128)S(1)}, u32[]{:S(2)}, u32[]{:S(2)}) collective-permute-start(f32[128,1024]{1,0:T(8,128)S(1)} %get-tuple-element.95), channel_id=1, source_target_pairs={{0,4},{4,8},{1,5},{5,9},{2,6},{6,10},{3,7},{7,11},{16,20},{20,24},... | collective-permute-start | bytes 1572872 | tf_op jit(solution)/shard_map/ppermute | solution.py:129
  153.0 9.3 %collective-permute-done.19 = f32[128,1024]{1,0:T(8,128)S(1)} collective-permute-done((f32[128,1024]{1,0:T(8,128)S(1)}, f32[128,1024]{1,0:T(8,128)S(1)}, u32[]{:S(2)}, u32[]{:S(2)}) %collective-permute-start.19) | collective-permute-done | bytes 524320 | tf_op jit(solution)/shard_map/ppermute | solution.py:129
  163.2 7.3 %collective-permute-start.20 = (f32[128,1024]{1,0:T(8,128)S(1)}, f32[128,1024]{1,0:T(8,128)S(1)}, u32[]{:S(2)}, u32[]{:S(2)}) collective-permute-start(f32[128,1024]{1,0:T(8,128)S(1)} %get-tuple-element.93), channel_id=1, source_target_pairs={{0,4},{4,8},{8,12},{1,5},{5,9},{9,13},{2,6},{6,10},{10,14},{3,7},{... | collective-permute-start | bytes 1572872 | tf_op jit(solution)/shard_map/ppermute | solution.py:129
  173.4 2.0 fusion.8
  177.7 4.4 %collective-permute-start.30 = (f32[128,1024]{1,0:T(8,128)S(1)}, f32[128,1024]{1,0:T(8,128)S(1)}, u32[]{:S(2)}, u32[]{:S(2)}) collective-permute-start(f32[128,1024]{1,0:T(8,128)S(1)} %get-tuple-element.90), channel_id=1, source_target_pairs={{0,4},{1,5},{2,6},{3,7},{16,20},{17,21},{18,22},{19,23}} | collective-permute-start | bytes 1572872 | tf_op jit(solution)/shard_map/ppermute | solution.py:129
  183.8 2.6 %collective-permute-done.23.refs_2_ = f32[128,1024]{1,0:T(8,128)S(1)} collective-permute-done((f32[128,1024]{1,0:T(8,128)S(1)}, f32[128,1024]{1,0:T(8,128)S(1)}, u32[]{:S(2)}, u32[]{:S(2)}) %collective-permute-start.23) | collective-permute-done | bytes 524320 | tf_op jit(solution)/shard_map/ppermute | solution.py:129
  186.4 7.5 %collective-permute-done.30 = f32[128,1024]{1,0:T(8,128)S(1)} collective-permute-done((f32[128,1024]{1,0:T(8,128)S(1)}, f32[128,1024]{1,0:T(8,128)S(1)}, u32[]{:S(2)}, u32[]{:S(2)}) %collective-permute-start.30) | collective-permute-done | bytes 524320 | tf_op jit(solution)/shard_map/ppermute | solution.py:129
  194.0 4.4 %collective-permute-start.31 = (f32[128,1024]{1,0:T(8,128)S(1)}, f32[128,1024]{1,0:T(8,128)S(1)}, u32[]{:S(2)}, u32[]{:S(2)}) collective-permute-start(f32[128,1024]{1,0:T(8,128)S(1)} %get-tuple-element.88), channel_id=1, source_target_pairs={{0,4},{4,8},{1,5},{5,9},{2,6},{6,10},{3,7},{7,11},{16,20},{20,24},... | collective-permute-start | bytes 1572872 | tf_op jit(solution)/shard_map/ppermute | solution.py:129
  200.2 9.3 %collective-permute-done.31 = f32[128,1024]{1,0:T(8,128)S(1)} collective-permute-done((f32[128,1024]{1,0:T(8,128)S(1)}, f32[128,1024]{1,0:T(8,128)S(1)}, u32[]{:S(2)}, u32[]{:S(2)}) %collective-permute-start.31) | collective-permute-done | bytes 524320 | tf_op jit(solution)/shard_map/ppermute | solution.py:129
  209.7 7.2 %collective-permute-start.32 = (f32[128,1024]{1,0:T(8,128)S(1)}, f32[128,1024]{1,0:T(8,128)S(1)}, u32[]{:S(2)}, u32[]{:S(2)}) collective-permute-start(f32[128,1024]{1,0:T(8,128)S(1)} %get-tuple-element.86), channel_id=1, source_target_pairs={{0,4},{4,8},{8,12},{1,5},{5,9},{9,13},{2,6},{6,10},{10,14},{3,7},{... | collective-permute-start | bytes 1572872 | tf_op jit(solution)/shard_map/ppermute | solution.py:129
  220.9 5.9 %collective-permute-done.32.refs_4_ = f32[128,1024]{1,0:T(8,128)S(1)} collective-permute-done((f32[128,1024]{1,0:T(8,128)S(1)}, f32[128,1024]{1,0:T(8,128)S(1)}, u32[]{:S(2)}, u32[]{:S(2)}) %collective-permute-start.32) | collective-permute-done | bytes 524320 | tf_op jit(solution)/shard_map/ppermute | solution.py:129
  226.8 4.1 %collective-permute-done.35.refs_5_ = f32[128,1024]{1,0:T(8,128)S(1)} collective-permute-done((f32[128,1024]{1,0:T(8,128)S(1)}, f32[128,1024]{1,0:T(8,128)S(1)}, u32[]{:S(2)}, u32[]{:S(2)}) %collective-permute-start.35) | collective-permute-done | bytes 524320 | tf_op jit(solution)/shard_map/ppermute | solution.py:129
  (123 shorter events, 43.3 us)
Async XLA Ops:
  5.6 15.2 %collective-permute-start = (bf16[128,1024]{1,0:T(8,128)(2,1)S(1)}, bf16[128,1024]{1,0:T(8,128)(2,1)}, u32[]{:S(2)}, u32[]{:S(2)}) collective-permute-start(bf16[128,1024]{1,0:T(8,128)(2,1)S(1)} %get-tuple-element.32), channel_id=1, source_target_pairs={{0,4},{4,8},{8,12},{12,0},{1,5},{5,9},{9,13},{13,1},{2,6},{6,10},{... | collective-permute-start | bytes 786440 | tf_op jit(solution)/shard_map/ppermute | solution.py:163
  8.6 20.6 %collective-permute-start.1 = (bf16[128,1024]{1,0:T(8,128)(2,1)S(1)}, bf16[128,1024]{1,0:T(8,128)(2,1)}, u32[]{:S(2)}, u32[]{:S(2)}) collective-permute-start(bf16[128,1024]{1,0:T(8,128)(2,1)S(1)} %get-tuple-element.33), channel_id=1, source_target_pairs={{0,8},{4,12},{8,0},{12,4},{1,9},{5,13},{9,1},{13,5},{2,10},{6,14},... | collective-permute-start | bytes 786440 | tf_op jit(solution)/shard_map/ppermute | solution.py:163
  11.2 19.0 %collective-permute-start.2 = (bf16[128,1024]{1,0:T(8,128)(2,1)S(1)}, bf16[128,1024]{1,0:T(8,128)(2,1)}, u32[]{:S(2)}, u32[]{:S(2)}) collective-permute-start(bf16[128,1024]{1,0:T(8,128)(2,1)S(1)} %get-tuple-element.34), channel_id=1, source_target_pairs={{0,12},{4,0},{8,4},{12,8},{1,13},{5,1},{9,5},{13,9},{2,14},{6,2},{... | collective-permute-start | bytes 786440 | tf_op jit(solution)/shard_map/ppermute | solution.py:163
  18.6 28.8 %collective-permute-start.3 = (bf16[128,1408]{1,0:T(8,128)(2,1)}, bf16[128,1408]{1,0:T(8,128)(2,1)}, u32[]{:S(2)}, u32[]{:S(2)}) collective-permute-start(bf16[128,1408]{1,0:T(8,128)(2,1)} %get-tuple-element.63), channel_id=1, source_target_pairs={{0,4},{4,8},{8,12},{12,0},{1,5},{5,9},{9,13},{13,1},{2,6},{6,10},{... | collective-permute-start | bytes 1081352 | tf_op jit(solution)/shard_map/ppermute | solution.py:163
  31.2 29.9 %collective-permute-start.6 = (bf16[512,1024]{1,0:T(8,128)(2,1)S(1)}, bf16[512,1024]{1,0:T(8,128)(2,1)}, u32[]{:S(2)}, u32[]{:S(2)}) collective-permute-start(bf16[512,1024]{1,0:T(8,128)(2,1)S(1)} %bitcast.74), channel_id=1, source_target_pairs={{0,2},{2,0},{1,3},{3,1},{4,6},{6,4},{5,7},{7,5},{8,10},{10,8},{9,1... | collective-permute-start | bytes 3145736 | tf_op jit(solution)/shard_map/ppermute | solution.py:166
  33.1 28.1 %collective-permute-start.7 = (bf16[512,1024]{1,0:T(8,128)(2,1)S(1)}, bf16[512,1024]{1,0:T(8,128)(2,1)}, u32[]{:S(2)}, u32[]{:S(2)}) collective-permute-start(bf16[512,1024]{1,0:T(8,128)(2,1)S(1)} %bitcast.75), channel_id=1, source_target_pairs={{0,1},{1,0},{2,3},{3,2},{4,5},{5,4},{6,7},{7,6},{8,9},{9,8},{10,11... | collective-permute-start | bytes 3145736 | tf_op jit(solution)/shard_map/ppermute | solution.py:167
  33.2 27.9 %collective-permute-start.4 = (bf16[128,1408]{1,0:T(8,128)(2,1)}, bf16[128,1408]{1,0:T(8,128)(2,1)S(1)}, u32[]{:S(2)}, u32[]{:S(2)}) collective-permute-start(bf16[128,1408]{1,0:T(8,128)(2,1)} %get-tuple-element.39), channel_id=1, source_target_pairs={{0,8},{4,12},{8,0},{12,4},{1,9},{5,13},{9,1},{13,5},{2,10},{6,14},... | collective-permute-start | bytes 1081352 | tf_op jit(solution)/shard_map/ppermute | solution.py:163
  43.9 25.6 %collective-permute-start.5 = (bf16[128,1408]{1,0:T(8,128)(2,1)}, bf16[128,1408]{1,0:T(8,128)(2,1)S(1)}, u32[]{:S(2)}, u32[]{:S(2)}) collective-permute-start(bf16[128,1408]{1,0:T(8,128)(2,1)} %get-tuple-element.41), channel_id=1, source_target_pairs={{0,12},{4,0},{8,4},{12,8},{1,13},{5,1},{9,5},{13,9},{2,14},{6,2},{... | collective-permute-start | bytes 1081352 | tf_op jit(solution)/shard_map/ppermute | solution.py:163
  61.2 19.8 %collective-permute-start.8 = (bf16[128,1280]{1,0:T(8,128)(2,1)}, bf16[128,1280]{1,0:T(8,128)(2,1)S(1)}, u32[]{:S(2)}, u32[]{:S(2)}) collective-permute-start(bf16[128,1280]{1,0:T(8,128)(2,1)} %get-tuple-element.44), channel_id=1, source_target_pairs={{0,4},{4,8},{8,12},{12,0},{1,5},{5,9},{9,13},{13,1},{2,6},{6,10},{... | collective-permute-start | bytes 983048 | tf_op jit(solution)/shard_map/ppermute | solution.py:163
  69.6 35.8 %collective-permute-start.15 = (bf16[512,1408]{1,0:T(8,128)(2,1)S(1)}, bf16[512,1408]{1,0:T(8,128)(2,1)S(1)}, u32[]{:S(2)}, u32[]{:S(2)}) collective-permute-start(bf16[512,1408]{1,0:T(8,128)(2,1)S(1)} %bitcast.88), channel_id=1, source_target_pairs={{0,1},{1,0},{2,3},{3,2},{4,5},{5,4},{6,7},{7,6},{8,9},{9,8},{10,11... | collective-permute-start | bytes 4325384 | tf_op jit(solution)/shard_map/ppermute | solution.py:167
  69.7 34.0 %collective-permute-start.24 = (bf16[512,1408]{1,0:T(8,128)(2,1)S(1)}, bf16[512,1408]{1,0:T(8,128)(2,1)S(1)}, u32[]{:S(2)}, u32[]{:S(2)}) collective-permute-start(bf16[512,1408]{1,0:T(8,128)(2,1)S(1)} %bitcast.89), channel_id=1, source_target_pairs={{0,2},{2,0},{1,3},{3,1},{4,6},{6,4},{5,7},{7,5},{8,10},{10,8},{9,1... | collective-permute-start | bytes 4325384 | tf_op jit(solution)/shard_map/ppermute | solution.py:166
  71.1 30.3 %collective-permute-start.10 = (bf16[128,1280]{1,0:T(8,128)(2,1)S(1)}, bf16[128,1280]{1,0:T(8,128)(2,1)S(1)}, u32[]{:S(2)}, u32[]{:S(2)}) collective-permute-start(bf16[128,1280]{1,0:T(8,128)(2,1)S(1)} %copy-done.6), channel_id=1, source_target_pairs={{0,12},{4,0},{8,4},{12,8},{1,13},{5,1},{9,5},{13,9},{2,14},{6,2},{... | collective-permute-start | bytes 983048 | tf_op jit(solution)/shard_map/ppermute | solution.py:163
  73.9 27.4 %collective-permute-start.9 = (bf16[128,1280]{1,0:T(8,128)(2,1)S(1)}, bf16[128,1280]{1,0:T(8,128)(2,1)S(1)}, u32[]{:S(2)}, u32[]{:S(2)}) collective-permute-start(bf16[128,1280]{1,0:T(8,128)(2,1)S(1)} %copy-done.7), channel_id=1, source_target_pairs={{0,8},{4,12},{8,0},{12,4},{1,9},{5,13},{9,1},{13,5},{2,10},{6,14},... | collective-permute-start | bytes 983048 | tf_op jit(solution)/shard_map/ppermute | solution.py:163
  81.0 28.5 %collective-permute-start.11 = (bf16[512,1024]{1,0:T(8,128)(2,1)}, bf16[512,1024]{1,0:T(8,128)(2,1)S(1)}, u32[]{:S(2)}, u32[]{:S(2)}) collective-permute-start(bf16[512,1024]{1,0:T(8,128)(2,1)} %collective-permute-done.6), channel_id=1, source_target_pairs={{0,1},{1,0},{2,3},{3,2},{4,5},{5,4},{6,7},{7,6},{8,9},{9,8},{10,11... | collective-permute-start | bytes 3145736 | tf_op jit(solution)/shard_map/ppermute | solution.py:171
  101.4 28.2 %collective-permute-start.16 = (bf16[512,1280]{1,0:T(8,128)(2,1)S(1)}, bf16[512,1280]{1,0:T(8,128)(2,1)S(1)}, u32[]{:S(2)}, u32[]{:S(2)}) collective-permute-start(bf16[512,1280]{1,0:T(8,128)(2,1)S(1)} %bitcast.98), channel_id=1, source_target_pairs={{0,1},{1,0},{2,3},{3,2},{4,5},{5,4},{6,7},{7,6},{8,9},{9,8},{10,11... | collective-permute-start | bytes 3932168 | tf_op jit(solution)/shard_map/ppermute | solution.py:167
  101.5 61.0 %collective-permute-start.25 = (bf16[512,1280]{1,0:T(8,128)(2,1)S(1)}, bf16[512,1280]{1,0:T(8,128)(2,1)S(1)}, u32[]{:S(2)}, u32[]{:S(2)}) collective-permute-start(bf16[512,1280]{1,0:T(8,128)(2,1)S(1)} %bitcast.99), channel_id=1, source_target_pairs={{0,2},{2,0},{1,3},{3,1},{4,6},{6,4},{5,7},{7,5},{8,10},{10,8},{9,1... | collective-permute-start | bytes 3932168 | tf_op jit(solution)/shard_map/ppermute | solution.py:166
  103.7 48.5 %collective-permute-start.27 = (bf16[512,1408]{1,0:T(8,128)(2,1)S(1)}, bf16[512,1408]{1,0:T(8,128)(2,1)S(1)}, u32[]{:S(2)}, u32[]{:S(2)}) collective-permute-start(bf16[512,1408]{1,0:T(8,128)(2,1)S(1)} %collective-permute-done.24), channel_id=1, source_target_pairs={{0,1},{1,0},{2,3},{3,2},{4,5},{5,4},{6,7},{7,6},{8,9},{9,8},{10,11... | collective-permute-start | bytes 4325384 | tf_op jit(solution)/shard_map/ppermute | solution.py:171
  111.0 17.3 %collective-permute-start.14 = (bf16[128,512]{1,0:T(8,128)(2,1)S(1)}, bf16[128,512]{1,0:T(8,128)(2,1)S(1)}, u32[]{:S(2)}, u32[]{:S(2)}) collective-permute-start(bf16[128,512]{1,0:T(8,128)(2,1)S(1)} %copy-done.8), channel_id=1, source_target_pairs={{0,12},{4,0},{8,4},{12,8},{1,13},{5,1},{9,5},{13,9},{2,14},{6,2},{... | collective-permute-start | bytes 393224 | tf_op jit(solution)/shard_map/ppermute | solution.py:163
  133.1 13.4 %collective-permute-start.18 = (f32[128,1024]{1,0:T(8,128)S(1)}, f32[128,1024]{1,0:T(8,128)S(1)}, u32[]{:S(2)}, u32[]{:S(2)}) collective-permute-start(f32[128,1024]{1,0:T(8,128)S(1)} %get-tuple-element.97), channel_id=1, source_target_pairs={{0,4},{1,5},{2,6},{3,7},{16,20},{17,21},{18,22},{19,23}} | collective-permute-start | bytes 1572872 | tf_op jit(solution)/shard_map/ppermute | solution.py:129
  134.4 12.1 %collective-permute-start.21 = (f32[128,1024]{1,0:T(8,128)S(1)}, f32[128,1024]{1,0:T(8,128)S(1)}, u32[]{:S(2)}, u32[]{:S(2)}) collective-permute-start(f32[128,1024]{1,0:T(8,128)S(1)} %get-tuple-element.96), channel_id=1, source_target_pairs={{12,8},{13,9},{14,10},{15,11},{28,24},{29,25},{30,26},{31,27}} | collective-permute-start | bytes 1572872 | tf_op jit(solution)/shard_map/ppermute | solution.py:129
  135.8 35.9 %collective-permute-start.26 = (bf16[512,512]{1,0:T(8,128)(2,1)S(1)}, bf16[512,512]{1,0:T(8,128)(2,1)S(1)}, u32[]{:S(2)}, u32[]{:S(2)}) collective-permute-start(bf16[512,512]{1,0:T(8,128)(2,1)S(1)} %bitcast.84), channel_id=1, source_target_pairs={{0,2},{2,0},{1,3},{3,1},{4,6},{6,4},{5,7},{7,5},{8,10},{10,8},{9,1... | collective-permute-start | bytes 1572872 | tf_op jit(solution)/shard_map/ppermute | solution.py:166
  146.6 15.6 %collective-permute-start.19 = (f32[128,1024]{1,0:T(8,128)S(1)}, f32[128,1024]{1,0:T(8,128)S(1)}, u32[]{:S(2)}, u32[]{:S(2)}) collective-permute-start(f32[128,1024]{1,0:T(8,128)S(1)} %get-tuple-element.95), channel_id=1, source_target_pairs={{0,4},{4,8},{1,5},{5,9},{2,6},{6,10},{3,7},{7,11},{16,20},{20,24},... | collective-permute-start | bytes 1572872 | tf_op jit(solution)/shard_map/ppermute | solution.py:129
  151.1 11.2 %collective-permute-start.22 = (f32[128,1024]{1,0:T(8,128)S(1)}, f32[128,1024]{1,0:T(8,128)S(1)}, u32[]{:S(2)}, u32[]{:S(2)}) collective-permute-start(f32[128,1024]{1,0:T(8,128)S(1)} %get-tuple-element.94), channel_id=1, source_target_pairs={{12,8},{8,4},{13,9},{9,5},{14,10},{10,6},{15,11},{11,7},{28,24},{2... | collective-permute-start | bytes 1572872 | tf_op jit(solution)/shard_map/ppermute | solution.py:129
  162.5 13.4 %collective-permute-start.28 = (bf16[512,1280]{1,0:T(8,128)(2,1)S(1)}, bf16[512,1280]{1,0:T(8,128)(2,1)S(1)}, u32[]{:S(2)}, u32[]{:S(2)}) collective-permute-start(bf16[512,1280]{1,0:T(8,128)(2,1)S(1)} %collective-permute-done.25), channel_id=1, source_target_pairs={{0,1},{1,0},{2,3},{3,2},{4,5},{5,4},{6,7},{7,6},{8,9},{9,8},{10,11... | collective-permute-start | bytes 3932168 | tf_op jit(solution)/shard_map/ppermute | solution.py:180
  163.2 20.6 %collective-permute-start.20 = (f32[128,1024]{1,0:T(8,128)S(1)}, f32[128,1024]{1,0:T(8,128)S(1)}, u32[]{:S(2)}, u32[]{:S(2)}) collective-permute-start(f32[128,1024]{1,0:T(8,128)S(1)} %get-tuple-element.93), channel_id=1, source_target_pairs={{0,4},{4,8},{8,12},{1,5},{5,9},{9,13},{2,6},{6,10},{10,14},{3,7},{... | collective-permute-start | bytes 1572872 | tf_op jit(solution)/shard_map/ppermute | solution.py:129
  170.4 15.9 %collective-permute-start.23 = (f32[128,1024]{1,0:T(8,128)S(1)}, f32[128,1024]{1,0:T(8,128)S(1)}, u32[]{:S(2)}, u32[]{:S(2)}) collective-permute-start(f32[128,1024]{1,0:T(8,128)S(1)} %get-tuple-element.91), channel_id=1, source_target_pairs={{12,8},{8,4},{4,0},{13,9},{9,5},{5,1},{14,10},{10,6},{6,2},{15,11}... | collective-permute-start | bytes 1572872 | tf_op jit(solution)/shard_map/ppermute | solution.py:129
  177.7 16.2 %collective-permute-start.30 = (f32[128,1024]{1,0:T(8,128)S(1)}, f32[128,1024]{1,0:T(8,128)S(1)}, u32[]{:S(2)}, u32[]{:S(2)}) collective-permute-start(f32[128,1024]{1,0:T(8,128)S(1)} %get-tuple-element.90), channel_id=1, source_target_pairs={{0,4},{1,5},{2,6},{3,7},{16,20},{17,21},{18,22},{19,23}} | collective-permute-start | bytes 1572872 | tf_op jit(solution)/shard_map/ppermute | solution.py:129
  182.1 11.8 %collective-permute-start.33 = (f32[128,1024]{1,0:T(8,128)S(1)}, f32[128,1024]{1,0:T(8,128)S(1)}, u32[]{:S(2)}, u32[]{:S(2)}) collective-permute-start(f32[128,1024]{1,0:T(8,128)S(1)} %get-tuple-element.89), channel_id=1, source_target_pairs={{12,8},{13,9},{14,10},{15,11},{28,24},{29,25},{30,26},{31,27}} | collective-permute-start | bytes 1572872 | tf_op jit(solution)/shard_map/ppermute | solution.py:129
  194.0 15.4 %collective-permute-start.31 = (f32[128,1024]{1,0:T(8,128)S(1)}, f32[128,1024]{1,0:T(8,128)S(1)}, u32[]{:S(2)}, u32[]{:S(2)}) collective-permute-start(f32[128,1024]{1,0:T(8,128)S(1)} %get-tuple-element.88), channel_id=1, source_target_pairs={{0,4},{4,8},{1,5},{5,9},{2,6},{6,10},{3,7},{7,11},{16,20},{20,24},... | collective-permute-start | bytes 1572872 | tf_op jit(solution)/shard_map/ppermute | solution.py:129
  198.5 11.0 %collective-permute-start.34 = (f32[128,1024]{1,0:T(8,128)S(1)}, f32[128,1024]{1,0:T(8,128)S(1)}, u32[]{:S(2)}, u32[]{:S(2)}) collective-permute-start(f32[128,1024]{1,0:T(8,128)S(1)} %get-tuple-element.87), channel_id=1, source_target_pairs={{12,8},{8,4},{13,9},{9,5},{14,10},{10,6},{15,11},{11,7},{28,24},{2... | collective-permute-start | bytes 1572872 | tf_op jit(solution)/shard_map/ppermute | solution.py:129
  209.7 17.1 %collective-permute-start.32 = (f32[128,1024]{1,0:T(8,128)S(1)}, f32[128,1024]{1,0:T(8,128)S(1)}, u32[]{:S(2)}, u32[]{:S(2)}) collective-permute-start(f32[128,1024]{1,0:T(8,128)S(1)} %get-tuple-element.86), channel_id=1, source_target_pairs={{0,4},{4,8},{8,12},{1,5},{5,9},{9,13},{2,6},{6,10},{10,14},{3,7},{... | collective-permute-start | bytes 1572872 | tf_op jit(solution)/shard_map/ppermute | solution.py:129
  217.0 14.0 %collective-permute-start.35 = (f32[128,1024]{1,0:T(8,128)S(1)}, f32[128,1024]{1,0:T(8,128)S(1)}, u32[]{:S(2)}, u32[]{:S(2)}) collective-permute-start(f32[128,1024]{1,0:T(8,128)S(1)} %get-tuple-element.84), channel_id=1, source_target_pairs={{12,8},{8,4},{4,0},{13,9},{9,5},{5,1},{14,10},{10,6},{6,2},{15,11}... | collective-permute-start | bytes 1572872 | tf_op jit(solution)/shard_map/ppermute | solution.py:129
  (15 other events, 76.0 us)

commit v10 on v7

--- a/solution.py
+++ b/solution.py
@@ -18,7 +18,7 @@
 
 def chunks_of(per_plane):
     unit = per_plane // 16
-    sizes = [4 * unit, 5 * unit, 5 * unit, 2 * unit] if unit else [1] * per_plane
+    sizes = [4 * unit, 4 * unit, 4 * unit, 2 * unit, 2 * unit] if unit else [1] * per_plane
     return [(sum(sizes[:i]), size) for i, size in enumerate(sizes)]
 
 
@@ -154,7 +154,13 @@
         for shift in range(1, planes):
             piece = pieces[j][shift]
             if len(sent) >= WINDOW:
-                piece = after(piece, sent[-WINDOW], *(waits[min(j, last - 1) - 2] if j > 1 else ()))
+                piece = after(
+                    piece,
+                    sent[-WINDOW],
+                    *(waits[min(j, last - 1) - 2] if j > 1 else ()),
+                    *(held[min(j, last - 1) - 3][3:] if j > 2 and last > 3 else ()),
+                    *((held[j - 3][3], held[j - 2][1]) if j == last > 3 and shift == planes - 1 else ()),
+                )
             sent.append(lax.ppermute(piece, "z", [(s, (s + shift) % planes) for s in range(planes)]))
             arrived.append(sent[-1])
         stack = stacked(arrived)
@@ -162,14 +168,17 @@
         beside = lax.ppermute(stack, "c", SWAP)
         waits.append((across, beside))
         held.append([stack, beside, across])
+        if j < last - 1:
+            held[j].append(lax.ppermute(across, "c", SWAP))
     flat = [[b[:, : size * cells] for b in held[j][:2]] for j, (_, size) in enumerate(chunks)]
     sums = [sum(nt_dot(flat[j][0], flat[j][k]) for j in range(last + 1)) for k in range(2)]
     parts, gate = [], None
     for half in range(2):
         if half:
             for j in range(last + 1):
-                across = after(held[j][2], *gate) if j >= last - 1 else held[j][2]
-                held[j].append(lax.ppermute(across, "c", SWAP))
+                if j >= last - 1:
+                    held[j][2] = after(held[j][2], *gate)
+                    held[j].append(lax.ppermute(held[j][2], "c", SWAP))
                 flat[j] += [b[:, : chunks[j][1] * cells] for b in held[j][2:]]
             sums = [sum(nt_dot(flat[j][0], flat[j][k]) for j in range(last + 1)) for k in range(2, 4)]
         both = jnp.concatenate(sums, axis=1)
@@ -177,12 +186,23 @@
         down, first_down = chain(planes, z, both, False)
         gate = (first_up, first_down)
         parts += [lax.dynamic_slice_in_dim(both, z * rows, rows, 0), up, down]
-    factors = after([b[:, chunks[1][1] * cells :] for b in held[1]], *gate)
     gram = finish(planes, total, place, parts)
     own = per_plane // 4
-    whole = [sum(tn_dot(flat[j][k], factors[k]) for k in range(4)) for j in range(last + 1)]
-    whole = jnp.concatenate(whole, axis=0)
-    core = lax.dynamic_slice_in_dim(whole, place * own * cells, own * cells, 0)
+
+    def kept(mine, held):
+        out = []
+        for j, (start, size) in enumerate(chunks):
+            low, high = max(start, mine * own) - start, min(start + size, (mine + 1) * own) - start
+            if low < high:
+                out.append(
+                    sum(
+                        tn_dot(held[j][k][:, low * cells : high * cells], held[1][k][:, chunks[1][1] * cells :])
+                        for k in range(4)
+                    )
+                )
+        return jnp.concatenate(out, axis=0)
+
+    core = lax.switch(place, [functools.partial(kept, mine) for mine in range(4)], after(held, *gate))
     return (gram, core)
 
 

time: 224 us -> 222 us (level)
  starting transfers between devices: 61.5 us -> 80.8 us
  waiting for transfers between devices: 106 us -> 88.5 us
  local copies, waits for them, and re-layouts: 23.5 us -> 17.8 us
    ppermute x4 -> x5, waiting for transfers between devices: 25.8 us -> 5.57 us  [on_device(): across = lax.ppermute(stack, 'y', SWAP)]
    ppermute x12 -> x15, starting transfers between devices: 28 us -> 44 us  [on_device(): lax.ppermute(piece, 'z', [(s, (s + shift) % planes) for s in range(planes)])]
    ppermute x12, waiting for transfers between devices: 13.8 us -> 23.5 us  [chain(): got = lax.ppermute(sent, 'z', pairs)]
    ppermute x12 -> x15, waiting for transfers between devices: 66.3 us -> 59 us  [on_device(): lax.ppermute(piece, 'z', [(s, (s + shift) % planes) for s in range(planes)])]
    slice x4 -> x0, local copies, waits for them, and re-layouts: 3.66 us -> none  [on_device(): factors = after([b[:, chunks[1][1] * cells:] for b in held[1]], *gate)]
    add x4, other arithmetic: 4.66 us -> 8 us  [chain(): sent = sent + got]
    ppermute x4 -> x5, starting transfers between devices: 3.71 us -> 6.13 us  [on_device(): across = lax.ppermute(stack, 'y', SWAP)]
    unnamed x86 -> x98, local copies, waits for them, and re-layouts: 9.51 us -> 7.32 us
  transfers between devices with their start and end apart: 36 -> 42, of which waited for: 11 -> 16; matrix products, arithmetic and copies ran while one was open for 18% -> 17% of each run, Pallas kernels for 0% -> 0%
where the time goes in v10:
time: 222 us; the launch traced here: 221 us
  waiting for transfers between devices  88.5 us (40%)
  starting transfers between devices  80.8 us (36%)
  matrix products  19.7 us (9%)
  local copies, waits for them, and re-layouts  17.8 us (8%)
  other arithmetic  9.14 us (4%)
  Pallas kernels  3.22 us (1%)
    ppermute x15, waiting for transfers between devices, on_device(): lax.ppermute(piece, 'z', [(s, (s + shift) % planes) for s in range(planes)])  59 us
    ppermute x15, starting transfers between devices, on_device(): lax.ppermute(piece, 'z', [(s, (s + shift) % planes) for s in range(planes)])  44 us
    ppermute x12, starting transfers between devices, chain(): got = lax.ppermute(sent, 'z', pairs)  29.9 us
    ppermute x12, waiting for transfers between devices, chain(): got = lax.ppermute(sent, 'z', pairs)  23.5 us
    dot_general x20, matrix products, nt_dot(): lax.dot_general(a, b, (((1,), (1,)), ((), ())), preferred_element_type=jn...  12.8 us
    add x4, other arithmetic, chain(): sent = sent + got  8 us
    unnamed x98, local copies, waits for them, and re-layouts  7.32 us
    dot_general x4, matrix products, tn_dot(): lax.dot_general(a, b, (((0,), (0,)), ((), ())), preferred_element_type=jn...  6.87 us
  transfers between devices with their start and end apart: 42, of which 16 were waited for; matrix products, arithmetic and copies ran while one was open for 17% of the time, Pallas kernels for 0%

profile of v10, /device:TPU:0, one launch (start us, length us, event | category | flops | bytes accessed | tf_op | source)
XLA Modules:
  0.0 220.8 jit_solution(15287732671771695680)
XLA Ops:
  0.6 2.2 copy-done
  5.6 3.1 %collective-permute-start = (bf16[128,1024]{1,0:T(8,128)(2,1)S(1)}, bf16[128,1024]{1,0:T(8,128)(2,1)}, u32[]{:S(2)}, u32[]{:S(2)}) collective-permute-start(bf16[128,1024]{1,0:T(8,128)(2,1)S(1)} %get-tuple-element.158), channel_id=1, source_target_pairs={{0,4},{4,8},{8,12},{12,0},{1,5},{5,9},{9,13},{13,1},{2,6},{6,10},{... | collective-permute-start | bytes 786440 | tf_op jit(solution)/shard_map/ppermute | solution.py:164
  8.6 2.6 %collective-permute-start.1 = (bf16[128,1024]{1,0:T(8,128)(2,1)S(1)}, bf16[128,1024]{1,0:T(8,128)(2,1)}, u32[]{:S(2)}, u32[]{:S(2)}) collective-permute-start(bf16[128,1024]{1,0:T(8,128)(2,1)S(1)} %get-tuple-element.159), channel_id=1, source_target_pairs={{0,8},{4,12},{8,0},{12,4},{1,9},{5,13},{9,1},{13,5},{2,10},{6,14},... | collective-permute-start | bytes 786440 | tf_op jit(solution)/shard_map/ppermute | solution.py:164
  12.7 5.8 %unfold.3 = (bf16[4,128,1152]{2,1,0:T(8,128)(2,1)S(1)}, bf16[128,1152]{1,0:T(8,128)(2,1)}, bf16[128,1152]{1,0:T(8,128)(2,1)S(1)}, bf16[128,1152]{1,0:T(8,128)(2,...) fusion(bf16[4,128,1152]{2,1,0:T(8,128)(2,1)S(1)} %broadcast_in_, ...), kind=kCustom, calls=%fused_computation.125 | custom fusion | bytes 7503880 | tf_op jit(solution)/shard_map/unfold/pallas_call | solution.py:67
  21.7 7.6 %collective-permute-done.1 = bf16[128,1024]{1,0:T(8,128)(2,1)} collective-permute-done((bf16[128,1024]{1,0:T(8,128)(2,1)S(1)}, bf16[128,1024]{1,0:T(8,128)(2,1)}, u32[]{:S(2)}, u32[]{:S(2)}) %collective-permute-start.1) | collective-permute-done | bytes 262176 | tf_op jit(solution)/shard_map/ppermute | solution.py:164
  33.2 9.1 %collective-permute-start.4 = (bf16[128,1152]{1,0:T(8,128)(2,1)S(1)}, bf16[128,1152]{1,0:T(8,128)(2,1)S(1)}, u32[]{:S(2)}, u32[]{:S(2)}) collective-permute-start(bf16[128,1152]{1,0:T(8,128)(2,1)S(1)} %get-tuple-element.165), channel_id=1, source_target_pairs={{0,8},{4,12},{8,0},{12,4},{1,9},{5,13},{9,1},{13,5},{2,10},{6,14},... | collective-permute-start | bytes 884744 | tf_op jit(solution)/shard_map/ppermute | solution.py:164
  42.3 3.5 %collective-permute-start.5 = (bf16[128,1152]{1,0:T(8,128)(2,1)S(1)}, bf16[128,1152]{1,0:T(8,128)(2,1)S(1)}, u32[]{:S(2)}, u32[]{:S(2)}) collective-permute-start(bf16[128,1152]{1,0:T(8,128)(2,1)S(1)} %get-tuple-element.167), channel_id=1, source_target_pairs={{0,12},{4,0},{8,4},{12,8},{1,13},{5,1},{9,5},{13,9},{2,14},{6,2},{... | collective-permute-start | bytes 884744 | tf_op jit(solution)/shard_map/ppermute | solution.py:164
  46.8 9.7 %collective-permute-done.4 = bf16[128,1152]{1,0:T(8,128)(2,1)S(1)} collective-permute-done((bf16[128,1152]{1,0:T(8,128)(2,1)S(1)}, bf16[128,1152]{1,0:T(8,128)(2,1)S(1)}, u32[]{:S(2)}, u32[]{:S(2)}) %collective-permute-start.4) | collective-permute-done | bytes 294944 | tf_op jit(solution)/shard_map/ppermute | solution.py:164
  57.2 10.8 %collective-permute-start.8 = (bf16[128,1024]{1,0:T(8,128)(2,1)S(1)}, bf16[128,1024]{1,0:T(8,128)(2,1)S(1)}, u32[]{:S(2)}, u32[]{:S(2)}) collective-permute-start(bf16[128,1024]{1,0:T(8,128)(2,1)S(1)} %copy-done.58), channel_id=1, source_target_pairs={{0,4},{4,8},{8,12},{12,0},{1,5},{5,9},{9,13},{13,1},{2,6},{6,10},{... | collective-permute-start | bytes 786440 | tf_op jit(solution)/shard_map/ppermute | solution.py:164
  68.9 2.3 %collective-permute-start.10 = (bf16[128,1024]{1,0:T(8,128)(2,1)S(1)}, bf16[128,1024]{1,0:T(8,128)(2,1)S(1)}, u32[]{:S(2)}, u32[]{:S(2)}) collective-permute-start(bf16[128,1024]{1,0:T(8,128)(2,1)S(1)} %copy-done.56), channel_id=1, source_target_pairs={{0,12},{4,0},{8,4},{12,8},{1,13},{5,1},{9,5},{13,9},{2,14},{6,2},{... | collective-permute-start | bytes 786440 | tf_op jit(solution)/shard_map/ppermute | solution.py:164
  71.3 3.5 %collective-permute-done.8 = bf16[128,1024]{1,0:T(8,128)(2,1)S(1)} collective-permute-done((bf16[128,1024]{1,0:T(8,128)(2,1)S(1)}, bf16[128,1024]{1,0:T(8,128)(2,1)S(1)}, u32[]{:S(2)}, u32[]{:S(2)}) %collective-permute-start.8) | collective-permute-done | bytes 262176 | tf_op jit(solution)/shard_map/ppermute | solution.py:164
  74.8 10.4 %collective-permute-done.9 = bf16[128,1024]{1,0:T(8,128)(2,1)S(1)} collective-permute-done((bf16[128,1024]{1,0:T(8,128)(2,1)S(1)}, bf16[128,1024]{1,0:T(8,128)(2,1)S(1)}, u32[]{:S(2)}, u32[]{:S(2)}) %collective-permute-start.9) | collective-permute-done | bytes 262176 | tf_op jit(solution)/shard_map/ppermute | solution.py:164
  89.2 6.1 %collective-permute-start.14 = (bf16[128,512]{1,0:T(8,128)(2,1)S(1)}, bf16[128,512]{1,0:T(8,128)(2,1)S(1)}, u32[]{:S(2)}, u32[]{:S(2)}) collective-permute-start(bf16[128,512]{1,0:T(8,128)(2,1)S(1)} %copy-done.64), channel_id=1, source_target_pairs={{0,4},{4,8},{8,12},{12,0},{1,5},{5,9},{9,13},{13,1},{2,6},{6,10},{... | collective-permute-start | bytes 393224 | tf_op jit(solution)/shard_map/ppermute | solution.py:164
  96.2 3.5 %collective-permute-done.14 = bf16[128,512]{1,0:T(8,128)(2,1)S(1)} collective-permute-done((bf16[128,512]{1,0:T(8,128)(2,1)S(1)}, bf16[128,512]{1,0:T(8,128)(2,1)S(1)}, u32[]{:S(2)}, u32[]{:S(2)}) %collective-permute-start.14) | collective-permute-done | bytes 131104 | tf_op jit(solution)/shard_map/ppermute | solution.py:164
  101.0 7.8 %collective-permute-done.15 = bf16[128,512]{1,0:T(8,128)(2,1)S(1)} collective-permute-done((bf16[128,512]{1,0:T(8,128)(2,1)S(1)}, bf16[128,512]{1,0:T(8,128)(2,1)S(1)}, u32[]{:S(2)}, u32[]{:S(2)}) %collective-permute-start.15) | collective-permute-done | bytes 131104 | tf_op jit(solution)/shard_map/ppermute | solution.py:164
  110.0 4.2 %collective-permute-done.16 = bf16[128,512]{1,0:T(8,128)(2,1)S(1)} collective-permute-done((bf16[128,512]{1,0:T(8,128)(2,1)S(1)}, bf16[128,512]{1,0:T(8,128)(2,1)S(1)}, u32[]{:S(2)}, u32[]{:S(2)}) %collective-permute-start.16) | collective-permute-done | bytes 131104 | tf_op jit(solution)/shard_map/ppermute | solution.py:164
  116.7 8.1 %collective-permute-done.18 = bf16[128,512]{1,0:T(8,128)(2,1)S(1)} collective-permute-done((bf16[128,512]{1,0:T(8,128)(2,1)S(1)}, bf16[128,512]{1,0:T(8,128)(2,1)S(1)}, u32[]{:S(2)}, u32[]{:S(2)}) %collective-permute-start.18) | collective-permute-done | bytes 131104 | tf_op jit(solution)/shard_map/ppermute | solution.py:164
  127.6 4.2 %collective-permute-done.21 = bf16[128,512]{1,0:T(8,128)(2,1)S(1)} collective-permute-done((bf16[128,512]{1,0:T(8,128)(2,1)S(1)}, bf16[128,512]{1,0:T(8,128)(2,1)S(1)}, u32[]{:S(2)}, u32[]{:S(2)}) %collective-permute-start.21) | collective-permute-done | bytes 131104 | tf_op jit(solution)/shard_map/ppermute | solution.py:164
  141.2 5.6 %collective-permute-done.32 = bf16[512,512]{1,0:T(8,128)(2,1)S(1)} collective-permute-done((bf16[512,512]{1,0:T(8,128)(2,1)S(1)}, bf16[512,512]{1,0:T(8,128)(2,1)S(1)}, u32[]{:S(2)}, u32[]{:S(2)}) %collective-permute-start.32) | collective-permute-done | bytes 524320 | tf_op jit(solution)/shard_map/ppermute | solution.py:167
  146.8 4.1 %collective-permute-done.24 = f32[128,1024]{1,0:T(8,128)S(1)} collective-permute-done((f32[128,1024]{1,0:T(8,128)S(1)}, f32[128,1024]{1,0:T(8,128)S(1)}, u32[]{:S(2)}, u32[]{:S(2)}) %collective-permute-start.24) | collective-permute-done | bytes 524320 | tf_op jit(solution)/shard_map/ppermute | solution.py:128
  158.3 5.2 %collective-permute-start.36 = (f32[128,1024]{1,0:T(8,128)}, f32[128,1024]{1,0:T(8,128)}, u32[]{:S(2)}, u32[]{:S(2)}) collective-permute-start(f32[128,1024]{1,0:T(8,128)} %get-tuple-element.249), channel_id=1, source_target_pairs={{0,4},{1,5},{2,6},{3,7},{16,20},{17,21},{18,22},{19,23}} | collective-permute-start | bytes 1572872 | tf_op jit(solution)/shard_map/ppermute | solution.py:128
  167.5 7.8 %collective-permute-done.36 = f32[128,1024]{1,0:T(8,128)} collective-permute-done((f32[128,1024]{1,0:T(8,128)}, f32[128,1024]{1,0:T(8,128)}, u32[]{:S(2)}, u32[]{:S(2)}) %collective-permute-start.36) | collective-permute-done | bytes 524320 | tf_op jit(solution)/shard_map/ppermute | solution.py:128
  175.3 2.2 fusion.62
  178.9 5.1 %collective-permute-start.37 = (f32[128,1024]{1,0:T(8,128)S(1)}, f32[128,1024]{1,0:T(8,128)}, u32[]{:S(2)}, u32[]{:S(2)}) collective-permute-start(f32[128,1024]{1,0:T(8,128)S(1)} %get-tuple-element.247), channel_id=1, source_target_pairs={{0,4},{4,8},{1,5},{5,9},{2,6},{6,10},{3,7},{7,11},{16,20},{20,24},... | collective-permute-start | bytes 1572872 | tf_op jit(solution)/shard_map/ppermute | solution.py:128
  186.5 2.4 %fusion.71 = (f32[128,1024]{1,0:T(8,128)}, f32[128,1024]{1,0:T(8,128)S(1)}, f32[128,1024]{1,0:T(8,128)}) fusion(f32[128,1024]{1,0:T(8,128)} %copy-done.55, s32[]{:T(128)S(6)} %select_n.119, f32[512,512]{1,0:T(8,128)S(1)} %copy-done.8, f32[512,512]{1,0:T(8,128)S(1)} %copy-done.10, s32[]{:T(128)S(6)} %select_n.115, f32[128,1024]{1,0:T(8,128)} %collective-permute-done.25, ...), kind=kLoop, calls=%fused_computation.119 | loop fusion | flops 655360 | bytes 4718604 | tf_op jit(solution)/shard_map/add | solution.py:126
  188.9 4.4 %collective-permute-start.26 = (f32[128,1024]{1,0:T(8,128)}, f32[128,1024]{1,0:T(8,128)S(1)}, u32[]{:S(2)}, u32[]{:S(2)}) collective-permute-start(f32[128,1024]{1,0:T(8,128)} %get-tuple-element.252), channel_id=1, source_target_pairs={{0,4},{4,8},{8,12},{1,5},{5,9},{9,13},{2,6},{6,10},{10,14},{3,7},{... | collective-permute-start | bytes 1572872 | tf_op jit(solution)/shard_map/ppermute | solution.py:128
  194.6 3.0 %collective-permute-done.37 = f32[128,1024]{1,0:T(8,128)} collective-permute-done((f32[128,1024]{1,0:T(8,128)S(1)}, f32[128,1024]{1,0:T(8,128)}, u32[]{:S(2)}, u32[]{:S(2)}) %collective-permute-start.37) | collective-permute-done | bytes 524320 | tf_op jit(solution)/shard_map/ppermute | solution.py:128
  197.7 2.4 %fusion.60 = (f32[128,1024]{1,0:T(8,128)}, f32[128,1024]{1,0:T(8,128)S(1)}, f32[128,1024]{1,0:T(8,128)}) fusion(f32[128,1024]{1,0:T(8,128)} %collective-permute-done.40, s32[]{:T(128)S(6)} %select_n.119, f32[512,512]{1,0:T(8,128)S(1)} %copy-done.13, f32[512,512]{1,0:T(8,128)S(1)} %copy-done.16, s32[]{:T(128)S(6)} %select_n.115, ...), kind=kLoop, calls=%fused_computation.108 | loop fusion | flops 655360 | bytes 4718604 | tf_op jit(solution)/shard_map/add | solution.py:126
  200.0 4.5 %collective-permute-start.38 = (f32[128,1024]{1,0:T(8,128)}, f32[128,1024]{1,0:T(8,128)S(1)}, u32[]{:S(2)}, u32[]{:S(2)}) collective-permute-start(f32[128,1024]{1,0:T(8,128)} %get-tuple-element.245), channel_id=1, source_target_pairs={{0,4},{4,8},{8,12},{1,5},{5,9},{9,13},{2,6},{6,10},{10,14},{3,7},{... | collective-permute-start | bytes 1572872 | tf_op jit(solution)/shard_map/ppermute | solution.py:128
  205.9 7.0 %conditional.1 = (f32[1024,128]{1,0:T(8,128)}) conditional(s32[]{:T(128)} %clamp.3, (bf16[512,1152]{1,0:T(8,128)(2,1)}, bf16[512,1024]{1,0:T(8,128)(2,1)}, bf16[512,1152]{1,0:T(8,128)(2,1)}, bf16[512,1024]{1,0:T(8,128)(2,1)}, bf16[512,1152]{1,0:T(8,128)(2,1)}, /*index=5*/bf16[512,1024]{1,0:T(8,128)(2,1)}, ...), branch_computations={%region_0.1_spmd, %region_1.2_spmd, %region_2.3_spmd, %region_3.4_... | conditional | flops 537395200 | bytes 24641740 | solution.py:205
  210.6 2.2 convolution_add_fusion
  212.8 6.7 %collective-permute-done.38.refs_4_ = f32[128,1024]{1,0:T(8,128)S(1)} collective-permute-done((f32[128,1024]{1,0:T(8,128)}, f32[128,1024]{1,0:T(8,128)S(1)}, u32[]{:S(2)}, u32[]{:S(2)}) %collective-permute-start.38) | collective-permute-done | bytes 524320 | tf_op jit(solution)/shard_map/ppermute | solution.py:128
  (214 shorter events, 59.2 us)
Async XLA Ops:
  5.6 15.1 %collective-permute-start = (bf16[128,1024]{1,0:T(8,128)(2,1)S(1)}, bf16[128,1024]{1,0:T(8,128)(2,1)}, u32[]{:S(2)}, u32[]{:S(2)}) collective-permute-start(bf16[128,1024]{1,0:T(8,128)(2,1)S(1)} %get-tuple-element.158), channel_id=1, source_target_pairs={{0,4},{4,8},{8,12},{12,0},{1,5},{5,9},{9,13},{13,1},{2,6},{6,10},{... | collective-permute-start | bytes 786440 | tf_op jit(solution)/shard_map/ppermute | solution.py:164
  8.6 20.6 %collective-permute-start.1 = (bf16[128,1024]{1,0:T(8,128)(2,1)S(1)}, bf16[128,1024]{1,0:T(8,128)(2,1)}, u32[]{:S(2)}, u32[]{:S(2)}) collective-permute-start(bf16[128,1024]{1,0:T(8,128)(2,1)S(1)} %get-tuple-element.159), channel_id=1, source_target_pairs={{0,8},{4,12},{8,0},{12,4},{1,9},{5,13},{9,1},{13,5},{2,10},{6,14},... | collective-permute-start | bytes 786440 | tf_op jit(solution)/shard_map/ppermute | solution.py:164
  11.2 19.1 %collective-permute-start.2 = (bf16[128,1024]{1,0:T(8,128)(2,1)S(1)}, bf16[128,1024]{1,0:T(8,128)(2,1)}, u32[]{:S(2)}, u32[]{:S(2)}) collective-permute-start(bf16[128,1024]{1,0:T(8,128)(2,1)S(1)} %get-tuple-element.160), channel_id=1, source_target_pairs={{0,12},{4,0},{8,4},{12,8},{1,13},{5,1},{9,5},{13,9},{2,14},{6,2},{... | collective-permute-start | bytes 786440 | tf_op jit(solution)/shard_map/ppermute | solution.py:164
  18.4 27.3 %collective-permute-start.3 = (bf16[128,1152]{1,0:T(8,128)(2,1)}, bf16[128,1152]{1,0:T(8,128)(2,1)}, u32[]{:S(2)}, u32[]{:S(2)}) collective-permute-start(bf16[128,1152]{1,0:T(8,128)(2,1)} %get-tuple-element.214), channel_id=1, source_target_pairs={{0,4},{4,8},{8,12},{12,0},{1,5},{5,9},{9,13},{13,1},{2,6},{6,10},{... | collective-permute-start | bytes 884744 | tf_op jit(solution)/shard_map/ppermute | solution.py:164
  31.3 25.9 %collective-permute-start.6 = (bf16[512,1024]{1,0:T(8,128)(2,1)S(1)}, bf16[512,1024]{1,0:T(8,128)(2,1)S(1)}, u32[]{:S(2)}, u32[]{:S(2)}) collective-permute-start(bf16[512,1024]{1,0:T(8,128)(2,1)S(1)} %bitcast.95), channel_id=1, source_target_pairs={{0,2},{2,0},{1,3},{3,1},{4,6},{6,4},{5,7},{7,5},{8,10},{10,8},{9,1... | collective-permute-start | bytes 3145736 | tf_op jit(solution)/shard_map/ppermute | solution.py:167
  33.2 24.0 %collective-permute-start.7 = (bf16[512,1024]{1,0:T(8,128)(2,1)S(1)}, bf16[512,1024]{1,0:T(8,128)(2,1)S(1)}, u32[]{:S(2)}, u32[]{:S(2)}) collective-permute-start(bf16[512,1024]{1,0:T(8,128)(2,1)S(1)} %bitcast.96), channel_id=1, source_target_pairs={{0,1},{1,0},{2,3},{3,2},{4,5},{5,4},{6,7},{7,6},{8,9},{9,8},{10,11... | collective-permute-start | bytes 3145736 | tf_op jit(solution)/shard_map/ppermute | solution.py:168
  33.2 23.3 %collective-permute-start.4 = (bf16[128,1152]{1,0:T(8,128)(2,1)S(1)}, bf16[128,1152]{1,0:T(8,128)(2,1)S(1)}, u32[]{:S(2)}, u32[]{:S(2)}) collective-permute-start(bf16[128,1152]{1,0:T(8,128)(2,1)S(1)} %get-tuple-element.165), channel_id=1, source_target_pairs={{0,8},{4,12},{8,0},{12,4},{1,9},{5,13},{9,1},{13,5},{2,10},{6,14},... | collective-permute-start | bytes 884744 | tf_op jit(solution)/shard_map/ppermute | solution.py:164
  42.3 14.2 %collective-permute-start.5 = (bf16[128,1152]{1,0:T(8,128)(2,1)S(1)}, bf16[128,1152]{1,0:T(8,128)(2,1)S(1)}, u32[]{:S(2)}, u32[]{:S(2)}) collective-permute-start(bf16[128,1152]{1,0:T(8,128)(2,1)S(1)} %get-tuple-element.167), channel_id=1, source_target_pairs={{0,12},{4,0},{8,4},{12,8},{1,13},{5,1},{9,5},{13,9},{2,14},{6,2},{... | collective-permute-start | bytes 884744 | tf_op jit(solution)/shard_map/ppermute | solution.py:164
  56.6 31.1 %collective-permute-start.11 = (bf16[512,1152]{1,0:T(8,128)(2,1)S(1)}, bf16[512,1152]{1,0:T(8,128)(2,1)S(1)}, u32[]{:S(2)}, u32[]{:S(2)}) collective-permute-start(bf16[512,1152]{1,0:T(8,128)(2,1)S(1)} %bitcast.123), channel_id=1, source_target_pairs={{0,2},{2,0},{1,3},{3,1},{4,6},{6,4},{5,7},{7,5},{8,10},{10,8},{9,1... | collective-permute-start | bytes 3538952 | tf_op jit(solution)/shard_map/ppermute | solution.py:167
  57.2 30.8 %collective-permute-start.12 = (bf16[512,1152]{1,0:T(8,128)(2,1)S(1)}, bf16[512,1152]{1,0:T(8,128)(2,1)S(1)}, u32[]{:S(2)}, u32[]{:S(2)}) collective-permute-start(bf16[512,1152]{1,0:T(8,128)(2,1)S(1)} %bitcast.124), channel_id=1, source_target_pairs={{0,1},{1,0},{2,3},{3,2},{4,5},{5,4},{6,7},{7,6},{8,9},{9,8},{10,11... | collective-permute-start | bytes 3538952 | tf_op jit(solution)/shard_map/ppermute | solution.py:168
  57.2 17.5 %collective-permute-start.8 = (bf16[128,1024]{1,0:T(8,128)(2,1)S(1)}, bf16[128,1024]{1,0:T(8,128)(2,1)S(1)}, u32[]{:S(2)}, u32[]{:S(2)}) collective-permute-start(bf16[128,1024]{1,0:T(8,128)(2,1)S(1)} %copy-done.58), channel_id=1, source_target_pairs={{0,4},{4,8},{8,12},{12,0},{1,5},{5,9},{9,13},{13,1},{2,6},{6,10},{... | collective-permute-start | bytes 786440 | tf_op jit(solution)/shard_map/ppermute | solution.py:164
  68.0 17.2 %collective-permute-start.9 = (bf16[128,1024]{1,0:T(8,128)(2,1)S(1)}, bf16[128,1024]{1,0:T(8,128)(2,1)S(1)}, u32[]{:S(2)}, u32[]{:S(2)}) collective-permute-start(bf16[128,1024]{1,0:T(8,128)(2,1)S(1)} %copy-done.57), channel_id=1, source_target_pairs={{0,8},{4,12},{8,0},{12,4},{1,9},{5,13},{9,1},{13,5},{2,10},{6,14},... | collective-permute-start | bytes 786440 | tf_op jit(solution)/shard_map/ppermute | solution.py:164
  68.9 16.3 %collective-permute-start.10 = (bf16[128,1024]{1,0:T(8,128)(2,1)S(1)}, bf16[128,1024]{1,0:T(8,128)(2,1)S(1)}, u32[]{:S(2)}, u32[]{:S(2)}) collective-permute-start(bf16[128,1024]{1,0:T(8,128)(2,1)S(1)} %copy-done.56), channel_id=1, source_target_pairs={{0,12},{4,0},{8,4},{12,8},{1,13},{5,1},{9,5},{13,9},{2,14},{6,2},{... | collective-permute-start | bytes 786440 | tf_op jit(solution)/shard_map/ppermute | solution.py:164
  74.8 14.4 %collective-permute-start.13 = (bf16[512,1024]{1,0:T(8,128)(2,1)S(1)}, bf16[512,1024]{1,0:T(8,128)(2,1)S(1)}, u32[]{:S(2)}, u32[]{:S(2)}) collective-permute-start(bf16[512,1024]{1,0:T(8,128)(2,1)S(1)} %collective-permute-done.6), channel_id=1, source_target_pairs={{0,1},{1,0},{2,3},{3,2},{4,5},{5,4},{6,7},{7,6},{8,9},{9,8},{10,11... | collective-permute-start | bytes 3145736 | tf_op jit(solution)/shard_map/ppermute | solution.py:172
  85.3 39.5 %collective-permute-start.20 = (bf16[512,1024]{1,0:T(8,128)(2,1)S(1)}, bf16[512,1024]{1,0:T(8,128)(2,1)S(1)}, u32[]{:S(2)}, u32[]{:S(2)}) collective-permute-start(bf16[512,1024]{1,0:T(8,128)(2,1)S(1)} %bitcast.116), channel_id=1, source_target_pairs={{0,1},{1,0},{2,3},{3,2},{4,5},{5,4},{6,7},{7,6},{8,9},{9,8},{10,11... | collective-permute-start | bytes 3145736 | tf_op jit(solution)/shard_map/ppermute | solution.py:168
  85.4 30.0 %collective-permute-start.30 = (bf16[512,1024]{1,0:T(8,128)(2,1)S(1)}, bf16[512,1024]{1,0:T(8,128)(2,1)S(1)}, u32[]{:S(2)}, u32[]{:S(2)}) collective-permute-start(bf16[512,1024]{1,0:T(8,128)(2,1)S(1)} %bitcast.117), channel_id=1, source_target_pairs={{0,2},{2,0},{1,3},{3,1},{4,6},{6,4},{5,7},{7,5},{8,10},{10,8},{9,1... | collective-permute-start | bytes 3145736 | tf_op jit(solution)/shard_map/ppermute | solution.py:167
  87.7 38.1 %collective-permute-start.19 = (bf16[512,1152]{1,0:T(8,128)(2,1)S(1)}, bf16[512,1152]{1,0:T(8,128)(2,1)S(1)}, u32[]{:S(2)}, u32[]{:S(2)}) collective-permute-start(bf16[512,1152]{1,0:T(8,128)(2,1)S(1)} %collective-permute-done.11), channel_id=1, source_target_pairs={{0,1},{1,0},{2,3},{3,2},{4,5},{5,4},{6,7},{7,6},{8,9},{9,8},{10,11... | collective-permute-start | bytes 3538952 | tf_op jit(solution)/shard_map/ppermute | solution.py:172
  96.0 18.3 %collective-permute-start.17 = (bf16[128,512]{1,0:T(8,128)(2,1)S(1)}, bf16[128,512]{1,0:T(8,128)(2,1)S(1)}, u32[]{:S(2)}, u32[]{:S(2)}) collective-permute-start(bf16[128,512]{1,0:T(8,128)(2,1)S(1)} %copy-done.61), channel_id=1, source_target_pairs={{0,4},{4,8},{8,12},{12,0},{1,5},{5,9},{9,13},{13,1},{2,6},{6,10},{... | collective-permute-start | bytes 393224 | tf_op jit(solution)/shard_map/ppermute | solution.py:164
  114.3 12.8 %collective-permute-start.22 = (bf16[512,512]{1,0:T(8,128)(2,1)S(1)}, bf16[512,512]{1,0:T(8,128)(2,1)S(1)}, u32[]{:S(2)}, u32[]{:S(2)}) collective-permute-start(bf16[512,512]{1,0:T(8,128)(2,1)S(1)} %bitcast.102), channel_id=1, source_target_pairs={{0,1},{1,0},{2,3},{3,2},{4,5},{5,4},{6,7},{7,6},{8,9},{9,8},{10,11... | collective-permute-start | bytes 1572872 | tf_op jit(solution)/shard_map/ppermute | solution.py:168
  114.4 37.0 %collective-permute-start.31 = (bf16[512,512]{1,0:T(8,128)(2,1)S(1)}, bf16[512,512]{1,0:T(8,128)(2,1)S(1)}, u32[]{:S(2)}, u32[]{:S(2)}) collective-permute-start(bf16[512,512]{1,0:T(8,128)(2,1)S(1)} %bitcast.103), channel_id=1, source_target_pairs={{0,2},{2,0},{1,3},{3,1},{4,6},{6,4},{5,7},{7,5},{8,10},{10,8},{9,1... | collective-permute-start | bytes 1572872 | tf_op jit(solution)/shard_map/ppermute | solution.py:167
  124.8 15.4 %collective-permute-start.33 = (bf16[512,1024]{1,0:T(8,128)(2,1)S(1)}, bf16[512,1024]{1,0:T(8,128)(2,1)S(1)}, u32[]{:S(2)}, u32[]{:S(2)}) collective-permute-start(bf16[512,1024]{1,0:T(8,128)(2,1)S(1)} %collective-permute-done.30), channel_id=1, source_target_pairs={{0,1},{1,0},{2,3},{3,2},{4,5},{5,4},{6,7},{7,6},{8,9},{9,8},{10,11... | collective-permute-start | bytes 3145736 | tf_op jit(solution)/shard_map/ppermute | solution.py:172
  132.4 14.4 %collective-permute-start.32 = (bf16[512,512]{1,0:T(8,128)(2,1)S(1)}, bf16[512,512]{1,0:T(8,128)(2,1)S(1)}, u32[]{:S(2)}, u32[]{:S(2)}) collective-permute-start(bf16[512,512]{1,0:T(8,128)(2,1)S(1)} %bitcast.111), channel_id=1, source_target_pairs={{0,2},{2,0},{1,3},{3,1},{4,6},{6,4},{5,7},{7,5},{8,10},{10,8},{9,1... | collective-permute-start | bytes 1572872 | tf_op jit(solution)/shard_map/ppermute | solution.py:167
  137.8 13.1 %collective-permute-start.24 = (f32[128,1024]{1,0:T(8,128)S(1)}, f32[128,1024]{1,0:T(8,128)S(1)}, u32[]{:S(2)}, u32[]{:S(2)}) collective-permute-start(f32[128,1024]{1,0:T(8,128)S(1)} %get-tuple-element.256), channel_id=1, source_target_pairs={{0,4},{1,5},{2,6},{3,7},{16,20},{17,21},{18,22},{19,23}} | collective-permute-start | bytes 1572872 | tf_op jit(solution)/shard_map/ppermute | solution.py:128
  158.3 17.0 %collective-permute-start.36 = (f32[128,1024]{1,0:T(8,128)}, f32[128,1024]{1,0:T(8,128)}, u32[]{:S(2)}, u32[]{:S(2)}) collective-permute-start(f32[128,1024]{1,0:T(8,128)} %get-tuple-element.249), channel_id=1, source_target_pairs={{0,4},{1,5},{2,6},{3,7},{16,20},{17,21},{18,22},{19,23}} | collective-permute-start | bytes 1572872 | tf_op jit(solution)/shard_map/ppermute | solution.py:128
  164.7 19.3 %collective-permute-start.28 = (f32[128,1024]{1,0:T(8,128)}, f32[128,1024]{1,0:T(8,128)S(1)}, u32[]{:S(2)}, u32[]{:S(2)}) collective-permute-start(f32[128,1024]{1,0:T(8,128)} %get-tuple-element.253), channel_id=1, source_target_pairs={{12,8},{8,4},{13,9},{9,5},{14,10},{10,6},{15,11},{11,7},{28,24},{2... | collective-permute-start | bytes 1572872 | tf_op jit(solution)/shard_map/ppermute | solution.py:128
  165.4 21.2 %collective-permute-start.25 = (f32[128,1024]{1,0:T(8,128)}, f32[128,1024]{1,0:T(8,128)}, u32[]{:S(2)}, u32[]{:S(2)}) collective-permute-start(f32[128,1024]{1,0:T(8,128)} %get-tuple-element.254), channel_id=1, source_target_pairs={{0,4},{4,8},{1,5},{5,9},{2,6},{6,10},{3,7},{7,11},{16,20},{20,24},... | collective-permute-start | bytes 1572872 | tf_op jit(solution)/shard_map/ppermute | solution.py:128
  177.5 17.2 %collective-permute-start.40 = (f32[128,1024]{1,0:T(8,128)}, f32[128,1024]{1,0:T(8,128)}, u32[]{:S(2)}, u32[]{:S(2)}) collective-permute-start(f32[128,1024]{1,0:T(8,128)} %get-tuple-element.246), channel_id=1, source_target_pairs={{12,8},{8,4},{13,9},{9,5},{14,10},{10,6},{15,11},{11,7},{28,24},{2... | collective-permute-start | bytes 1572872 | tf_op jit(solution)/shard_map/ppermute | solution.py:128
  178.9 18.7 %collective-permute-start.37 = (f32[128,1024]{1,0:T(8,128)S(1)}, f32[128,1024]{1,0:T(8,128)}, u32[]{:S(2)}, u32[]{:S(2)}) collective-permute-start(f32[128,1024]{1,0:T(8,128)S(1)} %get-tuple-element.247), channel_id=1, source_target_pairs={{0,4},{4,8},{1,5},{5,9},{2,6},{6,10},{3,7},{7,11},{16,20},{20,24},... | collective-permute-start | bytes 1572872 | tf_op jit(solution)/shard_map/ppermute | solution.py:128
  188.9 23.9 %collective-permute-start.26 = (f32[128,1024]{1,0:T(8,128)}, f32[128,1024]{1,0:T(8,128)S(1)}, u32[]{:S(2)}, u32[]{:S(2)}) collective-permute-start(f32[128,1024]{1,0:T(8,128)} %get-tuple-element.252), channel_id=1, source_target_pairs={{0,4},{4,8},{8,12},{1,5},{5,9},{9,13},{2,6},{6,10},{10,14},{3,7},{... | collective-permute-start | bytes 1572872 | tf_op jit(solution)/shard_map/ppermute | solution.py:128
  193.3 19.5 %collective-permute-start.29 = (f32[128,1024]{1,0:T(8,128)}, f32[128,1024]{1,0:T(8,128)S(1)}, u32[]{:S(2)}, u32[]{:S(2)}) collective-permute-start(f32[128,1024]{1,0:T(8,128)} %get-tuple-element.250), channel_id=1, source_target_pairs={{12,8},{8,4},{4,0},{13,9},{9,5},{5,1},{14,10},{10,6},{6,2},{15,11}... | collective-permute-start | bytes 1572872 | tf_op jit(solution)/shard_map/ppermute | solution.py:128
  200.0 19.5 %collective-permute-start.38 = (f32[128,1024]{1,0:T(8,128)}, f32[128,1024]{1,0:T(8,128)S(1)}, u32[]{:S(2)}, u32[]{:S(2)}) collective-permute-start(f32[128,1024]{1,0:T(8,128)} %get-tuple-element.245), channel_id=1, source_target_pairs={{0,4},{4,8},{8,12},{1,5},{5,9},{9,13},{2,6},{6,10},{10,14},{3,7},{... | collective-permute-start | bytes 1572872 | tf_op jit(solution)/shard_map/ppermute | solution.py:128
  204.5 15.0 %collective-permute-start.41 = (f32[128,1024]{1,0:T(8,128)}, f32[128,1024]{1,0:T(8,128)S(1)}, u32[]{:S(2)}, u32[]{:S(2)}) collective-permute-start(f32[128,1024]{1,0:T(8,128)} %get-tuple-element.243), channel_id=1, source_target_pairs={{12,8},{8,4},{4,0},{13,9},{9,5},{5,1},{14,10},{10,6},{6,2},{15,11}... | collective-permute-start | bytes 1572872 | tf_op jit(solution)/shard_map/ppermute | solution.py:128
  (62 other events, 916.2 us)

commit v11 on v10

--- a/solution.py
+++ b/solution.py
@@ -18,7 +18,7 @@
 
 def chunks_of(per_plane):
     unit = per_plane // 16
-    sizes = [4 * unit, 4 * unit, 4 * unit, 2 * unit, 2 * unit] if unit else [1] * per_plane
+    sizes = [6 * unit, 6 * unit, 4 * unit] if unit else [1] * per_plane
     return [(sum(sizes[:i]), size) for i, size in enumerate(sizes)]
 
 
@@ -150,16 +150,14 @@
 
     sent, waits, held = [], [], []
     for j in range(last + 1):
-        arrived = [pieces[j][0]]
+        arrived = [pieces[j][0] if j else after(pieces[0][0], pieces[1])]
         for shift in range(1, planes):
             piece = pieces[j][shift]
             if len(sent) >= WINDOW:
                 piece = after(
                     piece,
                     sent[-WINDOW],
-                    *(waits[min(j, last - 1) - 2] if j > 1 else ()),
-                    *(held[min(j, last - 1) - 3][3:] if j > 2 and last > 3 else ()),
-                    *((held[j - 3][3], held[j - 2][1]) if j == last > 3 and shift == planes - 1 else ()),
+                    *(waits[j - 2] if j > 1 else ()),
                 )
             sent.append(lax.ppermute(piece, "z", [(s, (s + shift) % planes) for s in range(planes)]))
             arrived.append(sent[-1])
@@ -168,7 +166,7 @@
         beside = lax.ppermute(stack, "c", SWAP)
         waits.append((across, beside))
         held.append([stack, beside, across])
-        if j < last - 1:
+        if j < last:
             held[j].append(lax.ppermute(across, "c", SWAP))
     flat = [[b[:, : size * cells] for b in held[j][:2]] for j, (_, size) in enumerate(chunks)]
     sums = [sum(nt_dot(flat[j][0], flat[j][k]) for j in range(last + 1)) for k in range(2)]
@@ -176,7 +174,7 @@
     for half in range(2):
         if half:
             for j in range(last + 1):
-                if j >= last - 1:
+                if j == last:
                     held[j][2] = after(held[j][2], *gate)
                     held[j].append(lax.ppermute(held[j][2], "c", SWAP))
                 flat[j] += [b[:, : chunks[j][1] * cells] for b in held[j][2:]]

time: 222 us -> 221 us (level)
  waiting for transfers between devices: 88.5 us -> 102 us
  starting transfers between devices: 80.8 us -> 71.3 us
  local copies, waits for them, and re-layouts: 17.8 us -> 12.6 us
  Pallas kernels: 3.22 us -> 6.66 us
    ppermute x5 -> x3, waiting for transfers between devices: 5.57 us -> 25.3 us  [on_device(): across = lax.ppermute(stack, 'y', SWAP)]
    ppermute x15 -> x9, starting transfers between devices: 44 us -> 32.7 us  [on_device(): lax.ppermute(piece, 'z', [(s, (s + shift) % planes) for s in range(planes)])]
    pallas_call x1 -> x0, local copies, waits for them, and re-layouts: 5.75 us -> none  [unfold(): pl.pallas_call(functools.partial(unfold_kernel, planes, per_plane, chunks...]
    ppermute x12, waiting for transfers between devices: 23.5 us -> 18.1 us  [chain(): got = lax.ppermute(sent, 'z', pairs)]
    ppermute x12, starting transfers between devices: 29.9 us -> 34.4 us  [chain(): got = lax.ppermute(sent, 'z', pairs)]
    pallas_call x1 -> x2, Pallas kernels: 1.96 us -> 5.41 us  [unfold(): pl.pallas_call(functools.partial(unfold_kernel, planes, per_plane, chunks...]
    ppermute x5 -> x3, starting transfers between devices: 6.13 us -> 3.99 us  [on_device(): across = lax.ppermute(stack, 'y', SWAP)]
    dot_general x20 -> x12, matrix products: 12.8 us -> 11 us  [nt_dot(): lax.dot_general(a, b, (((1,), (1,)), ((), ())), preferred_element_type=jn...]
  transfers between devices with their start and end apart: 42 -> 30, of which waited for: 16 -> 12; matrix products, arithmetic and copies ran while one was open for 17% -> 13% of each run, Pallas kernels for 0% -> 1%
where the time goes in v11:
time: 221 us
  waiting for transfers between devices  102 us (46%)
  starting transfers between devices  71.3 us (32%)
  matrix products  17.9 us (8%)
  local copies, waits for them, and re-layouts  12.6 us (6%)
  other arithmetic  9.22 us (4%)
  Pallas kernels  6.66 us (3%)
    ppermute x9, waiting for transfers between devices, on_device(): lax.ppermute(piece, 'z', [(s, (s + shift) % planes) for s in range(planes)])  58.2 us
    ppermute x12, starting transfers between devices, chain(): got = lax.ppermute(sent, 'z', pairs)  34.4 us
    ppermute x9, starting transfers between devices, on_device(): lax.ppermute(piece, 'z', [(s, (s + shift) % planes) for s in range(planes)])  32.7 us
    ppermute x3, waiting for transfers between devices, on_device(): across = lax.ppermute(stack, 'y', SWAP)  25.3 us
    ppermute x12, waiting for transfers between devices, chain(): got = lax.ppermute(sent, 'z', pairs)  18.1 us
    dot_general x12, matrix products, nt_dot(): lax.dot_general(a, b, (((1,), (1,)), ((), ())), preferred_element_type=jn...  11 us
    add x4, other arithmetic, chain(): sent = sent + got  8 us
    unnamed x54, local copies, waits for them, and re-layouts  7.91 us
  transfers between devices with their start and end apart: 30, of which 12 were waited for; matrix products, arithmetic and copies ran while one was open for 13% of the time, Pallas kernels for 1%

profile of v11, /device:TPU:0, one launch (start us, length us, event | category | flops | bytes accessed | tf_op | source)
XLA Modules:
  0.0 220.6 jit_solution(9928798191758817146)
XLA Ops:
  0.6 2.2 copy-done
  3.6 2.3 %unfold.2 = (bf16[128,1536]{1,0:T(8,128)(2,1)S(1)}, bf16[128,1536]{1,0:T(8,128)(2,1)S(1)}, bf16[128,1536]{1,0:T(8,128)(2,1)S(1)}, bf16[128,1536]{1,0:T(8,128)(2,1)S(1)}) custom-call(s32[1]{0:T(128)} %bitcast.1.z_ref, bf16[128,64,256]{2,1,0:T(8,128)(2,1)S(1)} %copy-done, bf16[128,64,256]{2,1,0:T(8,128)(2,1)S(1)} %copy-done, ...), custom_call_target="tpu_custom_call" | custom-call | bytes 5767168 | tf_op jit(solution)/shard_map/unfold/pallas_call | solution.py:67
  5.9 3.1 %collective-permute-start = (bf16[128,1536]{1,0:T(8,128)(2,1)S(1)}, bf16[128,1536]{1,0:T(8,128)(2,1)}, u32[]{:S(2)}, u32[]{:S(2)}) collective-permute-start(bf16[128,1536]{1,0:T(8,128)(2,1)S(1)} %get-tuple-element.124), channel_id=1, source_target_pairs={{0,4},{4,8},{8,12},{12,0},{1,5},{5,9},{9,13},{13,1},{2,6},{6,10},{... | collective-permute-start | bytes 1179656 | tf_op jit(solution)/shard_map/ppermute | solution.py:162
  9.0 2.6 %collective-permute-start.1 = (bf16[128,1536]{1,0:T(8,128)(2,1)S(1)}, bf16[128,1536]{1,0:T(8,128)(2,1)}, u32[]{:S(2)}, u32[]{:S(2)}) collective-permute-start(bf16[128,1536]{1,0:T(8,128)(2,1)S(1)} %get-tuple-element.125), channel_id=1, source_target_pairs={{0,8},{4,12},{8,0},{12,4},{1,9},{5,13},{9,1},{13,5},{2,10},{6,14},... | collective-permute-start | bytes 1179656 | tf_op jit(solution)/shard_map/ppermute | solution.py:162
  13.0 3.1 %unfold.3 = (bf16[128,1664]{1,0:T(8,128)(2,1)S(1)}, bf16[128,1664]{1,0:T(8,128)(2,1)S(1)}, bf16[128,1664]{1,0:T(8,128)(2,1)S(1)}, bf16[128,1664]{1,0:T(8,128)(2,...) custom-call(s32[1]{0:T(128)} %bitcast.1.z_ref, ...), custom_call_target="tpu_custom_call" | custom-call | bytes 6946816 | tf_op jit(solution)/shard_map/unfold/pallas_call | solution.py:67
  19.2 2.1 collective-permute-done
  22.3 15.8 %collective-permute-done.1 = bf16[128,1536]{1,0:T(8,128)(2,1)} collective-permute-done((bf16[128,1536]{1,0:T(8,128)(2,1)S(1)}, bf16[128,1536]{1,0:T(8,128)(2,1)}, u32[]{:S(2)}, u32[]{:S(2)}) %collective-permute-start.1) | collective-permute-done | bytes 393248 | tf_op jit(solution)/shard_map/ppermute | solution.py:162
  42.3 10.1 %collective-permute-start.5 = (bf16[128,1664]{1,0:T(8,128)(2,1)S(1)}, bf16[128,1664]{1,0:T(8,128)(2,1)S(1)}, u32[]{:S(2)}, u32[]{:S(2)}) collective-permute-start(bf16[128,1664]{1,0:T(8,128)(2,1)S(1)} %get-tuple-element.134), channel_id=1, source_target_pairs={{0,12},{4,0},{8,4},{12,8},{1,13},{5,1},{9,5},{13,9},{2,14},{6,2},{... | collective-permute-start | bytes 1277960 | tf_op jit(solution)/shard_map/ppermute | solution.py:162
  52.3 7.3 %collective-permute-start.4 = (bf16[128,1664]{1,0:T(8,128)(2,1)S(1)}, bf16[128,1664]{1,0:T(8,128)(2,1)S(1)}, u32[]{:S(2)}, u32[]{:S(2)}) collective-permute-start(bf16[128,1664]{1,0:T(8,128)(2,1)S(1)} %get-tuple-element.133), channel_id=1, source_target_pairs={{0,8},{4,12},{8,0},{12,4},{1,9},{5,13},{9,1},{13,5},{2,10},{6,14},... | collective-permute-start | bytes 1277960 | tf_op jit(solution)/shard_map/ppermute | solution.py:162
  60.7 27.1 %collective-permute-done.4 = bf16[128,1664]{1,0:T(8,128)(2,1)S(1)} collective-permute-done((bf16[128,1664]{1,0:T(8,128)(2,1)S(1)}, bf16[128,1664]{1,0:T(8,128)(2,1)S(1)}, u32[]{:S(2)}, u32[]{:S(2)}) %collective-permute-start.4) | collective-permute-done | bytes 426016 | tf_op jit(solution)/shard_map/ppermute | solution.py:162
  88.5 5.1 %collective-permute-start.8 = (bf16[128,1024]{1,0:T(8,128)(2,1)S(1)}, bf16[128,1024]{1,0:T(8,128)(2,1)S(1)}, u32[]{:S(2)}, u32[]{:S(2)}) collective-permute-start(bf16[128,1024]{1,0:T(8,128)(2,1)S(1)} %copy-done.7), channel_id=1, source_target_pairs={{0,4},{4,8},{8,12},{12,0},{1,5},{5,9},{9,13},{13,1},{2,6},{6,10},{... | collective-permute-start | bytes 786440 | tf_op jit(solution)/shard_map/ppermute | solution.py:162
  94.7 2.5 %collective-permute-start.10 = (bf16[128,1024]{1,0:T(8,128)(2,1)S(1)}, bf16[128,1024]{1,0:T(8,128)(2,1)S(1)}, u32[]{:S(2)}, u32[]{:S(2)}) collective-permute-start(bf16[128,1024]{1,0:T(8,128)(2,1)S(1)} %copy-done.3), channel_id=1, source_target_pairs={{0,12},{4,0},{8,4},{12,8},{1,13},{5,1},{9,5},{13,9},{2,14},{6,2},{... | collective-permute-start | bytes 786440 | tf_op jit(solution)/shard_map/ppermute | solution.py:162
  97.2 3.2 %collective-permute-done.8 = bf16[128,1024]{1,0:T(8,128)(2,1)S(1)} collective-permute-done((bf16[128,1024]{1,0:T(8,128)(2,1)S(1)}, bf16[128,1024]{1,0:T(8,128)(2,1)S(1)}, u32[]{:S(2)}, u32[]{:S(2)}) %collective-permute-start.8) | collective-permute-done | bytes 262176 | tf_op jit(solution)/shard_map/ppermute | solution.py:162
  100.4 10.0 %collective-permute-done.9 = bf16[128,1024]{1,0:T(8,128)(2,1)S(1)} collective-permute-done((bf16[128,1024]{1,0:T(8,128)(2,1)S(1)}, bf16[128,1024]{1,0:T(8,128)(2,1)S(1)}, u32[]{:S(2)}, u32[]{:S(2)}) %collective-permute-start.9) | collective-permute-done | bytes 262176 | tf_op jit(solution)/shard_map/ppermute | solution.py:162
  113.9 14.2 %collective-permute-done.19 = bf16[512,1664]{1,0:T(8,128)(2,1)S(1)} collective-permute-done((bf16[512,1664]{1,0:T(8,128)(2,1)S(1)}, bf16[512,1664]{1,0:T(8,128)(2,1)S(1)}, u32[]{:S(2)}, u32[]{:S(2)}) %collective-permute-start.19) | collective-permute-done | bytes 1703968 | tf_op jit(solution)/shard_map/ppermute | solution.py:165
  132.7 4.0 %collective-permute-start.13 = (f32[128,1024]{1,0:T(8,128)S(1)}, f32[128,1024]{1,0:T(8,128)S(1)}, u32[]{:S(2)}, u32[]{:S(2)}) collective-permute-start(f32[128,1024]{1,0:T(8,128)S(1)} %get-tuple-element.168), channel_id=1, source_target_pairs={{0,4},{1,5},{2,6},{3,7},{16,20},{17,21},{18,22},{19,23}} | collective-permute-start | bytes 1572872 | tf_op jit(solution)/shard_map/ppermute | solution.py:128
  137.8 11.1 %collective-permute-done.20 = bf16[512,1024]{1,0:T(8,128)(2,1)S(1)} collective-permute-done((bf16[512,1024]{1,0:T(8,128)(2,1)S(1)}, bf16[512,1024]{1,0:T(8,128)(2,1)S(1)}, u32[]{:S(2)}, u32[]{:S(2)}) %collective-permute-start.20) | collective-permute-done | bytes 1048608 | tf_op jit(solution)/shard_map/ppermute | solution.py:165
  157.2 6.0 %collective-permute-start.24 = (f32[128,1024]{1,0:T(8,128)}, f32[128,1024]{1,0:T(8,128)}, u32[]{:S(2)}, u32[]{:S(2)}) collective-permute-start(f32[128,1024]{1,0:T(8,128)} %get-tuple-element.161), channel_id=1, source_target_pairs={{0,4},{1,5},{2,6},{3,7},{16,20},{17,21},{18,22},{19,23}} | collective-permute-start | bytes 1572872 | tf_op jit(solution)/shard_map/ppermute | solution.py:128
  165.1 2.1 collective-permute-start.14
  167.2 7.7 %collective-permute-done.24 = f32[128,1024]{1,0:T(8,128)} collective-permute-done((f32[128,1024]{1,0:T(8,128)}, f32[128,1024]{1,0:T(8,128)}, u32[]{:S(2)}, u32[]{:S(2)}) %collective-permute-start.24) | collective-permute-done | bytes 524320 | tf_op jit(solution)/shard_map/ppermute | solution.py:128
  174.9 2.2 fusion.66
  178.6 5.1 %collective-permute-start.25 = (f32[128,1024]{1,0:T(8,128)S(1)}, f32[128,1024]{1,0:T(8,128)}, u32[]{:S(2)}, u32[]{:S(2)}) collective-permute-start(f32[128,1024]{1,0:T(8,128)S(1)} %get-tuple-element.159), channel_id=1, source_target_pairs={{0,4},{4,8},{1,5},{5,9},{2,6},{6,10},{3,7},{7,11},{16,20},{20,24},... | collective-permute-start | bytes 1572872 | tf_op jit(solution)/shard_map/ppermute | solution.py:128
  186.2 2.4 %fusion.75 = (f32[128,1024]{1,0:T(8,128)}, f32[128,1024]{1,0:T(8,128)S(1)}, f32[128,1024]{1,0:T(8,128)}) fusion(f32[128,1024]{1,0:T(8,128)} %copy-done.35, s32[]{:T(128)S(6)} %select_n.95, f32[512,512]{1,0:T(8,128)S(1)} %fusion.47, f32[512,512]{1,0:T(8,128)S(1)} %fusion.48, s32[]{:T(128)S(6)} %select_n.91, f32[128,1024]{1,0:T(8,128)} %collective-permute-done.14, ...), kind=kLoop, calls=%fused_computation.123 | loop fusion | flops 655360 | bytes 4718604 | tf_op jit(solution)/shard_map/add | solution.py:126
  189.8 5.0 %collective-permute-start.15 = (f32[128,1024]{1,0:T(8,128)}, f32[128,1024]{1,0:T(8,128)S(1)}, u32[]{:S(2)}, u32[]{:S(2)}) collective-permute-start(f32[128,1024]{1,0:T(8,128)} %get-tuple-element.164), channel_id=1, source_target_pairs={{0,4},{4,8},{8,12},{1,5},{5,9},{9,13},{2,6},{6,10},{10,14},{3,7},{... | collective-permute-start | bytes 1572872 | tf_op jit(solution)/shard_map/ppermute | solution.py:128
  194.9 2.4 %collective-permute-done.25 = f32[128,1024]{1,0:T(8,128)} collective-permute-done((f32[128,1024]{1,0:T(8,128)S(1)}, f32[128,1024]{1,0:T(8,128)}, u32[]{:S(2)}, u32[]{:S(2)}) %collective-permute-start.25) | collective-permute-done | bytes 524320 | tf_op jit(solution)/shard_map/ppermute | solution.py:128
  197.3 2.3 %fusion.64 = (f32[128,1024]{1,0:T(8,128)}, f32[128,1024]{1,0:T(8,128)S(1)}, f32[128,1024]{1,0:T(8,128)}) fusion(f32[128,1024]{1,0:T(8,128)} %collective-permute-done.28, s32[]{:T(128)S(6)} %select_n.95, f32[512,512]{1,0:T(8,128)S(1)} %copy-done.10, f32[512,512]{1,0:T(8,128)S(1)} %copy-done.13, s32[]{:T(128)S(6)} %select_n.91, ...), kind=kLoop, calls=%fused_computation.112 | loop fusion | flops 655360 | bytes 4718604 | tf_op jit(solution)/shard_map/add | solution.py:126
  200.9 5.2 %collective-permute-start.26 = (f32[128,1024]{1,0:T(8,128)}, f32[128,1024]{1,0:T(8,128)S(1)}, u32[]{:S(2)}, u32[]{:S(2)}) collective-permute-start(f32[128,1024]{1,0:T(8,128)} %get-tuple-element.157), channel_id=1, source_target_pairs={{0,4},{4,8},{8,12},{1,5},{5,9},{9,13},{2,6},{6,10},{10,14},{3,7},{... | collective-permute-start | bytes 1572872 | tf_op jit(solution)/shard_map/ppermute | solution.py:128
  206.1 7.0 %conditional.1 = (f32[1024,128]{1,0:T(8,128)}) conditional(s32[]{:T(128)} %clamp.3, (bf16[512,1536]{1,0:T(8,128)(2,1)}, bf16[512,1664]{1,0:T(8,128)(2,1)}, bf16[512,1536]{1,0:T(8,128)(2,1)}, bf16[512,1664]{1,0:T(8,128)(2,1)}, bf16[512,1536]{1,0:T(8,128)(2,1)}, /*index=5*/bf16[512,1664]{1,0:T(8,128)(2,1)}, ...), branch_computations={%region_0.1_spmd, %region_1.2_spmd, %region_2.3_spmd, %region_3.4_... | conditional | flops 537395200 | bytes 28835932 | solution.py:203
  206.1 1.8 fusion.3
  210.9 2.2 convolution_add_fusion
  213.1 2.4 %collective-permute-done.29.refs_5_ = f32[128,1024]{1,0:T(8,128)S(1)} collective-permute-done((f32[128,1024]{1,0:T(8,128)}, f32[128,1024]{1,0:T(8,128)S(1)}, u32[]{:S(2)}, u32[]{:S(2)}) %collective-permute-start.29) | collective-permute-done | bytes 524320 | tf_op jit(solution)/shard_map/ppermute | solution.py:128
  215.4 3.9 %collective-permute-done.26.refs_4_ = f32[128,1024]{1,0:T(8,128)S(1)} collective-permute-done((f32[128,1024]{1,0:T(8,128)}, f32[128,1024]{1,0:T(8,128)S(1)}, u32[]{:S(2)}, u32[]{:S(2)}) %collective-permute-start.26) | collective-permute-done | bytes 524320 | tf_op jit(solution)/shard_map/ppermute | solution.py:128
  (129 shorter events, 43.0 us)
Async XLA Ops:
  5.9 15.3 %collective-permute-start = (bf16[128,1536]{1,0:T(8,128)(2,1)S(1)}, bf16[128,1536]{1,0:T(8,128)(2,1)}, u32[]{:S(2)}, u32[]{:S(2)}) collective-permute-start(bf16[128,1536]{1,0:T(8,128)(2,1)S(1)} %get-tuple-element.124), channel_id=1, source_target_pairs={{0,4},{4,8},{8,12},{12,0},{1,5},{5,9},{9,13},{13,1},{2,6},{6,10},{... | collective-permute-start | bytes 1179656 | tf_op jit(solution)/shard_map/ppermute | solution.py:162
  9.0 29.1 %collective-permute-start.1 = (bf16[128,1536]{1,0:T(8,128)(2,1)S(1)}, bf16[128,1536]{1,0:T(8,128)(2,1)}, u32[]{:S(2)}, u32[]{:S(2)}) collective-permute-start(bf16[128,1536]{1,0:T(8,128)(2,1)S(1)} %get-tuple-element.125), channel_id=1, source_target_pairs={{0,8},{4,12},{8,0},{12,4},{1,9},{5,13},{9,1},{13,5},{2,10},{6,14},... | collective-permute-start | bytes 1179656 | tf_op jit(solution)/shard_map/ppermute | solution.py:162
  11.6 27.5 %collective-permute-start.2 = (bf16[128,1536]{1,0:T(8,128)(2,1)S(1)}, bf16[128,1536]{1,0:T(8,128)(2,1)}, u32[]{:S(2)}, u32[]{:S(2)}) collective-permute-start(bf16[128,1536]{1,0:T(8,128)(2,1)S(1)} %get-tuple-element.126), channel_id=1, source_target_pairs={{0,12},{4,0},{8,4},{12,8},{1,13},{5,1},{9,5},{13,9},{2,14},{6,2},{... | collective-permute-start | bytes 1179656 | tf_op jit(solution)/shard_map/ppermute | solution.py:162
  18.2 41.5 %collective-permute-start.3 = (bf16[128,1664]{1,0:T(8,128)(2,1)S(1)}, bf16[128,1664]{1,0:T(8,128)(2,1)}, u32[]{:S(2)}, u32[]{:S(2)}) collective-permute-start(bf16[128,1664]{1,0:T(8,128)(2,1)S(1)} %get-tuple-element.129), channel_id=1, source_target_pairs={{0,4},{4,8},{8,12},{12,0},{1,5},{5,9},{9,13},{13,1},{2,6},{6,10},{... | collective-permute-start | bytes 1277960 | tf_op jit(solution)/shard_map/ppermute | solution.py:162
  40.2 113.0 %copy-start.22 = (bf16[4,128,1536]{2,1,0:T(8,128)(2,1)}, bf16[4,128,1536]{2,1,0:T(8,128)(2,1)S(1)}, u32[]{:S(2)}) copy-start(bf16[4,128,1536]{2,1,0:T(8,128)(2,1)S(1)} %bitcast_dynamic-update-slice_fusion.4) | copy-start | bytes 4718596
  40.2 48.3 %collective-permute-start.7 = (bf16[512,1536]{1,0:T(8,128)(2,1)S(1)}, bf16[512,1536]{1,0:T(8,128)(2,1)S(1)}, u32[]{:S(2)}, u32[]{:S(2)}) collective-permute-start(bf16[512,1536]{1,0:T(8,128)(2,1)S(1)} %bitcast.66), channel_id=1, source_target_pairs={{0,1},{1,0},{2,3},{3,2},{4,5},{5,4},{6,7},{7,6},{8,9},{9,8},{10,11... | collective-permute-start | bytes 4718600 | tf_op jit(solution)/shard_map/ppermute | solution.py:166
  40.2 48.2 %collective-permute-start.6 = (bf16[512,1536]{1,0:T(8,128)(2,1)S(1)}, bf16[512,1536]{1,0:T(8,128)(2,1)S(1)}, u32[]{:S(2)}, u32[]{:S(2)}) collective-permute-start(bf16[512,1536]{1,0:T(8,128)(2,1)S(1)} %bitcast.67), channel_id=1, source_target_pairs={{0,2},{2,0},{1,3},{3,1},{4,6},{6,4},{5,7},{7,5},{8,10},{10,8},{9,1... | collective-permute-start | bytes 4718600 | tf_op jit(solution)/shard_map/ppermute | solution.py:165
  42.3 45.6 %collective-permute-start.5 = (bf16[128,1664]{1,0:T(8,128)(2,1)S(1)}, bf16[128,1664]{1,0:T(8,128)(2,1)S(1)}, u32[]{:S(2)}, u32[]{:S(2)}) collective-permute-start(bf16[128,1664]{1,0:T(8,128)(2,1)S(1)} %get-tuple-element.134), channel_id=1, source_target_pairs={{0,12},{4,0},{8,4},{12,8},{1,13},{5,1},{9,5},{13,9},{2,14},{6,2},{... | collective-permute-start | bytes 1277960 | tf_op jit(solution)/shard_map/ppermute | solution.py:162
  52.3 35.5 %collective-permute-start.4 = (bf16[128,1664]{1,0:T(8,128)(2,1)S(1)}, bf16[128,1664]{1,0:T(8,128)(2,1)S(1)}, u32[]{:S(2)}, u32[]{:S(2)}) collective-permute-start(bf16[128,1664]{1,0:T(8,128)(2,1)S(1)} %get-tuple-element.133), channel_id=1, source_target_pairs={{0,8},{4,12},{8,0},{12,4},{1,9},{5,13},{9,1},{13,5},{2,10},{6,14},... | collective-permute-start | bytes 1277960 | tf_op jit(solution)/shard_map/ppermute | solution.py:162
  87.9 63.0 %copy-start.21 = (bf16[4,128,1664]{2,1,0:T(8,128)(2,1)}, bf16[4,128,1664]{2,1,0:T(8,128)(2,1)S(1)}, u32[]{:S(2)}) copy-start(bf16[4,128,1664]{2,1,0:T(8,128)(2,1)S(1)} %bitcast_dynamic-update-slice_fusion) | copy-start | bytes 5111812
  87.9 40.2 %collective-permute-start.19 = (bf16[512,1664]{1,0:T(8,128)(2,1)S(1)}, bf16[512,1664]{1,0:T(8,128)(2,1)S(1)}, u32[]{:S(2)}, u32[]{:S(2)}) collective-permute-start(bf16[512,1664]{1,0:T(8,128)(2,1)S(1)} %bitcast.56), channel_id=1, source_target_pairs={{0,2},{2,0},{1,3},{3,1},{4,6},{6,4},{5,7},{7,5},{8,10},{10,8},{9,1... | collective-permute-start | bytes 5111816 | tf_op jit(solution)/shard_map/ppermute | solution.py:165
  88.5 39.6 %collective-permute-start.11 = (bf16[512,1664]{1,0:T(8,128)(2,1)S(1)}, bf16[512,1664]{1,0:T(8,128)(2,1)S(1)}, u32[]{:S(2)}, u32[]{:S(2)}) collective-permute-start(bf16[512,1664]{1,0:T(8,128)(2,1)S(1)} %bitcast.57), channel_id=1, source_target_pairs={{0,1},{1,0},{2,3},{3,2},{4,5},{5,4},{6,7},{7,6},{8,9},{9,8},{10,11... | collective-permute-start | bytes 5111816 | tf_op jit(solution)/shard_map/ppermute | solution.py:166
  88.5 11.9 %collective-permute-start.8 = (bf16[128,1024]{1,0:T(8,128)(2,1)S(1)}, bf16[128,1024]{1,0:T(8,128)(2,1)S(1)}, u32[]{:S(2)}, u32[]{:S(2)}) collective-permute-start(bf16[128,1024]{1,0:T(8,128)(2,1)S(1)} %copy-done.7), channel_id=1, source_target_pairs={{0,4},{4,8},{8,12},{12,0},{1,5},{5,9},{9,13},{13,1},{2,6},{6,10},{... | collective-permute-start | bytes 786440 | tf_op jit(solution)/shard_map/ppermute | solution.py:162
  93.7 16.8 %collective-permute-start.9 = (bf16[128,1024]{1,0:T(8,128)(2,1)S(1)}, bf16[128,1024]{1,0:T(8,128)(2,1)S(1)}, u32[]{:S(2)}, u32[]{:S(2)}) collective-permute-start(bf16[128,1024]{1,0:T(8,128)(2,1)S(1)} %copy-done.5), channel_id=1, source_target_pairs={{0,8},{4,12},{8,0},{12,4},{1,9},{5,13},{9,1},{13,5},{2,10},{6,14},... | collective-permute-start | bytes 786440 | tf_op jit(solution)/shard_map/ppermute | solution.py:162
  94.7 15.8 %collective-permute-start.10 = (bf16[128,1024]{1,0:T(8,128)(2,1)S(1)}, bf16[128,1024]{1,0:T(8,128)(2,1)S(1)}, u32[]{:S(2)}, u32[]{:S(2)}) collective-permute-start(bf16[128,1024]{1,0:T(8,128)(2,1)S(1)} %copy-done.3), channel_id=1, source_target_pairs={{0,12},{4,0},{8,4},{12,8},{1,13},{5,1},{9,5},{13,9},{2,14},{6,2},{... | collective-permute-start | bytes 786440 | tf_op jit(solution)/shard_map/ppermute | solution.py:162
  110.5 38.3 %collective-permute-start.20 = (bf16[512,1024]{1,0:T(8,128)(2,1)S(1)}, bf16[512,1024]{1,0:T(8,128)(2,1)S(1)}, u32[]{:S(2)}, u32[]{:S(2)}) collective-permute-start(bf16[512,1024]{1,0:T(8,128)(2,1)S(1)} %bitcast.49), channel_id=1, source_target_pairs={{0,2},{2,0},{1,3},{3,1},{4,6},{6,4},{5,7},{7,5},{8,10},{10,8},{9,1... | collective-permute-start | bytes 3145736 | tf_op jit(solution)/shard_map/ppermute | solution.py:165
  112.1 17.8 %collective-permute-start.12 = (bf16[512,1024]{1,0:T(8,128)(2,1)S(1)}, bf16[512,1024]{1,0:T(8,128)(2,1)S(1)}, u32[]{:S(2)}, u32[]{:S(2)}) collective-permute-start(bf16[512,1024]{1,0:T(8,128)(2,1)S(1)} %bitcast.50), channel_id=1, source_target_pairs={{0,1},{1,0},{2,3},{3,2},{4,5},{5,4},{6,7},{7,6},{8,9},{9,8},{10,11... | collective-permute-start | bytes 3145736 | tf_op jit(solution)/shard_map/ppermute | solution.py:166
  128.1 22.8 %collective-permute-start.22 = (bf16[512,1664]{1,0:T(8,128)(2,1)S(1)}, bf16[512,1664]{1,0:T(8,128)(2,1)S(1)}, u32[]{:S(2)}, u32[]{:S(2)}) collective-permute-start(bf16[512,1664]{1,0:T(8,128)(2,1)S(1)} %collective-permute-done.19), channel_id=1, source_target_pairs={{0,1},{1,0},{2,3},{3,2},{4,5},{5,4},{6,7},{7,6},{8,9},{9,8},{10,11... | collective-permute-start | bytes 5111816 | tf_op jit(solution)/shard_map/ppermute | solution.py:170
  132.0 16.9 %collective-permute-start.16 = (f32[128,1024]{1,0:T(8,128)S(1)}, f32[128,1024]{1,0:T(8,128)S(1)}, u32[]{:S(2)}, u32[]{:S(2)}) collective-permute-start(f32[128,1024]{1,0:T(8,128)S(1)} %get-tuple-element.167), channel_id=1, source_target_pairs={{12,8},{13,9},{14,10},{15,11},{28,24},{29,25},{30,26},{31,27}} | collective-permute-start | bytes 1572872 | tf_op jit(solution)/shard_map/ppermute | solution.py:128
  132.7 16.2 %collective-permute-start.13 = (f32[128,1024]{1,0:T(8,128)S(1)}, f32[128,1024]{1,0:T(8,128)S(1)}, u32[]{:S(2)}, u32[]{:S(2)}) collective-permute-start(f32[128,1024]{1,0:T(8,128)S(1)} %get-tuple-element.168), channel_id=1, source_target_pairs={{0,4},{1,5},{2,6},{3,7},{16,20},{17,21},{18,22},{19,23}} | collective-permute-start | bytes 1572872 | tf_op jit(solution)/shard_map/ppermute | solution.py:128
  136.7 16.5 %collective-permute-start.21 = (bf16[512,1536]{1,0:T(8,128)(2,1)S(1)}, bf16[512,1536]{1,0:T(8,128)(2,1)S(1)}, u32[]{:S(2)}, u32[]{:S(2)}) collective-permute-start(bf16[512,1536]{1,0:T(8,128)(2,1)S(1)} %collective-permute-done.6), channel_id=1, source_target_pairs={{0,1},{1,0},{2,3},{3,2},{4,5},{5,4},{6,7},{7,6},{8,9},{9,8},{10,11... | collective-permute-start | bytes 4718600 | tf_op jit(solution)/shard_map/ppermute | solution.py:170
  148.9 3.3 %collective-permute-start.23 = (bf16[512,1024]{1,0:T(8,128)(2,1)S(1)}, bf16[512,1024]{1,0:T(8,128)(2,1)S(1)}, u32[]{:S(2)}, u32[]{:S(2)}) collective-permute-start(bf16[512,1024]{1,0:T(8,128)(2,1)S(1)} %collective-permute-done.20), channel_id=1, source_target_pairs={{0,1},{1,0},{2,3},{3,2},{4,5},{5,4},{6,7},{7,6},{8,9},{9,8},{10,11... | collective-permute-start | bytes 3145736 | tf_op jit(solution)/shard_map/ppermute | solution.py:179
  155.7 11.5 %collective-permute-start.27 = (f32[128,1024]{1,0:T(8,128)}, f32[128,1024]{1,0:T(8,128)}, u32[]{:S(2)}, u32[]{:S(2)}) collective-permute-start(f32[128,1024]{1,0:T(8,128)} %get-tuple-element.160), channel_id=1, source_target_pairs={{12,8},{13,9},{14,10},{15,11},{28,24},{29,25},{30,26},{31,27}} | collective-permute-start | bytes 1572872 | tf_op jit(solution)/shard_map/ppermute | solution.py:128
  157.2 17.8 %collective-permute-start.24 = (f32[128,1024]{1,0:T(8,128)}, f32[128,1024]{1,0:T(8,128)}, u32[]{:S(2)}, u32[]{:S(2)}) collective-permute-start(f32[128,1024]{1,0:T(8,128)} %get-tuple-element.161), channel_id=1, source_target_pairs={{0,4},{1,5},{2,6},{3,7},{16,20},{17,21},{18,22},{19,23}} | collective-permute-start | bytes 1572872 | tf_op jit(solution)/shard_map/ppermute | solution.py:128
  164.3 19.3 %collective-permute-start.17 = (f32[128,1024]{1,0:T(8,128)}, f32[128,1024]{1,0:T(8,128)S(1)}, u32[]{:S(2)}, u32[]{:S(2)}) collective-permute-start(f32[128,1024]{1,0:T(8,128)} %get-tuple-element.165), channel_id=1, source_target_pairs={{12,8},{8,4},{13,9},{9,5},{14,10},{10,6},{15,11},{11,7},{28,24},{2... | collective-permute-start | bytes 1572872 | tf_op jit(solution)/shard_map/ppermute | solution.py:128
  165.1 21.0 %collective-permute-start.14 = (f32[128,1024]{1,0:T(8,128)}, f32[128,1024]{1,0:T(8,128)}, u32[]{:S(2)}, u32[]{:S(2)}) collective-permute-start(f32[128,1024]{1,0:T(8,128)} %get-tuple-element.166), channel_id=1, source_target_pairs={{0,4},{4,8},{1,5},{5,9},{2,6},{6,10},{3,7},{7,11},{16,20},{20,24},... | collective-permute-start | bytes 1572872 | tf_op jit(solution)/shard_map/ppermute | solution.py:128
  177.1 17.8 %collective-permute-start.28 = (f32[128,1024]{1,0:T(8,128)}, f32[128,1024]{1,0:T(8,128)}, u32[]{:S(2)}, u32[]{:S(2)}) collective-permute-start(f32[128,1024]{1,0:T(8,128)} %get-tuple-element.158), channel_id=1, source_target_pairs={{12,8},{8,4},{13,9},{9,5},{14,10},{10,6},{15,11},{11,7},{28,24},{2... | collective-permute-start | bytes 1572872 | tf_op jit(solution)/shard_map/ppermute | solution.py:128
  178.6 18.7 %collective-permute-start.25 = (f32[128,1024]{1,0:T(8,128)S(1)}, f32[128,1024]{1,0:T(8,128)}, u32[]{:S(2)}, u32[]{:S(2)}) collective-permute-start(f32[128,1024]{1,0:T(8,128)S(1)} %get-tuple-element.159), channel_id=1, source_target_pairs={{0,4},{4,8},{1,5},{5,9},{2,6},{6,10},{3,7},{7,11},{16,20},{20,24},... | collective-permute-start | bytes 1572872 | tf_op jit(solution)/shard_map/ppermute | solution.py:128
  188.5 24.5 %collective-permute-start.18 = (f32[128,1024]{1,0:T(8,128)}, f32[128,1024]{1,0:T(8,128)S(1)}, u32[]{:S(2)}, u32[]{:S(2)}) collective-permute-start(f32[128,1024]{1,0:T(8,128)} %get-tuple-element.162), channel_id=1, source_target_pairs={{12,8},{8,4},{4,0},{13,9},{9,5},{5,1},{14,10},{10,6},{6,2},{15,11}... | collective-permute-start | bytes 1572872 | tf_op jit(solution)/shard_map/ppermute | solution.py:128
  189.8 23.2 %collective-permute-start.15 = (f32[128,1024]{1,0:T(8,128)}, f32[128,1024]{1,0:T(8,128)S(1)}, u32[]{:S(2)}, u32[]{:S(2)}) collective-permute-start(f32[128,1024]{1,0:T(8,128)} %get-tuple-element.164), channel_id=1, source_target_pairs={{0,4},{4,8},{8,12},{1,5},{5,9},{9,13},{2,6},{6,10},{10,14},{3,7},{... | collective-permute-start | bytes 1572872 | tf_op jit(solution)/shard_map/ppermute | solution.py:128
  199.6 15.8 %collective-permute-start.29 = (f32[128,1024]{1,0:T(8,128)}, f32[128,1024]{1,0:T(8,128)S(1)}, u32[]{:S(2)}, u32[]{:S(2)}) collective-permute-start(f32[128,1024]{1,0:T(8,128)} %get-tuple-element.155), channel_id=1, source_target_pairs={{12,8},{8,4},{4,0},{13,9},{9,5},{5,1},{14,10},{10,6},{6,2},{15,11}... | collective-permute-start | bytes 1572872 | tf_op jit(solution)/shard_map/ppermute | solution.py:128
  200.9 18.4 %collective-permute-start.26 = (f32[128,1024]{1,0:T(8,128)}, f32[128,1024]{1,0:T(8,128)S(1)}, u32[]{:S(2)}, u32[]{:S(2)}) collective-permute-start(f32[128,1024]{1,0:T(8,128)} %get-tuple-element.157), channel_id=1, source_target_pairs={{0,4},{4,8},{8,12},{1,5},{5,9},{9,13},{2,6},{6,10},{10,14},{3,7},{... | collective-permute-start | bytes 1572872 | tf_op jit(solution)/shard_map/ppermute | solution.py:128
  (28 other events, 334.4 us)

commit v12 on v11

--- a/solution.py
+++ b/solution.py
@@ -116,18 +116,18 @@
     )(place.reshape(1).astype(jnp.int32), *parts)
 
 
-def chain(planes, z, sums, up):
+def chain(planes, z, sums, up, ahead):
     rows = sums.shape[0] // planes
-    got = first = None
+    got = early = None
     for step in range(1, planes):
         plane = planes - step + z if up else z - planes + step
         sent = lax.dynamic_slice_in_dim(sums, jnp.clip(plane, 0, planes - 1) * rows, rows, 0)
         if got is not None:
-            sent = sent + got
+            sent = sent + (after(got, *ahead) if step == 3 else got)
         pairs = [(i, i + 1) for i in range(step)] if up else [(planes - 1 - i, planes - 2 - i) for i in range(step)]
+        early = sent if step < 3 else early
         got = lax.ppermute(sent, "z", pairs)
-        first = got if first is None else first
-    return got, first
+    return got, early
 
 
 def on_device(planes, slab, factor):
@@ -166,7 +166,7 @@
         beside = lax.ppermute(stack, "c", SWAP)
         waits.append((across, beside))
         held.append([stack, beside, across])
-        if j < last:
+        if j < last - 1:
             held[j].append(lax.ppermute(across, "c", SWAP))
     flat = [[b[:, : size * cells] for b in held[j][:2]] for j, (_, size) in enumerate(chunks)]
     sums = [sum(nt_dot(flat[j][0], flat[j][k]) for j in range(last + 1)) for k in range(2)]
@@ -174,15 +174,15 @@
     for half in range(2):
         if half:
             for j in range(last + 1):
-                if j == last:
+                if j >= last - 1:
                     held[j][2] = after(held[j][2], *gate)
                     held[j].append(lax.ppermute(held[j][2], "c", SWAP))
                 flat[j] += [b[:, : chunks[j][1] * cells] for b in held[j][2:]]
             sums = [sum(nt_dot(flat[j][0], flat[j][k]) for j in range(last + 1)) for k in range(2, 4)]
         both = jnp.concatenate(sums, axis=1)
-        up, first_up = chain(planes, z, both, True)
-        down, first_down = chain(planes, z, both, False)
-        gate = (first_up, first_down)
+        up, early_up = chain(planes, z, both, True, parts[1:3])
+        down, early_down = chain(planes, z, both, False, parts[1:3])
+        gate = (early_up, early_down)
         parts += [lax.dynamic_slice_in_dim(both, z * rows, rows, 0), up, down]
     gram = finish(planes, total, place, parts)
     own = per_plane // 4

time: 221 us -> 234 us (1.059)
  matrix products: 17.9 us -> 32.5 us
  waiting for transfers between devices: 102 us -> 92.5 us
  local copies, waits for them, and re-layouts: 12.6 us -> 19 us
  starting transfers between devices: 71.3 us -> 73.9 us
    ppermute x3, waiting for transfers between devices: 25.3 us -> 6.08 us  [on_device(): across = lax.ppermute(stack, 'y', SWAP)]
    ppermute x12, waiting for transfers between devices: 18.1 us -> 33.1 us  [chain(): got = lax.ppermute(sent, 'z', pairs)]
    dot_general x12, matrix products: 11 us -> 25.6 us  [nt_dot(): lax.dot_general(a, b, (((1,), (1,)), ((), ())), preferred_element_type=jn...]
    dynamic_update_slice x12, local copies, waits for them, and re-layouts: 4.37 us -> 10.2 us  [stacked(): lax.dynamic_update_slice(stack, parts[shift][None], ((z - shift) % planes...]
    ppermute x9, waiting for transfers between devices: 58.2 us -> 53.3 us  [on_device(): lax.ppermute(piece, 'z', [(s, (s + shift) % planes) for s in range(planes)])]
    ppermute x12, starting transfers between devices: 34.4 us -> 38.6 us  [chain(): got = lax.ppermute(sent, 'z', pairs)]
    add x4, other arithmetic: 8 us -> 5.39 us  [chain(): sent = sent + (after(got, *ahead) if step == 3 else got)]
    unnamed x54 -> x46, local copies, waits for them, and re-layouts: 7.91 us -> 6.28 us
  transfers between devices with their start and end apart: 30 -> 30, of which waited for: 12 -> 12; matrix products, arithmetic and copies ran while one was open for 13% -> 22% of each run, Pallas kernels for 1% -> 1%
where the time goes in v12:
time: 234 us; the launch traced here: 233 us
  waiting for transfers between devices  92.5 us (40%)
  starting transfers between devices  73.9 us (32%)
  matrix products  32.5 us (14%)
  local copies, waits for them, and re-layouts  19 us (8%)
  other arithmetic  7.4 us (3%)
  Pallas kernels  6.66 us (3%)
    ppermute x9, waiting for transfers between devices, on_device(): lax.ppermute(piece, 'z', [(s, (s + shift) % planes) for s in range(planes)])  53.3 us
    ppermute x12, starting transfers between devices, chain(): got = lax.ppermute(sent, 'z', pairs)  38.6 us
    ppermute x12, waiting for transfers between devices, chain(): got = lax.ppermute(sent, 'z', pairs)  33.1 us
    ppermute x9, starting transfers between devices, on_device(): lax.ppermute(piece, 'z', [(s, (s + shift) % planes) for s in range(planes)])  30.7 us
    dot_general x12, matrix products, nt_dot(): lax.dot_general(a, b, (((1,), (1,)), ((), ())), preferred_element_type=jn...  25.6 us
    dynamic_update_slice x12, local copies, waits for them, and re-layouts, stacked(): lax.dynamic_update_slice(stack, parts[shift][None], ((z - shift) % planes...  10.2 us
    dot_general x4, matrix products, tn_dot(): lax.dot_general(a, b, (((0,), (0,)), ((), ())), preferred_element_type=jn...  6.88 us
    unnamed x46, local copies, waits for them, and re-layouts  6.28 us
  transfers between devices with their start and end apart: 30, of which 12 were waited for; matrix products, arithmetic and copies ran while one was open for 22% of the time, Pallas kernels for 1%

profile of v12, /device:TPU:0, one launch (start us, length us, event | category | flops | bytes accessed | tf_op | source)
XLA Modules:
  0.0 233.1 jit_solution(16217494718211932266)
XLA Ops:
  3.6 2.3 %unfold.2 = (bf16[128,1536]{1,0:T(8,128)(2,1)S(1)}, bf16[128,1536]{1,0:T(8,128)(2,1)S(1)}, bf16[128,1536]{1,0:T(8,128)(2,1)S(1)}, bf16[128,1536]{1,0:T(8,128)(2,1)S(1)}) custom-call(s32[1]{0:T(128)} %bitcast.1.z_ref, bf16[128,64,256]{2,1,0:T(8,128)(2,1)S(1)} %copy-done, bf16[128,64,256]{2,1,0:T(8,128)(2,1)S(1)} %copy-done, ...), custom_call_target="tpu_custom_call" | custom-call | bytes 5767168 | tf_op jit(solution)/shard_map/unfold/pallas_call | solution.py:67
  5.9 3.1 %collective-permute-start = (bf16[128,1536]{1,0:T(8,128)(2,1)S(1)}, bf16[128,1536]{1,0:T(8,128)(2,1)}, u32[]{:S(2)}, u32[]{:S(2)}) collective-permute-start(bf16[128,1536]{1,0:T(8,128)(2,1)S(1)} %get-tuple-element.127), channel_id=1, source_target_pairs={{0,4},{4,8},{8,12},{12,0},{1,5},{5,9},{9,13},{13,1},{2,6},{6,10},{... | collective-permute-start | bytes 1179656 | tf_op jit(solution)/shard_map/ppermute | solution.py:162
  9.0 2.6 %collective-permute-start.1 = (bf16[128,1536]{1,0:T(8,128)(2,1)S(1)}, bf16[128,1536]{1,0:T(8,128)(2,1)}, u32[]{:S(2)}, u32[]{:S(2)}) collective-permute-start(bf16[128,1536]{1,0:T(8,128)(2,1)S(1)} %get-tuple-element.128), channel_id=1, source_target_pairs={{0,8},{4,12},{8,0},{12,4},{1,9},{5,13},{9,1},{13,5},{2,10},{6,14},... | collective-permute-start | bytes 1179656 | tf_op jit(solution)/shard_map/ppermute | solution.py:162
  13.0 3.1 %unfold.3 = (bf16[128,1664]{1,0:T(8,128)(2,1)S(1)}, bf16[128,1664]{1,0:T(8,128)(2,1)S(1)}, bf16[128,1664]{1,0:T(8,128)(2,1)S(1)}, bf16[128,1664]{1,0:T(8,128)(2,...) custom-call(s32[1]{0:T(128)} %bitcast.1.z_ref, ...), custom_call_target="tpu_custom_call" | custom-call | bytes 6946816 | tf_op jit(solution)/shard_map/unfold/pallas_call | solution.py:67
  22.3 15.8 %collective-permute-done.1 = bf16[128,1536]{1,0:T(8,128)(2,1)} collective-permute-done((bf16[128,1536]{1,0:T(8,128)(2,1)S(1)}, bf16[128,1536]{1,0:T(8,128)(2,1)}, u32[]{:S(2)}, u32[]{:S(2)}) %collective-permute-start.1) | collective-permute-done | bytes 393248 | tf_op jit(solution)/shard_map/ppermute | solution.py:162
  43.9 10.0 %collective-permute-start.5 = (bf16[128,1664]{1,0:T(8,128)(2,1)S(1)}, bf16[128,1664]{1,0:T(8,128)(2,1)S(1)}, u32[]{:S(2)}, u32[]{:S(2)}) collective-permute-start(bf16[128,1664]{1,0:T(8,128)(2,1)S(1)} %get-tuple-element.137), channel_id=1, source_target_pairs={{0,12},{4,0},{8,4},{12,8},{1,13},{5,1},{9,5},{13,9},{2,14},{6,2},{... | collective-permute-start | bytes 1277960 | tf_op jit(solution)/shard_map/ppermute | solution.py:162
  53.9 7.3 %collective-permute-start.4 = (bf16[128,1664]{1,0:T(8,128)(2,1)S(1)}, bf16[128,1664]{1,0:T(8,128)(2,1)S(1)}, u32[]{:S(2)}, u32[]{:S(2)}) collective-permute-start(bf16[128,1664]{1,0:T(8,128)(2,1)S(1)} %get-tuple-element.136), channel_id=1, source_target_pairs={{0,8},{4,12},{8,0},{12,4},{1,9},{5,13},{9,1},{13,5},{2,10},{6,14},... | collective-permute-start | bytes 1277960 | tf_op jit(solution)/shard_map/ppermute | solution.py:162
  63.1 26.3 %collective-permute-done.4 = bf16[128,1664]{1,0:T(8,128)(2,1)S(1)} collective-permute-done((bf16[128,1664]{1,0:T(8,128)(2,1)S(1)}, bf16[128,1664]{1,0:T(8,128)(2,1)S(1)}, u32[]{:S(2)}, u32[]{:S(2)}) %collective-permute-start.4) | collective-permute-done | bytes 426016 | tf_op jit(solution)/shard_map/ppermute | solution.py:162
  91.0 2.2 collective-permute-start.8
  93.2 2.9 %fusion.54 = f32[512,512]{1,0:T(8,128)S(1)} fusion(bf16[512,1664]{1,0:T(8,128)(2,1)} %bitcast.11), kind=kOutput, calls=%fused_computation.102 | convolution fusion | flops 805306368 | bytes 2621440 | tf_op jit(solution)/shard_map/dot_general | solution.py:26
  97.8 3.5 %collective-permute-start.10 = (bf16[128,1024]{1,0:T(8,128)(2,1)S(1)}, bf16[128,1024]{1,0:T(8,128)(2,1)S(1)}, u32[]{:S(2)}, u32[]{:S(2)}) collective-permute-start(bf16[128,1024]{1,0:T(8,128)(2,1)S(1)} %copy-done.3), channel_id=1, source_target_pairs={{0,12},{4,0},{8,4},{12,8},{1,13},{5,1},{9,5},{13,9},{2,14},{6,2},{... | collective-permute-start | bytes 786440 | tf_op jit(solution)/shard_map/ppermute | solution.py:162
  102.8 10.1 %collective-permute-done.9 = bf16[128,1024]{1,0:T(8,128)(2,1)S(1)} collective-permute-done((bf16[128,1024]{1,0:T(8,128)(2,1)S(1)}, bf16[128,1024]{1,0:T(8,128)(2,1)S(1)}, u32[]{:S(2)}, u32[]{:S(2)}) %collective-permute-start.9) | collective-permute-done | bytes 262176 | tf_op jit(solution)/shard_map/ppermute | solution.py:162
  114.4 2.3 fusion.78
  117.7 3.0 %fusion.43 = f32[512,512]{1,0:T(8,128)S(1)} fusion(bf16[512,1664]{1,0:T(8,128)(2,1)S(1)} %collective-permute-done.11, bf16[512,1664]{1,0:T(8,128)(2,1)} %bitcast.11), kind=kOutput, calls=%fused_computation.87 | convolution fusion | flops 805306368 | bytes 4194304 | tf_op jit(solution)/shard_map/dot_general | solution.py:26
  120.8 2.3 %fusion.79 = f32[512,512]{1,0:T(8,128)S(1)} fusion(bf16[512,1024]{1,0:T(8,128)(2,1)} %bitcast.16, bf16[512,1024]{1,0:T(8,128)(2,1)S(1)} %collective-permute-done.12), kind=kOutput, calls=%fused_computation.139 | convolution fusion | flops 536870912 | bytes 3145728 | tf_op jit(solution)/shard_map/dot_general | solution.py:26
  125.7 8.2 %collective-permute-start.13 = (f32[128,1024]{1,0:T(8,128)S(1)}, f32[128,1024]{1,0:T(8,128)}, u32[]{:S(2)}, u32[]{:S(2)}) collective-permute-start(f32[128,1024]{1,0:T(8,128)S(1)} %get-tuple-element.174), channel_id=1, source_target_pairs={{0,4},{1,5},{2,6},{3,7},{16,20},{17,21},{18,22},{19,23}} | collective-permute-start | bytes 1572872 | tf_op jit(solution)/shard_map/ppermute | solution.py:129
  135.3 9.6 %collective-permute-done.13 = f32[128,1024]{1,0:T(8,128)} collective-permute-done((f32[128,1024]{1,0:T(8,128)S(1)}, f32[128,1024]{1,0:T(8,128)}, u32[]{:S(2)}, u32[]{:S(2)}) %collective-permute-start.13) | collective-permute-done | bytes 524320 | tf_op jit(solution)/shard_map/ppermute | solution.py:129
  148.3 5.1 %collective-permute-start.14 = (f32[128,1024]{1,0:T(8,128)S(1)}, f32[128,1024]{1,0:T(8,128)}, u32[]{:S(2)}, u32[]{:S(2)}) collective-permute-start(f32[128,1024]{1,0:T(8,128)S(1)} %get-tuple-element.172), channel_id=1, source_target_pairs={{0,4},{4,8},{1,5},{5,9},{2,6},{6,10},{3,7},{7,11},{16,20},{20,24},... | collective-permute-start | bytes 1572872 | tf_op jit(solution)/shard_map/ppermute | solution.py:129
  153.4 6.1 %collective-permute-done.20 = bf16[512,1024]{1,0:T(8,128)(2,1)} collective-permute-done((bf16[512,1024]{1,0:T(8,128)(2,1)}, bf16[512,1024]{1,0:T(8,128)(2,1)}, u32[]{:S(2)}, u32[]{:S(2)}) %collective-permute-start.20) | collective-permute-done | bytes 1048608 | tf_op jit(solution)/shard_map/ppermute | solution.py:165
  159.5 2.3 fusion.80
  161.8 3.0 %fusion.45 = f32[512,512]{1,0:T(8,128)S(1)} fusion(bf16[512,1664]{1,0:T(8,128)(2,1)} %collective-permute-done.19, bf16[512,1664]{1,0:T(8,128)(2,1)} %bitcast.11), kind=kOutput, calls=%fused_computation.89 | convolution fusion | flops 805306368 | bytes 4194304 | tf_op jit(solution)/shard_map/dot_general | solution.py:26
  165.8 2.7 %fusion.81 = f32[512,512]{1,0:T(8,128)S(1)} fusion(bf16[512,1024]{1,0:T(8,128)(2,1)} %bitcast.16, bf16[512,1024]{1,0:T(8,128)(2,1)S(1)} %collective-permute-done.23), kind=kOutput, calls=%fused_computation.141 | convolution fusion | flops 536870912 | bytes 3145728 | tf_op jit(solution)/shard_map/dot_general | solution.py:26
  168.6 3.0 %fusion.41 = f32[512,512]{1,0:T(8,128)S(1)} fusion(bf16[512,1664]{1,0:T(8,128)(2,1)S(1)} %collective-permute-done.22, bf16[512,1664]{1,0:T(8,128)(2,1)} %bitcast.11), kind=kOutput, calls=%fused_computation.85 | convolution fusion | flops 805306368 | bytes 4194304 | tf_op jit(solution)/shard_map/dot_general | solution.py:26
  175.8 3.6 %collective-permute-start.24 = (f32[128,1024]{1,0:T(8,128)}, f32[128,1024]{1,0:T(8,128)}, u32[]{:S(2)}, u32[]{:S(2)}) collective-permute-start(f32[128,1024]{1,0:T(8,128)} %get-tuple-element.167), channel_id=1, source_target_pairs={{0,4},{1,5},{2,6},{3,7},{16,20},{17,21},{18,22},{19,23}} | collective-permute-start | bytes 1572872 | tf_op jit(solution)/shard_map/ppermute | solution.py:129
  182.2 4.6 %collective-permute-start.15 = (f32[128,1024]{1,0:T(8,128)S(1)}, f32[128,1024]{1,0:T(8,128)S(1)}, u32[]{:S(2)}, u32[]{:S(2)}) collective-permute-start(f32[128,1024]{1,0:T(8,128)S(1)} %get-tuple-element.170), channel_id=1, source_target_pairs={{0,4},{4,8},{8,12},{1,5},{5,9},{9,13},{2,6},{6,10},{10,14},{3,7},{... | collective-permute-start | bytes 1572872 | tf_op jit(solution)/shard_map/ppermute | solution.py:129
  186.8 4.3 %collective-permute-done.24 = f32[128,1024]{1,0:T(8,128)} collective-permute-done((f32[128,1024]{1,0:T(8,128)}, f32[128,1024]{1,0:T(8,128)}, u32[]{:S(2)}, u32[]{:S(2)}) %collective-permute-start.24) | collective-permute-done | bytes 524320 | tf_op jit(solution)/shard_map/ppermute | solution.py:129
  193.1 5.0 %collective-permute-start.25 = (f32[128,1024]{1,0:T(8,128)S(1)}, f32[128,1024]{1,0:T(8,128)S(1)}, u32[]{:S(2)}, u32[]{:S(2)}) collective-permute-start(f32[128,1024]{1,0:T(8,128)S(1)} %get-tuple-element.165), channel_id=1, source_target_pairs={{0,4},{4,8},{1,5},{5,9},{2,6},{6,10},{3,7},{7,11},{16,20},{20,24},... | collective-permute-start | bytes 1572872 | tf_op jit(solution)/shard_map/ppermute | solution.py:129
  198.1 4.0 %collective-permute-done.15.refs_1_ = f32[128,1024]{1,0:T(8,128)S(1)} collective-permute-done((f32[128,1024]{1,0:T(8,128)S(1)}, f32[128,1024]{1,0:T(8,128)S(1)}, u32[]{:S(2)}, u32[]{:S(2)}) %collective-permute-start.15) | collective-permute-done | bytes 524320 | tf_op jit(solution)/shard_map/ppermute | solution.py:129
  202.2 10.8 %collective-permute-done.25 = f32[128,1024]{1,0:T(8,128)S(1)} collective-permute-done((f32[128,1024]{1,0:T(8,128)S(1)}, f32[128,1024]{1,0:T(8,128)S(1)}, u32[]{:S(2)}, u32[]{:S(2)}) %collective-permute-start.25) | collective-permute-done | bytes 524320 | tf_op jit(solution)/shard_map/ppermute | solution.py:129
  215.5 5.0 %collective-permute-start.26 = (f32[128,1024]{1,0:T(8,128)}, f32[128,1024]{1,0:T(8,128)S(1)}, u32[]{:S(2)}, u32[]{:S(2)}) collective-permute-start(f32[128,1024]{1,0:T(8,128)} %get-tuple-element.163), channel_id=1, source_target_pairs={{0,4},{4,8},{8,12},{1,5},{5,9},{9,13},{2,6},{6,10},{10,14},{3,7},{... | collective-permute-start | bytes 1572872 | tf_op jit(solution)/shard_map/ppermute | solution.py:129
  220.5 7.0 %conditional.1 = (f32[1024,128]{1,0:T(8,128)}) conditional(s32[]{:T(128)} %clamp.3, (bf16[512,1536]{1,0:T(8,128)(2,1)}, bf16[512,1664]{1,0:T(8,128)(2,1)}, bf16[512,1536]{1,0:T(8,128)(2,1)}, bf16[512,1664]{1,0:T(8,128)(2,1)}, bf16[512,1536]{1,0:T(8,128)(2,1)}, /*index=5*/bf16[512,1664]{1,0:T(8,128)(2,1)}, ...), branch_computations={%region_0.1_spmd, %region_1.2_spmd, %region_2.3_spmd, %region_3.4_... | conditional | flops 537395200 | bytes 27263068 | solution.py:203
  227.5 3.1 %collective-permute-done.29.refs_5_ = f32[128,1024]{1,0:T(8,128)S(1)} collective-permute-done((f32[128,1024]{1,0:T(8,128)}, f32[128,1024]{1,0:T(8,128)S(1)}, u32[]{:S(2)}, u32[]{:S(2)}) %collective-permute-start.29) | collective-permute-done | bytes 524320 | tf_op jit(solution)/shard_map/ppermute | solution.py:129
  (121 shorter events, 54.4 us)
Async XLA Ops:
  5.9 15.3 %collective-permute-start = (bf16[128,1536]{1,0:T(8,128)(2,1)S(1)}, bf16[128,1536]{1,0:T(8,128)(2,1)}, u32[]{:S(2)}, u32[]{:S(2)}) collective-permute-start(bf16[128,1536]{1,0:T(8,128)(2,1)S(1)} %get-tuple-element.127), channel_id=1, source_target_pairs={{0,4},{4,8},{8,12},{12,0},{1,5},{5,9},{9,13},{13,1},{2,6},{6,10},{... | collective-permute-start | bytes 1179656 | tf_op jit(solution)/shard_map/ppermute | solution.py:162
  9.0 29.1 %collective-permute-start.1 = (bf16[128,1536]{1,0:T(8,128)(2,1)S(1)}, bf16[128,1536]{1,0:T(8,128)(2,1)}, u32[]{:S(2)}, u32[]{:S(2)}) collective-permute-start(bf16[128,1536]{1,0:T(8,128)(2,1)S(1)} %get-tuple-element.128), channel_id=1, source_target_pairs={{0,8},{4,12},{8,0},{12,4},{1,9},{5,13},{9,1},{13,5},{2,10},{6,14},... | collective-permute-start | bytes 1179656 | tf_op jit(solution)/shard_map/ppermute | solution.py:162
  11.6 27.5 %collective-permute-start.2 = (bf16[128,1536]{1,0:T(8,128)(2,1)S(1)}, bf16[128,1536]{1,0:T(8,128)(2,1)}, u32[]{:S(2)}, u32[]{:S(2)}) collective-permute-start(bf16[128,1536]{1,0:T(8,128)(2,1)S(1)} %get-tuple-element.129), channel_id=1, source_target_pairs={{0,12},{4,0},{8,4},{12,8},{1,13},{5,1},{9,5},{13,9},{2,14},{6,2},{... | collective-permute-start | bytes 1179656 | tf_op jit(solution)/shard_map/ppermute | solution.py:162
  18.2 43.1 %collective-permute-start.3 = (bf16[128,1664]{1,0:T(8,128)(2,1)S(1)}, bf16[128,1664]{1,0:T(8,128)(2,1)}, u32[]{:S(2)}, u32[]{:S(2)}) collective-permute-start(bf16[128,1664]{1,0:T(8,128)(2,1)S(1)} %get-tuple-element.132), channel_id=1, source_target_pairs={{0,4},{4,8},{8,12},{12,0},{1,5},{5,9},{9,13},{13,1},{2,6},{6,10},{... | collective-permute-start | bytes 1277960 | tf_op jit(solution)/shard_map/ppermute | solution.py:162
  40.2 83.0 %copy-start.16 = (bf16[4,128,1536]{2,1,0:T(8,128)(2,1)}, bf16[4,128,1536]{2,1,0:T(8,128)(2,1)S(1)}, u32[]{:S(2)}) copy-start(bf16[4,128,1536]{2,1,0:T(8,128)(2,1)S(1)} %bitcast_dynamic-update-slice_fusion.4) | copy-start | bytes 4718596
  40.2 50.8 %collective-permute-start.7 = (bf16[512,1536]{1,0:T(8,128)(2,1)S(1)}, bf16[512,1536]{1,0:T(8,128)(2,1)S(1)}, u32[]{:S(2)}, u32[]{:S(2)}) collective-permute-start(bf16[512,1536]{1,0:T(8,128)(2,1)S(1)} %bitcast.49), channel_id=1, source_target_pairs={{0,1},{1,0},{2,3},{3,2},{4,5},{5,4},{6,7},{7,6},{8,9},{9,8},{10,11... | collective-permute-start | bytes 4718600 | tf_op jit(solution)/shard_map/ppermute | solution.py:166
  40.2 50.7 %collective-permute-start.6 = (bf16[512,1536]{1,0:T(8,128)(2,1)S(1)}, bf16[512,1536]{1,0:T(8,128)(2,1)S(1)}, u32[]{:S(2)}, u32[]{:S(2)}) collective-permute-start(bf16[512,1536]{1,0:T(8,128)(2,1)S(1)} %bitcast.50), channel_id=1, source_target_pairs={{0,2},{2,0},{1,3},{3,1},{4,6},{6,4},{5,7},{7,5},{8,10},{10,8},{9,1... | collective-permute-start | bytes 4718600 | tf_op jit(solution)/shard_map/ppermute | solution.py:165
  43.2 50.0 %copy-start.5 = (bf16[128,1024]{1,0:T(8,128)(2,1)S(1)}, bf16[128,1024]{1,0:T(8,128)(2,1)}, u32[]{:S(2)}) copy-start(bf16[128,1024]{1,0:T(8,128)(2,1)} %copy-done.4) | copy-start | bytes 786436
  43.9 46.3 %collective-permute-start.5 = (bf16[128,1664]{1,0:T(8,128)(2,1)S(1)}, bf16[128,1664]{1,0:T(8,128)(2,1)S(1)}, u32[]{:S(2)}, u32[]{:S(2)}) collective-permute-start(bf16[128,1664]{1,0:T(8,128)(2,1)S(1)} %get-tuple-element.137), channel_id=1, source_target_pairs={{0,12},{4,0},{8,4},{12,8},{1,13},{5,1},{9,5},{13,9},{2,14},{6,2},{... | collective-permute-start | bytes 1277960 | tf_op jit(solution)/shard_map/ppermute | solution.py:162
  53.9 35.5 %collective-permute-start.4 = (bf16[128,1664]{1,0:T(8,128)(2,1)S(1)}, bf16[128,1664]{1,0:T(8,128)(2,1)S(1)}, u32[]{:S(2)}, u32[]{:S(2)}) collective-permute-start(bf16[128,1664]{1,0:T(8,128)(2,1)S(1)} %get-tuple-element.136), channel_id=1, source_target_pairs={{0,8},{4,12},{8,0},{12,4},{1,9},{5,13},{9,1},{13,5},{2,10},{6,14},... | collective-permute-start | bytes 1277960 | tf_op jit(solution)/shard_map/ppermute | solution.py:162
  91.0 26.7 %collective-permute-start.11 = (bf16[512,1664]{1,0:T(8,128)(2,1)}, bf16[512,1664]{1,0:T(8,128)(2,1)S(1)}, u32[]{:S(2)}, u32[]{:S(2)}) collective-permute-start(bf16[512,1664]{1,0:T(8,128)(2,1)} %bitcast.11), channel_id=1, source_target_pairs={{0,1},{1,0},{2,3},{3,2},{4,5},{5,4},{6,7},{7,6},{8,9},{9,8},{10,11... | collective-permute-start | bytes 5111816 | tf_op jit(solution)/shard_map/ppermute | solution.py:166
  91.0 11.1 %collective-permute-start.8 = (bf16[128,1024]{1,0:T(8,128)(2,1)S(1)}, bf16[128,1024]{1,0:T(8,128)(2,1)S(1)}, u32[]{:S(2)}, u32[]{:S(2)}) collective-permute-start(bf16[128,1024]{1,0:T(8,128)(2,1)S(1)} %copy-done.7), channel_id=1, source_target_pairs={{0,4},{4,8},{8,12},{12,0},{1,5},{5,9},{9,13},{13,1},{2,6},{6,10},{... | collective-permute-start | bytes 786440 | tf_op jit(solution)/shard_map/ppermute | solution.py:162
  93.2 19.7 %collective-permute-start.9 = (bf16[128,1024]{1,0:T(8,128)(2,1)S(1)}, bf16[128,1024]{1,0:T(8,128)(2,1)S(1)}, u32[]{:S(2)}, u32[]{:S(2)}) collective-permute-start(bf16[128,1024]{1,0:T(8,128)(2,1)S(1)} %copy-done.5), channel_id=1, source_target_pairs={{0,8},{4,12},{8,0},{12,4},{1,9},{5,13},{9,1},{13,5},{2,10},{6,14},... | collective-permute-start | bytes 786440 | tf_op jit(solution)/shard_map/ppermute | solution.py:162
  96.2 50.0 %collective-permute-start.19 = (bf16[512,1664]{1,0:T(8,128)(2,1)}, bf16[512,1664]{1,0:T(8,128)(2,1)}, u32[]{:S(2)}, u32[]{:S(2)}) collective-permute-start(bf16[512,1664]{1,0:T(8,128)(2,1)} %bitcast.11), channel_id=1, source_target_pairs={{0,2},{2,0},{1,3},{3,1},{4,6},{6,4},{5,7},{7,5},{8,10},{10,8},{9,1... | collective-permute-start | bytes 5111816 | tf_op jit(solution)/shard_map/ppermute | solution.py:165
  97.8 15.9 %collective-permute-start.10 = (bf16[128,1024]{1,0:T(8,128)(2,1)S(1)}, bf16[128,1024]{1,0:T(8,128)(2,1)S(1)}, u32[]{:S(2)}, u32[]{:S(2)}) collective-permute-start(bf16[128,1024]{1,0:T(8,128)(2,1)S(1)} %copy-done.3), channel_id=1, source_target_pairs={{0,12},{4,0},{8,4},{12,8},{1,13},{5,1},{9,5},{13,9},{2,14},{6,2},{... | collective-permute-start | bytes 786440 | tf_op jit(solution)/shard_map/ppermute | solution.py:162
  114.4 6.4 %collective-permute-start.12 = (bf16[512,1024]{1,0:T(8,128)(2,1)}, bf16[512,1024]{1,0:T(8,128)(2,1)S(1)}, u32[]{:S(2)}, u32[]{:S(2)}) collective-permute-start(bf16[512,1024]{1,0:T(8,128)(2,1)} %bitcast.16), channel_id=1, source_target_pairs={{0,1},{1,0},{2,3},{3,2},{4,5},{5,4},{6,7},{7,6},{8,9},{9,8},{10,11... | collective-permute-start | bytes 3145736 | tf_op jit(solution)/shard_map/ppermute | solution.py:166
  125.1 9.4 %collective-permute-start.16 = (f32[128,1024]{1,0:T(8,128)}, f32[128,1024]{1,0:T(8,128)S(1)}, u32[]{:S(2)}, u32[]{:S(2)}) collective-permute-start(f32[128,1024]{1,0:T(8,128)} %get-tuple-element.173), channel_id=1, source_target_pairs={{12,8},{13,9},{14,10},{15,11},{28,24},{29,25},{30,26},{31,27}} | collective-permute-start | bytes 1572872 | tf_op jit(solution)/shard_map/ppermute | solution.py:129
  125.7 19.1 %collective-permute-start.13 = (f32[128,1024]{1,0:T(8,128)S(1)}, f32[128,1024]{1,0:T(8,128)}, u32[]{:S(2)}, u32[]{:S(2)}) collective-permute-start(f32[128,1024]{1,0:T(8,128)S(1)} %get-tuple-element.174), channel_id=1, source_target_pairs={{0,4},{1,5},{2,6},{3,7},{16,20},{17,21},{18,22},{19,23}} | collective-permute-start | bytes 1572872 | tf_op jit(solution)/shard_map/ppermute | solution.py:129
  134.0 25.5 %collective-permute-start.20 = (bf16[512,1024]{1,0:T(8,128)(2,1)}, bf16[512,1024]{1,0:T(8,128)(2,1)}, u32[]{:S(2)}, u32[]{:S(2)}) collective-permute-start(bf16[512,1024]{1,0:T(8,128)(2,1)} %bitcast.16), channel_id=1, source_target_pairs={{0,2},{2,0},{1,3},{3,1},{4,6},{6,4},{5,7},{7,5},{8,10},{10,8},{9,1... | collective-permute-start | bytes 3145736 | tf_op jit(solution)/shard_map/ppermute | solution.py:165
  146.2 22.3 %collective-permute-start.22 = (bf16[512,1664]{1,0:T(8,128)(2,1)}, bf16[512,1664]{1,0:T(8,128)(2,1)S(1)}, u32[]{:S(2)}, u32[]{:S(2)}) collective-permute-start(bf16[512,1664]{1,0:T(8,128)(2,1)} %collective-permute-done.19), channel_id=1, source_target_pairs={{0,1},{1,0},{2,3},{3,2},{4,5},{5,4},{6,7},{7,6},{8,9},{9,8},{10,11... | collective-permute-start | bytes 5111816 | tf_op jit(solution)/shard_map/ppermute | solution.py:179
  146.3 25.3 %collective-permute-start.21 = (bf16[512,1536]{1,0:T(8,128)(2,1)S(1)}, bf16[512,1536]{1,0:T(8,128)(2,1)S(1)}, u32[]{:S(2)}, u32[]{:S(2)}) collective-permute-start(bf16[512,1536]{1,0:T(8,128)(2,1)S(1)} %copy-done.21), channel_id=1, source_target_pairs={{0,1},{1,0},{2,3},{3,2},{4,5},{5,4},{6,7},{7,6},{8,9},{9,8},{10,11... | collective-permute-start | bytes 4718600 | tf_op jit(solution)/shard_map/ppermute | solution.py:170
  146.8 32.5 %collective-permute-start.17 = (f32[128,1024]{1,0:T(8,128)S(1)}, f32[128,1024]{1,0:T(8,128)}, u32[]{:S(2)}, u32[]{:S(2)}) collective-permute-start(f32[128,1024]{1,0:T(8,128)S(1)} %get-tuple-element.171), channel_id=1, source_target_pairs={{12,8},{8,4},{13,9},{9,5},{14,10},{10,6},{15,11},{11,7},{28,24},{2... | collective-permute-start | bytes 1572872 | tf_op jit(solution)/shard_map/ppermute | solution.py:129
  148.3 31.1 %collective-permute-start.14 = (f32[128,1024]{1,0:T(8,128)S(1)}, f32[128,1024]{1,0:T(8,128)}, u32[]{:S(2)}, u32[]{:S(2)}) collective-permute-start(f32[128,1024]{1,0:T(8,128)S(1)} %get-tuple-element.172), channel_id=1, source_target_pairs={{0,4},{4,8},{1,5},{5,9},{2,6},{6,10},{3,7},{7,11},{16,20},{20,24},... | collective-permute-start | bytes 1572872 | tf_op jit(solution)/shard_map/ppermute | solution.py:129
  159.5 6.3 %collective-permute-start.23 = (bf16[512,1024]{1,0:T(8,128)(2,1)}, bf16[512,1024]{1,0:T(8,128)(2,1)S(1)}, u32[]{:S(2)}, u32[]{:S(2)}) collective-permute-start(bf16[512,1024]{1,0:T(8,128)(2,1)} %collective-permute-done.20), channel_id=1, source_target_pairs={{0,1},{1,0},{2,3},{3,2},{4,5},{5,4},{6,7},{7,6},{8,9},{9,8},{10,11... | collective-permute-start | bytes 3145736 | tf_op jit(solution)/shard_map/ppermute | solution.py:179
  174.1 12.6 %collective-permute-start.27 = (f32[128,1024]{1,0:T(8,128)}, f32[128,1024]{1,0:T(8,128)}, u32[]{:S(2)}, u32[]{:S(2)}) collective-permute-start(f32[128,1024]{1,0:T(8,128)} %get-tuple-element.166), channel_id=1, source_target_pairs={{12,8},{13,9},{14,10},{15,11},{28,24},{29,25},{30,26},{31,27}} | collective-permute-start | bytes 1572872 | tf_op jit(solution)/shard_map/ppermute | solution.py:129
  175.8 15.3 %collective-permute-start.24 = (f32[128,1024]{1,0:T(8,128)}, f32[128,1024]{1,0:T(8,128)}, u32[]{:S(2)}, u32[]{:S(2)}) collective-permute-start(f32[128,1024]{1,0:T(8,128)} %get-tuple-element.167), channel_id=1, source_target_pairs={{0,4},{1,5},{2,6},{3,7},{16,20},{17,21},{18,22},{19,23}} | collective-permute-start | bytes 1572872 | tf_op jit(solution)/shard_map/ppermute | solution.py:129
  180.9 17.3 %collective-permute-start.18 = (f32[128,1024]{1,0:T(8,128)S(1)}, f32[128,1024]{1,0:T(8,128)S(1)}, u32[]{:S(2)}, u32[]{:S(2)}) collective-permute-start(f32[128,1024]{1,0:T(8,128)S(1)} %get-tuple-element.168), channel_id=1, source_target_pairs={{12,8},{8,4},{4,0},{13,9},{9,5},{5,1},{14,10},{10,6},{6,2},{15,11}... | collective-permute-start | bytes 1572872 | tf_op jit(solution)/shard_map/ppermute | solution.py:129
  182.2 20.0 %collective-permute-start.15 = (f32[128,1024]{1,0:T(8,128)S(1)}, f32[128,1024]{1,0:T(8,128)S(1)}, u32[]{:S(2)}, u32[]{:S(2)}) collective-permute-start(f32[128,1024]{1,0:T(8,128)S(1)} %get-tuple-element.170), channel_id=1, source_target_pairs={{0,4},{4,8},{8,12},{1,5},{5,9},{9,13},{2,6},{6,10},{10,14},{3,7},{... | collective-permute-start | bytes 1572872 | tf_op jit(solution)/shard_map/ppermute | solution.py:129
  192.4 9.8 %collective-permute-start.28 = (f32[128,1024]{1,0:T(8,128)S(1)}, f32[128,1024]{1,0:T(8,128)S(1)}, u32[]{:S(2)}, u32[]{:S(2)}) collective-permute-start(f32[128,1024]{1,0:T(8,128)S(1)} %get-tuple-element.164), channel_id=1, source_target_pairs={{12,8},{8,4},{13,9},{9,5},{14,10},{10,6},{15,11},{11,7},{28,24},{2... | collective-permute-start | bytes 1572872 | tf_op jit(solution)/shard_map/ppermute | solution.py:129
  193.1 19.9 %collective-permute-start.25 = (f32[128,1024]{1,0:T(8,128)S(1)}, f32[128,1024]{1,0:T(8,128)S(1)}, u32[]{:S(2)}, u32[]{:S(2)}) collective-permute-start(f32[128,1024]{1,0:T(8,128)S(1)} %get-tuple-element.165), channel_id=1, source_target_pairs={{0,4},{4,8},{1,5},{5,9},{2,6},{6,10},{3,7},{7,11},{16,20},{20,24},... | collective-permute-start | bytes 1572872 | tf_op jit(solution)/shard_map/ppermute | solution.py:129
  214.2 16.4 %collective-permute-start.29 = (f32[128,1024]{1,0:T(8,128)}, f32[128,1024]{1,0:T(8,128)S(1)}, u32[]{:S(2)}, u32[]{:S(2)}) collective-permute-start(f32[128,1024]{1,0:T(8,128)} %get-tuple-element.161), channel_id=1, source_target_pairs={{12,8},{8,4},{4,0},{13,9},{9,5},{5,1},{14,10},{10,6},{6,2},{15,11}... | collective-permute-start | bytes 1572872 | tf_op jit(solution)/shard_map/ppermute | solution.py:129
  215.5 16.4 %collective-permute-start.26 = (f32[128,1024]{1,0:T(8,128)}, f32[128,1024]{1,0:T(8,128)S(1)}, u32[]{:S(2)}, u32[]{:S(2)}) collective-permute-start(f32[128,1024]{1,0:T(8,128)} %get-tuple-element.163), channel_id=1, source_target_pairs={{0,4},{4,8},{8,12},{1,5},{5,9},{9,13},{2,6},{6,10},{10,14},{3,7},{... | collective-permute-start | bytes 1572872 | tf_op jit(solution)/shard_map/ppermute | solution.py:129
  (24 other events, 161.8 us)

commit v13 on v11

--- a/solution.py
+++ b/solution.py
@@ -12,7 +12,7 @@
 AXES = ("groups", "z", "y", "c")
 BLOCK = 16
 LANES = 128
-WINDOW = 4
+WINDOW = 6
 SWAP = [(0, 1), (1, 0)]
 
 

time: 221 us -> 245 us (1.11)
  waiting for transfers between devices: 102 us -> 79.8 us
  starting transfers between devices: 71.3 us -> 92.3 us
  matrix products: 17.9 us -> 34.5 us
  local copies, waits for them, and re-layouts: 12.6 us -> 20.7 us
    ppermute x3, waiting for transfers between devices: 25.3 us -> 6.01 us  [on_device(): across = lax.ppermute(stack, 'y', SWAP)]
    dot_general x12, matrix products: 11 us -> 27.1 us  [nt_dot(): lax.dot_general(a, b, (((1,), (1,)), ((), ())), preferred_element_type=jn...]
    ppermute x12, starting transfers between devices: 34.4 us -> 47.4 us  [chain(): got = lax.ppermute(sent, 'z', pairs)]
    ppermute x9, waiting for transfers between devices: 58.2 us -> 47.5 us  [on_device(): lax.ppermute(piece, 'z', [(s, (s + shift) % planes) for s in range(planes)])]
    ppermute x12, waiting for transfers between devices: 18.1 us -> 26.2 us  [chain(): got = lax.ppermute(sent, 'z', pairs)]
    ppermute x9, starting transfers between devices: 32.7 us -> 39.9 us  [on_device(): lax.ppermute(piece, 'z', [(s, (s + shift) % planes) for s in range(planes)])]
    dynamic_update_slice x12, local copies, waits for them, and re-layouts: 4.37 us -> 11.5 us  [stacked(): lax.dynamic_update_slice(stack, parts[shift][None], ((z - shift) % planes...]
    unnamed x54 -> x44, local copies, waits for them, and re-layouts: 7.91 us -> 6.47 us
  transfers between devices with their start and end apart: 30 -> 30, of which waited for: 12 -> 12; matrix products, arithmetic and copies ran while one was open for 13% -> 22% of each run, Pallas kernels for 1% -> 1%
where the time goes in v13:
time: 245 us; the launch traced here: 244 us
  starting transfers between devices  92.3 us (38%)
  waiting for transfers between devices  79.8 us (33%)
  matrix products  34.5 us (14%)
  local copies, waits for them, and re-layouts  20.7 us (8%)
  other arithmetic  9.28 us (4%)
  Pallas kernels  6.66 us (3%)
    ppermute x9, waiting for transfers between devices, on_device(): lax.ppermute(piece, 'z', [(s, (s + shift) % planes) for s in range(planes)])  47.5 us
    ppermute x12, starting transfers between devices, chain(): got = lax.ppermute(sent, 'z', pairs)  47.4 us
    ppermute x9, starting transfers between devices, on_device(): lax.ppermute(piece, 'z', [(s, (s + shift) % planes) for s in range(planes)])  39.9 us
    dot_general x12, matrix products, nt_dot(): lax.dot_general(a, b, (((1,), (1,)), ((), ())), preferred_element_type=jn...  27.1 us
    ppermute x12, waiting for transfers between devices, chain(): got = lax.ppermute(sent, 'z', pairs)  26.2 us
    dynamic_update_slice x12, local copies, waits for them, and re-layouts, stacked(): lax.dynamic_update_slice(stack, parts[shift][None], ((z - shift) % planes...  11.5 us
    add x4, other arithmetic, chain(): sent = sent + got  8.05 us
    dot_general x4, matrix products, tn_dot(): lax.dot_general(a, b, (((0,), (0,)), ((), ())), preferred_element_type=jn...  7.37 us
  transfers between devices with their start and end apart: 30, of which 12 were waited for; matrix products, arithmetic and copies ran while one was open for 22% of the time, Pallas kernels for 1%

profile of v13, /device:TPU:0, one launch (start us, length us, event | category | flops | bytes accessed | tf_op | source)
XLA Modules:
  0.0 244.3 jit_solution(9470682959526870605)
XLA Ops:
  3.6 2.3 unfold.2
  5.9 3.1 %collective-permute-start = (bf16[128,1536]{1,0:T(8,128)(2,1)S(1)}, bf16[128,1536]{1,0:T(8,128)(2,1)}, u32[]{:S(2)}, u32[]{:S(2)}) collective-permute-start(bf16[128,1536]{1,0:T(8,128)(2,1)S(1)} %get-tuple-element.122), channel_id=1, source_target_pairs={{0,4},{4,8},{8,12},{12,0},{1,5},{5,9},{9,13},{13,1},{2,6},{6,10},{... | collective-permute-start | bytes 1179656 | tf_op jit(solution)/shard_map/ppermute | solution.py:162
  9.0 2.6 %collective-permute-start.1 = (bf16[128,1536]{1,0:T(8,128)(2,1)S(1)}, bf16[128,1536]{1,0:T(8,128)(2,1)}, u32[]{:S(2)}, u32[]{:S(2)}) collective-permute-start(bf16[128,1536]{1,0:T(8,128)(2,1)S(1)} %get-tuple-element.123), channel_id=1, source_target_pairs={{0,8},{4,12},{8,0},{12,4},{1,9},{5,13},{9,1},{13,5},{2,10},{6,14},... | collective-permute-start | bytes 1179656 | tf_op jit(solution)/shard_map/ppermute | solution.py:162
  13.0 3.1 %unfold.3 = (bf16[128,1664]{1,0:T(8,128)(2,1)S(1)}, bf16[128,1664]{1,0:T(8,128)(2,1)S(1)}, bf16[128,1664]{1,0:T(8,128)(2,1)S(1)}, bf16[128,1664]{1,0:T(8,128)(2,...) custom-call(s32[1]{0:T(128)} %bitcast.1.z_ref, ...), custom_call_target="tpu_custom_call" | custom-call | bytes 6946816 | tf_op jit(solution)/shard_map/unfold/pallas_call | solution.py:67
  23.3 2.8 %collective-permute-start.5 = (bf16[128,1664]{1,0:T(8,128)(2,1)S(1)}, bf16[128,1664]{1,0:T(8,128)(2,1)S(1)}, u32[]{:S(2)}, u32[]{:S(2)}) collective-permute-start(bf16[128,1664]{1,0:T(8,128)(2,1)S(1)} %get-tuple-element.129), channel_id=1, source_target_pairs={{0,12},{4,0},{8,4},{12,8},{1,13},{5,1},{9,5},{13,9},{2,14},{6,2},{... | collective-permute-start | bytes 1277960 | tf_op jit(solution)/shard_map/ppermute | solution.py:162
  27.9 10.2 %collective-permute-done.1 = bf16[128,1536]{1,0:T(8,128)(2,1)} collective-permute-done((bf16[128,1536]{1,0:T(8,128)(2,1)S(1)}, bf16[128,1536]{1,0:T(8,128)(2,1)}, u32[]{:S(2)}, u32[]{:S(2)}) %collective-permute-start.1) | collective-permute-done | bytes 393248 | tf_op jit(solution)/shard_map/ppermute | solution.py:162
  43.5 3.7 %collective-permute-done.3 = bf16[128,1664]{1,0:T(8,128)(2,1)} collective-permute-done((bf16[128,1664]{1,0:T(8,128)(2,1)S(1)}, bf16[128,1664]{1,0:T(8,128)(2,1)}, u32[]{:S(2)}, u32[]{:S(2)}) %collective-permute-start.3) | collective-permute-done | bytes 426016 | tf_op jit(solution)/shard_map/ppermute | solution.py:162
  49.1 24.1 %collective-permute-done.4 = bf16[128,1664]{1,0:T(8,128)(2,1)} collective-permute-done((bf16[128,1664]{1,0:T(8,128)(2,1)S(1)}, bf16[128,1664]{1,0:T(8,128)(2,1)}, u32[]{:S(2)}, u32[]{:S(2)}) %collective-permute-start.4) | collective-permute-done | bytes 426016 | tf_op jit(solution)/shard_map/ppermute | solution.py:162
  79.3 25.4 %collective-permute-start.8 = (bf16[128,1024]{1,0:T(8,128)(2,1)S(1)}, bf16[128,1024]{1,0:T(8,128)(2,1)S(1)}, u32[]{:S(2)}, u32[]{:S(2)}) collective-permute-start(bf16[128,1024]{1,0:T(8,128)(2,1)S(1)} %copy-done.7), channel_id=1, source_target_pairs={{0,4},{4,8},{8,12},{12,0},{1,5},{5,9},{9,13},{13,1},{2,6},{6,10},{... | collective-permute-start | bytes 786440 | tf_op jit(solution)/shard_map/ppermute | solution.py:162
  104.6 3.7 %collective-permute-start.9 = (bf16[128,1024]{1,0:T(8,128)(2,1)S(1)}, bf16[128,1024]{1,0:T(8,128)(2,1)S(1)}, u32[]{:S(2)}, u32[]{:S(2)}) collective-permute-start(bf16[128,1024]{1,0:T(8,128)(2,1)S(1)} %copy-done.5), channel_id=1, source_target_pairs={{0,8},{4,12},{8,0},{12,4},{1,9},{5,13},{9,1},{13,5},{2,10},{6,14},... | collective-permute-start | bytes 786440 | tf_op jit(solution)/shard_map/ppermute | solution.py:162
  108.3 2.9 %fusion.54 = f32[512,512]{1,0:T(8,128)S(1)} fusion(bf16[512,1664]{1,0:T(8,128)(2,1)} %bitcast.11), kind=kOutput, calls=%fused_computation.102 | convolution fusion | flops 805306368 | bytes 2621440 | tf_op jit(solution)/shard_map/dot_general | solution.py:26
  111.3 4.1 %collective-permute-done.19 = bf16[512,1664]{1,0:T(8,128)(2,1)} collective-permute-done((bf16[512,1664]{1,0:T(8,128)(2,1)}, bf16[512,1664]{1,0:T(8,128)(2,1)}, u32[]{:S(2)}, u32[]{:S(2)}) %collective-permute-start.19) | collective-permute-done | bytes 1703968 | tf_op jit(solution)/shard_map/ppermute | solution.py:165
  115.5 9.5 %collective-permute-done.9 = bf16[128,1024]{1,0:T(8,128)(2,1)S(1)} collective-permute-done((bf16[128,1024]{1,0:T(8,128)(2,1)S(1)}, bf16[128,1024]{1,0:T(8,128)(2,1)S(1)}, u32[]{:S(2)}, u32[]{:S(2)}) %collective-permute-start.9) | collective-permute-done | bytes 262176 | tf_op jit(solution)/shard_map/ppermute | solution.py:162
  125.1 3.3 %fusion.45 = f32[512,512]{1,0:T(8,128)S(1)} fusion(bf16[512,1664]{1,0:T(8,128)(2,1)S(1)} %collective-permute-done.11, bf16[512,1664]{1,0:T(8,128)(2,1)} %bitcast.11), kind=kOutput, calls=%fused_computation.89 | convolution fusion | flops 805306368 | bytes 4194304 | tf_op jit(solution)/shard_map/dot_general | solution.py:26
  130.8 2.9 %fusion.47 = f32[512,512]{1,0:T(8,128)S(1)} fusion(f32[512,512]{1,0:T(8,128)S(1)} %fusion.78, f32[512,512]{1,0:T(8,128)S(1)} %fusion.54, bf16[512,1536]{1,0:T(8,128)(2,1)} %bitcast.6), kind=kOutput, calls=%fused_computation.95 | convolution fusion | flops 805830656 | bytes 4718592 | tf_op jit(solution)/shard_map/dot_general | solution.py:26
  134.7 2.9 %fusion.48 = f32[512,512]{1,0:T(8,128)S(1)} fusion(f32[512,512]{1,0:T(8,128)S(1)} %fusion.79, f32[512,512]{1,0:T(8,128)S(1)} %fusion.45, bf16[512,1536]{1,0:T(8,128)(2,1)} %bitcast.6, bf16[512,1536]{1,0:T(8,128)(2,1)} %collective-permute-done.7), kind=kOutput, calls=%fused_computation.96 | convolution fusion | flops 805830656 | bytes 6291456 | tf_op jit(solution)/shard_map/dot_general | solution.py:26
  138.4 18.0 %collective-permute-start.13 = (f32[128,1024]{1,0:T(8,128)S(1)}, f32[128,1024]{1,0:T(8,128)S(1)}, u32[]{:S(2)}, u32[]{:S(2)}) collective-permute-start(f32[128,1024]{1,0:T(8,128)S(1)} %get-tuple-element.164), channel_id=1, source_target_pairs={{0,4},{1,5},{2,6},{3,7},{16,20},{17,21},{18,22},{19,23}} | collective-permute-start | bytes 1572872 | tf_op jit(solution)/shard_map/ppermute | solution.py:128
  156.5 2.9 %fusion.43 = f32[512,512]{1,0:T(8,128)S(1)} fusion(bf16[512,1664]{1,0:T(8,128)(2,1)} %collective-permute-done.19, bf16[512,1664]{1,0:T(8,128)(2,1)} %bitcast.11), kind=kOutput, calls=%fused_computation.87 | convolution fusion | flops 805306368 | bytes 4194304 | tf_op jit(solution)/shard_map/dot_general | solution.py:26
  159.4 8.3 %collective-permute-done.13 = f32[128,1024]{1,0:T(8,128)S(1)} collective-permute-done((f32[128,1024]{1,0:T(8,128)S(1)}, f32[128,1024]{1,0:T(8,128)S(1)}, u32[]{:S(2)}, u32[]{:S(2)}) %collective-permute-start.13) | collective-permute-done | bytes 524320 | tf_op jit(solution)/shard_map/ppermute | solution.py:128
  168.5 2.9 %fusion.49 = f32[512,512]{1,0:T(8,128)S(1)} fusion(f32[512,512]{1,0:T(8,128)S(1)} %fusion.80, f32[512,512]{1,0:T(8,128)S(1)} %fusion.43, bf16[512,1536]{1,0:T(8,128)(2,1)} %bitcast.6, bf16[512,1536]{1,0:T(8,128)(2,1)} %collective-permute-done.6), kind=kOutput, calls=%fused_computation.97 | convolution fusion | flops 805830656 | bytes 6291456 | tf_op jit(solution)/shard_map/dot_general | solution.py:26
  171.4 3.4 %fusion.41 = f32[512,512]{1,0:T(8,128)S(1)} fusion(bf16[512,1664]{1,0:T(8,128)(2,1)S(1)} %collective-permute-done.22, bf16[512,1664]{1,0:T(8,128)(2,1)} %bitcast.11), kind=kOutput, calls=%fused_computation.85 | convolution fusion | flops 805306368 | bytes 4194304 | tf_op jit(solution)/shard_map/dot_general | solution.py:26
  175.8 3.0 %fusion.50 = f32[512,512]{1,0:T(8,128)S(1)} fusion(f32[512,512]{1,0:T(8,128)S(1)} %fusion.81, f32[512,512]{1,0:T(8,128)S(1)} %fusion.41, bf16[512,1536]{1,0:T(8,128)(2,1)} %bitcast.6, bf16[512,1536]{1,0:T(8,128)(2,1)S(1)} %collective-permute-done.21), kind=kOutput, calls=%fused_computation.98 | convolution fusion | flops 805830656 | bytes 6291456 | tf_op jit(solution)/shard_map/dot_general | solution.py:26
  181.6 5.2 %collective-permute-start.24 = (f32[128,1024]{1,0:T(8,128)}, f32[128,1024]{1,0:T(8,128)}, u32[]{:S(2)}, u32[]{:S(2)}) collective-permute-start(f32[128,1024]{1,0:T(8,128)} %get-tuple-element.157), channel_id=1, source_target_pairs={{0,4},{1,5},{2,6},{3,7},{16,20},{17,21},{18,22},{19,23}} | collective-permute-start | bytes 1572872 | tf_op jit(solution)/shard_map/ppermute | solution.py:128
  190.7 7.8 %collective-permute-done.24 = f32[128,1024]{1,0:T(8,128)} collective-permute-done((f32[128,1024]{1,0:T(8,128)}, f32[128,1024]{1,0:T(8,128)}, u32[]{:S(2)}, u32[]{:S(2)}) %collective-permute-start.24) | collective-permute-done | bytes 524320 | tf_op jit(solution)/shard_map/ppermute | solution.py:128
  202.1 5.0 %collective-permute-start.25 = (f32[128,1024]{1,0:T(8,128)S(1)}, f32[128,1024]{1,0:T(8,128)}, u32[]{:S(2)}, u32[]{:S(2)}) collective-permute-start(f32[128,1024]{1,0:T(8,128)S(1)} %get-tuple-element.155), channel_id=1, source_target_pairs={{0,4},{4,8},{1,5},{5,9},{2,6},{6,10},{3,7},{7,11},{16,20},{20,24},... | collective-permute-start | bytes 1572872 | tf_op jit(solution)/shard_map/ppermute | solution.py:128
  209.7 2.4 fusion.75
  213.4 5.0 %collective-permute-start.15 = (f32[128,1024]{1,0:T(8,128)}, f32[128,1024]{1,0:T(8,128)S(1)}, u32[]{:S(2)}, u32[]{:S(2)}) collective-permute-start(f32[128,1024]{1,0:T(8,128)} %get-tuple-element.160), channel_id=1, source_target_pairs={{0,4},{4,8},{8,12},{1,5},{5,9},{9,13},{2,6},{6,10},{10,14},{3,7},{... | collective-permute-start | bytes 1572872 | tf_op jit(solution)/shard_map/ppermute | solution.py:128
  218.5 2.4 collective-permute-done.25
  220.9 2.4 fusion.64
  224.5 5.2 %collective-permute-start.26 = (f32[128,1024]{1,0:T(8,128)}, f32[128,1024]{1,0:T(8,128)S(1)}, u32[]{:S(2)}, u32[]{:S(2)}) collective-permute-start(f32[128,1024]{1,0:T(8,128)} %get-tuple-element.153), channel_id=1, source_target_pairs={{0,4},{4,8},{8,12},{1,5},{5,9},{9,13},{2,6},{6,10},{10,14},{3,7},{... | collective-permute-start | bytes 1572872 | tf_op jit(solution)/shard_map/ppermute | solution.py:128
  229.7 7.4 %conditional.1 = (f32[1024,128]{1,0:T(8,128)}) conditional(s32[]{:T(128)} %clamp.3, (bf16[512,1536]{1,0:T(8,128)(2,1)}, bf16[512,1664]{1,0:T(8,128)(2,1)}, bf16[512,1536]{1,0:T(8,128)(2,1)}, bf16[512,1664]{1,0:T(8,128)(2,1)}, bf16[512,1536]{1,0:T(8,128)(2,1)}, /*index=5*/bf16[512,1664]{1,0:T(8,128)(2,1)}, ...), branch_computations={%region_0.1_spmd, %region_1.2_spmd, %region_2.3_spmd, %region_3.4_... | conditional | flops 537395200 | bytes 22020160 | solution.py:203
  239.4 3.7 %collective-permute-done.26.refs_4_ = f32[128,1024]{1,0:T(8,128)S(1)} collective-permute-done((f32[128,1024]{1,0:T(8,128)}, f32[128,1024]{1,0:T(8,128)S(1)}, u32[]{:S(2)}, u32[]{:S(2)}) %collective-permute-start.26) | collective-permute-done | bytes 524320 | tf_op jit(solution)/shard_map/ppermute | solution.py:128
  (115 shorter events, 59.1 us)
Async XLA Ops:
  5.9 17.4 %collective-permute-start = (bf16[128,1536]{1,0:T(8,128)(2,1)S(1)}, bf16[128,1536]{1,0:T(8,128)(2,1)}, u32[]{:S(2)}, u32[]{:S(2)}) collective-permute-start(bf16[128,1536]{1,0:T(8,128)(2,1)S(1)} %get-tuple-element.122), channel_id=1, source_target_pairs={{0,4},{4,8},{8,12},{12,0},{1,5},{5,9},{9,13},{13,1},{2,6},{6,10},{... | collective-permute-start | bytes 1179656 | tf_op jit(solution)/shard_map/ppermute | solution.py:162
  9.0 29.1 %collective-permute-start.1 = (bf16[128,1536]{1,0:T(8,128)(2,1)S(1)}, bf16[128,1536]{1,0:T(8,128)(2,1)}, u32[]{:S(2)}, u32[]{:S(2)}) collective-permute-start(bf16[128,1536]{1,0:T(8,128)(2,1)S(1)} %get-tuple-element.123), channel_id=1, source_target_pairs={{0,8},{4,12},{8,0},{12,4},{1,9},{5,13},{9,1},{13,5},{2,10},{6,14},... | collective-permute-start | bytes 1179656 | tf_op jit(solution)/shard_map/ppermute | solution.py:162
  11.6 28.3 %collective-permute-start.2 = (bf16[128,1536]{1,0:T(8,128)(2,1)S(1)}, bf16[128,1536]{1,0:T(8,128)(2,1)}, u32[]{:S(2)}, u32[]{:S(2)}) collective-permute-start(bf16[128,1536]{1,0:T(8,128)(2,1)S(1)} %get-tuple-element.124), channel_id=1, source_target_pairs={{0,12},{4,0},{8,4},{12,8},{1,13},{5,1},{9,5},{13,9},{2,14},{6,2},{... | collective-permute-start | bytes 1179656 | tf_op jit(solution)/shard_map/ppermute | solution.py:162
  18.1 29.1 %collective-permute-start.3 = (bf16[128,1664]{1,0:T(8,128)(2,1)S(1)}, bf16[128,1664]{1,0:T(8,128)(2,1)}, u32[]{:S(2)}, u32[]{:S(2)}) collective-permute-start(bf16[128,1664]{1,0:T(8,128)(2,1)S(1)} %get-tuple-element.127), channel_id=1, source_target_pairs={{0,4},{4,8},{8,12},{12,0},{1,5},{5,9},{9,13},{13,1},{2,6},{6,10},{... | collective-permute-start | bytes 1277960 | tf_op jit(solution)/shard_map/ppermute | solution.py:162
  18.8 54.3 %collective-permute-start.4 = (bf16[128,1664]{1,0:T(8,128)(2,1)S(1)}, bf16[128,1664]{1,0:T(8,128)(2,1)}, u32[]{:S(2)}, u32[]{:S(2)}) collective-permute-start(bf16[128,1664]{1,0:T(8,128)(2,1)S(1)} %get-tuple-element.128), channel_id=1, source_target_pairs={{0,8},{4,12},{8,0},{12,4},{1,9},{5,13},{9,1},{13,5},{2,10},{6,14},... | collective-permute-start | bytes 1277960 | tf_op jit(solution)/shard_map/ppermute | solution.py:162
  23.3 51.6 %collective-permute-start.5 = (bf16[128,1664]{1,0:T(8,128)(2,1)S(1)}, bf16[128,1664]{1,0:T(8,128)(2,1)S(1)}, u32[]{:S(2)}, u32[]{:S(2)}) collective-permute-start(bf16[128,1664]{1,0:T(8,128)(2,1)S(1)} %get-tuple-element.129), channel_id=1, source_target_pairs={{0,12},{4,0},{8,4},{12,8},{1,13},{5,1},{9,5},{13,9},{2,14},{6,2},{... | collective-permute-start | bytes 1277960 | tf_op jit(solution)/shard_map/ppermute | solution.py:162
  41.8 35.6 %collective-permute-start.7 = (bf16[512,1536]{1,0:T(8,128)(2,1)}, bf16[512,1536]{1,0:T(8,128)(2,1)}, u32[]{:S(2)}, u32[]{:S(2)}) collective-permute-start(bf16[512,1536]{1,0:T(8,128)(2,1)} %bitcast.6), channel_id=1, source_target_pairs={{0,1},{1,0},{2,3},{3,2},{4,5},{5,4},{6,7},{7,6},{8,9},{9,8},{10,11... | collective-permute-start | bytes 4718600 | tf_op jit(solution)/shard_map/ppermute | solution.py:166
  41.8 37.5 %collective-permute-start.6 = (bf16[512,1536]{1,0:T(8,128)(2,1)}, bf16[512,1536]{1,0:T(8,128)(2,1)}, u32[]{:S(2)}, u32[]{:S(2)}) collective-permute-start(bf16[512,1536]{1,0:T(8,128)(2,1)} %bitcast.6), channel_id=1, source_target_pairs={{0,2},{2,0},{1,3},{3,1},{4,6},{6,4},{5,7},{7,5},{8,10},{10,8},{9,1... | collective-permute-start | bytes 4718600 | tf_op jit(solution)/shard_map/ppermute | solution.py:165
  49.0 55.6 %copy-start.5 = (bf16[128,1024]{1,0:T(8,128)(2,1)S(1)}, bf16[128,1024]{1,0:T(8,128)(2,1)}, u32[]{:S(2)}) copy-start(bf16[128,1024]{1,0:T(8,128)(2,1)} %copy-done.4) | copy-start | bytes 786436
  75.7 39.7 %collective-permute-start.19 = (bf16[512,1664]{1,0:T(8,128)(2,1)}, bf16[512,1664]{1,0:T(8,128)(2,1)}, u32[]{:S(2)}, u32[]{:S(2)}) collective-permute-start(bf16[512,1664]{1,0:T(8,128)(2,1)} %bitcast.11), channel_id=1, source_target_pairs={{0,2},{2,0},{1,3},{3,1},{4,6},{6,4},{5,7},{7,5},{8,10},{10,8},{9,1... | collective-permute-start | bytes 5111816 | tf_op jit(solution)/shard_map/ppermute | solution.py:165
  77.2 47.9 %collective-permute-start.11 = (bf16[512,1664]{1,0:T(8,128)(2,1)}, bf16[512,1664]{1,0:T(8,128)(2,1)S(1)}, u32[]{:S(2)}, u32[]{:S(2)}) collective-permute-start(bf16[512,1664]{1,0:T(8,128)(2,1)} %bitcast.11), channel_id=1, source_target_pairs={{0,1},{1,0},{2,3},{3,2},{4,5},{5,4},{6,7},{7,6},{8,9},{9,8},{10,11... | collective-permute-start | bytes 5111816 | tf_op jit(solution)/shard_map/ppermute | solution.py:166
  79.3 36.2 %collective-permute-start.8 = (bf16[128,1024]{1,0:T(8,128)(2,1)S(1)}, bf16[128,1024]{1,0:T(8,128)(2,1)S(1)}, u32[]{:S(2)}, u32[]{:S(2)}) collective-permute-start(bf16[128,1024]{1,0:T(8,128)(2,1)S(1)} %copy-done.7), channel_id=1, source_target_pairs={{0,4},{4,8},{8,12},{12,0},{1,5},{5,9},{9,13},{13,1},{2,6},{6,10},{... | collective-permute-start | bytes 786440 | tf_op jit(solution)/shard_map/ppermute | solution.py:162
  104.6 20.3 %collective-permute-start.9 = (bf16[128,1024]{1,0:T(8,128)(2,1)S(1)}, bf16[128,1024]{1,0:T(8,128)(2,1)S(1)}, u32[]{:S(2)}, u32[]{:S(2)}) collective-permute-start(bf16[128,1024]{1,0:T(8,128)(2,1)S(1)} %copy-done.5), channel_id=1, source_target_pairs={{0,8},{4,12},{8,0},{12,4},{1,9},{5,13},{9,1},{13,5},{2,10},{6,14},... | collective-permute-start | bytes 786440 | tf_op jit(solution)/shard_map/ppermute | solution.py:162
  111.2 13.8 %collective-permute-start.10 = (bf16[128,1024]{1,0:T(8,128)(2,1)S(1)}, bf16[128,1024]{1,0:T(8,128)(2,1)S(1)}, u32[]{:S(2)}, u32[]{:S(2)}) collective-permute-start(bf16[128,1024]{1,0:T(8,128)(2,1)S(1)} %copy-done.3), channel_id=1, source_target_pairs={{0,12},{4,0},{8,4},{12,8},{1,13},{5,1},{9,5},{13,9},{2,14},{6,2},{... | collective-permute-start | bytes 786440 | tf_op jit(solution)/shard_map/ppermute | solution.py:162
  115.4 56.0 %collective-permute-start.22 = (bf16[512,1664]{1,0:T(8,128)(2,1)}, bf16[512,1664]{1,0:T(8,128)(2,1)S(1)}, u32[]{:S(2)}, u32[]{:S(2)}) collective-permute-start(bf16[512,1664]{1,0:T(8,128)(2,1)} %collective-permute-done.19), channel_id=1, source_target_pairs={{0,1},{1,0},{2,3},{3,2},{4,5},{5,4},{6,7},{7,6},{8,9},{9,8},{10,11... | collective-permute-start | bytes 5111816 | tf_op jit(solution)/shard_map/ppermute | solution.py:170
  125.0 49.8 %copy-start.14 = (bf16[4,128,1024]{2,1,0:T(8,128)(2,1)}, bf16[4,128,1024]{2,1,0:T(8,128)(2,1)S(1)}, u32[]{:S(2)}) copy-start(bf16[4,128,1024]{2,1,0:T(8,128)(2,1)S(1)} %bitcast_dynamic-update-slice_fusion.8) | copy-start | bytes 3145732
  125.0 8.7 %collective-permute-start.12 = (bf16[512,1024]{1,0:T(8,128)(2,1)S(1)}, bf16[512,1024]{1,0:T(8,128)(2,1)S(1)}, u32[]{:S(2)}, u32[]{:S(2)}) collective-permute-start(bf16[512,1024]{1,0:T(8,128)(2,1)S(1)} %bitcast.49), channel_id=1, source_target_pairs={{0,1},{1,0},{2,3},{3,2},{4,5},{5,4},{6,7},{7,6},{8,9},{9,8},{10,11... | collective-permute-start | bytes 3145736 | tf_op jit(solution)/shard_map/ppermute | solution.py:166
  128.4 30.9 %collective-permute-start.20 = (bf16[512,1024]{1,0:T(8,128)(2,1)S(1)}, bf16[512,1024]{1,0:T(8,128)(2,1)S(1)}, u32[]{:S(2)}, u32[]{:S(2)}) collective-permute-start(bf16[512,1024]{1,0:T(8,128)(2,1)S(1)} %bitcast.50), channel_id=1, source_target_pairs={{0,2},{2,0},{1,3},{3,1},{4,6},{6,4},{5,7},{7,5},{8,10},{10,8},{9,1... | collective-permute-start | bytes 3145736 | tf_op jit(solution)/shard_map/ppermute | solution.py:165
  137.7 21.7 %collective-permute-start.16 = (f32[128,1024]{1,0:T(8,128)S(1)}, f32[128,1024]{1,0:T(8,128)S(1)}, u32[]{:S(2)}, u32[]{:S(2)}) collective-permute-start(f32[128,1024]{1,0:T(8,128)S(1)} %get-tuple-element.163), channel_id=1, source_target_pairs={{12,8},{13,9},{14,10},{15,11},{28,24},{29,25},{30,26},{31,27}} | collective-permute-start | bytes 1572872 | tf_op jit(solution)/shard_map/ppermute | solution.py:128
  138.4 29.3 %collective-permute-start.13 = (f32[128,1024]{1,0:T(8,128)S(1)}, f32[128,1024]{1,0:T(8,128)S(1)}, u32[]{:S(2)}, u32[]{:S(2)}) collective-permute-start(f32[128,1024]{1,0:T(8,128)S(1)} %get-tuple-element.164), channel_id=1, source_target_pairs={{0,4},{1,5},{2,6},{3,7},{16,20},{17,21},{18,22},{19,23}} | collective-permute-start | bytes 1572872 | tf_op jit(solution)/shard_map/ppermute | solution.py:128
  156.4 19.4 %collective-permute-start.21 = (bf16[512,1536]{1,0:T(8,128)(2,1)}, bf16[512,1536]{1,0:T(8,128)(2,1)S(1)}, u32[]{:S(2)}, u32[]{:S(2)}) collective-permute-start(bf16[512,1536]{1,0:T(8,128)(2,1)} %collective-permute-done.6), channel_id=1, source_target_pairs={{0,1},{1,0},{2,3},{3,2},{4,5},{5,4},{6,7},{7,6},{8,9},{9,8},{10,11... | collective-permute-start | bytes 4718600 | tf_op jit(solution)/shard_map/ppermute | solution.py:170
  167.7 7.1 %collective-permute-start.23 = (bf16[512,1024]{1,0:T(8,128)(2,1)S(1)}, bf16[512,1024]{1,0:T(8,128)(2,1)S(1)}, u32[]{:S(2)}, u32[]{:S(2)}) collective-permute-start(bf16[512,1024]{1,0:T(8,128)(2,1)S(1)} %collective-permute-done.20), channel_id=1, source_target_pairs={{0,1},{1,0},{2,3},{3,2},{4,5},{5,4},{6,7},{7,6},{8,9},{9,8},{10,11... | collective-permute-start | bytes 3145736 | tf_op jit(solution)/shard_map/ppermute | solution.py:179
  180.1 10.6 %collective-permute-start.27 = (f32[128,1024]{1,0:T(8,128)}, f32[128,1024]{1,0:T(8,128)}, u32[]{:S(2)}, u32[]{:S(2)}) collective-permute-start(f32[128,1024]{1,0:T(8,128)} %get-tuple-element.156), channel_id=1, source_target_pairs={{12,8},{13,9},{14,10},{15,11},{28,24},{29,25},{30,26},{31,27}} | collective-permute-start | bytes 1572872 | tf_op jit(solution)/shard_map/ppermute | solution.py:128
  181.6 16.9 %collective-permute-start.24 = (f32[128,1024]{1,0:T(8,128)}, f32[128,1024]{1,0:T(8,128)}, u32[]{:S(2)}, u32[]{:S(2)}) collective-permute-start(f32[128,1024]{1,0:T(8,128)} %get-tuple-element.157), channel_id=1, source_target_pairs={{0,4},{1,5},{2,6},{3,7},{16,20},{17,21},{18,22},{19,23}} | collective-permute-start | bytes 1572872 | tf_op jit(solution)/shard_map/ppermute | solution.py:128
  187.9 19.3 %collective-permute-start.17 = (f32[128,1024]{1,0:T(8,128)}, f32[128,1024]{1,0:T(8,128)S(1)}, u32[]{:S(2)}, u32[]{:S(2)}) collective-permute-start(f32[128,1024]{1,0:T(8,128)} %get-tuple-element.161), channel_id=1, source_target_pairs={{12,8},{8,4},{13,9},{9,5},{14,10},{10,6},{15,11},{11,7},{28,24},{2... | collective-permute-start | bytes 1572872 | tf_op jit(solution)/shard_map/ppermute | solution.py:128
  188.6 21.1 %collective-permute-start.14 = (f32[128,1024]{1,0:T(8,128)}, f32[128,1024]{1,0:T(8,128)}, u32[]{:S(2)}, u32[]{:S(2)}) collective-permute-start(f32[128,1024]{1,0:T(8,128)} %get-tuple-element.162), channel_id=1, source_target_pairs={{0,4},{4,8},{1,5},{5,9},{2,6},{6,10},{3,7},{7,11},{16,20},{20,24},... | collective-permute-start | bytes 1572872 | tf_op jit(solution)/shard_map/ppermute | solution.py:128
  200.7 17.8 %collective-permute-start.28 = (f32[128,1024]{1,0:T(8,128)}, f32[128,1024]{1,0:T(8,128)}, u32[]{:S(2)}, u32[]{:S(2)}) collective-permute-start(f32[128,1024]{1,0:T(8,128)} %get-tuple-element.154), channel_id=1, source_target_pairs={{12,8},{8,4},{13,9},{9,5},{14,10},{10,6},{15,11},{11,7},{28,24},{2... | collective-permute-start | bytes 1572872 | tf_op jit(solution)/shard_map/ppermute | solution.py:128
  202.1 18.7 %collective-permute-start.25 = (f32[128,1024]{1,0:T(8,128)S(1)}, f32[128,1024]{1,0:T(8,128)}, u32[]{:S(2)}, u32[]{:S(2)}) collective-permute-start(f32[128,1024]{1,0:T(8,128)S(1)} %get-tuple-element.155), channel_id=1, source_target_pairs={{0,4},{4,8},{1,5},{5,9},{2,6},{6,10},{3,7},{7,11},{16,20},{20,24},... | collective-permute-start | bytes 1572872 | tf_op jit(solution)/shard_map/ppermute | solution.py:128
  212.1 25.0 %collective-permute-start.18 = (f32[128,1024]{1,0:T(8,128)}, f32[128,1024]{1,0:T(8,128)S(1)}, u32[]{:S(2)}, u32[]{:S(2)}) collective-permute-start(f32[128,1024]{1,0:T(8,128)} %get-tuple-element.158), channel_id=1, source_target_pairs={{12,8},{8,4},{4,0},{13,9},{9,5},{5,1},{14,10},{10,6},{6,2},{15,11}... | collective-permute-start | bytes 1572872 | tf_op jit(solution)/shard_map/ppermute | solution.py:128
  213.4 23.7 %collective-permute-start.15 = (f32[128,1024]{1,0:T(8,128)}, f32[128,1024]{1,0:T(8,128)S(1)}, u32[]{:S(2)}, u32[]{:S(2)}) collective-permute-start(f32[128,1024]{1,0:T(8,128)} %get-tuple-element.160), channel_id=1, source_target_pairs={{0,4},{4,8},{8,12},{1,5},{5,9},{9,13},{2,6},{6,10},{10,14},{3,7},{... | collective-permute-start | bytes 1572872 | tf_op jit(solution)/shard_map/ppermute | solution.py:128
  223.2 16.1 %collective-permute-start.29 = (f32[128,1024]{1,0:T(8,128)}, f32[128,1024]{1,0:T(8,128)S(1)}, u32[]{:S(2)}, u32[]{:S(2)}) collective-permute-start(f32[128,1024]{1,0:T(8,128)} %get-tuple-element.151), channel_id=1, source_target_pairs={{12,8},{8,4},{4,0},{13,9},{9,5},{5,1},{14,10},{10,6},{6,2},{15,11}... | collective-permute-start | bytes 1572872 | tf_op jit(solution)/shard_map/ppermute | solution.py:128
  224.5 18.5 %collective-permute-start.26 = (f32[128,1024]{1,0:T(8,128)}, f32[128,1024]{1,0:T(8,128)S(1)}, u32[]{:S(2)}, u32[]{:S(2)}) collective-permute-start(f32[128,1024]{1,0:T(8,128)} %get-tuple-element.153), channel_id=1, source_target_pairs={{0,4},{4,8},{8,12},{1,5},{5,9},{9,13},{2,6},{6,10},{10,14},{3,7},{... | collective-permute-start | bytes 1572872 | tf_op jit(solution)/shard_map/ppermute | solution.py:128
  (21 other events, 151.9 us)
